TPU v7x, 32 devices: a whole 2x2x4 slice. The times are simulated.
32 devices in a mesh: freq: 2 (over y), col: 4 (over z), row: 2 (over x), help: 2 (over core).
Axes of the slice: x: 2, y: 2, z: 4, core: 2. Of those that a mesh axis runs over, the one named last changes fastest.
Arguments:
- wavefield: bfloat16 [4, 64, 512, 128], P('freq', 'col', ('row', 'help')), parts along dimension 0, may hold values from -6 to 6
- basis_factor: bfloat16 [4, 8, 64, 80, 512], P('freq', 'row', 'col', 'help'), parts along dimension 0, may hold values from -0.0625 to 0.0625
- second_factor: bfloat16 [4, 8, 64, 80, 512], P('freq', 'row', 'col', 'help'), parts along dimension 0, may hold values from -0.1875 to 0.1875
- tile_ranks: int32 [16, 64], P(('freq', 'row'), 'col'), parts along dimension 0, may hold values from 16 to 80
- observed: bfloat16 [4, 8, 512, 128], P('freq', 'row', ('col', 'help')), parts along dimension 0, may hold values from -6 to 6
- amplitude: bfloat16 [16, 512, 128], P(('freq', 'row'), ('col', 'help')), parts along dimension 0, may hold values from 0.29882812 to 3
Outputs:
- residual: bfloat16 [4, 8, 512, 128], P('freq', 'row', ('col', 'help')), parts along dimension 0
- adjoint: bfloat16 [4, 64, 512, 128], P('freq', 'col', ('row', 'help')), parts along dimension 0
There are 2 independent parts, one for each index of `freq`. A program takes and returns all parts, laid end to end along the dimension named above; each array names one. Nothing has to cross between parts.
Inputs may be any that keep to these rules, and one draw needn't show every extreme that they name: `tile_ranks`: entries of a tile's factors at rank terms from its rank on are not part of the kernel.
All inputs are finite; a program needn't handle non-finite values.
Results may differ from a plain program's by a relative error of at most 0.006.
Values may be sent and summed in bfloat16 or wider, within the bound.
No kernel may reach another device: no remote copies, remote signals or barrier semaphores. Data moves between devices by JAX's collectives and lax.ppermute only.
A program may use at most 128 MiB of HBM per device.

v0:
```python
import jax
import jax.numpy as jnp
from jax import lax
from jax.sharding import PartitionSpec as P


def body(wavefield, basis_factor, second_factor, tile_ranks, observed, amplitude):
    half = second_factor.shape[3]
    order = lax.broadcasted_iota(jnp.int32, (1, 1, half), 2) + lax.axis_index("help") * half
    keep = (order < tile_ranks[:, :, None]).astype(jnp.float32)[:, :, :, None]
    piece = lax.all_gather(wavefield, ("row", "help"), axis=2, tiled=True)
    block = second_factor
    swapped = jnp.stack([piece[1], -piece[0]])
    real_part = jnp.einsum("pijkt,pjtn->ijkn", block, piece, preferred_element_type=jnp.float32)
    imag_part = jnp.einsum("pijkt,pjtn->ijkn", block, swapped, preferred_element_type=jnp.float32)
    coef_real = real_part
    coef_imag = imag_part
    coef = (jnp.stack([coef_real, coef_imag]) * keep[None]).astype(jnp.bfloat16)
    flipped = jnp.stack([coef[0], -coef[1]])
    crossed = jnp.stack([coef[1], coef[0]])
    forward_real = jnp.einsum(
        "pijks,pijkn->isn", basis_factor, flipped, preferred_element_type=jnp.float32
    )
    forward_imag = jnp.einsum(
        "pijks,pijkn->isn", basis_factor, crossed, preferred_element_type=jnp.float32
    )
    partial_value = jnp.stack([forward_real, forward_imag])
    stacked = jnp.concatenate([observed, amplitude[None]], 0)
    whole = lax.all_gather(stacked, ("col", "help"), axis=2, tiled=True)
    total = lax.psum(partial_value, ("col", "help"))
    full = (whole[2].astype(jnp.float32)[None] * (total - whole[:2].astype(jnp.float32))).astype(
        jnp.bfloat16
    )
    span = observed.shape[2]
    residual = lax.dynamic_slice_in_dim(full, lax.axis_index(("col", "help")) * span, span, 2)
    block = basis_factor
    swapped = jnp.stack([full[1], -full[0]])
    real_part = jnp.einsum("pijks,pisn->ijkn", block, full, preferred_element_type=jnp.float32)
    imag_part = jnp.einsum("pijks,pisn->ijkn", block, swapped, preferred_element_type=jnp.float32)
    back = (jnp.stack([real_part, imag_part]) * keep[None]).astype(jnp.bfloat16)
    back_flipped = jnp.stack([back[0], -back[1]])
    back_crossed = jnp.stack([back[1], back[0]])
    adjoint_real = jnp.einsum(
        "pijkt,pijkn->jtn", second_factor, back_flipped, preferred_element_type=jnp.float32
    )
    adjoint_imag = jnp.einsum(
        "pijkt,pijkn->jtn", second_factor, back_crossed, preferred_element_type=jnp.float32
    )
    adjoint_terms = jnp.stack([adjoint_real, adjoint_imag])
    adjoint = lax.psum_scatter(
        adjoint_terms, ("row", "help"), scatter_dimension=2, tiled=True
    ).astype(jnp.bfloat16)
    return (residual, adjoint)


def solution(mesh):
    return jax.shard_map(
        body,
        mesh=mesh,
        in_specs=(
            P("freq", "col", ("row", "help"), None),
            P("freq", "row", "col", "help", None),
            P("freq", "row", "col", "help", None),
            P(("freq", "row"), "col"),
            P("freq", "row", ("col", "help"), None),
            P(("freq", "row"), ("col", "help"), None),
        ),
        out_specs=(
            P("freq", "row", ("col", "help"), None),
            P("freq", "col", ("row", "help"), None),
        ),
        check_vma=False,
    )
```

profile of v0, /device:TPU:0, one launch (start us, length us, event | category | flops | bytes accessed | tf_op | source)
XLA Modules:
  0.0 237.8 jit_solution(18379420434144310951)
XLA Ops:
  7.2 0.0 all-gather.5.cloned.1.call-start
  7.2 2.3 copy.33
  9.6 0.0 all-gather.5.cloned.1.call-update
  9.6 0.0 all-gather.3.cloned.1.call-start
  9.7 0.1 copy.132
  9.7 0.1 copy.31
  9.8 0.8 pad_maximum_fusion.4
  10.7 0.0 all-gather.3.cloned.1.call-update
  10.7 0.0 all-reduce.2.cloned.1.call-start
  10.8 0.1 copy.36
  10.9 0.1 compare_convert_fusion
  10.9 36.5 %all-gather.5.cloned.1.call-done = bf16[2,16,512,128]{3,2,0,1:T(8,128)(2,1)} async-done(((bf16[2,16,128,128]{3,2,0,1:T(8,128)(2,1)}), bf16[2,16,512,128]{3,2,0,1:T(8,128)(2,1)}) %all-gather.5.cloned.1.call-update) | async-done | bytes 4194320 | tf_op jit(solution)/shard_map/all_gather | solution.py:11
  47.4 2.8 %fusion.61 = (bf16[1,16,512,128]{3,2,0,1:T(8,128)(2,1)S(1)}, bf16[1,16,512,128]{3,2,0,1:T(8,128)(2,1)S(1)}) fusion(bf16[2,16,512,128]{3,2,0,1:T(8,128)(2,1)} %all-gather.5.cloned.1.call-done), kind=kLoop, calls=%fused_computation.62 | loop fusion | flops 1048576 | bytes 8388608 | tf_op jit(solution)/shard_map/slice | solution.py:13
  50.2 0.0 slice-start.6
  50.2 3.7 %fusion.27 = f32[1,4,16,40,128]{4,3,1,2,0:T(8,128)S(1)} fusion(bf16[2,4,16,40,512]{4,3,2,1,0:T(8,128)(2,1)} %param.8, bf16[1,16,512,128]{3,2,0,1:T(8,128)(2,1)S(1)} %get-tuple-element.7, bf16[1,16,512,128]{3,2,0,1:T(8,128)(2,1)S(1)} %get-tuple-element.6), kind=kOutput, calls=%fused_computation.30 | convolution fusion | flops 679477248 | bytes 10747904 | tf_op jit(solution)/shard_map/pijkt,pjtn->ijkn/dot_general | solution.py:15
  53.9 0.2 copy-done
  54.1 0.2 slice-done.6
  54.3 1.5 fusion.30
  55.9 0.4 fusion.19
  56.3 0.2 slice_negate_fusion.3
  56.5 0.2 pad_maximum_fusion.2
  56.7 1.5 slice-done.1
  58.2 0.4 slice-done.2
  58.6 1.0 fusion.41
  59.5 1.0 fusion.44
  60.5 1.6 pad_maximum_fusion.1
  62.1 0.0 all-reduce.2.cloned.1.call-update
  62.1 0.2 reduce-scatter.2.cloned.1.call-start
  62.4 11.8 %all-gather.3.cloned.1.call-done = bf16[3,4,512,128]{3,1,0,2:T(4,128)(2,1)} async-done(((bf16[3,4,64,128]{3,1,0,2:T(4,128)(2,1)}), bf16[3,4,512,128]{3,1,0,2:T(4,128)(2,1)}) %all-gather.3.cloned.1.call-update) | async-done | bytes 1572880 | tf_op jit(solution)/shard_map/all_gather | solution.py:29
  74.1 1.2 fusion.57
  75.4 0.4 copy.32
  75.8 1.0 copy.90
  76.7 64.3 %all-reduce.2.cloned.1.call-done = f32[2,4,512,128]{2,3,1,0:T(8,128)} async-done(((f32[2,4,512,128]{2,3,1,0:T(8,128)}), f32[2,4,512,128]{2,3,1,0:T(8,128)}) %all-reduce.2.cloned.1.call-update) | async-done | bytes 2097168 | tf_op jit(solution)/shard_map/psum | solution.py:30
  141.0 2.1 multiply_convert_fusion
  143.1 0.1 fusion.62
  143.2 4.2 %fusion.35 = f32[1,4,16,40,128]{4,3,1,2,0:T(8,128)S(1)} fusion(bf16[2,4,16,40,512]{4,3,2,1,0:T(8,128)(2,1)} %param.7, bf16[2,4,512,128]{2,3,1,0:T(8,128)(2,1)S(1)} %multiply_convert_fusion), kind=kOutput, calls=%fused_computation.32 | convolution fusion | flops 671088640 | bytes 7602176 | tf_op jit(solution)/shard_map/pijks,pisn->ijkn/dot_general | solution.py:38
  147.4 1.6 fusion.38
  149.0 0.4 fusion.20
  149.5 0.2 slice_negate_fusion.2
  149.7 1.3 fusion.21
  151.0 1.3 fusion.24
  152.3 4.3 %pad_maximum_fusion = f32[2,16,512,128]{2,3,1,0:T(8,128)} fusion(f32[1,16,512,128]{2,3,1,0:T(8,128)S(1)} %fusion.24, f32[1,16,512,128]{2,3,1,0:T(8,128)S(1)} %fusion.21), kind=kLoop, calls=%fused_computation | loop fusion | flops 2097152 | bytes 16777216 | tf_op jit(solution)/shard_map/stack | solution.py:49
  156.6 0.0 reduce-scatter.2.cloned.1.call-update
  156.6 0.1 constant_dynamic-slice_fusion
  156.8 0.8 copy.52
  157.5 70.6 %reduce-scatter.2.cloned.1.call-done = f32[2,16,128,128]{2,3,1,0:T(8,128)} async-done(((f32[2,16,512,128]{2,3,1,0:T(8,128)}), f32[2,16,128,128]{2,3,1,0:T(8,128)}) %reduce-scatter.2.cloned.1.call-update) | async-done | bytes 2097168 | tf_op jit(solution)/shard_map/reduce_scatter | solution.py:50
  228.1 1.7 convert_element_type.29
  229.9 1.3 copy.53
  (26 shorter events, 0.1 us)
Async XLA Ops:
  7.2 2.5 %copy-start.2 = (bf16[4,64,128]{2,1,0:T(8,128)(2,1)S(1)}, bf16[4,64,128]{2,1,0:T(8,128)(2,1)}, u32[]{:S(2)}) copy-start(bf16[4,64,128]{2,1,0:T(8,128)(2,1)} %param.11) | copy-start | bytes 196612
  7.2 2.6 %copy-start.1 = (bf16[2,4,64,128]{3,2,1,0:T(8,128)(2,1)S(1)}, bf16[2,4,64,128]{3,2,1,0:T(8,128)(2,1)}, u32[]{:S(2)}) copy-start(bf16[2,4,64,128]{3,2,1,0:T(8,128)(2,1)} %param.10) | copy-start | bytes 393220
  7.2 3.6 %copy-start.3 = (s32[4,16]{1,0:T(4,128)S(1)}, s32[4,16]{1,0:T(4,128)}, u32[]{:S(2)}) copy-start(s32[4,16]{1,0:T(4,128)} %param.9) | copy-start | bytes 772
  7.2 40.2 %all-gather.5.cloned.1.call-start = ((), (), s32[]{:S(2)}) async-start(), calls=%async_computation.2 | async-start | bytes 5242880 | tf_op jit(solution)/shard_map/all_gather | solution.py:11
  9.6 64.5 %all-gather.3.cloned.1.call-start = ((), (), s32[]{:S(2)}) async-start(), calls=%async_computation.1 | async-start | bytes 1769472 | tf_op jit(solution)/shard_map/all_gather | solution.py:29
  10.7 130.3 %all-reduce.2.cloned.1.call-start = ((), (), s32[]{:S(2)}) async-start(), calls=%async_computation.3 | async-start | bytes 4194304 | tf_op jit(solution)/shard_map/psum | solution.py:30
  47.4 6.5 %slice-start.5 = ((s8[5242880]{0:T(1024)(128)(4,1)}), s8[4194304]{0:T(1024)(128)(4,1)S(1)}, s32[]{:S(2)}) async-start(s8[5242880]{0:T(1024)(128)(4,1)} %bitcast.93), calls=%async_computation.10 | async-start | bytes 8388608
  50.2 3.9 %copy-start = (bf16[2,16,512,128]{3,2,0,1:T(8,128)(2,1)S(1)}, bf16[2,16,512,128]{3,2,0,1:T(8,128)(2,1)}, u32[]{:S(2)}) copy-start(bf16[2,16,512,128]{3,2,0,1:T(8,128)(2,1)} %all-gather.5.cloned.1.call-done) | copy-start | bytes 12582916
  50.2 4.1 %slice-start.6 = ((s8[5242880]{0:T(1024)(128)(4,1)}), s8[1048576]{0:T(1024)(128)(4,1)S(1)}, s32[]{:S(2)}) async-start(s8[5242880]{0:T(1024)(128)(4,1)} %bitcast.93), calls=%async_computation.11 | async-start | bytes 2097152
  55.9 2.3 slice-start.1
  56.3 2.3 slice-start.2
  62.1 166.0 %reduce-scatter.2.cloned.1.call-start = ((), (), s32[]{:S(2)}) async-start(), calls=%async_computation.4 | async-start | bytes 10485760 | tf_op jit(solution)/shard_map/reduce_scatter | solution.py:50
  74.1 1.6 slice-start
  143.1 4.3 %slice-start.3 = ((s8[5242880]{0:T(1024)(128)(4,1)}), s8[4194304]{0:T(1024)(128)(4,1)S(1)}, s32[]{:S(2)}) async-start(s8[5242880]{0:T(1024)(128)(4,1)} %bitcast.91), calls=%async_computation.8 | async-start | bytes 8388608
  143.2 4.2 %slice-start.4 = ((s8[5242880]{0:T(1024)(128)(4,1)}), s8[1048576]{0:T(1024)(128)(4,1)S(1)}, s32[]{:S(2)}) async-start(s8[5242880]{0:T(1024)(128)(4,1)} %bitcast.91), calls=%async_computation.9 | async-start | bytes 2097152
  143.2 6.5 %slice-start.7 = ((s8[5242880]{0:T(1024)(128)(4,1)}), s8[4194304]{0:T(1024)(128)(4,1)S(1)}, s32[]{:S(2)}) async-start(s8[5242880]{0:T(1024)(128)(4,1)} %bitcast.95), calls=%async_computation.12 | async-start | bytes 8388608
  147.4 2.2 slice-start.8
Sparse Core Ops, SparseCore 0:
  10.2 37.1 all-gather.4
  49.0 25.0 all-gather.2
  76.5 64.4 all-reduce.1
  156.7 71.3 reduce-scatter.1
where the time goes:
time: 238 us
  waiting for transfers between devices  183 us (77%)
  other arithmetic  16.1 us (7%)
  matrix products  15.5 us (7%)
  between operations  14.1 us (6%)
  local copies, waits for them, and re-layouts  8.49 us (4%)
    reduce_scatter x1, waiting for transfers between devices, body(): lax.psum_scatter(adjoint_terms, ('row', 'help'), scatter_dimension=2, til...  70.6 us
    psum x1, waiting for transfers between devices, body(): total = lax.psum(partial_value, ('col', 'help'))  64.3 us
    all_gather x1, waiting for transfers between devices, body(): piece = lax.all_gather(wavefield, ('row', 'help'), axis=2, tiled=True)  36.5 us
    all_gather x1, waiting for transfers between devices, body(): whole = lax.all_gather(stacked, ('col', 'help'), axis=2, tiled=True)  11.8 us
    unnamed x31, local copies, waits for them, and re-layouts  7.98 us
  transfers between devices with their start and end apart: 4, of which 4 were waited for; matrix products, arithmetic and copies ran while one was open for 7% of the time, Pallas kernels for 0%

commit v1 on v0

v1 whole, which is shorter than its diff:
```python
import functools

import jax
import jax.numpy as jnp
from jax import lax
from jax.experimental import pallas as pl
from jax.experimental.pallas import tpu as pltpu
from jax.sharding import PartitionSpec as P

BF16 = jnp.bfloat16
F32 = jnp.float32
CHUNKS = 2
STEP_TILES = 4


def swap(axis_name, step, value):
    size = lax.axis_size(axis_name)
    return lax.ppermute(value, axis_name, [(i, i ^ step) for i in range(size)])


def gather_pieces(value, axis_name):
    size = lax.axis_size(axis_name)
    return [value] + [swap(axis_name, step, value) for step in range(1, size)]


def turn(value, first, second):
    width = value.shape[-1]
    lane = lax.broadcasted_iota(jnp.int32, value.shape, value.ndim - 1)
    sign = jnp.where(lane < width // 2, first, second).astype(F32)
    return pltpu.roll(value, width // 2, value.ndim - 1) * sign


def forward_kernel(dims, scalars, *refs):
    tiles, rows, terms, rest, zs, helps, n_pieces, steps, peers = dims
    pieces = refs[:n_pieces]
    second, basis, keep_out, send_out, waves, coef, both = refs[n_pieces:]
    step = pl.program_id(0)
    here = scalars[0]
    quarter = pieces[0].shape[1]
    width = pieces[0].shape[2]

    @pl.when(step < steps)
    def _():
        row_index = lax.broadcasted_iota(jnp.int32, (terms, width), 0)
        for jj in range(tiles):
            for n, piece in enumerate(pieces):
                at = pl.multiple_of(scalars[1 + n] * quarter, quarter)
                waves[jj, pl.ds(at, quarter), :] = piece[jj]
            out = jnp.dot(second[jj], waves[jj], preferred_element_type=F32)
            half = rows * terms
            value = out[:half] + turn(out[half:], 1.0, -1.0)
            j = step * tiles + jj
            at = pl.multiple_of(j * terms, 8)
            for i in range(rows):
                left = scalars[rest + i * steps * tiles + j] - here * terms
                part = value[i * terms : (i + 1) * terms]
                coef[i, pl.ds(at, terms), :] = jnp.where(row_index < left, part, 0.0)

    @pl.when(step >= steps)
    def _():
        i = step - steps
        depth = coef.shape[1]
        value = coef[i]
        both[:depth, :] = value.astype(BF16)
        both[depth:, :] = turn(value, -1.0, 1.0).astype(BF16)
        span = keep_out.shape[2]
        for out_ref, h in ((keep_out, here), (send_out, 1 - here)):
            left = jnp.concatenate(
                [
                    basis[0, pl.ds(pl.multiple_of((scalars[peers + z] * helps + h) * span, span), span), :]
                    for z in range(zs)
                ],
                axis=0,
            )
            out = jnp.dot(left, both[...], preferred_element_type=F32)
            for z in range(zs):
                out_ref[z, 0] = out[z * span : (z + 1) * span].astype(out_ref.dtype)


def adjoint_kernel(dims, scalars, *refs):
    tiles, rows, terms, rest, rs, helps, n_pieces, steps, peers, places = dims
    pieces = refs[:n_pieces]
    basis, second, keep_out, send_out, resid, back, both = refs[n_pieces:]
    step = pl.program_id(0)
    here = scalars[0]
    span = pieces[0].shape[1]
    width = pieces[0].shape[2]
    columns = back.shape[0]

    @pl.when(step < rows)
    def _():
        for n, piece in enumerate(pieces):
            at = pl.multiple_of(scalars[places + n] * span, span)
            resid[pl.ds(at, span), :] = piece[0]
        value = resid[...]
        turned = turn(value.astype(F32), 1.0, -1.0).astype(BF16)
        out = jnp.dot(basis[0, 0], value, preferred_element_type=F32)
        out = out + jnp.dot(basis[1, 0], turned, preferred_element_type=F32)
        row_index = lax.broadcasted_iota(jnp.int32, (terms, width), 0)
        at = pl.multiple_of(step * terms, 8)
        for j in range(columns):
            left = scalars[rest + step * columns + j] - here * terms
            part = out[j * terms : (j + 1) * terms]
            back[j, pl.ds(at, terms), :] = jnp.where(row_index < left, part, 0.0)

    @pl.when(step >= rows)
    def _():
        depth = back.shape[1]
        quarter = keep_out.shape[2]
        for jj in range(tiles):
            value = back[(step - rows) * tiles + jj]
            both[jj, :depth, :] = value.astype(BF16)
            both[jj, depth:, :] = turn(value, -1.0, 1.0).astype(BF16)
            for out_ref, h in ((keep_out, here), (send_out, 1 - here)):
                left = jnp.concatenate(
                    [
                        second[
                            jj,
                            pl.ds(pl.multiple_of((scalars[peers + r] * helps + h) * quarter, quarter), quarter),
                            :,
                        ]
                        for r in range(rs)
                    ],
                    axis=0,
                )
                out = jnp.dot(left, both[jj], preferred_element_type=F32)
                for r in range(rs):
                    out_ref[r, jj] = out[r * quarter : (r + 1) * quarter].astype(out_ref.dtype)


def body(wavefield, basis_factor, second_factor, tile_ranks, observed, amplitude):
    _, columns, quarter, rhs = wavefield.shape
    _, rows, _, terms, tile = basis_factor.shape
    span = observed.shape[2]
    zs, rs, helps = lax.axis_size("col"), lax.axis_size("row"), lax.axis_size("help")
    z, r, h = lax.axis_index("col"), lax.axis_index("row"), lax.axis_index("help")
    part = rhs // CHUNKS
    width = 2 * part
    tiles = STEP_TILES
    steps = columns // tiles

    z_peers = [z ^ d for d in range(zs)]
    r_peers = [r ^ d for d in range(rs)]
    wave_places = [p * helps + (h ^ d) for d in range(helps) for p in r_peers]
    resid_places = [p * helps + (h ^ d) for d in range(helps) for p in z_peers]
    head = [h] + wave_places + z_peers + resid_places + r_peers
    z_at = 1 + len(wave_places)
    resid_at = z_at + zs
    r_at = resid_at + len(resid_places)
    rest = len(head)
    scalars = jnp.concatenate([jnp.stack(head).astype(jnp.int32), tile_ranks.reshape(-1)])

    def split(value, c):
        return jnp.concatenate(
            [value[0, ..., c * part : (c + 1) * part], value[1, ..., c * part : (c + 1) * part]], -1
        )

    second_rows = second_factor.transpose(2, 0, 1, 3, 4).reshape(columns, 2 * rows * terms, tile)
    second_cols = second_factor.transpose(2, 4, 0, 1, 3).reshape(columns, tile, 2 * rows * terms)
    basis_rows = basis_factor.reshape(2, rows, columns * terms, tile)
    basis_cols = basis_factor.transpose(1, 4, 0, 2, 3).reshape(rows, tile, 2 * columns * terms)

    def run_forward(pieces):
        n = len(pieces)
        dims = (tiles, rows, terms, rest, zs, helps, n, steps, z_at)
        out_block = pl.BlockSpec((zs, 1, span, width), lambda g, s: (0, jnp.maximum(g - steps, 0), 0, 0))
        return pl.pallas_call(
            functools.partial(forward_kernel, dims),
            out_shape=(
                jax.ShapeDtypeStruct((zs, rows, span, width), F32),
                jax.ShapeDtypeStruct((zs, rows, span, width), BF16),
            ),
            grid_spec=pltpu.PrefetchScalarGridSpec(
                num_scalar_prefetch=1,
                grid=(steps + rows,),
                in_specs=[
                    pl.BlockSpec((tiles, quarter, width), lambda g, s: (jnp.minimum(g, steps - 1), 0, 0))
                    for _ in range(n)
                ]
                + [
                    pl.BlockSpec(
                        (tiles, 2 * rows * terms, tile), lambda g, s: (jnp.minimum(g, steps - 1), 0, 0)
                    ),
                    pl.BlockSpec(
                        (1, tile, 2 * columns * terms), lambda g, s: (jnp.maximum(g - steps, 0), 0, 0)
                    ),
                ],
                out_specs=(out_block, out_block),
                scratch_shapes=[
                    pltpu.VMEM((tiles, tile, width), BF16),
                    pltpu.VMEM((rows, columns * terms, width), F32),
                    pltpu.VMEM((2 * columns * terms, width), BF16),
                ],
            ),
            compiler_params=pltpu.CompilerParams(vmem_limit_bytes=40 * 1024 * 1024),
            cost_estimate=pl.CostEstimate(
                flops=8 * 2 * rows * columns * terms * tile * width // 2,
                bytes_accessed=8 * rows * columns * terms * tile,
                transcendentals=0,
            ),
            name="forward_product",
        )(scalars, *pieces, second_rows, basis_cols)

    def run_adjoint(pieces):
        n = len(pieces)
        dims = (tiles, rows, terms, rest, rs, helps, n, rows, r_at, resid_at)
        out_block = pl.BlockSpec((rs, tiles, quarter, width), lambda g, s: (0, jnp.maximum(g - rows, 0), 0, 0))
        return pl.pallas_call(
            functools.partial(adjoint_kernel, dims),
            out_shape=(
                jax.ShapeDtypeStruct((rs, columns, quarter, width), F32),
                jax.ShapeDtypeStruct((rs, columns, quarter, width), BF16),
            ),
            grid_spec=pltpu.PrefetchScalarGridSpec(
                num_scalar_prefetch=1,
                grid=(rows + steps,),
                in_specs=[
                    pl.BlockSpec((1, span, width), lambda g, s: (jnp.minimum(g, rows - 1), 0, 0))
                    for _ in range(n)
                ]
                + [
                    pl.BlockSpec(
                        (2, 1, columns * terms, tile), lambda g, s: (0, jnp.minimum(g, rows - 1), 0, 0)
                    ),
                    pl.BlockSpec(
                        (tiles, tile, 2 * rows * terms), lambda g, s: (jnp.maximum(g - rows, 0), 0, 0)
                    ),
                ],
                out_specs=(out_block, out_block),
                scratch_shapes=[
                    pltpu.VMEM((tile, width), BF16),
                    pltpu.VMEM((columns, rows * terms, width), F32),
                    pltpu.VMEM((tiles, 2 * rows * terms, width), BF16),
                ],
            ),
            compiler_params=pltpu.CompilerParams(vmem_limit_bytes=40 * 1024 * 1024),
            cost_estimate=pl.CostEstimate(
                flops=8 * 2 * rows * columns * terms * tile * width // 2,
                bytes_accessed=8 * rows * columns * terms * tile,
                transcendentals=0,
            ),
            name="adjoint_product",
        )(scalars, *pieces, basis_rows, second_cols)

    waves = [split(wavefield, c) for c in range(CHUNKS)]
    gathered = [gather_pieces(w, "row") for w in waves]
    residuals, adjoints = [], []
    for c in range(CHUNKS):
        mine = gathered[c]
        pieces = mine + [swap("help", d, m) for d in range(1, helps) for m in mine]
        keep, send = run_forward(pieces)
        summed = keep + swap("help", 1, send).astype(F32)
        total = summed[0]
        for d in range(1, zs):
            total = total + swap("col", d, summed[d].astype(BF16)).astype(F32)
        weight = amplitude[..., c * part : (c + 1) * part].astype(F32)
        weight = jnp.concatenate([weight, weight], -1)
        resid = (weight * (total - split(observed, c).astype(F32))).astype(BF16)
        residuals.append(resid)
        mine = gather_pieces(resid, "col")
        pieces = mine + [swap("help", d, m) for d in range(1, helps) for m in mine]
        keep, send = run_adjoint(pieces)
        summed = keep + swap("help", 1, send).astype(F32)
        total = summed[0]
        for d in range(1, rs):
            total = total + swap("row", d, summed[d].astype(BF16)).astype(F32)
        adjoints.append(total.astype(BF16))

    def join(values):
        return jnp.stack(
            [
                jnp.concatenate([v[..., p * part : (p + 1) * part] for v in values], -1)
                for p in range(2)
            ]
        )

    return join(residuals), join(adjoints)


def solution(mesh):
    return jax.shard_map(
        body,
        mesh=mesh,
        in_specs=(
            P("freq", "col", ("row", "help"), None),
            P("freq", "row", "col", "help", None),
            P("freq", "row", "col", "help", None),
            P(("freq", "row"), "col"),
            P("freq", "row", ("col", "help"), None),
            P(("freq", "row"), ("col", "help"), None),
        ),
        out_specs=(
            P("freq", "row", ("col", "help"), None),
            P("freq", "col", ("row", "help"), None),
        ),
        check_vma=False,
    )
```

time: 238 us -> 166 us (0.70)
  waiting for transfers between devices: 183 us -> 54.5 us
  local copies, waits for them, and re-layouts: 8.49 us -> 45.9 us
  Pallas kernels: 0 us -> 32.5 us
  starting transfers between devices: 0.34 us -> 26.5 us
  matrix products: 15.5 us -> 0 us
  between operations: 14.1 us -> 1.01 us
  other arithmetic: 16.1 us -> 4.23 us
    reduce_scatter x1 -> x0, waiting for transfers between devices: 70.6 us -> none  [body(): lax.psum_scatter(adjoint_terms, ('row', 'help'), scatter_dimension=2, til...]
    psum x1 -> x0, waiting for transfers between devices: 64.3 us -> none  [body(): total = lax.psum(partial_value, ('col', 'help'))]
    ppermute x0 -> x32, waiting for transfers between devices: none -> 54.5 us  [swap(): return lax.ppermute(value, axis_name, [(i, i ^ step) for i in range(size)])]
    all_gather x2 -> x0, waiting for transfers between devices: 48.2 us -> none  [the longest x1 36.5 us: body(): piece = lax.all_gather(wavefield, ('row', 'help'), axis=2, tiled=True)]
    pallas_call x0 -> x4, Pallas kernels: none -> 32.5 us  [the longest x2 18.1 us: run_adjoint(): pl.pallas_call(functools.partial(adjoint_kernel, dims), out_shape=(jax.Sh...]
    ppermute x0 -> x32, starting transfers between devices: none -> 26.5 us  [swap(): return lax.ppermute(value, axis_name, [(i, i ^ step) for i in range(size)])]
    reshape x0 -> x3, local copies, waits for them, and re-layouts: none -> 16.2 us  [the longest x1 8.11 us: body(): second_factor.transpose(2, 4, 0, 1, 3)]
    dot_general x8 -> x0, matrix products: 15.5 us -> none  [the longest x1 4.18 us: body(): jnp.einsum('pijks,pisn->ijkn', block, full, preferred_element_type=jnp.fl...]
  transfers between devices with their start and end apart: 4 -> 32, of which waited for: 4 -> 10; matrix products, arithmetic and copies ran while one was open for 7% -> 20% of each run, Pallas kernels for 0% -> 20%
where the time goes in v1:
time: 166 us; the launch traced here: 165 us
  waiting for transfers between devices  54.5 us (33%)
  local copies, waits for them, and re-layouts  45.9 us (28%)
  Pallas kernels  32.5 us (20%)
  starting transfers between devices  26.5 us (16%)
  other arithmetic  4.23 us (3%)
    ppermute x32, waiting for transfers between devices, swap(): return lax.ppermute(value, axis_name, [(i, i ^ step) for i in range(size)])  54.5 us
    ppermute x32, starting transfers between devices, swap(): return lax.ppermute(value, axis_name, [(i, i ^ step) for i in range(size)])  26.5 us
    unnamed x26, local copies, waits for them, and re-layouts  20.8 us
    pallas_call x2, Pallas kernels, run_adjoint(): pl.pallas_call(functools.partial(adjoint_kernel, dims), out_shape=(jax.Sh...  18.1 us
    pallas_call x2, Pallas kernels, run_forward(): pl.pallas_call(functools.partial(forward_kernel, dims), out_shape=(jax.Sh...  14.3 us
    reshape x1, local copies, waits for them, and re-layouts, body(): second_factor.transpose(2, 4, 0, 1, 3)  8.11 us
    reshape x1, local copies, waits for them, and re-layouts, body(): basis_factor.transpose(1, 4, 0, 2, 3)  8 us
    transpose x1, local copies, waits for them, and re-layouts, body(): second_factor.transpose(2, 0, 1, 3, 4)  5.71 us
  transfers between devices with their start and end apart: 32, of which 10 were waited for; matrix products, arithmetic and copies ran while one was open for 20% of the time, Pallas kernels for 20%

profile of v1, /device:TPU:0, one launch (start us, length us, event | category | flops | bytes accessed | tf_op | source)
XLA Modules:
  0.0 164.6 jit_solution(8636561543613117920)
XLA Ops:
  0.6 2.0 %slice_bitcast_fusion.5 = (bf16[16,128,64]{2,1,0:T(8,128)(2,1)S(1)}, bf16[16,128,64]{2,1,0:T(8,128)(2,1)S(1)}, bf16[16,128,64]{2,1,0:T(8,128)(2,1)S(1)}, bf16[16,128,64]{2,1,0:T(8,128)(2,1)S(1)}) fusion(bf16[2,16,128,128]{3,2,1,0:T(8,128)(2,1)} %param.6), kind=kLoop, calls=%fused_computation.22 | loop fusion | bytes 2097152 | tf_op jit(solution)/shard_map/squeeze | solution.py:155
  2.7 0.3 pad_maximum_fusion.2.refs_0_
  3.0 3.0 %collective-permute-start.7 = (bf16[16,128,128]{2,1,0:T(8,128)(2,1)S(1)}, bf16[16,128,128]{2,1,0:T(8,128)(2,1)S(1)}, u32[]{:S(2)}, u32[]{:S(2)}) collective-permute-start(bf16[16,128,128]{2,1,0:T(8,128)(2,1)S(1)} %pad_maximum_fusion.2.refs_0_), channel_id=1, source_target_pairs={{0,2},{2,0},{1,3},{3,1},{4,6},{6,4},{5,7},{7,5},{8,10},{10,8},{9,1... | collective-permute-start | bytes 1572872 | tf_op jit(solution)/shard_map/ppermute | solution.py:18
  6.0 0.3 pad_maximum_fusion.1.refs_0_
  6.4 12.3 %collective-permute-done.7.refs_1_ = bf16[16,128,128]{2,1,0:T(8,128)(2,1)S(1)} collective-permute-done((bf16[16,128,128]{2,1,0:T(8,128)(2,1)S(1)}, bf16[16,128,128]{2,1,0:T(8,128)(2,1)S(1)}, u32[]{:S(2)}, u32[]{:S(2)}) %collective-permute-start.7) | collective-permute-done | bytes 524320 | tf_op jit(solution)/shard_map/ppermute | solution.py:18
  18.7 0.5 collective-permute-start.1
  19.2 9.9 %collective-permute-done.refs_1_ = bf16[16,128,128]{2,1,0:T(8,128)(2,1)S(1)} collective-permute-done((bf16[16,128,128]{2,1,0:T(8,128)(2,1)S(1)}, bf16[16,128,128]{2,1,0:T(8,128)(2,1)S(1)}, u32[]{:S(2)}, u32[]{:S(2)}) %collective-permute-start) | collective-permute-done | bytes 524320 | tf_op jit(solution)/shard_map/ppermute | solution.py:18
  29.2 5.7 %copy.11 = bf16[16,2,4,40,512]{4,3,2,1,0:T(8,128)(2,1)} copy(bf16[16,2,4,40,512]{4,3,0,2,1:T(8,128)(2,1)} %bitcast.116) | data formatting | bytes 10485760 | tf_op jit(solution)/shard_map/transpose | solution.py:158
  34.9 2.8 %copy.12 = bf16[2,4,16,40,512]{4,3,2,0,1:T(8,128)(2,1)} copy(bf16[2,4,16,40,512]{4,3,2,1,0:T(8,128)(2,1)S(1)} %bitcast.113) | data formatting | bytes 10485760 | tf_op args[1]
  37.8 8.0 %copy.13.refs_5_ = bf16[4,512,1280]{2,1,0:T(8,128)(2,1)} copy(bf16[4,512,1280]{1,2,0:T(8,128)(2,1)} %bitcast.117) | data formatting | bytes 10485760 | tf_op jit(solution)/shard_map/reshape | solution.py:161
  45.9 2.5 %copy-done = bf16[16,2,4,40,512]{4,3,2,1,0:T(8,128)(2,1)S(1)} copy-done((bf16[16,2,4,40,512]{4,3,2,1,0:T(8,128)(2,1)S(1)}, bf16[16,2,4,40,512]{4,3,2,1,0:T(8,128)(2,1)}, u32[]{:S(2)}) %copy-start) | copy-done | bytes 5242904
  48.4 2.5 %copy-done.1 = bf16[4,512,1280]{2,1,0:T(8,128)(2,1)S(1)} copy-done((bf16[4,512,1280]{2,1,0:T(8,128)(2,1)S(1)}, bf16[4,512,1280]{2,1,0:T(8,128)(2,1)}, u32[]{:S(2)}) %copy-start.1) | copy-done | bytes 5242904
  50.9 7.3 %forward_product.3 = (f32[4,4,64,128]{3,2,1,0:T(8,128)S(1)}, bf16[4,4,64,128]{3,2,1,0:T(8,128)(2,1)S(1)}) custom-call(s32[83]{0:T(128)S(1)} %concatenate.41.scalars, bf16[16,128,128]{2,1,0:T(8,128)(2,1)S(1)} %pad_maximum_fusion.2.refs_0_, bf16[16,128,128]{2,1,0:T(8,128)(2,1)S(1)} %collective-permute-done.7.refs_1_, ...), custom_call_target="tpu_custom_call" | custom-call | flops 1342177280 | bytes 10485760 | tf_op jit(solution)/shard_map/forward_product/pallas_call | solution.py:167
  58.2 0.6 collective-permute-start.10
  58.9 2.5 %copy-done.2 = bf16[4,512,1280]{2,1,0:T(8,128)(2,1)S(1)} copy-done((bf16[4,512,1280]{2,1,0:T(8,128)(2,1)S(1)}, bf16[4,512,1280]{2,1,0:T(8,128)(2,1)}, u32[]{:S(2)}) %copy-start.2) | copy-done | bytes 5242904
  61.4 7.0 %forward_product.2 = (f32[4,4,64,128]{3,2,1,0:T(8,128)S(1)}, bf16[4,4,64,128]{3,2,1,0:T(8,128)(2,1)S(1)}) custom-call(s32[83]{0:T(128)S(1)} %concatenate.41.scalars, bf16[16,128,128]{2,1,0:T(8,128)(2,1)S(1)} %pad_maximum_fusion.1.refs_0_, bf16[16,128,128]{2,1,0:T(8,128)(2,1)S(1)} %collective-permute-done.refs_1_, ...), custom_call_target="tpu_custom_call" | custom-call | flops 1342177280 | bytes 10485760 | tf_op jit(solution)/shard_map/forward_product/pallas_call | solution.py:167
  68.7 3.9 %collective-permute-start.13 = (bf16[4,64,128]{2,1,0:T(8,128)(2,1)S(1)}, bf16[4,64,128]{2,1,0:T(8,128)(2,1)S(1)}, u32[]{:S(2)}, u32[]{:S(2)}) collective-permute-start(bf16[4,64,128]{2,1,0:T(8,128)(2,1)S(1)} %get-tuple-element.34), channel_id=1, source_target_pairs={{0,12},{4,8},{8,4},{12,0},{1,13},{5,9},{9,5},{13,1},{2,14},{6,10},... | collective-permute-start | bytes 196616 | tf_op jit(solution)/shard_map/ppermute | solution.py:18
  72.6 0.6 collective-permute-start.11
  73.3 5.5 %copy.15 = bf16[2,4,16,40,512]{4,3,1,0,2:T(8,128)(2,1)} copy(bf16[2,4,16,40,512]{4,3,2,1,0:T(8,128)(2,1)} %param.8) | data formatting | bytes 10485760 | tf_op args[2]
  78.8 8.1 %copy.16.refs_9_ = bf16[16,512,320]{2,1,0:T(8,128)(2,1)} copy(bf16[16,512,320]{1,2,0:T(8,128)(2,1)} %bitcast.118) | data formatting | bytes 10485760 | tf_op jit(solution)/shard_map/reshape | solution.py:159
  87.1 1.5 collective-permute-start.23
  88.5 2.9 %collective-permute-start.24 = (bf16[4,64,128]{2,1,0:T(8,128)(2,1)S(1)}, bf16[4,64,128]{2,1,0:T(8,128)(2,1)S(1)}, u32[]{:S(2)}, u32[]{:S(2)}) collective-permute-start(bf16[4,64,128]{2,1,0:T(8,128)(2,1)S(1)} %fusion.11.refs_0_), channel_id=1, source_target_pairs={{0,8},{4,12},{8,0},{12,4},{1,9},{5,13},{9,1},{13,5},{2,10},{6,14},... | collective-permute-start | bytes 196616 | tf_op jit(solution)/shard_map/ppermute | solution.py:18
  91.7 0.5 collective-permute-start.27
  92.2 3.7 %collective-permute-done.24.refs_2_ = bf16[4,64,128]{2,1,0:T(8,128)(2,1)S(1)} collective-permute-done((bf16[4,64,128]{2,1,0:T(8,128)(2,1)S(1)}, bf16[4,64,128]{2,1,0:T(8,128)(2,1)S(1)}, u32[]{:S(2)}, u32[]{:S(2)}) %collective-permute-start.24) | collective-permute-done | bytes 65568 | tf_op jit(solution)/shard_map/ppermute | solution.py:18
  95.9 1.6 collective-permute-done.25.refs_3_
  97.5 2.1 %collective-permute-start.6 = (bf16[4,64,128]{2,1,0:T(8,128)(2,1)S(1)}, bf16[4,64,128]{2,1,0:T(8,128)(2,1)S(1)}, u32[]{:S(2)}, u32[]{:S(2)}) collective-permute-start(bf16[4,64,128]{2,1,0:T(8,128)(2,1)S(1)} %get-tuple-element.31), channel_id=1, source_target_pairs={{0,12},{4,8},{8,4},{12,0},{1,13},{5,9},{9,5},{13,1},{2,14},{6,10},... | collective-permute-start | bytes 196616 | tf_op jit(solution)/shard_map/ppermute | solution.py:18
  99.6 2.4 %collective-permute-start.4 = (bf16[4,64,128]{2,1,0:T(8,128)(2,1)S(1)}, bf16[4,64,128]{2,1,0:T(8,128)(2,1)S(1)}, u32[]{:S(2)}, u32[]{:S(2)}) collective-permute-start(bf16[4,64,128]{2,1,0:T(8,128)(2,1)S(1)} %get-tuple-element.30), channel_id=1, source_target_pairs={{0,4},{4,0},{8,12},{12,8},{1,5},{5,1},{9,13},{13,9},{2,6},{6,2},{1... | collective-permute-start | bytes 196616 | tf_op jit(solution)/shard_map/ppermute | solution.py:18
  102.0 2.5 %copy-done.3 = bf16[2,4,16,40,512]{4,3,2,1,0:T(8,128)(2,1)S(1)} copy-done((bf16[2,4,16,40,512]{4,3,2,1,0:T(8,128)(2,1)S(1)}, bf16[2,4,16,40,512]{4,3,2,1,0:T(8,128)(2,1)}, u32[]{:S(2)}) %copy-start.3) | copy-done | bytes 5242904
  104.5 9.1 %adjoint_product.3 = (f32[2,16,128,128]{3,2,1,0:T(8,128)S(1)}, bf16[2,16,128,128]{3,2,1,0:T(8,128)(2,1)S(1)}) custom-call(s32[83]{0:T(128)S(1)} %concatenate.41.scalars, bf16[4,64,128]{2,1,0:T(8,128)(2,1)S(1)} %fusion.11.refs_0_, bf16[4,64,128]{2,1,0:T(8,128)(2,1)S(1)} %collective-permute-done.23.refs_1_, ...), custom_call_target="tpu_custom_call" | custom-call | flops 1342177280 | bytes 10485760 | tf_op jit(solution)/shard_map/adjoint_product/pallas_call | solution.py:208
  113.9 2.6 %collective-permute-start.15 = (bf16[4,64,128]{2,1,0:T(8,128)(2,1)S(1)}, bf16[4,64,128]{2,1,0:T(8,128)(2,1)S(1)}, u32[]{:S(2)}, u32[]{:S(2)}) collective-permute-start(bf16[4,64,128]{2,1,0:T(8,128)(2,1)S(1)} %fusion.17.refs_0_), channel_id=1, source_target_pairs={{0,8},{4,12},{8,0},{12,4},{1,9},{5,13},{9,1},{13,5},{2,10},{6,14},... | collective-permute-start | bytes 196616 | tf_op jit(solution)/shard_map/ppermute | solution.py:18
  116.4 1.8 %collective-permute-start.16 = (bf16[4,64,128]{2,1,0:T(8,128)(2,1)S(1)}, bf16[4,64,128]{2,1,0:T(8,128)(2,1)S(1)}, u32[]{:S(2)}, u32[]{:S(2)}) collective-permute-start(bf16[4,64,128]{2,1,0:T(8,128)(2,1)S(1)} %fusion.17.refs_0_), channel_id=1, source_target_pairs={{0,12},{4,8},{8,4},{12,0},{1,13},{5,9},{9,5},{13,1},{2,14},{6,10},... | collective-permute-start | bytes 196616 | tf_op jit(solution)/shard_map/ppermute | solution.py:18
  118.2 1.2 collective-permute-done.14.refs_1_
  119.4 3.2 %collective-permute-done.15.refs_2_ = bf16[4,64,128]{2,1,0:T(8,128)(2,1)S(1)} collective-permute-done((bf16[4,64,128]{2,1,0:T(8,128)(2,1)S(1)}, bf16[4,64,128]{2,1,0:T(8,128)(2,1)S(1)}, u32[]{:S(2)}, u32[]{:S(2)}) %collective-permute-start.15) | collective-permute-done | bytes 65568 | tf_op jit(solution)/shard_map/ppermute | solution.py:18
  122.6 0.5 collective-permute-start.20
  123.2 0.6 collective-permute-done.19.refs_6_
  124.0 2.5 %copy-done.4 = bf16[2,4,16,40,512]{4,3,2,1,0:T(8,128)(2,1)S(1)} copy-done((bf16[2,4,16,40,512]{4,3,2,1,0:T(8,128)(2,1)S(1)}, bf16[2,4,16,40,512]{4,3,2,1,0:T(8,128)(2,1)}, u32[]{:S(2)}) %copy-start.4) | copy-done | bytes 5242904
  126.5 9.1 %adjoint_product.2 = (f32[2,16,128,128]{3,2,1,0:T(8,128)S(1)}, bf16[2,16,128,128]{3,2,1,0:T(8,128)(2,1)S(1)}) custom-call(s32[83]{0:T(128)S(1)} %concatenate.41.scalars, bf16[4,64,128]{2,1,0:T(8,128)(2,1)S(1)} %fusion.17.refs_0_, bf16[4,64,128]{2,1,0:T(8,128)(2,1)S(1)} %collective-permute-done.14.refs_1_, ...), custom_call_target="tpu_custom_call" | custom-call | flops 1342177280 | bytes 10485760 | tf_op jit(solution)/shard_map/adjoint_product/pallas_call | solution.py:208
  135.6 0.4 collective-permute-start.21
  136.2 0.7 pad_maximum_fusion.3
  136.9 0.3 convert_add_fusion
  137.2 1.6 collective-permute-start.31
  138.8 0.3 convert_add_fusion.1
  139.2 1.1 collective-permute-start.22
  140.3 11.8 %collective-permute-done.31 = bf16[16,128,128]{2,1,0:T(8,128)(2,1)S(1)} collective-permute-done((bf16[16,128,128]{2,1,0:T(8,128)(2,1)S(1)}, bf16[16,128,128]{2,1,0:T(8,128)(2,1)S(1)}, u32[]{:S(2)}, u32[]{:S(2)}) %collective-permute-start.31) | collective-permute-done | bytes 524320 | tf_op jit(solution)/shard_map/ppermute | solution.py:18
  152.2 0.2 fusion.21
  152.4 10.1 %collective-permute-done.22 = bf16[16,128,128]{2,1,0:T(8,128)(2,1)S(1)} collective-permute-done((bf16[16,128,128]{2,1,0:T(8,128)(2,1)S(1)}, bf16[16,128,128]{2,1,0:T(8,128)(2,1)S(1)}, u32[]{:S(2)}, u32[]{:S(2)}) %collective-permute-start.22) | collective-permute-done | bytes 524320 | tf_op jit(solution)/shard_map/ppermute | solution.py:18
  162.9 0.6 maximum_bitcast_fusion
  163.5 1.1 pad_maximum_fusion
  (78 shorter events, 2.6 us)
Async XLA Ops:
  2.6 26.5 %copy-start.7 = (s32[4,16]{1,0:T(4,128)S(1)}, s32[4,16]{1,0:T(4,128)}, u32[]{:S(2)}) copy-start(s32[4,16]{1,0:T(4,128)} %param.9) | copy-start | bytes 772
  3.0 15.8 %collective-permute-start.7 = (bf16[16,128,128]{2,1,0:T(8,128)(2,1)S(1)}, bf16[16,128,128]{2,1,0:T(8,128)(2,1)S(1)}, u32[]{:S(2)}, u32[]{:S(2)}) collective-permute-start(bf16[16,128,128]{2,1,0:T(8,128)(2,1)S(1)} %pad_maximum_fusion.2.refs_0_), channel_id=1, source_target_pairs={{0,2},{2,0},{1,3},{3,1},{4,6},{6,4},{5,7},{7,5},{8,10},{10,8},{9,1... | collective-permute-start | bytes 1572872 | tf_op jit(solution)/shard_map/ppermute | solution.py:18
  6.0 29.0 %slice-start.2 = ((s8[5242880]{0:T(1024)(128)(4,1)}), s8[1048576]{0:T(1024)(128)(4,1)S(1)}, s32[]{:S(2)}) async-start(s8[5242880]{0:T(1024)(128)(4,1)} %bitcast.112), calls=%async_computation.2 | async-start | bytes 2097152
  6.3 22.9 %collective-permute-start = (bf16[16,128,128]{2,1,0:T(8,128)(2,1)S(1)}, bf16[16,128,128]{2,1,0:T(8,128)(2,1)S(1)}, u32[]{:S(2)}, u32[]{:S(2)}) collective-permute-start(bf16[16,128,128]{2,1,0:T(8,128)(2,1)S(1)} %pad_maximum_fusion.1.refs_0_), channel_id=1, source_target_pairs={{0,2},{2,0},{1,3},{3,1},{4,6},{6,4},{5,7},{7,5},{8,10},{10,8},{9,1... | collective-permute-start | bytes 1572872 | tf_op jit(solution)/shard_map/ppermute | solution.py:18
  6.4 39.5 %collective-permute-start.8 = (bf16[16,128,128]{2,1,0:T(8,128)(2,1)S(1)}, bf16[16,128,128]{2,1,0:T(8,128)(2,1)}, u32[]{:S(2)}, u32[]{:S(2)}) collective-permute-start(bf16[16,128,128]{2,1,0:T(8,128)(2,1)S(1)} %pad_maximum_fusion.2.refs_0_), channel_id=1, source_target_pairs={{0,1},{1,0},{2,3},{3,2},{4,5},{5,4},{6,7},{7,6},{8,9},{9,8},{10,11... | collective-permute-start | bytes 1572872 | tf_op jit(solution)/shard_map/ppermute | solution.py:18
  18.7 27.2 %collective-permute-start.9 = (bf16[16,128,128]{2,1,0:T(8,128)(2,1)S(1)}, bf16[16,128,128]{2,1,0:T(8,128)(2,1)}, u32[]{:S(2)}, u32[]{:S(2)}) collective-permute-start(bf16[16,128,128]{2,1,0:T(8,128)(2,1)S(1)} %collective-permute-done.7.refs_1_), channel_id=1, source_target_pairs={{0,1},{1,0},{2,3},{3,2},{4,5},{5,4},{6,7},{7,6},{8,9},{9,8},{10,11... | collective-permute-start | bytes 1572872 | tf_op jit(solution)/shard_map/ppermute | solution.py:18
  18.7 40.2 %collective-permute-start.1 = (bf16[16,128,128]{2,1,0:T(8,128)(2,1)S(1)}, bf16[16,128,128]{2,1,0:T(8,128)(2,1)}, u32[]{:S(2)}, u32[]{:S(2)}) collective-permute-start(bf16[16,128,128]{2,1,0:T(8,128)(2,1)S(1)} %pad_maximum_fusion.1.refs_0_), channel_id=1, source_target_pairs={{0,1},{1,0},{2,3},{3,2},{4,5},{5,4},{6,7},{7,6},{8,9},{9,8},{10,11... | collective-permute-start | bytes 1572872 | tf_op jit(solution)/shard_map/ppermute | solution.py:18
  29.1 29.8 %collective-permute-start.2 = (bf16[16,128,128]{2,1,0:T(8,128)(2,1)S(1)}, bf16[16,128,128]{2,1,0:T(8,128)(2,1)}, u32[]{:S(2)}, u32[]{:S(2)}) collective-permute-start(bf16[16,128,128]{2,1,0:T(8,128)(2,1)S(1)} %collective-permute-done.refs_1_), channel_id=1, source_target_pairs={{0,1},{1,0},{2,3},{3,2},{4,5},{5,4},{6,7},{7,6},{8,9},{9,8},{10,11... | collective-permute-start | bytes 1572872 | tf_op jit(solution)/shard_map/ppermute | solution.py:18
  29.2 5.7 %slice-start.3 = ((s8[5242880]{0:T(1024)(128)(4,1)}), s8[4194304]{0:T(1024)(128)(4,1)S(1)}, s32[]{:S(2)}) async-start(s8[5242880]{0:T(1024)(128)(4,1)} %bitcast.112), calls=%async_computation.3 | async-start | bytes 8388608
  37.8 21.1 %slice-start = ((s8[5242880]{0:T(1024)(128)(4,1)}), s8[1048576]{0:T(1024)(128)(4,1)S(1)}, s32[]{:S(2)}) async-start(s8[5242880]{0:T(1024)(128)(4,1)} %bitcast.109), calls=%async_computation | async-start | bytes 2097152
  45.9 2.5 %copy-start = (bf16[16,2,4,40,512]{4,3,2,1,0:T(8,128)(2,1)S(1)}, bf16[16,2,4,40,512]{4,3,2,1,0:T(8,128)(2,1)}, u32[]{:S(2)}) copy-start(bf16[16,2,4,40,512]{4,3,2,1,0:T(8,128)(2,1)} %copy.11) | copy-start | bytes 15728644
  48.4 2.5 %copy-start.1 = (bf16[4,512,1280]{2,1,0:T(8,128)(2,1)S(1)}, bf16[4,512,1280]{2,1,0:T(8,128)(2,1)}, u32[]{:S(2)}) copy-start(bf16[4,512,1280]{2,1,0:T(8,128)(2,1)} %copy.13.refs_5_) | copy-start | bytes 15728644
  50.9 7.9 %copy-start.5 = (bf16[2,4,64,128]{3,2,1,0:T(8,128)(2,1)S(1)}, bf16[2,4,64,128]{3,2,1,0:T(8,128)(2,1)}, u32[]{:S(2)}) copy-start(bf16[2,4,64,128]{3,2,1,0:T(8,128)(2,1)} %param.10) | copy-start | bytes 393220
  50.9 8.0 %slice-start.1 = ((s8[5242880]{0:T(1024)(128)(4,1)}), s8[4194304]{0:T(1024)(128)(4,1)S(1)}, s32[]{:S(2)}) async-start(s8[5242880]{0:T(1024)(128)(4,1)} %bitcast.109), calls=%async_computation.1 | async-start | bytes 8388608
  58.2 10.4 %collective-permute-start.10 = (bf16[4,4,64,128]{3,2,1,0:T(8,128)(2,1)S(1)}, bf16[4,4,64,128]{3,2,1,0:T(8,128)(2,1)S(1)}, u32[]{:S(2)}, u32[]{:S(2)}) collective-permute-start(bf16[4,4,64,128]{3,2,1,0:T(8,128)(2,1)S(1)} %get-tuple-element.13), channel_id=1, source_target_pairs={{0,1},{1,0},{2,3},{3,2},{4,5},{5,4},{6,7},{7,6},{8,9},{9,8},{10,11... | collective-permute-start | bytes 786440 | tf_op jit(solution)/shard_map/ppermute | solution.py:18
  58.8 14.5 %copy-start.6 = (bf16[4,64,128]{2,1,0:T(8,128)(2,1)S(1)}, bf16[4,64,128]{2,1,0:T(8,128)(2,1)}, u32[]{:S(2)}) copy-start(bf16[4,64,128]{2,1,0:T(8,128)(2,1)} %param.11) | copy-start | bytes 196612
  58.9 2.5 %copy-start.2 = (bf16[4,512,1280]{2,1,0:T(8,128)(2,1)S(1)}, bf16[4,512,1280]{2,1,0:T(8,128)(2,1)}, u32[]{:S(2)}) copy-start(bf16[4,512,1280]{2,1,0:T(8,128)(2,1)} %copy.13.refs_5_) | copy-start | bytes 15728644
  68.4 23.1 %collective-permute-start.3 = (bf16[4,4,64,128]{3,2,1,0:T(8,128)(2,1)S(1)}, bf16[4,4,64,128]{3,2,1,0:T(8,128)(2,1)S(1)}, u32[]{:S(2)}, u32[]{:S(2)}) collective-permute-start(bf16[4,4,64,128]{3,2,1,0:T(8,128)(2,1)S(1)} %get-tuple-element.11), channel_id=1, source_target_pairs={{0,1},{1,0},{2,3},{3,2},{4,5},{5,4},{6,7},{7,6},{8,9},{9,8},{10,11... | collective-permute-start | bytes 786440 | tf_op jit(solution)/shard_map/ppermute | solution.py:18
  68.7 18.3 %collective-permute-start.13 = (bf16[4,64,128]{2,1,0:T(8,128)(2,1)S(1)}, bf16[4,64,128]{2,1,0:T(8,128)(2,1)S(1)}, u32[]{:S(2)}, u32[]{:S(2)}) collective-permute-start(bf16[4,64,128]{2,1,0:T(8,128)(2,1)S(1)} %get-tuple-element.34), channel_id=1, source_target_pairs={{0,12},{4,8},{8,4},{12,0},{1,13},{5,9},{9,5},{13,1},{2,14},{6,10},... | collective-permute-start | bytes 196616 | tf_op jit(solution)/shard_map/ppermute | solution.py:18
  72.6 14.4 %collective-permute-start.12 = (bf16[4,64,128]{2,1,0:T(8,128)(2,1)S(1)}, bf16[4,64,128]{2,1,0:T(8,128)(2,1)S(1)}, u32[]{:S(2)}, u32[]{:S(2)}) collective-permute-start(bf16[4,64,128]{2,1,0:T(8,128)(2,1)S(1)} %get-tuple-element.35), channel_id=1, source_target_pairs={{0,8},{4,12},{8,0},{12,4},{1,9},{5,13},{9,1},{13,5},{2,10},{6,14},... | collective-permute-start | bytes 196616 | tf_op jit(solution)/shard_map/ppermute | solution.py:18
  72.6 14.4 %collective-permute-start.11 = (bf16[4,64,128]{2,1,0:T(8,128)(2,1)S(1)}, bf16[4,64,128]{2,1,0:T(8,128)(2,1)S(1)}, u32[]{:S(2)}, u32[]{:S(2)}) collective-permute-start(bf16[4,64,128]{2,1,0:T(8,128)(2,1)S(1)} %get-tuple-element.33), channel_id=1, source_target_pairs={{0,4},{4,0},{8,12},{12,8},{1,5},{5,1},{9,13},{13,9},{2,6},{6,2},{1... | collective-permute-start | bytes 196616 | tf_op jit(solution)/shard_map/ppermute | solution.py:18
  87.1 4.6 %collective-permute-start.23 = (bf16[4,64,128]{2,1,0:T(8,128)(2,1)S(1)}, bf16[4,64,128]{2,1,0:T(8,128)(2,1)S(1)}, u32[]{:S(2)}, u32[]{:S(2)}) collective-permute-start(bf16[4,64,128]{2,1,0:T(8,128)(2,1)S(1)} %fusion.11.refs_0_), channel_id=1, source_target_pairs={{0,4},{4,0},{8,12},{12,8},{1,5},{5,1},{9,13},{13,9},{2,6},{6,2},{1... | collective-permute-start | bytes 196616 | tf_op jit(solution)/shard_map/ppermute | solution.py:18
  88.5 7.3 %collective-permute-start.24 = (bf16[4,64,128]{2,1,0:T(8,128)(2,1)S(1)}, bf16[4,64,128]{2,1,0:T(8,128)(2,1)S(1)}, u32[]{:S(2)}, u32[]{:S(2)}) collective-permute-start(bf16[4,64,128]{2,1,0:T(8,128)(2,1)S(1)} %fusion.11.refs_0_), channel_id=1, source_target_pairs={{0,8},{4,12},{8,0},{12,4},{1,9},{5,13},{9,1},{13,5},{2,10},{6,14},... | collective-permute-start | bytes 196616 | tf_op jit(solution)/shard_map/ppermute | solution.py:18
  91.4 6.1 %collective-permute-start.25 = (bf16[4,64,128]{2,1,0:T(8,128)(2,1)S(1)}, bf16[4,64,128]{2,1,0:T(8,128)(2,1)S(1)}, u32[]{:S(2)}, u32[]{:S(2)}) collective-permute-start(bf16[4,64,128]{2,1,0:T(8,128)(2,1)S(1)} %fusion.11.refs_0_), channel_id=1, source_target_pairs={{0,12},{4,8},{8,4},{12,0},{1,13},{5,9},{9,5},{13,1},{2,14},{6,10},... | collective-permute-start | bytes 196616 | tf_op jit(solution)/shard_map/ppermute | solution.py:18
  91.6 8.0 %collective-permute-start.26 = (bf16[4,64,128]{2,1,0:T(8,128)(2,1)S(1)}, bf16[4,64,128]{2,1,0:T(8,128)(2,1)S(1)}, u32[]{:S(2)}, u32[]{:S(2)}) collective-permute-start(bf16[4,64,128]{2,1,0:T(8,128)(2,1)S(1)} %fusion.11.refs_0_), channel_id=1, source_target_pairs={{0,1},{1,0},{2,3},{3,2},{4,5},{5,4},{6,7},{7,6},{8,9},{9,8},{10,11... | collective-permute-start | bytes 196616 | tf_op jit(solution)/shard_map/ppermute | solution.py:18
  91.7 7.9 %collective-permute-start.27 = (bf16[4,64,128]{2,1,0:T(8,128)(2,1)S(1)}, bf16[4,64,128]{2,1,0:T(8,128)(2,1)S(1)}, u32[]{:S(2)}, u32[]{:S(2)}) collective-permute-start(bf16[4,64,128]{2,1,0:T(8,128)(2,1)S(1)} %collective-permute-done.23.refs_1_), channel_id=1, source_target_pairs={{0,1},{1,0},{2,3},{3,2},{4,5},{5,4},{6,7},{7,6},{8,9},{9,8},{10,11... | collective-permute-start | bytes 196616 | tf_op jit(solution)/shard_map/ppermute | solution.py:18
  95.9 6.1 %collective-permute-start.28 = (bf16[4,64,128]{2,1,0:T(8,128)(2,1)S(1)}, bf16[4,64,128]{2,1,0:T(8,128)(2,1)S(1)}, u32[]{:S(2)}, u32[]{:S(2)}) collective-permute-start(bf16[4,64,128]{2,1,0:T(8,128)(2,1)S(1)} %collective-permute-done.24.refs_2_), channel_id=1, source_target_pairs={{0,1},{1,0},{2,3},{3,2},{4,5},{5,4},{6,7},{7,6},{8,9},{9,8},{10,11... | collective-permute-start | bytes 196616 | tf_op jit(solution)/shard_map/ppermute | solution.py:18
  97.5 4.5 %collective-permute-start.29 = (bf16[4,64,128]{2,1,0:T(8,128)(2,1)S(1)}, bf16[4,64,128]{2,1,0:T(8,128)(2,1)S(1)}, u32[]{:S(2)}, u32[]{:S(2)}) collective-permute-start(bf16[4,64,128]{2,1,0:T(8,128)(2,1)S(1)} %collective-permute-done.25.refs_3_), channel_id=1, source_target_pairs={{0,1},{1,0},{2,3},{3,2},{4,5},{5,4},{6,7},{7,6},{8,9},{9,8},{10,11... | collective-permute-start | bytes 196616 | tf_op jit(solution)/shard_map/ppermute | solution.py:18
  97.5 16.1 %collective-permute-start.6 = (bf16[4,64,128]{2,1,0:T(8,128)(2,1)S(1)}, bf16[4,64,128]{2,1,0:T(8,128)(2,1)S(1)}, u32[]{:S(2)}, u32[]{:S(2)}) collective-permute-start(bf16[4,64,128]{2,1,0:T(8,128)(2,1)S(1)} %get-tuple-element.31), channel_id=1, source_target_pairs={{0,12},{4,8},{8,4},{12,0},{1,13},{5,9},{9,5},{13,1},{2,14},{6,10},... | collective-permute-start | bytes 196616 | tf_op jit(solution)/shard_map/ppermute | solution.py:18
  99.6 14.1 %collective-permute-start.5 = (bf16[4,64,128]{2,1,0:T(8,128)(2,1)S(1)}, bf16[4,64,128]{2,1,0:T(8,128)(2,1)S(1)}, u32[]{:S(2)}, u32[]{:S(2)}) collective-permute-start(bf16[4,64,128]{2,1,0:T(8,128)(2,1)S(1)} %get-tuple-element.32), channel_id=1, source_target_pairs={{0,8},{4,12},{8,0},{12,4},{1,9},{5,13},{9,1},{13,5},{2,10},{6,14},... | collective-permute-start | bytes 196616 | tf_op jit(solution)/shard_map/ppermute | solution.py:18
  99.6 14.1 %collective-permute-start.4 = (bf16[4,64,128]{2,1,0:T(8,128)(2,1)S(1)}, bf16[4,64,128]{2,1,0:T(8,128)(2,1)S(1)}, u32[]{:S(2)}, u32[]{:S(2)}) collective-permute-start(bf16[4,64,128]{2,1,0:T(8,128)(2,1)S(1)} %get-tuple-element.30), channel_id=1, source_target_pairs={{0,4},{4,0},{8,12},{12,8},{1,5},{5,1},{9,13},{13,9},{2,6},{6,2},{1... | collective-permute-start | bytes 196616 | tf_op jit(solution)/shard_map/ppermute | solution.py:18
  102.0 2.5 %copy-start.3 = (bf16[2,4,16,40,512]{4,3,2,1,0:T(8,128)(2,1)S(1)}, bf16[2,4,16,40,512]{4,3,2,1,0:T(8,128)(2,1)}, u32[]{:S(2)}) copy-start(bf16[2,4,16,40,512]{4,3,2,1,0:T(8,128)(2,1)} %param.7) | copy-start | bytes 15728644
  113.6 23.3 %collective-permute-start.30 = (bf16[2,16,128,128]{3,2,1,0:T(8,128)(2,1)S(1)}, bf16[2,16,128,128]{3,2,1,0:T(8,128)(2,1)S(1)}, u32[]{:S(2)}, u32[]{:S(2)}) collective-permute-start(bf16[2,16,128,128]{3,2,1,0:T(8,128)(2,1)S(1)} %get-tuple-element.17), channel_id=1, source_target_pairs={{0,1},{1,0},{2,3},{3,2},{4,5},{5,4},{6,7},{7,6},{8,9},{9,8},{10,11... | collective-permute-start | bytes 3145736 | tf_op jit(solution)/shard_map/ppermute | solution.py:18
  113.8 5.6 %collective-permute-start.14 = (bf16[4,64,128]{2,1,0:T(8,128)(2,1)S(1)}, bf16[4,64,128]{2,1,0:T(8,128)(2,1)S(1)}, u32[]{:S(2)}, u32[]{:S(2)}) collective-permute-start(bf16[4,64,128]{2,1,0:T(8,128)(2,1)S(1)} %fusion.17.refs_0_), channel_id=1, source_target_pairs={{0,4},{4,0},{8,12},{12,8},{1,5},{5,1},{9,13},{13,9},{2,6},{6,2},{1... | collective-permute-start | bytes 196616 | tf_op jit(solution)/shard_map/ppermute | solution.py:18
  113.9 8.7 %collective-permute-start.15 = (bf16[4,64,128]{2,1,0:T(8,128)(2,1)S(1)}, bf16[4,64,128]{2,1,0:T(8,128)(2,1)S(1)}, u32[]{:S(2)}, u32[]{:S(2)}) collective-permute-start(bf16[4,64,128]{2,1,0:T(8,128)(2,1)S(1)} %fusion.17.refs_0_), channel_id=1, source_target_pairs={{0,8},{4,12},{8,0},{12,4},{1,9},{5,13},{9,1},{13,5},{2,10},{6,14},... | collective-permute-start | bytes 196616 | tf_op jit(solution)/shard_map/ppermute | solution.py:18
  116.4 6.2 %collective-permute-start.16 = (bf16[4,64,128]{2,1,0:T(8,128)(2,1)S(1)}, bf16[4,64,128]{2,1,0:T(8,128)(2,1)S(1)}, u32[]{:S(2)}, u32[]{:S(2)}) collective-permute-start(bf16[4,64,128]{2,1,0:T(8,128)(2,1)S(1)} %fusion.17.refs_0_), channel_id=1, source_target_pairs={{0,12},{4,8},{8,4},{12,0},{1,13},{5,9},{9,5},{13,1},{2,14},{6,10},... | collective-permute-start | bytes 196616 | tf_op jit(solution)/shard_map/ppermute | solution.py:18
  118.2 4.9 %collective-permute-start.17 = (bf16[4,64,128]{2,1,0:T(8,128)(2,1)S(1)}, bf16[4,64,128]{2,1,0:T(8,128)(2,1)S(1)}, u32[]{:S(2)}, u32[]{:S(2)}) collective-permute-start(bf16[4,64,128]{2,1,0:T(8,128)(2,1)S(1)} %fusion.17.refs_0_), channel_id=1, source_target_pairs={{0,1},{1,0},{2,3},{3,2},{4,5},{5,4},{6,7},{7,6},{8,9},{9,8},{10,11... | collective-permute-start | bytes 196616 | tf_op jit(solution)/shard_map/ppermute | solution.py:18
  119.4 3.8 %collective-permute-start.18 = (bf16[4,64,128]{2,1,0:T(8,128)(2,1)S(1)}, bf16[4,64,128]{2,1,0:T(8,128)(2,1)S(1)}, u32[]{:S(2)}, u32[]{:S(2)}) collective-permute-start(bf16[4,64,128]{2,1,0:T(8,128)(2,1)S(1)} %collective-permute-done.14.refs_1_), channel_id=1, source_target_pairs={{0,1},{1,0},{2,3},{3,2},{4,5},{5,4},{6,7},{7,6},{8,9},{9,8},{10,11... | collective-permute-start | bytes 196616 | tf_op jit(solution)/shard_map/ppermute | solution.py:18
  122.6 1.3 collective-permute-start.19
  122.6 1.4 collective-permute-start.20
  124.0 2.5 %copy-start.4 = (bf16[2,4,16,40,512]{4,3,2,1,0:T(8,128)(2,1)S(1)}, bf16[2,4,16,40,512]{4,3,2,1,0:T(8,128)(2,1)}, u32[]{:S(2)}) copy-start(bf16[2,4,16,40,512]{4,3,2,1,0:T(8,128)(2,1)} %param.7) | copy-start | bytes 15728644
  135.6 3.2 %collective-permute-start.21 = (bf16[2,16,128,128]{3,2,1,0:T(8,128)(2,1)S(1)}, bf16[2,16,128,128]{3,2,1,0:T(8,128)(2,1)S(1)}, u32[]{:S(2)}, u32[]{:S(2)}) collective-permute-start(bf16[2,16,128,128]{3,2,1,0:T(8,128)(2,1)S(1)} %get-tuple-element.15), channel_id=1, source_target_pairs={{0,1},{1,0},{2,3},{3,2},{4,5},{5,4},{6,7},{7,6},{8,9},{9,8},{10,11... | collective-permute-start | bytes 3145736 | tf_op jit(solution)/shard_map/ppermute | solution.py:18
  137.2 14.8 %collective-permute-start.31 = (bf16[16,128,128]{2,1,0:T(8,128)(2,1)S(1)}, bf16[16,128,128]{2,1,0:T(8,128)(2,1)S(1)}, u32[]{:S(2)}, u32[]{:S(2)}) collective-permute-start(bf16[16,128,128]{2,1,0:T(8,128)(2,1)S(1)} %fusion.5), channel_id=1, source_target_pairs={{0,2},{2,0},{1,3},{3,1},{4,6},{6,4},{5,7},{7,5},{8,10},{10,8},{9,1... | collective-permute-start | bytes 1572872 | tf_op jit(solution)/shard_map/ppermute | solution.py:18
  139.2 23.3 %collective-permute-start.22 = (bf16[16,128,128]{2,1,0:T(8,128)(2,1)S(1)}, bf16[16,128,128]{2,1,0:T(8,128)(2,1)S(1)}, u32[]{:S(2)}, u32[]{:S(2)}) collective-permute-start(bf16[16,128,128]{2,1,0:T(8,128)(2,1)S(1)} %fusion.4), channel_id=1, source_target_pairs={{0,2},{2,0},{1,3},{3,1},{4,6},{6,4},{5,7},{7,5},{8,10},{10,8},{9,1... | collective-permute-start | bytes 1572872 | tf_op jit(solution)/shard_map/ppermute | solution.py:18

commit v2 on v0

v2 whole, which is shorter than its diff:
```python
import functools

import jax
import jax.numpy as jnp
from jax import lax
from jax.experimental import pallas as pl
from jax.experimental.pallas import tpu as pltpu
from jax.sharding import PartitionSpec as P

BF16 = jnp.bfloat16
F32 = jnp.float32
CHUNKS = 2
LANES = 128
VM = pl.BlockSpec(memory_space=pltpu.VMEM)
SM = pl.BlockSpec(memory_space=pltpu.SMEM)


def swap(axis_name, step, value):
    size = lax.axis_size(axis_name)
    return lax.ppermute(value, axis_name, [(i, i ^ step) for i in range(size)])


def turn(value, first, second):
    width = value.shape[-1]
    lane = lax.broadcasted_iota(jnp.int32, value.shape, value.ndim - 1)
    sign = jnp.where(lane < width // 2, first, second).astype(F32)
    return pltpu.roll(value, width // 2, value.ndim - 1) * sign


def forward_kernel(at_waves, at_ranks, at_z, helps, n_pieces, scalars, *refs):
    pieces = refs[:n_pieces]
    second, basis, keep_out, send_out, waves, coef, fwd = refs[n_pieces:]
    here = scalars[0]
    columns, quarter, width = pieces[0].shape
    rows = basis.shape[1]
    terms = second.shape[1] // (2 * rows)
    half = rows * terms
    row_index = lax.broadcasted_iota(jnp.int32, (terms, width), 0)
    for j in range(columns):
        for n, piece in enumerate(pieces):
            at = pl.multiple_of(scalars[at_waves + n] * quarter, quarter)
            waves[j, pl.ds(at, quarter), :] = piece[j]
        out = jnp.dot(second[j], waves[j], preferred_element_type=F32)
        value = out[:half] + turn(out[half:], 1.0, -1.0)
        for i in range(rows):
            left = scalars[at_ranks + i * columns + j] - here * terms
            part = value[i * terms : (i + 1) * terms]
            coef[i, j * terms : (j + 1) * terms, :] = jnp.where(row_index < left, part, 0.0)
    zs, _, span, _ = keep_out.shape
    dims = (((0,), (0,)), ((), ()))
    for i in range(rows):
        value = coef[i]
        turned = turn(value, -1.0, 1.0)
        out = lax.dot_general(value.astype(BF16), basis[0, i], dims, preferred_element_type=F32)
        out = out + lax.dot_general(turned.astype(BF16), basis[1, i], dims, preferred_element_type=F32)
        fwd[i] = out.T
        for z in range(zs):
            block = scalars[at_z + z] * helps
            at = pl.multiple_of((block + here) * span, span)
            keep_out[z, i] = fwd[i, pl.ds(at, span), :].astype(keep_out.dtype)
            at = pl.multiple_of((block + 1 - here) * span, span)
            send_out[z, i] = fwd[i, pl.ds(at, span), :].astype(send_out.dtype)


def adjoint_kernel(at_resid, at_ranks, at_r, helps, n_pieces, scalars, *refs):
    pieces = refs[:n_pieces]
    basis, second, keep_out, send_out, resid, back = refs[n_pieces:]
    here = scalars[0]
    blocks, rows, span, width = pieces[0].shape
    columns = second.shape[0]
    terms = second.shape[1] // (2 * rows)
    row_index = lax.broadcasted_iota(jnp.int32, (terms, width), 0)
    for i in range(rows):
        for n, piece in enumerate(pieces):
            for e in range(blocks):
                at = pl.multiple_of(scalars[at_resid + n * blocks + e] * span, span)
                resid[i, pl.ds(at, span), :] = piece[e, i]
        value = resid[i]
        turned = turn(value.astype(F32), 1.0, -1.0).astype(BF16)
        out = jnp.dot(basis[0, i], value, preferred_element_type=F32)
        out = out + jnp.dot(basis[1, i], turned, preferred_element_type=F32)
        for j in range(columns):
            left = scalars[at_ranks + i * columns + j] - here * terms
            part = out[j * terms : (j + 1) * terms]
            back[j, i * terms : (i + 1) * terms, :] = jnp.where(row_index < left, part, 0.0)
    rs, _, _, quarter = keep_out.shape
    for j in range(columns):
        value = back[j]
        left = jnp.concatenate([value, turn(value, -1.0, 1.0)], 0).T.astype(BF16)
        if quarter % LANES == 0:
            for out_ref, h in ((keep_out, here), (send_out, 1 - here)):
                for r in range(rs):
                    at = pl.multiple_of((scalars[at_r + r] * helps + h) * quarter, quarter)
                    out = jnp.dot(left, second[j, :, pl.ds(at, quarter)], preferred_element_type=F32)
                    out_ref[r, j] = out.astype(out_ref.dtype)
        else:
            out = jnp.dot(left, second[j], preferred_element_type=F32)
            for r in range(rs):
                for h in range(helps):
                    part = out[:, (r * helps + h) * quarter : (r * helps + h + 1) * quarter]
                    to = r ^ scalars[at_r]

                    @pl.when(here == h)
                    def _(part=part, to=to):
                        keep_out[to, j] = part.astype(keep_out.dtype)

                    @pl.when(here != h)
                    def _(part=part, to=to):
                        send_out[to, j] = part.astype(send_out.dtype)


def final_kernel(n_each, *refs):
    out_ref = refs[-1]
    groups = [refs[k : k + n_each] for k in range(0, len(refs) - 1, n_each)]
    part = groups[0][0].shape[1] // 2
    for j in range(out_ref.shape[1]):
        for p in range(2):
            pieces = []
            for group in groups:
                total = group[0][j, p * part : (p + 1) * part, :]
                for ref in group[1:]:
                    total = total + ref[j, p * part : (p + 1) * part, :].astype(F32)
                pieces.append(total)
            out_ref[p, j] = jnp.concatenate(pieces, 0).T.astype(out_ref.dtype)


def body(wavefield, basis_factor, second_factor, tile_ranks, observed, amplitude):
    _, columns, quarter, rhs = wavefield.shape
    _, rows, _, terms, tile = basis_factor.shape
    span = observed.shape[2]
    zs, rs, helps = lax.axis_size("col"), lax.axis_size("row"), lax.axis_size("help")
    z, r, h = lax.axis_index("col"), lax.axis_index("row"), lax.axis_index("help")
    part = rhs // CHUNKS
    width = 2 * part
    bits = zs.bit_length() - 1
    far = zs // 2
    near = [1 << b for b in range(bits - 1)]

    z_offsets = [int(format(n, f"0{bits}b")[::-1], 2) for n in range(zs)]
    r_offsets = list(range(rs))
    wave_places = [(r ^ d) * helps + (h ^ e) for e in range(helps) for d in r_offsets]
    z_places = [z ^ d for d in z_offsets]
    r_places = [r ^ d for d in r_offsets]
    offsets = [0]
    for d in reversed(near):
        offsets = offsets + [o ^ d for o in offsets]
    resid_places = [
        (z ^ o ^ f) * helps + (h ^ e) for e in range(helps) for o in offsets for f in (0, far)
    ]
    head = [h] + wave_places + z_places + resid_places + r_places
    at_waves = 1
    at_z = at_waves + len(wave_places)
    at_resid = at_z + len(z_places)
    at_r = at_resid + len(resid_places)
    at_ranks = at_r + len(r_places)
    scalars = jnp.concatenate([jnp.stack(head).astype(jnp.int32), tile_ranks.reshape(-1)])

    def split(value, c):
        return jnp.concatenate(
            [value[0, ..., c * part : (c + 1) * part], value[1, ..., c * part : (c + 1) * part]], -1
        )

    second_rows = second_factor.transpose(2, 0, 1, 3, 4).reshape(columns, 2 * rows * terms, tile)
    basis_rows = basis_factor.reshape(2, rows, columns * terms, tile)
    params = pltpu.CompilerParams(vmem_limit_bytes=20 * 1024 * 1024)
    cost = pl.CostEstimate(flops=4 * 10**9, bytes_accessed=10**6, transcendentals=0)

    def run_forward(pieces):
        shape = (zs, rows, span, width)
        return pl.pallas_call(
            functools.partial(forward_kernel, at_waves, at_ranks, at_z, helps, len(pieces)),
            out_shape=(jax.ShapeDtypeStruct(shape, F32), jax.ShapeDtypeStruct(shape, BF16)),
            in_specs=[SM] + [VM] * (len(pieces) + 2),
            out_specs=(VM, VM),
            scratch_shapes=[
                pltpu.VMEM((columns, tile, width), BF16),
                pltpu.VMEM((rows, columns * terms, width), F32),
                pltpu.VMEM((rows, tile, width), F32),
            ],
            compiler_params=params,
            cost_estimate=cost,
            name="forward_product",
        )(scalars, *pieces, second_rows, basis_rows)

    def run_adjoint(pieces):
        shape = (rs, columns, width, quarter)
        return pl.pallas_call(
            functools.partial(adjoint_kernel, at_resid, at_ranks, at_r, helps, len(pieces)),
            out_shape=(jax.ShapeDtypeStruct(shape, F32), jax.ShapeDtypeStruct(shape, BF16)),
            in_specs=[SM] + [VM] * (len(pieces) + 2),
            out_specs=(VM, VM),
            scratch_shapes=[
                pltpu.VMEM((rows, tile, width), BF16),
                pltpu.VMEM((columns, rows * terms, width), F32),
            ],
            compiler_params=params,
            cost_estimate=cost,
            name="adjoint_product",
        )(scalars, *pieces, basis_rows, second_rows)

    def share(pieces):
        return pieces + [swap("help", d, m) for d in range(1, helps) for m in pieces]

    waves = [split(wavefield, c) for c in range(CHUNKS)]
    gathered = [[w] + [swap("row", d, w) for d in range(1, rs)] for w in waves]
    data = jnp.concatenate([observed, amplitude[None]], 0)
    data = jnp.stack([data, swap("col", far, data)], 1).astype(F32)

    residuals, ends = [], []
    for c in range(CHUNKS):
        keep, send = run_forward(share(gathered[c]))
        total = keep + swap("help", 1, send).astype(F32)
        for d in near:
            n = total.shape[0] // 2
            total = total[:n] + swap("col", d, total[n:].astype(BF16)).astype(F32)
        total = total + swap("col", far, total[::-1].astype(BF16)).astype(F32)
        weight = data[2, ..., c * part : (c + 1) * part]
        weight = jnp.concatenate([weight, weight], -1)
        resid = (weight * (total - split(data[:2], c))).astype(BF16)
        residuals.append(resid[0])
        pieces = [resid]
        for d in reversed(near):
            pieces = pieces + [swap("col", d, m) for m in pieces]
        keep, send = run_adjoint(share(pieces))
        total = keep + swap("help", 1, send).astype(F32)
        ends += [total[0]] + [swap("row", d, total[d].astype(BF16)) for d in range(1, rs)]

    adjoint = pl.pallas_call(
        functools.partial(final_kernel, rs),
        out_shape=jax.ShapeDtypeStruct(wavefield.shape, BF16),
        in_specs=[VM] * len(ends),
        out_specs=VM,
        compiler_params=params,
        cost_estimate=pl.CostEstimate(flops=10**9, bytes_accessed=10**6, transcendentals=0),
        name="adjoint_sum",
    )(*ends)
    residual = jnp.stack(
        [jnp.concatenate([v[..., p * part : (p + 1) * part] for v in residuals], -1) for p in range(2)]
    )
    return residual, adjoint


def solution(mesh):
    return jax.shard_map(
        body,
        mesh=mesh,
        in_specs=(
            P("freq", "col", ("row", "help"), None),
            P("freq", "row", "col", "help", None),
            P("freq", "row", "col", "help", None),
            P(("freq", "row"), "col"),
            P("freq", "row", ("col", "help"), None),
            P(("freq", "row"), ("col", "help"), None),
        ),
        out_specs=(
            P("freq", "row", ("col", "help"), None),
            P("freq", "col", ("row", "help"), None),
        ),
        check_vma=False,
    )
```

time: 238 us -> 123 us (0.52)
  waiting for transfers between devices: 183 us -> 58.6 us
  starting transfers between devices: 0.34 us -> 20.2 us
  Pallas kernels: 0 us -> 18.4 us
  matrix products: 15.5 us -> 0 us
  between operations: 14.1 us -> 0.95 us
  other arithmetic: 16.1 us -> 3.33 us
  local copies, waits for them, and re-layouts: 8.49 us -> 21.1 us
    reduce_scatter x1 -> x0, waiting for transfers between devices: 70.6 us -> none  [body(): lax.psum_scatter(adjoint_terms, ('row', 'help'), scatter_dimension=2, til...]
    psum x1 -> x0, waiting for transfers between devices: 64.3 us -> none  [body(): total = lax.psum(partial_value, ('col', 'help'))]
    ppermute x0 -> x23, waiting for transfers between devices: none -> 58.6 us  [swap(): return lax.ppermute(value, axis_name, [(i, i ^ step) for i in range(size)])]
    all_gather x2 -> x0, waiting for transfers between devices: 48.2 us -> none  [the longest x1 36.5 us: body(): piece = lax.all_gather(wavefield, ('row', 'help'), axis=2, tiled=True)]
    ppermute x0 -> x23, starting transfers between devices: none -> 20.2 us  [swap(): return lax.ppermute(value, axis_name, [(i, i ^ step) for i in range(size)])]
    pallas_call x0 -> x5, Pallas kernels: none -> 18.4 us  [the longest x2 8.7 us: run_adjoint(): pl.pallas_call(functools.partial(adjoint_kernel, at_resid, at_ranks, at_r...]
    dot_general x8 -> x0, matrix products: 15.5 us -> none  [the longest x1 4.18 us: body(): jnp.einsum('pijks,pisn->ijkn', block, full, preferred_element_type=jnp.fl...]
    transpose x0 -> x1, local copies, waits for them, and re-layouts: none -> 5.53 us  [body(): second_factor.transpose(2, 0, 1, 3, 4)]
  transfers between devices with their start and end apart: 4 -> 23, of which waited for: 4 -> 10; matrix products, arithmetic and copies ran while one was open for 7% -> 8% of each run, Pallas kernels for 0% -> 14%
where the time goes in v2:
time: 123 us; the launch traced here: 122 us
  waiting for transfers between devices  58.6 us (48%)
  local copies, waits for them, and re-layouts  21.1 us (17%)
  starting transfers between devices  20.2 us (16%)
  Pallas kernels  18.4 us (15%)
  other arithmetic  3.33 us (3%)
    ppermute x23, waiting for transfers between devices, swap(): return lax.ppermute(value, axis_name, [(i, i ^ step) for i in range(size)])  58.6 us
    ppermute x23, starting transfers between devices, swap(): return lax.ppermute(value, axis_name, [(i, i ^ step) for i in range(size)])  20.2 us
    unnamed x18, local copies, waits for them, and re-layouts  12.4 us
    pallas_call x2, Pallas kernels, run_adjoint(): pl.pallas_call(functools.partial(adjoint_kernel, at_resid, at_ranks, at_r...  8.7 us
    pallas_call x2, Pallas kernels, run_forward(): pl.pallas_call(functools.partial(forward_kernel, at_waves, at_ranks, at_z...  8.33 us
    transpose x1, local copies, waits for them, and re-layouts, body(): second_factor.transpose(2, 0, 1, 3, 4)  5.53 us
  transfers between devices with their start and end apart: 23, of which 10 were waited for; matrix products, arithmetic and copies ran while one was open for 8% of the time, Pallas kernels for 14%

profile of v2, /device:TPU:0, one launch (start us, length us, event | category | flops | bytes accessed | tf_op | source)
XLA Modules:
  0.0 122.5 jit_solution(12230999805148012895)
XLA Ops:
  0.6 2.0 %slice_bitcast_fusion.5 = (bf16[16,128,64]{2,1,0:T(8,128)(2,1)S(1)}, bf16[16,128,64]{2,1,0:T(8,128)(2,1)S(1)}, bf16[16,128,64]{2,1,0:T(8,128)(2,1)S(1)}, bf16[16,128,64]{2,1,0:T(8,128)(2,1)S(1)}) fusion(bf16[2,16,128,128]{3,2,1,0:T(8,128)(2,1)} %param.6), kind=kLoop, calls=%fused_computation.15 | loop fusion | bytes 2097152 | tf_op jit(solution)/shard_map/squeeze | solution.py:160
  2.7 0.3 pad_maximum_fusion.1.refs_0_
  3.0 3.0 %collective-permute-start.7 = (bf16[16,128,128]{2,1,0:T(8,128)(2,1)S(1)}, bf16[16,128,128]{2,1,0:T(8,128)(2,1)S(1)}, u32[]{:S(2)}, u32[]{:S(2)}) collective-permute-start(bf16[16,128,128]{2,1,0:T(8,128)(2,1)S(1)} %pad_maximum_fusion.1.refs_0_), channel_id=1, source_target_pairs={{0,2},{2,0},{1,3},{3,1},{4,6},{6,4},{5,7},{7,5},{8,10},{10,8},{9,1... | collective-permute-start | bytes 1572872 | tf_op jit(solution)/shard_map/ppermute | solution.py:20
  6.0 0.3 pad_maximum_fusion.refs_0_
  6.5 12.3 %collective-permute-done.7.refs_1_ = bf16[16,128,128]{2,1,0:T(8,128)(2,1)S(1)} collective-permute-done((bf16[16,128,128]{2,1,0:T(8,128)(2,1)S(1)}, bf16[16,128,128]{2,1,0:T(8,128)(2,1)S(1)}, u32[]{:S(2)}, u32[]{:S(2)}) %collective-permute-start.7) | collective-permute-done | bytes 524320 | tf_op jit(solution)/shard_map/ppermute | solution.py:20
  18.8 0.7 fusion.4
  19.5 3.2 %collective-permute-start = (bf16[3,4,64,128]{3,2,1,0:T(8,128)(2,1)}, bf16[3,4,64,128]{3,2,1,0:T(8,128)(2,1)S(1)}, u32[]{:S(2)}, u32[]{:S(2)}) collective-permute-start(bf16[3,4,64,128]{3,2,1,0:T(8,128)(2,1)} %get-tuple-element.29), channel_id=1, source_target_pairs={{0,8},{4,12},{8,0},{12,4},{1,9},{5,13},{9,1},{13,5},{2,10},{6,14},... | collective-permute-start | bytes 589832 | tf_op jit(solution)/shard_map/ppermute | solution.py:20
  22.6 0.2 collective-permute-start.2
  22.9 6.3 %collective-permute-done.1.refs_1_ = bf16[16,128,128]{2,1,0:T(8,128)(2,1)S(1)} collective-permute-done((bf16[16,128,128]{2,1,0:T(8,128)(2,1)S(1)}, bf16[16,128,128]{2,1,0:T(8,128)(2,1)S(1)}, u32[]{:S(2)}, u32[]{:S(2)}) %collective-permute-start.1) | collective-permute-done | bytes 524320 | tf_op jit(solution)/shard_map/ppermute | solution.py:20
  29.3 5.5 %copy.9 = bf16[16,2,4,40,512]{4,3,2,1,0:T(8,128)(2,1)} copy(bf16[16,2,4,40,512]{4,3,0,2,1:T(8,128)(2,1)} %bitcast.72) | data formatting | bytes 10485760 | tf_op jit(solution)/shard_map/transpose | solution.py:163
  34.8 0.1 concatenate.32.scalars
  35.0 2.5 %copy-done = bf16[16,2,4,40,512]{4,3,2,1,0:T(8,128)(2,1)S(1)} copy-done((bf16[16,2,4,40,512]{4,3,2,1,0:T(8,128)(2,1)S(1)}, bf16[16,2,4,40,512]{4,3,2,1,0:T(8,128)(2,1)}, u32[]{:S(2)}) %copy-start) | copy-done | bytes 5242904
  37.5 2.5 %copy-done.3 = bf16[2,4,16,40,512]{4,3,2,1,0:T(8,128)(2,1)S(1)} copy-done((bf16[2,4,16,40,512]{4,3,2,1,0:T(8,128)(2,1)S(1)}, bf16[2,4,16,40,512]{4,3,2,1,0:T(8,128)(2,1)}, u32[]{:S(2)}) %copy-start.3) | copy-done | bytes 5242904
  40.0 4.2 %forward_product.3 = (f32[4,4,64,128]{3,2,1,0:T(8,128)S(1)}, bf16[4,4,64,128]{3,2,1,0:T(8,128)(2,1)S(1)}) custom-call(s32[83]{0:T(128)S(1)} %concatenate.32.scalars, bf16[16,128,128]{2,1,0:T(8,128)(2,1)S(1)} %pad_maximum_fusion.1.refs_0_, bf16[16,128,128]{2,1,0:T(8,128)(2,1)S(1)} %collective-permute-done.7.refs_1_, ...), custom_call_target="tpu_custom_call" | custom-call | flops 4000000000 | bytes 1000000 | tf_op jit(solution)/shard_map/forward_product/pallas_call | solution.py:170
  44.2 0.6 collective-permute-start.10
  44.8 2.5 %copy-done.4 = bf16[2,4,16,40,512]{4,3,2,1,0:T(8,128)(2,1)S(1)} copy-done((bf16[2,4,16,40,512]{4,3,2,1,0:T(8,128)(2,1)S(1)}, bf16[2,4,16,40,512]{4,3,2,1,0:T(8,128)(2,1)}, u32[]{:S(2)}) %copy-start.4) | copy-done | bytes 5242904
  47.3 4.1 %forward_product.2 = (f32[4,4,64,128]{3,2,1,0:T(8,128)S(1)}, bf16[4,4,64,128]{3,2,1,0:T(8,128)(2,1)S(1)}) custom-call(s32[83]{0:T(128)S(1)} %concatenate.32.scalars, bf16[16,128,128]{2,1,0:T(8,128)(2,1)S(1)} %pad_maximum_fusion.refs_0_, bf16[16,128,128]{2,1,0:T(8,128)(2,1)S(1)} %collective-permute-done.1.refs_1_, ...), custom_call_target="tpu_custom_call" | custom-call | flops 4000000000 | bytes 1000000 | tf_op jit(solution)/shard_map/forward_product/pallas_call | solution.py:170
  51.4 0.1 collective-permute-start.4
  51.5 0.3 slice_bitcast_fusion.10
  51.8 1.2 collective-permute-done.4
  53.1 1.9 %collective-permute-start.5 = (bf16[2,4,64,128]{3,2,1,0:T(8,128)(2,1)S(1)}, bf16[2,4,64,128]{3,2,1,0:T(8,128)(2,1)S(1)}, u32[]{:S(2)}, u32[]{:S(2)}) collective-permute-start(bf16[2,4,64,128]{3,2,1,0:T(8,128)(2,1)S(1)} %slice.151), channel_id=1, source_target_pairs={{0,4},{4,0},{8,12},{12,8},{1,5},{5,1},{9,13},{13,9},{2,6},{6,2},{1... | collective-permute-start | bytes 393224 | tf_op jit(solution)/shard_map/ppermute | solution.py:20
  55.1 0.3 collective-permute-start.11
  55.3 4.1 %collective-permute-done.5 = bf16[2,4,64,128]{3,2,1,0:T(8,128)(2,1)S(1)} collective-permute-done((bf16[2,4,64,128]{3,2,1,0:T(8,128)(2,1)S(1)}, bf16[2,4,64,128]{3,2,1,0:T(8,128)(2,1)S(1)}, u32[]{:S(2)}, u32[]{:S(2)}) %collective-permute-start.5) | collective-permute-done | bytes 131104 | tf_op jit(solution)/shard_map/ppermute | solution.py:20
  59.5 2.9 %collective-permute-start.6 = (bf16[2,4,64,128]{3,2,1,0:T(8,128)(2,1)S(1)}, bf16[2,4,64,128]{3,2,1,0:T(8,128)(2,1)S(1)}, u32[]{:S(2)}, u32[]{:S(2)}) collective-permute-start(bf16[2,4,64,128]{3,2,1,0:T(8,128)(2,1)S(1)} %rev.11), channel_id=1, source_target_pairs={{0,8},{4,12},{8,0},{12,4},{1,9},{5,13},{9,1},{13,5},{2,10},{6,14},... | collective-permute-start | bytes 393224 | tf_op jit(solution)/shard_map/ppermute | solution.py:20
  62.5 2.7 %collective-permute-start.12 = (bf16[2,4,64,128]{3,2,1,0:T(8,128)(2,1)S(1)}, bf16[2,4,64,128]{3,2,1,0:T(8,128)(2,1)S(1)}, u32[]{:S(2)}, u32[]{:S(2)}) collective-permute-start(bf16[2,4,64,128]{3,2,1,0:T(8,128)(2,1)S(1)} %rev.10), channel_id=1, source_target_pairs={{0,8},{4,12},{8,0},{12,4},{1,9},{5,13},{9,1},{13,5},{2,10},{6,14},... | collective-permute-start | bytes 393224 | tf_op jit(solution)/shard_map/ppermute | solution.py:20
  65.3 6.5 %collective-permute-done.6 = bf16[2,4,64,128]{3,2,1,0:T(8,128)(2,1)S(1)} collective-permute-done((bf16[2,4,64,128]{3,2,1,0:T(8,128)(2,1)S(1)}, bf16[2,4,64,128]{3,2,1,0:T(8,128)(2,1)S(1)}, u32[]{:S(2)}, u32[]{:S(2)}) %collective-permute-start.6) | collective-permute-done | bytes 131104 | tf_op jit(solution)/shard_map/ppermute | solution.py:20
  71.7 0.2 fusion.2.refs_0_
  71.9 0.5 collective-permute-start.13
  72.5 1.0 collective-permute-done.12
  73.4 0.2 fusion.3.refs_0_
  73.7 0.7 collective-permute-start.18
  74.3 0.2 collective-permute-start.19
  74.6 3.6 %collective-permute-done.13.refs_1_ = bf16[2,4,64,128]{3,2,1,0:T(8,128)(2,1)S(1)} collective-permute-done((bf16[2,4,64,128]{3,2,1,0:T(8,128)(2,1)S(1)}, bf16[2,4,64,128]{3,2,1,0:T(8,128)(2,1)S(1)}, u32[]{:S(2)}, u32[]{:S(2)}) %collective-permute-start.13) | collective-permute-done | bytes 131104 | tf_op jit(solution)/shard_map/ppermute | solution.py:20
  78.2 1.6 %collective-permute-done.18.refs_1_ = bf16[2,4,64,128]{3,2,1,0:T(8,128)(2,1)S(1)} collective-permute-done((bf16[2,4,64,128]{3,2,1,0:T(8,128)(2,1)S(1)}, bf16[2,4,64,128]{3,2,1,0:T(8,128)(2,1)S(1)}, u32[]{:S(2)}, u32[]{:S(2)}) %collective-permute-start.18) | collective-permute-done | bytes 131104 | tf_op jit(solution)/shard_map/ppermute | solution.py:20
  79.8 2.5 %copy-done.2 = bf16[16,2,4,40,512]{4,3,2,1,0:T(8,128)(2,1)S(1)} copy-done((bf16[16,2,4,40,512]{4,3,2,1,0:T(8,128)(2,1)S(1)}, bf16[16,2,4,40,512]{4,3,2,1,0:T(8,128)(2,1)}, u32[]{:S(2)}) %copy-start.2) | copy-done | bytes 5242904
  82.3 2.5 %copy-done.5 = bf16[2,4,16,40,512]{4,3,2,1,0:T(8,128)(2,1)S(1)} copy-done((bf16[2,4,16,40,512]{4,3,2,1,0:T(8,128)(2,1)S(1)}, bf16[2,4,16,40,512]{4,3,2,1,0:T(8,128)(2,1)}, u32[]{:S(2)}) %copy-start.5) | copy-done | bytes 5242904
  84.8 4.4 %adjoint_product.2 = (f32[2,16,128,128]{3,2,1,0:T(8,128)S(1)}, bf16[2,16,128,128]{3,2,1,0:T(8,128)(2,1)S(1)}) custom-call(s32[83]{0:T(128)S(1)} %concatenate.32.scalars, bf16[2,4,64,128]{3,2,1,0:T(8,128)(2,1)S(1)} %fusion.2.refs_0_, bf16[2,4,64,128]{3,2,1,0:T(8,128)(2,1)S(1)} %collective-permute-done.13.refs_1_, ...), custom_call_target="tpu_custom_call" | custom-call | flops 4000000000 | bytes 1000000 | tf_op jit(solution)/shard_map/adjoint_product/pallas_call | solution.py:187
  89.2 0.6 collective-permute-start.16
  89.8 4.3 %adjoint_product.3 = (f32[2,16,128,128]{3,2,1,0:T(8,128)S(1)}, bf16[2,16,128,128]{3,2,1,0:T(8,128)(2,1)S(1)}) custom-call(s32[83]{0:T(128)S(1)} %concatenate.32.scalars, bf16[2,4,64,128]{3,2,1,0:T(8,128)(2,1)S(1)} %fusion.3.refs_0_, bf16[2,4,64,128]{3,2,1,0:T(8,128)(2,1)S(1)} %collective-permute-done.18.refs_1_, ...), custom_call_target="tpu_custom_call" | custom-call | flops 4000000000 | bytes 1000000 | tf_op jit(solution)/shard_map/adjoint_product/pallas_call | solution.py:187
  94.3 0.1 maximum_bitcast_fusion
  94.4 0.7 pad_maximum_fusion.3
  95.1 0.4 convert_add_fusion.1
  95.5 1.8 %collective-permute-start.17 = (bf16[16,128,128]{2,1,0:T(8,128)(2,1)S(1)}, bf16[16,128,128]{2,1,0:T(8,128)(2,1)S(1)}, u32[]{:S(2)}, u32[]{:S(2)}) collective-permute-start(bf16[16,128,128]{2,1,0:T(8,128)(2,1)S(1)} %fusion), channel_id=1, source_target_pairs={{0,2},{2,0},{1,3},{3,1},{4,6},{6,4},{5,7},{7,5},{8,10},{10,8},{9,1... | collective-permute-start | bytes 1572872 | tf_op jit(solution)/shard_map/ppermute | solution.py:20
  97.3 0.3 convert_add_fusion
  97.7 1.3 %collective-permute-start.22 = (bf16[16,128,128]{2,1,0:T(8,128)(2,1)S(1)}, bf16[16,128,128]{2,1,0:T(8,128)(2,1)S(1)}, u32[]{:S(2)}, u32[]{:S(2)}) collective-permute-start(bf16[16,128,128]{2,1,0:T(8,128)(2,1)S(1)} %fusion.1), channel_id=1, source_target_pairs={{0,2},{2,0},{1,3},{3,1},{4,6},{6,4},{5,7},{7,5},{8,10},{10,8},{9,1... | collective-permute-start | bytes 1572872 | tf_op jit(solution)/shard_map/ppermute | solution.py:20
  99.2 11.2 %collective-permute-done.17.refs_1_ = bf16[16,128,128]{2,1,0:T(8,128)(2,1)S(1)} collective-permute-done((bf16[16,128,128]{2,1,0:T(8,128)(2,1)S(1)}, bf16[16,128,128]{2,1,0:T(8,128)(2,1)S(1)}, u32[]{:S(2)}, u32[]{:S(2)}) %collective-permute-start.17) | collective-permute-done | bytes 524320 | tf_op jit(solution)/shard_map/ppermute | solution.py:20
  110.3 10.8 %collective-permute-done.22.refs_3_ = bf16[16,128,128]{2,1,0:T(8,128)(2,1)S(1)} collective-permute-done((bf16[16,128,128]{2,1,0:T(8,128)(2,1)S(1)}, bf16[16,128,128]{2,1,0:T(8,128)(2,1)S(1)}, u32[]{:S(2)}, u32[]{:S(2)}) %collective-permute-start.22) | collective-permute-done | bytes 524320 | tf_op jit(solution)/shard_map/ppermute | solution.py:20
  121.1 1.4 %adjoint_sum.1 = bf16[2,16,128,128]{3,2,1,0:T(8,128)(2,1)} custom-call(f32[16,128,128]{2,1,0:T(8,128)S(1)} %slice_bitcast_fusion.1.refs_0_, bf16[16,128,128]{2,1,0:T(8,128)(2,1)S(1)} %collective-permute-done.17.refs_1_, f32[16,128,128]{2,1,0:T(8,128)S(1)} %slice_bitcast_fusion.refs_2_, bf16[16,128,128]{2,1,0:T(8,128)(2,1)S(1)} %collective-permute-done.22.refs_3_), custom_call_target="tpu_custom_call" | custom-call | flops 1000000000 | bytes 1000000 | tf_op jit(solution)/shard_map/adjoint_sum/pallas_call | solution.py:228
  (52 shorter events, 1.2 us)
Async XLA Ops:
  2.7 16.1 %copy-start.6 = (bf16[2,4,64,128]{3,2,1,0:T(8,128)(2,1)S(1)}, bf16[2,4,64,128]{3,2,1,0:T(8,128)(2,1)}, u32[]{:S(2)}) copy-start(bf16[2,4,64,128]{3,2,1,0:T(8,128)(2,1)} %param.10) | copy-start | bytes 393220
  2.7 16.1 %copy-start.7 = (bf16[4,64,128]{2,1,0:T(8,128)(2,1)S(1)}, bf16[4,64,128]{2,1,0:T(8,128)(2,1)}, u32[]{:S(2)}) copy-start(bf16[4,64,128]{2,1,0:T(8,128)(2,1)} %param.11) | copy-start | bytes 196612
  2.7 26.5 %copy-start.8 = (s32[4,16]{1,0:T(4,128)S(1)}, s32[4,16]{1,0:T(4,128)}, u32[]{:S(2)}) copy-start(s32[4,16]{1,0:T(4,128)} %param.9) | copy-start | bytes 772
  3.0 15.8 %collective-permute-start.7 = (bf16[16,128,128]{2,1,0:T(8,128)(2,1)S(1)}, bf16[16,128,128]{2,1,0:T(8,128)(2,1)S(1)}, u32[]{:S(2)}, u32[]{:S(2)}) collective-permute-start(bf16[16,128,128]{2,1,0:T(8,128)(2,1)S(1)} %pad_maximum_fusion.1.refs_0_), channel_id=1, source_target_pairs={{0,2},{2,0},{1,3},{3,1},{4,6},{6,4},{5,7},{7,5},{8,10},{10,8},{9,1... | collective-permute-start | bytes 1572872 | tf_op jit(solution)/shard_map/ppermute | solution.py:20
  6.3 22.9 %collective-permute-start.1 = (bf16[16,128,128]{2,1,0:T(8,128)(2,1)S(1)}, bf16[16,128,128]{2,1,0:T(8,128)(2,1)S(1)}, u32[]{:S(2)}, u32[]{:S(2)}) collective-permute-start(bf16[16,128,128]{2,1,0:T(8,128)(2,1)S(1)} %pad_maximum_fusion.refs_0_), channel_id=1, source_target_pairs={{0,2},{2,0},{1,3},{3,1},{4,6},{6,4},{5,7},{7,5},{8,10},{10,8},{9,1... | collective-permute-start | bytes 1572872 | tf_op jit(solution)/shard_map/ppermute | solution.py:20
  6.4 28.6 %collective-permute-start.8 = (bf16[16,128,128]{2,1,0:T(8,128)(2,1)S(1)}, bf16[16,128,128]{2,1,0:T(8,128)(2,1)S(1)}, u32[]{:S(2)}, u32[]{:S(2)}) collective-permute-start(bf16[16,128,128]{2,1,0:T(8,128)(2,1)S(1)} %pad_maximum_fusion.1.refs_0_), channel_id=1, source_target_pairs={{0,1},{1,0},{2,3},{3,2},{4,5},{5,4},{6,7},{7,6},{8,9},{9,8},{10,11... | collective-permute-start | bytes 1572872 | tf_op jit(solution)/shard_map/ppermute | solution.py:20
  18.8 16.2 %collective-permute-start.9 = (bf16[16,128,128]{2,1,0:T(8,128)(2,1)S(1)}, bf16[16,128,128]{2,1,0:T(8,128)(2,1)}, u32[]{:S(2)}, u32[]{:S(2)}) collective-permute-start(bf16[16,128,128]{2,1,0:T(8,128)(2,1)S(1)} %collective-permute-done.7.refs_1_), channel_id=1, source_target_pairs={{0,1},{1,0},{2,3},{3,2},{4,5},{5,4},{6,7},{7,6},{8,9},{9,8},{10,11... | collective-permute-start | bytes 1572872 | tf_op jit(solution)/shard_map/ppermute | solution.py:20
  19.5 15.4 %collective-permute-start = (bf16[3,4,64,128]{3,2,1,0:T(8,128)(2,1)}, bf16[3,4,64,128]{3,2,1,0:T(8,128)(2,1)S(1)}, u32[]{:S(2)}, u32[]{:S(2)}) collective-permute-start(bf16[3,4,64,128]{3,2,1,0:T(8,128)(2,1)} %get-tuple-element.29), channel_id=1, source_target_pairs={{0,8},{4,12},{8,0},{12,4},{1,9},{5,13},{9,1},{13,5},{2,10},{6,14},... | collective-permute-start | bytes 589832 | tf_op jit(solution)/shard_map/ppermute | solution.py:20
  22.6 22.1 %collective-permute-start.2 = (bf16[16,128,128]{2,1,0:T(8,128)(2,1)S(1)}, bf16[16,128,128]{2,1,0:T(8,128)(2,1)S(1)}, u32[]{:S(2)}, u32[]{:S(2)}) collective-permute-start(bf16[16,128,128]{2,1,0:T(8,128)(2,1)S(1)} %pad_maximum_fusion.refs_0_), channel_id=1, source_target_pairs={{0,1},{1,0},{2,3},{3,2},{4,5},{5,4},{6,7},{7,6},{8,9},{9,8},{10,11... | collective-permute-start | bytes 1572872 | tf_op jit(solution)/shard_map/ppermute | solution.py:20
  29.2 15.6 %collective-permute-start.3 = (bf16[16,128,128]{2,1,0:T(8,128)(2,1)S(1)}, bf16[16,128,128]{2,1,0:T(8,128)(2,1)}, u32[]{:S(2)}, u32[]{:S(2)}) collective-permute-start(bf16[16,128,128]{2,1,0:T(8,128)(2,1)S(1)} %collective-permute-done.1.refs_1_), channel_id=1, source_target_pairs={{0,1},{1,0},{2,3},{3,2},{4,5},{5,4},{6,7},{7,6},{8,9},{9,8},{10,11... | collective-permute-start | bytes 1572872 | tf_op jit(solution)/shard_map/ppermute | solution.py:20
  35.0 2.5 %copy-start = (bf16[16,2,4,40,512]{4,3,2,1,0:T(8,128)(2,1)S(1)}, bf16[16,2,4,40,512]{4,3,2,1,0:T(8,128)(2,1)}, u32[]{:S(2)}) copy-start(bf16[16,2,4,40,512]{4,3,2,1,0:T(8,128)(2,1)} %copy.9) | copy-start | bytes 15728644
  37.5 2.5 %copy-start.3 = (bf16[2,4,16,40,512]{4,3,2,1,0:T(8,128)(2,1)S(1)}, bf16[2,4,16,40,512]{4,3,2,1,0:T(8,128)(2,1)}, u32[]{:S(2)}) copy-start(bf16[2,4,16,40,512]{4,3,2,1,0:T(8,128)(2,1)} %param.7) | copy-start | bytes 15728644
  40.0 4.8 %copy-start.1 = (bf16[16,2,4,40,512]{4,3,2,1,0:T(8,128)(2,1)S(1)}, bf16[16,2,4,40,512]{4,3,2,1,0:T(8,128)(2,1)}, u32[]{:S(2)}) copy-start(bf16[16,2,4,40,512]{4,3,2,1,0:T(8,128)(2,1)} %copy.9) | copy-start | bytes 15728644
  44.2 10.8 %collective-permute-start.10 = (bf16[4,4,64,128]{3,2,1,0:T(8,128)(2,1)S(1)}, bf16[4,4,64,128]{3,2,1,0:T(8,128)(2,1)S(1)}, u32[]{:S(2)}, u32[]{:S(2)}) collective-permute-start(bf16[4,4,64,128]{3,2,1,0:T(8,128)(2,1)S(1)} %get-tuple-element.13), channel_id=1, source_target_pairs={{0,1},{1,0},{2,3},{3,2},{4,5},{5,4},{6,7},{7,6},{8,9},{9,8},{10,11... | collective-permute-start | bytes 786440 | tf_op jit(solution)/shard_map/ppermute | solution.py:20
  44.8 2.5 %copy-start.4 = (bf16[2,4,16,40,512]{4,3,2,1,0:T(8,128)(2,1)S(1)}, bf16[2,4,16,40,512]{4,3,2,1,0:T(8,128)(2,1)}, u32[]{:S(2)}) copy-start(bf16[2,4,16,40,512]{4,3,2,1,0:T(8,128)(2,1)} %param.7) | copy-start | bytes 15728644
  51.4 1.6 %collective-permute-start.4 = (bf16[4,4,64,128]{3,2,1,0:T(8,128)(2,1)S(1)}, bf16[4,4,64,128]{3,2,1,0:T(8,128)(2,1)S(1)}, u32[]{:S(2)}, u32[]{:S(2)}) collective-permute-start(bf16[4,4,64,128]{3,2,1,0:T(8,128)(2,1)S(1)} %get-tuple-element.11), channel_id=1, source_target_pairs={{0,1},{1,0},{2,3},{3,2},{4,5},{5,4},{6,7},{7,6},{8,9},{9,8},{10,11... | collective-permute-start | bytes 786440 | tf_op jit(solution)/shard_map/ppermute | solution.py:20
  53.1 6.4 %collective-permute-start.5 = (bf16[2,4,64,128]{3,2,1,0:T(8,128)(2,1)S(1)}, bf16[2,4,64,128]{3,2,1,0:T(8,128)(2,1)S(1)}, u32[]{:S(2)}, u32[]{:S(2)}) collective-permute-start(bf16[2,4,64,128]{3,2,1,0:T(8,128)(2,1)S(1)} %slice.151), channel_id=1, source_target_pairs={{0,4},{4,0},{8,12},{12,8},{1,5},{5,1},{9,13},{13,9},{2,6},{6,2},{1... | collective-permute-start | bytes 393224 | tf_op jit(solution)/shard_map/ppermute | solution.py:20
  55.1 7.4 %collective-permute-start.11 = (bf16[2,4,64,128]{3,2,1,0:T(8,128)(2,1)S(1)}, bf16[2,4,64,128]{3,2,1,0:T(8,128)(2,1)S(1)}, u32[]{:S(2)}, u32[]{:S(2)}) collective-permute-start(bf16[2,4,64,128]{3,2,1,0:T(8,128)(2,1)S(1)} %slice.150), channel_id=1, source_target_pairs={{0,4},{4,0},{8,12},{12,8},{1,5},{5,1},{9,13},{13,9},{2,6},{6,2},{1... | collective-permute-start | bytes 393224 | tf_op jit(solution)/shard_map/ppermute | solution.py:20
  59.5 12.2 %collective-permute-start.6 = (bf16[2,4,64,128]{3,2,1,0:T(8,128)(2,1)S(1)}, bf16[2,4,64,128]{3,2,1,0:T(8,128)(2,1)S(1)}, u32[]{:S(2)}, u32[]{:S(2)}) collective-permute-start(bf16[2,4,64,128]{3,2,1,0:T(8,128)(2,1)S(1)} %rev.11), channel_id=1, source_target_pairs={{0,8},{4,12},{8,0},{12,4},{1,9},{5,13},{9,1},{13,5},{2,10},{6,14},... | collective-permute-start | bytes 393224 | tf_op jit(solution)/shard_map/ppermute | solution.py:20
  62.5 10.9 %collective-permute-start.12 = (bf16[2,4,64,128]{3,2,1,0:T(8,128)(2,1)S(1)}, bf16[2,4,64,128]{3,2,1,0:T(8,128)(2,1)S(1)}, u32[]{:S(2)}, u32[]{:S(2)}) collective-permute-start(bf16[2,4,64,128]{3,2,1,0:T(8,128)(2,1)S(1)} %rev.10), channel_id=1, source_target_pairs={{0,8},{4,12},{8,0},{12,4},{1,9},{5,13},{9,1},{13,5},{2,10},{6,14},... | collective-permute-start | bytes 393224 | tf_op jit(solution)/shard_map/ppermute | solution.py:20
  71.9 6.2 %collective-permute-start.13 = (bf16[2,4,64,128]{3,2,1,0:T(8,128)(2,1)S(1)}, bf16[2,4,64,128]{3,2,1,0:T(8,128)(2,1)S(1)}, u32[]{:S(2)}, u32[]{:S(2)}) collective-permute-start(bf16[2,4,64,128]{3,2,1,0:T(8,128)(2,1)S(1)} %fusion.2.refs_0_), channel_id=1, source_target_pairs={{0,4},{4,0},{8,12},{12,8},{1,5},{5,1},{9,13},{13,9},{2,6},{6,2},{1... | collective-permute-start | bytes 393224 | tf_op jit(solution)/shard_map/ppermute | solution.py:20
  72.5 7.3 %collective-permute-start.14 = (bf16[2,4,64,128]{3,2,1,0:T(8,128)(2,1)S(1)}, bf16[2,4,64,128]{3,2,1,0:T(8,128)(2,1)S(1)}, u32[]{:S(2)}, u32[]{:S(2)}) collective-permute-start(bf16[2,4,64,128]{3,2,1,0:T(8,128)(2,1)S(1)} %fusion.2.refs_0_), channel_id=1, source_target_pairs={{0,1},{1,0},{2,3},{3,2},{4,5},{5,4},{6,7},{7,6},{8,9},{9,8},{10,11... | collective-permute-start | bytes 393224 | tf_op jit(solution)/shard_map/ppermute | solution.py:20
  73.7 6.1 %collective-permute-start.18 = (bf16[2,4,64,128]{3,2,1,0:T(8,128)(2,1)S(1)}, bf16[2,4,64,128]{3,2,1,0:T(8,128)(2,1)S(1)}, u32[]{:S(2)}, u32[]{:S(2)}) collective-permute-start(bf16[2,4,64,128]{3,2,1,0:T(8,128)(2,1)S(1)} %fusion.3.refs_0_), channel_id=1, source_target_pairs={{0,4},{4,0},{8,12},{12,8},{1,5},{5,1},{9,13},{13,9},{2,6},{6,2},{1... | collective-permute-start | bytes 393224 | tf_op jit(solution)/shard_map/ppermute | solution.py:20
  74.3 15.5 %collective-permute-start.19 = (bf16[2,4,64,128]{3,2,1,0:T(8,128)(2,1)S(1)}, bf16[2,4,64,128]{3,2,1,0:T(8,128)(2,1)S(1)}, u32[]{:S(2)}, u32[]{:S(2)}) collective-permute-start(bf16[2,4,64,128]{3,2,1,0:T(8,128)(2,1)S(1)} %fusion.3.refs_0_), channel_id=1, source_target_pairs={{0,1},{1,0},{2,3},{3,2},{4,5},{5,4},{6,7},{7,6},{8,9},{9,8},{10,11... | collective-permute-start | bytes 393224 | tf_op jit(solution)/shard_map/ppermute | solution.py:20
  78.1 1.7 %collective-permute-start.15 = (bf16[2,4,64,128]{3,2,1,0:T(8,128)(2,1)S(1)}, bf16[2,4,64,128]{3,2,1,0:T(8,128)(2,1)S(1)}, u32[]{:S(2)}, u32[]{:S(2)}) collective-permute-start(bf16[2,4,64,128]{3,2,1,0:T(8,128)(2,1)S(1)} %collective-permute-done.13.refs_1_), channel_id=1, source_target_pairs={{0,1},{1,0},{2,3},{3,2},{4,5},{5,4},{6,7},{7,6},{8,9},{9,8},{10,11... | collective-permute-start | bytes 393224 | tf_op jit(solution)/shard_map/ppermute | solution.py:20
  79.8 10.0 %collective-permute-start.20 = (bf16[2,4,64,128]{3,2,1,0:T(8,128)(2,1)S(1)}, bf16[2,4,64,128]{3,2,1,0:T(8,128)(2,1)S(1)}, u32[]{:S(2)}, u32[]{:S(2)}) collective-permute-start(bf16[2,4,64,128]{3,2,1,0:T(8,128)(2,1)S(1)} %collective-permute-done.18.refs_1_), channel_id=1, source_target_pairs={{0,1},{1,0},{2,3},{3,2},{4,5},{5,4},{6,7},{7,6},{8,9},{9,8},{10,11... | collective-permute-start | bytes 393224 | tf_op jit(solution)/shard_map/ppermute | solution.py:20
  79.8 2.5 %copy-start.2 = (bf16[16,2,4,40,512]{4,3,2,1,0:T(8,128)(2,1)S(1)}, bf16[16,2,4,40,512]{4,3,2,1,0:T(8,128)(2,1)}, u32[]{:S(2)}) copy-start(bf16[16,2,4,40,512]{4,3,2,1,0:T(8,128)(2,1)} %copy.9) | copy-start | bytes 15728644
  82.3 2.5 %copy-start.5 = (bf16[2,4,16,40,512]{4,3,2,1,0:T(8,128)(2,1)S(1)}, bf16[2,4,16,40,512]{4,3,2,1,0:T(8,128)(2,1)}, u32[]{:S(2)}) copy-start(bf16[2,4,16,40,512]{4,3,2,1,0:T(8,128)(2,1)} %param.7) | copy-start | bytes 15728644
  89.2 5.8 %collective-permute-start.16 = (bf16[2,16,128,128]{3,2,1,0:T(8,128)(2,1)S(1)}, bf16[2,16,128,128]{3,2,1,0:T(8,128)(2,1)S(1)}, u32[]{:S(2)}, u32[]{:S(2)}) collective-permute-start(bf16[2,16,128,128]{3,2,1,0:T(8,128)(2,1)S(1)} %get-tuple-element.15), channel_id=1, source_target_pairs={{0,1},{1,0},{2,3},{3,2},{4,5},{5,4},{6,7},{7,6},{8,9},{9,8},{10,11... | collective-permute-start | bytes 3145736 | tf_op jit(solution)/shard_map/ppermute | solution.py:20
  94.1 3.2 %collective-permute-start.21 = (bf16[2,16,128,128]{3,2,1,0:T(8,128)(2,1)S(1)}, bf16[2,16,128,128]{3,2,1,0:T(8,128)(2,1)S(1)}, u32[]{:S(2)}, u32[]{:S(2)}) collective-permute-start(bf16[2,16,128,128]{3,2,1,0:T(8,128)(2,1)S(1)} %get-tuple-element.17), channel_id=1, source_target_pairs={{0,1},{1,0},{2,3},{3,2},{4,5},{5,4},{6,7},{7,6},{8,9},{9,8},{10,11... | collective-permute-start | bytes 3145736 | tf_op jit(solution)/shard_map/ppermute | solution.py:20
  95.5 14.8 %collective-permute-start.17 = (bf16[16,128,128]{2,1,0:T(8,128)(2,1)S(1)}, bf16[16,128,128]{2,1,0:T(8,128)(2,1)S(1)}, u32[]{:S(2)}, u32[]{:S(2)}) collective-permute-start(bf16[16,128,128]{2,1,0:T(8,128)(2,1)S(1)} %fusion), channel_id=1, source_target_pairs={{0,2},{2,0},{1,3},{3,1},{4,6},{6,4},{5,7},{7,5},{8,10},{10,8},{9,1... | collective-permute-start | bytes 1572872 | tf_op jit(solution)/shard_map/ppermute | solution.py:20
  97.7 23.5 %collective-permute-start.22 = (bf16[16,128,128]{2,1,0:T(8,128)(2,1)S(1)}, bf16[16,128,128]{2,1,0:T(8,128)(2,1)S(1)}, u32[]{:S(2)}, u32[]{:S(2)}) collective-permute-start(bf16[16,128,128]{2,1,0:T(8,128)(2,1)S(1)} %fusion.1), channel_id=1, source_target_pairs={{0,2},{2,0},{1,3},{3,1},{4,6},{6,4},{5,7},{7,5},{8,10},{10,8},{9,1... | collective-permute-start | bytes 1572872 | tf_op jit(solution)/shard_map/ppermute | solution.py:20

commit v3 on v0

v3 whole, which is shorter than its diff:
```python
import functools

import jax
import jax.numpy as jnp
from jax import lax
from jax.experimental import pallas as pl
from jax.experimental.pallas import tpu as pltpu
from jax.sharding import PartitionSpec as P

BF16 = jnp.bfloat16
F32 = jnp.float32
CHUNKS = 2
LANES = 128
VM = pl.BlockSpec(memory_space=pltpu.VMEM)
SM = pl.BlockSpec(memory_space=pltpu.SMEM)
ANY = pl.BlockSpec(memory_space=pl.ANY)
MIB = 1024 * 1024
LARGE = 10**10
SPLIT = 2


def call(kernel, name, outs, ins, in_specs=None, scratch=(), limit=6 * MIB, cost=10**6):
    return pl.pallas_call(
        kernel,
        out_shape=[jax.ShapeDtypeStruct(shape, kind) for shape, kind in outs],
        in_specs=in_specs or [VM] * len(ins),
        out_specs=[VM] * len(outs),
        scratch_shapes=list(scratch),
        compiler_params=pltpu.CompilerParams(vmem_limit_bytes=limit),
        cost_estimate=pl.CostEstimate(flops=cost, bytes_accessed=10**4, transcendentals=0),
        name=name,
    )(*ins)


def swap(axis_name, step, value):
    size = lax.axis_size(axis_name)
    return lax.ppermute(value, axis_name, [(i, i ^ step) for i in range(size)])


def after(value, *earlier):
    return lax.optimization_barrier((value, *earlier))[0]


def turn(value, first, second):
    width = value.shape[-1]
    lane = lax.broadcasted_iota(jnp.int32, value.shape, value.ndim - 1)
    sign = jnp.where(lane < width // 2, first, second).astype(F32)
    return pltpu.roll(value, width // 2, value.ndim - 1) * sign


def waves_kernel(source, *outs):
    part = source.shape[-1] // len(outs)
    for j in range(source.shape[1]):
        for c, out in enumerate(outs):
            lanes = slice(c * part, (c + 1) * part)
            out[j] = jnp.concatenate([source[0, j, :, lanes], source[1, j, :, lanes]], -1)


def load_kernel(second_in, basis_in, second, basis, sems):
    rows = second_in.shape[1]
    copies = []
    for p in range(2):
        for i in range(rows):
            n = p * rows + i
            copies.append(pltpu.make_async_copy(second_in.at[p, i], second.at[:, n], sems.at[0, n]))
            copies.append(pltpu.make_async_copy(basis_in.at[p, i], basis.at[p, i], sems.at[1, n]))
    for copy in copies:
        copy.start()
    for copy in copies:
        copy.wait()


def halve_kernel(mine, other, keep, send):
    n = keep.shape[0]
    keep[...] = mine[:n] + other[:n].astype(F32)
    send[...] = (mine[n:] + other[n:].astype(F32)).astype(BF16)


def mirror_kernel(mine, other, keep, send):
    total = mine[...] + other[...].astype(F32)
    keep[...] = total
    n = keep.shape[0]
    for e in range(n):
        send[e] = total[n - 1 - e].astype(BF16)


def residual_kernel(c, mine, other, *refs):
    observed, amplitude, out = refs[:2], refs[2:4], refs[4]
    part = out.shape[-1] // 2
    lanes = slice(c * part, (c + 1) * part)
    for e in range(2):
        total = mine[e] + other[e].astype(F32)
        data = jnp.concatenate([observed[e][0, :, :, lanes], observed[e][1, :, :, lanes]], -1)
        weight = jnp.concatenate([amplitude[e][:, :, lanes]] * 2, -1)
        out[e] = (weight.astype(F32) * (total - data.astype(F32))).astype(BF16)


def join_kernel(*refs):
    out = refs[-1]
    part = out.shape[-1] // (len(refs) - 1)
    for p in range(2):
        out[p] = jnp.concatenate([ref[0, :, :, p * part : (p + 1) * part] for ref in refs[:-1]], -1)


def share_kernel(mine, *refs):
    others, out = refs[:-1], refs[-1]
    n = out.shape[0] // len(others)
    for k, other in enumerate(others):
        out[k * n : (k + 1) * n] = (mine[k * n : (k + 1) * n] + other[...].astype(F32)).astype(BF16)


def total_kernel(mine, *refs):
    others, out = refs[:-1], refs[-1]
    first, rest = others[:SPLIT], others[SPLIT:]
    n = out.shape[0] // len(first)
    for k, other in enumerate(first):
        total = mine[k * n : (k + 1) * n] + other[...].astype(F32)
        for ref in rest:
            total = total + ref[k * n : (k + 1) * n].astype(F32)
        out[k * n : (k + 1) * n] = total


def final_kernel(*refs):
    *done, mine = refs[: CHUNKS]
    others, out_ref = refs[CHUNKS:-1], refs[-1]
    first, rest = others[:SPLIT], others[SPLIT:]
    part = mine.shape[1] // 2
    n = mine.shape[0] // SPLIT
    for j in range(out_ref.shape[1]):
        for p in range(2):
            lanes = slice(p * part, (p + 1) * part)
            total = mine[j, lanes, :] + first[j // n][j % n, lanes, :].astype(F32)
            for ref in rest:
                total = total + ref[j, lanes, :].astype(F32)
            pieces = [ref[j, lanes, :] for ref in done] + [total]
            out_ref[p, j] = jnp.concatenate(pieces, 0).T.astype(out_ref.dtype)


def forward_kernel(rs, helps, z_offsets, ranks, *refs):
    n_pieces = rs * helps
    pieces = refs[:n_pieces]
    second, basis, keep_out, send_out, waves, coef, fwd = refs[n_pieces:]
    z, r, here = lax.axis_index("col"), lax.axis_index("row"), lax.axis_index("help")
    columns, quarter, width = pieces[0].shape
    rows = basis.shape[1]
    terms = second.shape[1] // (2 * rows)
    half = rows * terms
    row_index = lax.broadcasted_iota(jnp.int32, (terms, width), 0)
    for j in range(columns):
        for n, piece in enumerate(pieces):
            spot = (r ^ (n % rs)) * helps + (here ^ (n // rs))
            waves[j, pl.ds(pl.multiple_of(spot * quarter, quarter), quarter), :] = piece[j]
        out = jnp.dot(second[j], waves[j], preferred_element_type=F32)
        value = out[:half] + turn(out[half:], 1.0, -1.0)
        for i in range(rows):
            left = ranks[i, j] - here * terms
            part = value[i * terms : (i + 1) * terms]
            coef[i, j * terms : (j + 1) * terms, :] = jnp.where(row_index < left, part, 0.0)
    _, _, span, _ = keep_out.shape
    dims = (((0,), (0,)), ((), ()))
    for i in range(rows):
        value = coef[i]
        turned = turn(value, -1.0, 1.0)
        out = lax.dot_general(value.astype(BF16), basis[0, i], dims, preferred_element_type=F32)
        out = out + lax.dot_general(turned.astype(BF16), basis[1, i], dims, preferred_element_type=F32)
        fwd[i] = out.T
        for n, offset in enumerate(z_offsets):
            block = (z ^ offset) * helps
            at = pl.multiple_of((block + here) * span, span)
            keep_out[n, i] = fwd[i, pl.ds(at, span), :].astype(keep_out.dtype)
            at = pl.multiple_of((block + 1 - here) * span, span)
            send_out[n, i] = fwd[i, pl.ds(at, span), :].astype(send_out.dtype)


def adjoint_kernel(rs, helps, spots, ranks, *refs):
    n_pieces = len(spots)
    pieces, (basis, second) = refs[:n_pieces], refs[n_pieces : n_pieces + 2]
    keeps, sends = refs[n_pieces + 2 : n_pieces + 2 + rs], refs[n_pieces + 2 + rs : -2]
    resid, back = refs[-2:]
    z, r, here = lax.axis_index("col"), lax.axis_index("row"), lax.axis_index("help")
    blocks, rows, span, width = pieces[0].shape
    columns = second.shape[0]
    terms = second.shape[1] // (2 * rows)
    row_index = lax.broadcasted_iota(jnp.int32, (terms, width), 0)
    for i in range(rows):
        for piece, (z_offsets, h_offset) in zip(pieces, spots):
            for e, offset in enumerate(z_offsets):
                spot = (z ^ offset) * helps + (here ^ h_offset)
                resid[i, pl.ds(pl.multiple_of(spot * span, span), span), :] = piece[e, i]
        value = resid[i]
        turned = turn(value.astype(F32), 1.0, -1.0).astype(BF16)
        out = jnp.dot(basis[0, i], value, preferred_element_type=F32)
        out = out + jnp.dot(basis[1, i], turned, preferred_element_type=F32)
        for j in range(columns):
            left = ranks[i, j] - here * terms
            part = out[j * terms : (j + 1) * terms]
            back[j, i * terms : (i + 1) * terms, :] = jnp.where(row_index < left, part, 0.0)
    quarter = keeps[0].shape[2]

    def keep(d, j, value):
        keeps[d][j] = value

    def send(d, j, value):
        refs = sends[d * SPLIT : (d + 1) * SPLIT]
        n = refs[0].shape[0]
        refs[j // n][j % n] = value.astype(BF16)

    for j in range(columns):
        value = back[j]
        left = jnp.concatenate([value, turn(value, -1.0, 1.0)], 0).T.astype(BF16)
        if quarter % LANES == 0:
            for put, h in ((keep, here), (send, 1 - here)):
                for d in range(rs):
                    at = pl.multiple_of(((r ^ d) * helps + h) * quarter, quarter)
                    out = jnp.dot(left, second[j, :, pl.ds(at, quarter)], preferred_element_type=F32)
                    put(d, j, out)
        else:
            out = jnp.dot(left, second[j], preferred_element_type=F32)
            for n in range(rs):
                for h in range(helps):
                    part = out[:, (n * helps + h) * quarter : (n * helps + h + 1) * quarter]
                    for d in range(rs):
                        pl.when((here == h) & (n ^ r == d))(functools.partial(keep, d, j, part))
                        pl.when((here != h) & (n ^ r == d))(functools.partial(send, d, j, part))


def body(wavefield, basis_factor, second_factor, tile_ranks, observed, amplitude):
    _, columns, quarter, rhs = wavefield.shape
    _, rows, _, terms, tile = basis_factor.shape
    span = observed.shape[2]
    zs, rs, helps = lax.axis_size("col"), lax.axis_size("row"), lax.axis_size("help")
    width = 2 * rhs // CHUNKS
    bits = zs.bit_length() - 1
    far = zs // 2
    near = [1 << b for b in range(bits - 1)]
    z_offsets = [int(format(n, f"0{bits}b")[::-1], 2) for n in range(zs)]

    def share(pieces):
        return pieces + [swap("help", d, m) for d in range(1, helps) for m in pieces]

    waves = call(
        waves_kernel, "split_waves", [((columns, quarter, width), BF16)] * CHUNKS, [wavefield]
    )
    gathered = [[w] + [swap("row", d, w) for d in range(1, rs)] for w in waves]
    data = [observed, swap("col", far, observed), amplitude, swap("col", far, amplitude)]
    second, basis = call(
        load_kernel,
        "load_factors",
        [((columns, 2 * rows, terms, tile), BF16), ((2, rows, columns, terms, tile), BF16)],
        [second_factor, basis_factor],
        in_specs=[pl.BlockSpec(memory_space=pltpu.HBM)] * 2,
        scratch=[pltpu.SemaphoreType.DMA((2, 2 * rows))],
        cost=LARGE,
    )
    second = second.reshape(columns, 2 * rows * terms, tile)
    basis = basis.reshape(2, rows, columns * terms, tile)

    def forward(c, mine):
        shape = (zs, rows, span, width)
        pieces = share(mine)
        return call(
            functools.partial(forward_kernel, rs, helps, z_offsets),
            "forward_product",
            [(shape, F32), (shape, BF16)],
            [tile_ranks, *pieces, second, basis],
            in_specs=[SM] + [VM] * (len(pieces) + 2),
            scratch=[
                pltpu.VMEM((columns, tile, width), BF16),
                pltpu.VMEM((rows, columns * terms, width), F32),
                pltpu.VMEM((rows, tile, width), F32),
            ],
            limit=16 * MIB,
            cost=LARGE if c else 1,
        )

    def backward(pieces, spots):
        whole, piece = (columns, width, quarter), (columns // SPLIT, width, quarter)
        outs = call(
            functools.partial(adjoint_kernel, rs, helps, spots),
            "adjoint_product",
            [(whole, F32)] * rs + [(piece, BF16)] * (rs * SPLIT),
            [tile_ranks, *pieces, basis, second],
            in_specs=[SM] + [VM] * (len(pieces) + 2),
            scratch=[
                pltpu.VMEM((rows, tile, width), BF16),
                pltpu.VMEM((columns, rows * terms, width), F32),
            ],
            limit=16 * MIB,
            cost=LARGE,
        )
        sends = outs[rs:]
        return outs[:rs], [sends[d * SPLIT : (d + 1) * SPLIT] for d in range(rs)]

    halved, mirrored, residuals, shared, totals = [], [], [], [], []

    def front(c):
        earlier = (halved[-1],) if c else (second, data[1], data[3])
        mine = [gathered[c][0]] + [after(m, *earlier) for m in gathered[c][1:]]
        if c:
            mine[0] = after(mine[0], mirrored[-1][1])
        keep, send = forward(c, mine)
        if c:
            residual_of(c - 1, send)
            keep = after(keep, residuals[c - 1])
        other = swap("help", 1, send)
        for d in near:
            shape = (keep.shape[0] // 2, rows, span, width)
            keep, send = call(
                halve_kernel, "halve", [(shape, F32), (shape, BF16)], [keep, other], cost=LARGE if c else 1
            )
            other = swap("col", d, send)
        halved.append(send)
        mirrored.append(call(mirror_kernel, "mirror", [(shape, F32), (shape, BF16)], [keep, other]))

    def residual_of(c, *earlier):
        keep, send = mirrored[c]
        residuals.extend(
            call(
                functools.partial(residual_kernel, c),
                "residual",
                [((2, rows, span, width), BF16)],
                [after(keep, *earlier), swap("col", far, send), *data],
                cost=LARGE,
            )
        )

    def rear(c):
        pieces, offsets = [residuals[c]], [0]
        for d in reversed(near):
            pieces = pieces + [swap("col", d, m) for m in pieces]
            offsets = offsets + [o ^ d for o in offsets]
        pieces = share(pieces)
        spots = [((o, o ^ far), e) for e in range(helps) for o in offsets]
        last = c + 1 == CHUNKS
        pieces[0] = after(pieces[0], *(shared[-1] if last else [mirrored[c + 1][1]]))
        keeps, sends = backward(pieces, spots)
        if not last:
            residual_of(c + 1, sends[-1][-1])
            keeps = [keeps[0]] + [after(k, residuals[c + 1]) for k in keeps[1:]]
        shape = (columns, width, quarter)
        shared.append(
            [
                call(
                    share_kernel, "adjoint_share", [(shape, BF16)], [k, *[swap("help", 1, m) for m in s]]
                )[0]
                for k, s in zip(keeps[1:], sends[1:])
            ]
        )
        if last:
            totals[-1] = [after(totals[-1][0], *shared[-1])] + totals[-1][1:]
            totals[-1] = call(total_kernel, "total", [(shape, F32)], totals[-1], cost=LARGE)
        totals.append(
            [keeps[0], *[swap("help", 1, m) for m in sends[0]]]
            + [swap("row", d + 1, m) for d, m in enumerate(shared[-1])]
        )

    for c in range(CHUNKS):
        front(c)
    for c in range(CHUNKS):
        rear(c)

    residual = call(join_kernel, "join", [(observed.shape, BF16)], residuals, cost=LARGE)[0]
    adjoint = call(
        final_kernel, "adjoint_sum", [(wavefield.shape, BF16)], [*totals[0], *totals[1]]
    )[0]
    return residual, adjoint


def solution(mesh):
    return jax.shard_map(
        body,
        mesh=mesh,
        in_specs=(
            P("freq", "col", ("row", "help"), None),
            P("freq", "row", "col", "help", None),
            P("freq", "row", "col", "help", None),
            P(("freq", "row"), "col"),
            P("freq", "row", ("col", "help"), None),
            P(("freq", "row"), ("col", "help"), None),
        ),
        out_specs=(
            P("freq", "row", ("col", "help"), None),
            P("freq", "col", ("row", "help"), None),
        ),
        check_vma=False,
    )
```

time: 238 us -> 92.1 us (0.39)
  waiting for transfers between devices: 183 us -> 39.6 us
  starting transfers between devices: 0.34 us -> 23.6 us
  Pallas kernels: 0 us -> 21.7 us
  other arithmetic: 16.1 us -> 0 us
  matrix products: 15.5 us -> 0 us
  between operations: 14.1 us -> 0.83 us
    reduce_scatter x1 -> x0, waiting for transfers between devices: 70.6 us -> none  [body(): lax.psum_scatter(adjoint_terms, ('row', 'help'), scatter_dimension=2, til...]
    psum x1 -> x0, waiting for transfers between devices: 64.3 us -> none  [body(): total = lax.psum(partial_value, ('col', 'help'))]
    all_gather x2 -> x0, waiting for transfers between devices: 48.2 us -> none  [the longest x1 36.5 us: body(): piece = lax.all_gather(wavefield, ('row', 'help'), axis=2, tiled=True)]
    ppermute x0 -> x30, waiting for transfers between devices: none -> 39.6 us  [swap(): return lax.ppermute(value, axis_name, [(i, i ^ step) for i in range(size)])]
    ppermute x0 -> x30, starting transfers between devices: none -> 23.6 us  [swap(): return lax.ppermute(value, axis_name, [(i, i ^ step) for i in range(size)])]
    pallas_call x0 -> x17, Pallas kernels: none -> 21.7 us  [call(): pl.pallas_call(kernel, out_shape=[jax.ShapeDtypeStruct(shape, kind) for s...]
    dot_general x8 -> x0, matrix products: 15.5 us -> none  [the longest x1 4.18 us: body(): jnp.einsum('pijks,pisn->ijkn', block, full, preferred_element_type=jnp.fl...]
    another operation x3 -> x0, other arithmetic: 6.13 us -> none  [the longest x1 4.29 us: body(): adjoint_terms = jnp.stack([adjoint_real, adjoint_imag])]
  transfers between devices with their start and end apart: 4 -> 30, of which waited for: 4 -> 14; matrix products, arithmetic and copies ran while one was open for 7% -> 0% of each run, Pallas kernels for 0% -> 22%
where the time goes in v3:
time: 92.1 us; the launch traced here: 91.9 us
  waiting for transfers between devices  39.6 us (43%)
  starting transfers between devices  23.6 us (26%)
  Pallas kernels  21.7 us (24%)
  local copies, waits for them, and re-layouts  6.21 us (7%)
    ppermute x30, waiting for transfers between devices, swap(): return lax.ppermute(value, axis_name, [(i, i ^ step) for i in range(size)])  39.6 us
    ppermute x30, starting transfers between devices, swap(): return lax.ppermute(value, axis_name, [(i, i ^ step) for i in range(size)])  23.6 us
    pallas_call x17, Pallas kernels, call(): pl.pallas_call(kernel, out_shape=[jax.ShapeDtypeStruct(shape, kind) for s...  21.7 us
    unnamed x12, local copies, waits for them, and re-layouts  6.21 us
  transfers between devices with their start and end apart: 30, of which 14 were waited for; matrix products, arithmetic and copies ran while one was open for 0% of the time, Pallas kernels for 22%

profile of v3, /device:TPU:0, one launch (start us, length us, event | category | flops | bytes accessed | tf_op | source)
XLA Modules:
  0.0 91.9 jit_solution(14711972323220142776)
XLA Ops:
  0.6 1.2 %copy-done = bf16[2,16,128,128]{3,2,1,0:T(8,128)(2,1)S(1)} copy-done((bf16[2,16,128,128]{3,2,1,0:T(8,128)(2,1)S(1)}, bf16[2,16,128,128]{3,2,1,0:T(8,128)(2,1)}, u32[]{:S(2)}) %copy-start) | copy-done | bytes 1048600
  1.9 0.3 split_waves.1
  2.2 0.5 collective-permute-start.3
  2.7 2.6 %collective-permute-start = (bf16[16,128,128]{2,1,0:T(8,128)(2,1)S(1)}, bf16[16,128,128]{2,1,0:T(8,128)(2,1)S(1)}, u32[]{:S(2)}, u32[]{:S(2)}) collective-permute-start(bf16[16,128,128]{2,1,0:T(8,128)(2,1)S(1)} %get-tuple-element.40.refs_0_), channel_id=1, source_target_pairs={{0,2},{2,0},{1,3},{3,1},{4,6},{6,4},{5,7},{7,5},{8,10},{10,8},{9,1... | collective-permute-start | bytes 1572872 | tf_op jit(solution)/shard_map/ppermute | solution.py:37
  5.3 2.6 %collective-permute-start.2 = (bf16[4,64,128]{2,1,0:T(8,128)(2,1)}, bf16[4,64,128]{2,1,0:T(8,128)(2,1)S(1)}, u32[]{:S(2)}, u32[]{:S(2)}) collective-permute-start(bf16[4,64,128]{2,1,0:T(8,128)(2,1)} %refs_2_.3), channel_id=1, source_target_pairs={{0,8},{4,12},{8,0},{12,4},{1,9},{5,13},{9,1},{13,5},{2,10},{6,14},... | collective-permute-start | bytes 196616 | tf_op jit(solution)/shard_map/ppermute | solution.py:37
  7.9 0.3 collective-permute-start.1
  8.2 2.5 %copy-done.2 = bf16[2,4,16,40,512]{4,3,2,1,0:T(8,128)(2,1)S(1)} copy-done((bf16[2,4,16,40,512]{4,3,2,1,0:T(8,128)(2,1)S(1)}, bf16[2,4,16,40,512]{4,3,2,1,0:T(8,128)(2,1)}, u32[]{:S(2)}) %copy-start.2) | copy-done | bytes 5242904
  10.7 2.5 %copy-done.3 = bf16[2,4,16,40,512]{4,3,2,1,0:T(8,128)(2,1)S(1)} copy-done((bf16[2,4,16,40,512]{4,3,2,1,0:T(8,128)(2,1)S(1)}, bf16[2,4,16,40,512]{4,3,2,1,0:T(8,128)(2,1)}, u32[]{:S(2)}) %copy-start.3) | copy-done | bytes 5242904
  13.2 2.2 %load_factors.1 = (bf16[16,8,40,512]{3,2,1,0:T(8,128)(2,1)S(1)}, bf16[2,4,16,40,512]{4,3,2,1,0:T(8,128)(2,1)S(1)}) custom-call(bf16[2,4,16,40,512]{4,3,2,1,0:T(8,128)(2,1)S(1)} %copy-done.2, bf16[2,4,16,40,512]{4,3,2,1,0:T(8,128)(2,1)S(1)} %copy-done.3), custom_call_target="tpu_custom_call" | custom-call | flops 10000000000 | bytes 10000 | tf_op jit(solution)/shard_map/load_factors/pallas_call | solution.py:23
  15.4 2.3 %collective-permute-done.1.refs_1_ = bf16[2,4,64,128]{3,2,1,0:T(8,128)(2,1)S(1)} collective-permute-done((bf16[2,4,64,128]{3,2,1,0:T(8,128)(2,1)}, bf16[2,4,64,128]{3,2,1,0:T(8,128)(2,1)S(1)}, u32[]{:S(2)}, u32[]{:S(2)}) %collective-permute-start.1) | collective-permute-done | bytes 131104 | tf_op jit(solution)/shard_map/ppermute | solution.py:37
  17.8 1.8 %collective-permute-start.7 = (bf16[16,128,128]{2,1,0:T(8,128)(2,1)S(1)}, bf16[16,128,128]{2,1,0:T(8,128)(2,1)S(1)}, u32[]{:S(2)}, u32[]{:S(2)}) collective-permute-start(bf16[16,128,128]{2,1,0:T(8,128)(2,1)S(1)} %get-tuple-element.51.refs_0_), channel_id=1, source_target_pairs={{0,2},{2,0},{1,3},{3,1},{4,6},{6,4},{5,7},{7,5},{8,10},{10,8},{9,1... | collective-permute-start | bytes 1572872 | tf_op jit(solution)/shard_map/ppermute | solution.py:37
  19.6 0.1 collective-permute-done.4.refs_3_
  19.7 3.7 %forward_product.2 = (f32[4,4,64,128]{3,2,1,0:T(8,128)S(1)}, bf16[4,4,64,128]{3,2,1,0:T(8,128)(2,1)S(1)}) custom-call(s32[4,16]{1,0:T(4,128)S(1)} %copy-done.1, bf16[16,128,128]{2,1,0:T(8,128)(2,1)S(1)} %get-tuple-element.40.refs_0_, bf16[16,128,128]{2,1,0:T(8,128)(2,1)S(1)} %collective-permute-done.refs_1_, ...), custom_call_target="tpu_custom_call" | custom-call | flops 1 | bytes 10000 | tf_op jit(solution)/shard_map/forward_product/pallas_call | solution.py:23
  23.4 0.2 collective-permute-start.5
  23.6 1.4 %collective-permute-done.5.other = bf16[4,4,64,128]{3,2,1,0:T(8,128)(2,1)S(1)} collective-permute-done((bf16[4,4,64,128]{3,2,1,0:T(8,128)(2,1)S(1)}, bf16[4,4,64,128]{3,2,1,0:T(8,128)(2,1)S(1)}, u32[]{:S(2)}, u32[]{:S(2)}) %collective-permute-start.5) | collective-permute-done | bytes 262176 | tf_op jit(solution)/shard_map/ppermute | solution.py:37
  25.1 1.9 %collective-permute-start.6 = (bf16[2,4,64,128]{3,2,1,0:T(8,128)(2,1)S(1)}, bf16[2,4,64,128]{3,2,1,0:T(8,128)(2,1)S(1)}, u32[]{:S(2)}, u32[]{:S(2)}) collective-permute-start(bf16[2,4,64,128]{3,2,1,0:T(8,128)(2,1)S(1)} %get-tuple-element.47), channel_id=1, source_target_pairs={{0,4},{4,0},{8,12},{12,8},{1,5},{5,1},{9,13},{13,9},{2,6},{6,2},{1... | collective-permute-start | bytes 393224 | tf_op jit(solution)/shard_map/ppermute | solution.py:37
  27.0 5.1 %collective-permute-done.7.refs_1_ = bf16[16,128,128]{2,1,0:T(8,128)(2,1)S(1)} collective-permute-done((bf16[16,128,128]{2,1,0:T(8,128)(2,1)S(1)}, bf16[16,128,128]{2,1,0:T(8,128)(2,1)S(1)}, u32[]{:S(2)}, u32[]{:S(2)}) %collective-permute-start.7) | collective-permute-done | bytes 524320 | tf_op jit(solution)/shard_map/ppermute | solution.py:37
  32.2 0.6 collective-permute-start.8
  32.8 2.8 %collective-permute-start.10 = (bf16[2,4,64,128]{3,2,1,0:T(8,128)(2,1)S(1)}, bf16[2,4,64,128]{3,2,1,0:T(8,128)(2,1)S(1)}, u32[]{:S(2)}, u32[]{:S(2)}) collective-permute-start(bf16[2,4,64,128]{3,2,1,0:T(8,128)(2,1)S(1)} %get-tuple-element.50), channel_id=1, source_target_pairs={{0,8},{4,12},{8,0},{12,4},{1,9},{5,13},{9,1},{13,5},{2,10},{6,14},... | collective-permute-start | bytes 393224 | tf_op jit(solution)/shard_map/ppermute | solution.py:37
  35.6 3.7 %forward_product.3 = (f32[4,4,64,128]{3,2,1,0:T(8,128)S(1)}, bf16[4,4,64,128]{3,2,1,0:T(8,128)(2,1)S(1)}) custom-call(s32[4,16]{1,0:T(4,128)S(1)} %copy-done.1, bf16[16,128,128]{2,1,0:T(8,128)(2,1)S(1)} %get-tuple-element.51.refs_0_, bf16[16,128,128]{2,1,0:T(8,128)(2,1)S(1)} %collective-permute-done.7.refs_1_, ...), custom_call_target="tpu_custom_call" | custom-call | flops 10000000000 | bytes 10000 | tf_op jit(solution)/shard_map/forward_product/pallas_call | solution.py:23
  39.5 2.7 %collective-permute-done.10.other = bf16[2,4,64,128]{3,2,1,0:T(8,128)(2,1)S(1)} collective-permute-done((bf16[2,4,64,128]{3,2,1,0:T(8,128)(2,1)S(1)}, bf16[2,4,64,128]{3,2,1,0:T(8,128)(2,1)S(1)}, u32[]{:S(2)}, u32[]{:S(2)}) %collective-permute-start.10) | collective-permute-done | bytes 131104 | tf_op jit(solution)/shard_map/ppermute | solution.py:37
  42.2 0.1 residual.2.refs_0_
  42.3 0.8 collective-permute-start.13
  43.2 1.4 %collective-permute-start.12 = (bf16[2,4,64,128]{3,2,1,0:T(8,128)(2,1)S(1)}, bf16[2,4,64,128]{3,2,1,0:T(8,128)(2,1)S(1)}, u32[]{:S(2)}, u32[]{:S(2)}) collective-permute-start(bf16[2,4,64,128]{3,2,1,0:T(8,128)(2,1)S(1)} %get-tuple-element.58), channel_id=1, source_target_pairs={{0,4},{4,0},{8,12},{12,8},{1,5},{5,1},{9,13},{13,9},{2,6},{6,2},{1... | collective-permute-start | bytes 393224 | tf_op jit(solution)/shard_map/ppermute | solution.py:37
  44.6 4.1 %collective-permute-done.13.refs_1_ = bf16[2,4,64,128]{3,2,1,0:T(8,128)(2,1)S(1)} collective-permute-done((bf16[2,4,64,128]{3,2,1,0:T(8,128)(2,1)S(1)}, bf16[2,4,64,128]{3,2,1,0:T(8,128)(2,1)S(1)}, u32[]{:S(2)}, u32[]{:S(2)}) %collective-permute-start.13) | collective-permute-done | bytes 131104 | tf_op jit(solution)/shard_map/ppermute | solution.py:37
  48.7 1.4 %collective-permute-done.12.other = bf16[2,4,64,128]{3,2,1,0:T(8,128)(2,1)S(1)} collective-permute-done((bf16[2,4,64,128]{3,2,1,0:T(8,128)(2,1)S(1)}, bf16[2,4,64,128]{3,2,1,0:T(8,128)(2,1)S(1)}, u32[]{:S(2)}, u32[]{:S(2)}) %collective-permute-start.12) | collective-permute-done | bytes 131104 | tf_op jit(solution)/shard_map/ppermute | solution.py:37
  50.1 3.0 %collective-permute-start.16 = (bf16[2,4,64,128]{3,2,1,0:T(8,128)(2,1)S(1)}, bf16[2,4,64,128]{3,2,1,0:T(8,128)(2,1)S(1)}, u32[]{:S(2)}, u32[]{:S(2)}) collective-permute-start(bf16[2,4,64,128]{3,2,1,0:T(8,128)(2,1)S(1)} %get-tuple-element.60), channel_id=1, source_target_pairs={{0,8},{4,12},{8,0},{12,4},{1,9},{5,13},{9,1},{13,5},{2,10},{6,14},... | collective-permute-start | bytes 393224 | tf_op jit(solution)/shard_map/ppermute | solution.py:37
  53.1 4.3 %adjoint_product.2 = (f32[16,128,128]{2,1,0:T(8,128)S(1)}, f32[16,128,128]{2,1,0:T(8,128)S(1)}, bf16[8,128,128]{2,1,0:T(8,128)(2,1)S(1)}, bf16[8,128,128]{2,1,0:...) custom-call(s32[4,16]{1,0:T(4,128)S(1)} %copy-done.1, ...), custom_call_target="tpu_custom_call" | custom-call | flops 10000000000 | bytes 10000 | tf_op jit(solution)/shard_map/adjoint_product/pallas_call | solution.py:23
  57.5 0.5 collective-permute-start.17
  58.0 1.1 %collective-permute-done.16.other = bf16[2,4,64,128]{3,2,1,0:T(8,128)(2,1)S(1)} collective-permute-done((bf16[2,4,64,128]{3,2,1,0:T(8,128)(2,1)S(1)}, bf16[2,4,64,128]{3,2,1,0:T(8,128)(2,1)S(1)}, u32[]{:S(2)}, u32[]{:S(2)}) %collective-permute-start.16) | collective-permute-done | bytes 131104 | tf_op jit(solution)/shard_map/ppermute | solution.py:37
  59.1 0.1 residual.3.refs_1_.refs_0_
  59.2 0.7 collective-permute-start.19
  60.0 4.3 %collective-permute-done.19.refs_1_ = bf16[2,4,64,128]{3,2,1,0:T(8,128)(2,1)S(1)} collective-permute-done((bf16[2,4,64,128]{3,2,1,0:T(8,128)(2,1)S(1)}, bf16[2,4,64,128]{3,2,1,0:T(8,128)(2,1)S(1)}, u32[]{:S(2)}, u32[]{:S(2)}) %collective-permute-start.19) | collective-permute-done | bytes 131104 | tf_op jit(solution)/shard_map/ppermute | solution.py:37
  64.3 0.5 collective-permute-start.24
  64.9 1.6 %collective-permute-start.26 = (bf16[16,128,128]{2,1,0:T(8,128)(2,1)S(1)}, bf16[16,128,128]{2,1,0:T(8,128)(2,1)S(1)}, u32[]{:S(2)}, u32[]{:S(2)}) collective-permute-start(bf16[16,128,128]{2,1,0:T(8,128)(2,1)S(1)} %adjoint_share.2), channel_id=1, source_target_pairs={{0,2},{2,0},{1,3},{3,1},{4,6},{6,4},{5,7},{7,5},{8,10},{10,8},{9,1... | collective-permute-start | bytes 1572872 | tf_op jit(solution)/shard_map/ppermute | solution.py:37
  66.5 4.5 %adjoint_product.3 = (f32[16,128,128]{2,1,0:T(8,128)S(1)}, f32[16,128,128]{2,1,0:T(8,128)S(1)}, bf16[8,128,128]{2,1,0:T(8,128)(2,1)S(1)}, bf16[8,128,128]{2,1,0:...) custom-call(s32[4,16]{1,0:T(4,128)S(1)} %copy-done.1, ...), custom_call_target="tpu_custom_call" | custom-call | flops 10000000000 | bytes 10000 | tf_op jit(solution)/shard_map/adjoint_product/pallas_call | solution.py:23
  70.9 0.3 collective-permute-start.22
  71.2 0.3 collective-permute-start.23
  71.5 0.8 join.1
  72.3 0.3 collective-permute-done.22.refs_0_
  72.5 0.2 collective-permute-start.27
  72.8 0.2 collective-permute-done.23.refs_1_
  72.9 0.2 collective-permute-start.28
  73.3 0.7 collective-permute-start.29
  73.9 5.8 %collective-permute-done.26.refs_2_ = bf16[16,128,128]{2,1,0:T(8,128)(2,1)S(1)} collective-permute-done((bf16[16,128,128]{2,1,0:T(8,128)(2,1)S(1)}, bf16[16,128,128]{2,1,0:T(8,128)(2,1)S(1)}, u32[]{:S(2)}, u32[]{:S(2)}) %collective-permute-start.26) | collective-permute-done | bytes 524320 | tf_op jit(solution)/shard_map/ppermute | solution.py:37
  79.7 0.1 total.1.refs_0_
  79.8 10.7 %collective-permute-done.29.refs_4_ = bf16[16,128,128]{2,1,0:T(8,128)(2,1)S(1)} collective-permute-done((bf16[16,128,128]{2,1,0:T(8,128)(2,1)S(1)}, bf16[16,128,128]{2,1,0:T(8,128)(2,1)S(1)}, u32[]{:S(2)}, u32[]{:S(2)}) %collective-permute-start.29) | collective-permute-done | bytes 524320 | tf_op jit(solution)/shard_map/ppermute | solution.py:37
  90.5 1.4 %adjoint_sum.1 = bf16[2,16,128,128]{3,2,1,0:T(8,128)(2,1)} custom-call(f32[16,128,128]{2,1,0:T(8,128)S(1)} %total.1.refs_0_, f32[16,128,128]{2,1,0:T(8,128)S(1)} %get-tuple-element.75.refs_1_, bf16[8,128,128]{2,1,0:T(8,128)(2,1)S(1)} %collective-permute-done.27.refs_2_, bf16[8,128,128]{2,1,0:T(8,128)(2,1)S(1)} %collective-permute-done.28.refs_3_, ...), custom_call_target="tpu_custom_call" | custom-call | flops 1000000 | bytes 10000 | tf_op jit(solution)/shard_map/adjoint_sum/pallas_call | solution.py:23
  (41 shorter events, 0.7 us)
Async XLA Ops:
  0.6 1.2 %copy-start = (bf16[2,16,128,128]{3,2,1,0:T(8,128)(2,1)S(1)}, bf16[2,16,128,128]{3,2,1,0:T(8,128)(2,1)}, u32[]{:S(2)}) copy-start(bf16[2,16,128,128]{3,2,1,0:T(8,128)(2,1)} %source.1) | copy-start | bytes 3145732
  2.2 17.5 %copy-start.1 = (s32[4,16]{1,0:T(4,128)S(1)}, s32[4,16]{1,0:T(4,128)}, u32[]{:S(2)}) copy-start(s32[4,16]{1,0:T(4,128)} %ranks.7) | copy-start | bytes 772
  2.2 17.4 %collective-permute-start.3 = (bf16[16,128,128]{2,1,0:T(8,128)(2,1)S(1)}, bf16[16,128,128]{2,1,0:T(8,128)(2,1)S(1)}, u32[]{:S(2)}, u32[]{:S(2)}) collective-permute-start(bf16[16,128,128]{2,1,0:T(8,128)(2,1)S(1)} %get-tuple-element.40.refs_0_), channel_id=1, source_target_pairs={{0,1},{1,0},{2,3},{3,2},{4,5},{5,4},{6,7},{7,6},{8,9},{9,8},{10,11... | collective-permute-start | bytes 1572872 | tf_op jit(solution)/shard_map/ppermute | solution.py:37
  2.7 15.1 %collective-permute-start = (bf16[16,128,128]{2,1,0:T(8,128)(2,1)S(1)}, bf16[16,128,128]{2,1,0:T(8,128)(2,1)S(1)}, u32[]{:S(2)}, u32[]{:S(2)}) collective-permute-start(bf16[16,128,128]{2,1,0:T(8,128)(2,1)S(1)} %get-tuple-element.40.refs_0_), channel_id=1, source_target_pairs={{0,2},{2,0},{1,3},{3,1},{4,6},{6,4},{5,7},{7,5},{8,10},{10,8},{9,1... | collective-permute-start | bytes 1572872 | tf_op jit(solution)/shard_map/ppermute | solution.py:37
  5.3 10.1 %collective-permute-start.2 = (bf16[4,64,128]{2,1,0:T(8,128)(2,1)}, bf16[4,64,128]{2,1,0:T(8,128)(2,1)S(1)}, u32[]{:S(2)}, u32[]{:S(2)}) collective-permute-start(bf16[4,64,128]{2,1,0:T(8,128)(2,1)} %refs_2_.3), channel_id=1, source_target_pairs={{0,8},{4,12},{8,0},{12,4},{1,9},{5,13},{9,1},{13,5},{2,10},{6,14},... | collective-permute-start | bytes 196616 | tf_op jit(solution)/shard_map/ppermute | solution.py:37
  7.9 9.8 %collective-permute-start.1 = (bf16[2,4,64,128]{3,2,1,0:T(8,128)(2,1)}, bf16[2,4,64,128]{3,2,1,0:T(8,128)(2,1)S(1)}, u32[]{:S(2)}, u32[]{:S(2)}) collective-permute-start(bf16[2,4,64,128]{3,2,1,0:T(8,128)(2,1)} %refs_0_.3), channel_id=1, source_target_pairs={{0,8},{4,12},{8,0},{12,4},{1,9},{5,13},{9,1},{13,5},{2,10},{6,14},... | collective-permute-start | bytes 393224 | tf_op jit(solution)/shard_map/ppermute | solution.py:37
  8.2 2.5 %copy-start.2 = (bf16[2,4,16,40,512]{4,3,2,1,0:T(8,128)(2,1)S(1)}, bf16[2,4,16,40,512]{4,3,2,1,0:T(8,128)(2,1)}, u32[]{:S(2)}) copy-start(bf16[2,4,16,40,512]{4,3,2,1,0:T(8,128)(2,1)} %second_in.1) | copy-start | bytes 15728644
  10.7 2.5 %copy-start.3 = (bf16[2,4,16,40,512]{4,3,2,1,0:T(8,128)(2,1)S(1)}, bf16[2,4,16,40,512]{4,3,2,1,0:T(8,128)(2,1)}, u32[]{:S(2)}) copy-start(bf16[2,4,16,40,512]{4,3,2,1,0:T(8,128)(2,1)} %basis_in.1) | copy-start | bytes 15728644
  17.8 1.9 %collective-permute-start.4 = (bf16[16,128,128]{2,1,0:T(8,128)(2,1)S(1)}, bf16[16,128,128]{2,1,0:T(8,128)(2,1)S(1)}, u32[]{:S(2)}, u32[]{:S(2)}) collective-permute-start(bf16[16,128,128]{2,1,0:T(8,128)(2,1)S(1)} %collective-permute-done.refs_1_), channel_id=1, source_target_pairs={{0,1},{1,0},{2,3},{3,2},{4,5},{5,4},{6,7},{7,6},{8,9},{9,8},{10,11... | collective-permute-start | bytes 1572872 | tf_op jit(solution)/shard_map/ppermute | solution.py:37
  17.8 14.4 %collective-permute-start.7 = (bf16[16,128,128]{2,1,0:T(8,128)(2,1)S(1)}, bf16[16,128,128]{2,1,0:T(8,128)(2,1)S(1)}, u32[]{:S(2)}, u32[]{:S(2)}) collective-permute-start(bf16[16,128,128]{2,1,0:T(8,128)(2,1)S(1)} %get-tuple-element.51.refs_0_), channel_id=1, source_target_pairs={{0,2},{2,0},{1,3},{3,1},{4,6},{6,4},{5,7},{7,5},{8,10},{10,8},{9,1... | collective-permute-start | bytes 1572872 | tf_op jit(solution)/shard_map/ppermute | solution.py:37
  23.4 1.6 %collective-permute-start.5 = (bf16[4,4,64,128]{3,2,1,0:T(8,128)(2,1)S(1)}, bf16[4,4,64,128]{3,2,1,0:T(8,128)(2,1)S(1)}, u32[]{:S(2)}, u32[]{:S(2)}) collective-permute-start(bf16[4,4,64,128]{3,2,1,0:T(8,128)(2,1)S(1)} %get-tuple-element.45), channel_id=1, source_target_pairs={{0,1},{1,0},{2,3},{3,2},{4,5},{5,4},{6,7},{7,6},{8,9},{9,8},{10,11... | collective-permute-start | bytes 786440 | tf_op jit(solution)/shard_map/ppermute | solution.py:37
  25.1 7.1 %collective-permute-start.6 = (bf16[2,4,64,128]{3,2,1,0:T(8,128)(2,1)S(1)}, bf16[2,4,64,128]{3,2,1,0:T(8,128)(2,1)S(1)}, u32[]{:S(2)}, u32[]{:S(2)}) collective-permute-start(bf16[2,4,64,128]{3,2,1,0:T(8,128)(2,1)S(1)} %get-tuple-element.47), channel_id=1, source_target_pairs={{0,4},{4,0},{8,12},{12,8},{1,5},{5,1},{9,13},{13,9},{2,6},{6,2},{1... | collective-permute-start | bytes 393224 | tf_op jit(solution)/shard_map/ppermute | solution.py:37
  32.2 3.5 %collective-permute-start.9 = (bf16[16,128,128]{2,1,0:T(8,128)(2,1)S(1)}, bf16[16,128,128]{2,1,0:T(8,128)(2,1)S(1)}, u32[]{:S(2)}, u32[]{:S(2)}) collective-permute-start(bf16[16,128,128]{2,1,0:T(8,128)(2,1)S(1)} %collective-permute-done.7.refs_1_), channel_id=1, source_target_pairs={{0,1},{1,0},{2,3},{3,2},{4,5},{5,4},{6,7},{7,6},{8,9},{9,8},{10,11... | collective-permute-start | bytes 1572872 | tf_op jit(solution)/shard_map/ppermute | solution.py:37
  32.2 10.0 %copy-start.4 = (bf16[2,4,64,128]{3,2,1,0:T(8,128)(2,1)S(1)}, bf16[2,4,64,128]{3,2,1,0:T(8,128)(2,1)}, u32[]{:S(2)}) copy-start(bf16[2,4,64,128]{3,2,1,0:T(8,128)(2,1)} %refs_0_.3) | copy-start | bytes 393220
  32.2 10.0 %copy-start.5 = (bf16[4,64,128]{2,1,0:T(8,128)(2,1)S(1)}, bf16[4,64,128]{2,1,0:T(8,128)(2,1)}, u32[]{:S(2)}) copy-start(bf16[4,64,128]{2,1,0:T(8,128)(2,1)} %refs_2_.3) | copy-start | bytes 196612
  32.2 3.4 %collective-permute-start.8 = (bf16[16,128,128]{2,1,0:T(8,128)(2,1)S(1)}, bf16[16,128,128]{2,1,0:T(8,128)(2,1)S(1)}, u32[]{:S(2)}, u32[]{:S(2)}) collective-permute-start(bf16[16,128,128]{2,1,0:T(8,128)(2,1)S(1)} %get-tuple-element.51.refs_0_), channel_id=1, source_target_pairs={{0,1},{1,0},{2,3},{3,2},{4,5},{5,4},{6,7},{7,6},{8,9},{9,8},{10,11... | collective-permute-start | bytes 1572872 | tf_op jit(solution)/shard_map/ppermute | solution.py:37
  32.8 9.4 %collective-permute-start.10 = (bf16[2,4,64,128]{3,2,1,0:T(8,128)(2,1)S(1)}, bf16[2,4,64,128]{3,2,1,0:T(8,128)(2,1)S(1)}, u32[]{:S(2)}, u32[]{:S(2)}) collective-permute-start(bf16[2,4,64,128]{3,2,1,0:T(8,128)(2,1)S(1)} %get-tuple-element.50), channel_id=1, source_target_pairs={{0,8},{4,12},{8,0},{12,4},{1,9},{5,13},{9,1},{13,5},{2,10},{6,14},... | collective-permute-start | bytes 393224 | tf_op jit(solution)/shard_map/ppermute | solution.py:37
  39.4 3.8 %collective-permute-start.11 = (bf16[4,4,64,128]{3,2,1,0:T(8,128)(2,1)S(1)}, bf16[4,4,64,128]{3,2,1,0:T(8,128)(2,1)S(1)}, u32[]{:S(2)}, u32[]{:S(2)}) collective-permute-start(bf16[4,4,64,128]{3,2,1,0:T(8,128)(2,1)S(1)} %get-tuple-element.53), channel_id=1, source_target_pairs={{0,1},{1,0},{2,3},{3,2},{4,5},{5,4},{6,7},{7,6},{8,9},{9,8},{10,11... | collective-permute-start | bytes 786440 | tf_op jit(solution)/shard_map/ppermute | solution.py:37
  42.3 6.3 %collective-permute-start.13 = (bf16[2,4,64,128]{3,2,1,0:T(8,128)(2,1)S(1)}, bf16[2,4,64,128]{3,2,1,0:T(8,128)(2,1)S(1)}, u32[]{:S(2)}, u32[]{:S(2)}) collective-permute-start(bf16[2,4,64,128]{3,2,1,0:T(8,128)(2,1)S(1)} %residual.2.refs_0_), channel_id=1, source_target_pairs={{0,4},{4,0},{8,12},{12,8},{1,5},{5,1},{9,13},{13,9},{2,6},{6,2},{1... | collective-permute-start | bytes 393224 | tf_op jit(solution)/shard_map/ppermute | solution.py:37
  43.2 6.9 %collective-permute-start.12 = (bf16[2,4,64,128]{3,2,1,0:T(8,128)(2,1)S(1)}, bf16[2,4,64,128]{3,2,1,0:T(8,128)(2,1)S(1)}, u32[]{:S(2)}, u32[]{:S(2)}) collective-permute-start(bf16[2,4,64,128]{3,2,1,0:T(8,128)(2,1)S(1)} %get-tuple-element.58), channel_id=1, source_target_pairs={{0,4},{4,0},{8,12},{12,8},{1,5},{5,1},{9,13},{13,9},{2,6},{6,2},{1... | collective-permute-start | bytes 393224 | tf_op jit(solution)/shard_map/ppermute | solution.py:37
  44.6 8.6 %collective-permute-start.14 = (bf16[2,4,64,128]{3,2,1,0:T(8,128)(2,1)S(1)}, bf16[2,4,64,128]{3,2,1,0:T(8,128)(2,1)S(1)}, u32[]{:S(2)}, u32[]{:S(2)}) collective-permute-start(bf16[2,4,64,128]{3,2,1,0:T(8,128)(2,1)S(1)} %residual.2.refs_0_), channel_id=1, source_target_pairs={{0,1},{1,0},{2,3},{3,2},{4,5},{5,4},{6,7},{7,6},{8,9},{9,8},{10,11... | collective-permute-start | bytes 393224 | tf_op jit(solution)/shard_map/ppermute | solution.py:37
  48.7 4.4 %collective-permute-start.15 = (bf16[2,4,64,128]{3,2,1,0:T(8,128)(2,1)S(1)}, bf16[2,4,64,128]{3,2,1,0:T(8,128)(2,1)S(1)}, u32[]{:S(2)}, u32[]{:S(2)}) collective-permute-start(bf16[2,4,64,128]{3,2,1,0:T(8,128)(2,1)S(1)} %collective-permute-done.13.refs_1_), channel_id=1, source_target_pairs={{0,1},{1,0},{2,3},{3,2},{4,5},{5,4},{6,7},{7,6},{8,9},{9,8},{10,11... | collective-permute-start | bytes 393224 | tf_op jit(solution)/shard_map/ppermute | solution.py:37
  50.1 9.0 %collective-permute-start.16 = (bf16[2,4,64,128]{3,2,1,0:T(8,128)(2,1)S(1)}, bf16[2,4,64,128]{3,2,1,0:T(8,128)(2,1)S(1)}, u32[]{:S(2)}, u32[]{:S(2)}) collective-permute-start(bf16[2,4,64,128]{3,2,1,0:T(8,128)(2,1)S(1)} %get-tuple-element.60), channel_id=1, source_target_pairs={{0,8},{4,12},{8,0},{12,4},{1,9},{5,13},{9,1},{13,5},{2,10},{6,14},... | collective-permute-start | bytes 393224 | tf_op jit(solution)/shard_map/ppermute | solution.py:37
  57.4 7.4 %collective-permute-start.18 = (bf16[8,128,128]{2,1,0:T(8,128)(2,1)S(1)}, bf16[8,128,128]{2,1,0:T(8,128)(2,1)S(1)}, u32[]{:S(2)}, u32[]{:S(2)}) collective-permute-start(bf16[8,128,128]{2,1,0:T(8,128)(2,1)S(1)} %get-tuple-element.62), channel_id=1, source_target_pairs={{0,1},{1,0},{2,3},{3,2},{4,5},{5,4},{6,7},{7,6},{8,9},{9,8},{10,11... | collective-permute-start | bytes 786440 | tf_op jit(solution)/shard_map/ppermute | solution.py:37
  57.5 7.3 %collective-permute-start.17 = (bf16[8,128,128]{2,1,0:T(8,128)(2,1)S(1)}, bf16[8,128,128]{2,1,0:T(8,128)(2,1)S(1)}, u32[]{:S(2)}, u32[]{:S(2)}) collective-permute-start(bf16[8,128,128]{2,1,0:T(8,128)(2,1)S(1)} %get-tuple-element.67), channel_id=1, source_target_pairs={{0,1},{1,0},{2,3},{3,2},{4,5},{5,4},{6,7},{7,6},{8,9},{9,8},{10,11... | collective-permute-start | bytes 786440 | tf_op jit(solution)/shard_map/ppermute | solution.py:37
  59.2 5.0 %collective-permute-start.19 = (bf16[2,4,64,128]{3,2,1,0:T(8,128)(2,1)S(1)}, bf16[2,4,64,128]{3,2,1,0:T(8,128)(2,1)S(1)}, u32[]{:S(2)}, u32[]{:S(2)}) collective-permute-start(bf16[2,4,64,128]{3,2,1,0:T(8,128)(2,1)S(1)} %residual.3.refs_1_.refs_0_), channel_id=1, source_target_pairs={{0,4},{4,0},{8,12},{12,8},{1,5},{5,1},{9,13},{13,9},{2,6},{6,2},{1... | collective-permute-start | bytes 393224 | tf_op jit(solution)/shard_map/ppermute | solution.py:37
  60.0 6.5 %collective-permute-start.20 = (bf16[2,4,64,128]{3,2,1,0:T(8,128)(2,1)S(1)}, bf16[2,4,64,128]{3,2,1,0:T(8,128)(2,1)S(1)}, u32[]{:S(2)}, u32[]{:S(2)}) collective-permute-start(bf16[2,4,64,128]{3,2,1,0:T(8,128)(2,1)S(1)} %residual.3.refs_1_.refs_0_), channel_id=1, source_target_pairs={{0,1},{1,0},{2,3},{3,2},{4,5},{5,4},{6,7},{7,6},{8,9},{9,8},{10,11... | collective-permute-start | bytes 393224 | tf_op jit(solution)/shard_map/ppermute | solution.py:37
  64.3 2.2 %collective-permute-start.21 = (bf16[2,4,64,128]{3,2,1,0:T(8,128)(2,1)S(1)}, bf16[2,4,64,128]{3,2,1,0:T(8,128)(2,1)S(1)}, u32[]{:S(2)}, u32[]{:S(2)}) collective-permute-start(bf16[2,4,64,128]{3,2,1,0:T(8,128)(2,1)S(1)} %collective-permute-done.19.refs_1_), channel_id=1, source_target_pairs={{0,1},{1,0},{2,3},{3,2},{4,5},{5,4},{6,7},{7,6},{8,9},{9,8},{10,11... | collective-permute-start | bytes 393224 | tf_op jit(solution)/shard_map/ppermute | solution.py:37
  64.3 9.0 %collective-permute-start.24 = (bf16[8,128,128]{2,1,0:T(8,128)(2,1)S(1)}, bf16[8,128,128]{2,1,0:T(8,128)(2,1)S(1)}, u32[]{:S(2)}, u32[]{:S(2)}) collective-permute-start(bf16[8,128,128]{2,1,0:T(8,128)(2,1)S(1)} %get-tuple-element.73), channel_id=1, source_target_pairs={{0,1},{1,0},{2,3},{3,2},{4,5},{5,4},{6,7},{7,6},{8,9},{9,8},{10,11... | collective-permute-start | bytes 786440 | tf_op jit(solution)/shard_map/ppermute | solution.py:37
  64.8 9.1 %collective-permute-start.25 = (bf16[8,128,128]{2,1,0:T(8,128)(2,1)S(1)}, bf16[8,128,128]{2,1,0:T(8,128)(2,1)S(1)}, u32[]{:S(2)}, u32[]{:S(2)}) collective-permute-start(bf16[8,128,128]{2,1,0:T(8,128)(2,1)S(1)} %get-tuple-element.74), channel_id=1, source_target_pairs={{0,1},{1,0},{2,3},{3,2},{4,5},{5,4},{6,7},{7,6},{8,9},{9,8},{10,11... | collective-permute-start | bytes 786440 | tf_op jit(solution)/shard_map/ppermute | solution.py:37
  64.9 14.8 %collective-permute-start.26 = (bf16[16,128,128]{2,1,0:T(8,128)(2,1)S(1)}, bf16[16,128,128]{2,1,0:T(8,128)(2,1)S(1)}, u32[]{:S(2)}, u32[]{:S(2)}) collective-permute-start(bf16[16,128,128]{2,1,0:T(8,128)(2,1)S(1)} %adjoint_share.2), channel_id=1, source_target_pairs={{0,2},{2,0},{1,3},{3,1},{4,6},{6,4},{5,7},{7,5},{8,10},{10,8},{9,1... | collective-permute-start | bytes 1572872 | tf_op jit(solution)/shard_map/ppermute | solution.py:37
  70.9 1.6 %collective-permute-start.22 = (bf16[8,128,128]{2,1,0:T(8,128)(2,1)S(1)}, bf16[8,128,128]{2,1,0:T(8,128)(2,1)S(1)}, u32[]{:S(2)}, u32[]{:S(2)}) collective-permute-start(bf16[8,128,128]{2,1,0:T(8,128)(2,1)S(1)} %get-tuple-element.70), channel_id=1, source_target_pairs={{0,1},{1,0},{2,3},{3,2},{4,5},{5,4},{6,7},{7,6},{8,9},{9,8},{10,11... | collective-permute-start | bytes 786440 | tf_op jit(solution)/shard_map/ppermute | solution.py:37
  71.2 1.7 %collective-permute-start.23 = (bf16[8,128,128]{2,1,0:T(8,128)(2,1)S(1)}, bf16[8,128,128]{2,1,0:T(8,128)(2,1)S(1)}, u32[]{:S(2)}, u32[]{:S(2)}) collective-permute-start(bf16[8,128,128]{2,1,0:T(8,128)(2,1)S(1)} %get-tuple-element.71), channel_id=1, source_target_pairs={{0,1},{1,0},{2,3},{3,2},{4,5},{5,4},{6,7},{7,6},{8,9},{9,8},{10,11... | collective-permute-start | bytes 786440 | tf_op jit(solution)/shard_map/ppermute | solution.py:37
  72.5 7.3 %collective-permute-start.27 = (bf16[8,128,128]{2,1,0:T(8,128)(2,1)S(1)}, bf16[8,128,128]{2,1,0:T(8,128)(2,1)S(1)}, u32[]{:S(2)}, u32[]{:S(2)}) collective-permute-start(bf16[8,128,128]{2,1,0:T(8,128)(2,1)S(1)} %get-tuple-element.76), channel_id=1, source_target_pairs={{0,1},{1,0},{2,3},{3,2},{4,5},{5,4},{6,7},{7,6},{8,9},{9,8},{10,11... | collective-permute-start | bytes 786440 | tf_op jit(solution)/shard_map/ppermute | solution.py:37
  72.9 6.9 %collective-permute-start.28 = (bf16[8,128,128]{2,1,0:T(8,128)(2,1)S(1)}, bf16[8,128,128]{2,1,0:T(8,128)(2,1)S(1)}, u32[]{:S(2)}, u32[]{:S(2)}) collective-permute-start(bf16[8,128,128]{2,1,0:T(8,128)(2,1)S(1)} %get-tuple-element.77), channel_id=1, source_target_pairs={{0,1},{1,0},{2,3},{3,2},{4,5},{5,4},{6,7},{7,6},{8,9},{9,8},{10,11... | collective-permute-start | bytes 786440 | tf_op jit(solution)/shard_map/ppermute | solution.py:37
  73.3 17.3 %collective-permute-start.29 = (bf16[16,128,128]{2,1,0:T(8,128)(2,1)S(1)}, bf16[16,128,128]{2,1,0:T(8,128)(2,1)S(1)}, u32[]{:S(2)}, u32[]{:S(2)}) collective-permute-start(bf16[16,128,128]{2,1,0:T(8,128)(2,1)S(1)} %adjoint_share.3), channel_id=1, source_target_pairs={{0,2},{2,0},{1,3},{3,1},{4,6},{6,4},{5,7},{7,5},{8,10},{10,8},{9,1... | collective-permute-start | bytes 1572872 | tf_op jit(solution)/shard_map/ppermute | solution.py:37

commit v4 on v3

--- a/solution.py
+++ b/solution.py
@@ -49,11 +49,14 @@
 
 
 def waves_kernel(source, *outs):
-    part = source.shape[-1] // len(outs)
-    for j in range(source.shape[1]):
-        for c, out in enumerate(outs):
+    part = outs[0].shape[-1] // 2
+    at = 0
+    for out in outs:
+        for j in range(out.shape[0]):
+            c, row = divmod(at, source.shape[1])
             lanes = slice(c * part, (c + 1) * part)
-            out[j] = jnp.concatenate([source[0, j, :, lanes], source[1, j, :, lanes]], -1)
+            out[j] = jnp.concatenate([source[0, row, :, lanes], source[1, row, :, lanes]], -1)
+            at += 1
 
 
 def load_kernel(second_in, basis_in, second, basis, sems):
@@ -70,14 +73,17 @@
         copy.wait()
 
 
-def halve_kernel(mine, other, keep, send):
+def halve_kernel(mine, *refs):
+    others, keep, send = refs[:-2], refs[-2], refs[-1]
     n = keep.shape[0]
-    keep[...] = mine[:n] + other[:n].astype(F32)
-    send[...] = (mine[n:] + other[n:].astype(F32)).astype(BF16)
-
-
-def mirror_kernel(mine, other, keep, send):
-    total = mine[...] + other[...].astype(F32)
+    total = jnp.concatenate([other[...] for other in others], 0).astype(F32) + mine[...]
+    keep[...] = total[:n]
+    send[...] = total[n:].astype(BF16)
+
+
+def mirror_kernel(mine, *refs):
+    others, keep, send = refs[:-2], refs[-2], refs[-1]
+    total = jnp.concatenate([other[...] for other in others], 0).astype(F32) + mine[...]
     keep[...] = total
     n = keep.shape[0]
     for e in range(n):
@@ -104,53 +110,56 @@
 
 def share_kernel(mine, *refs):
     others, out = refs[:-1], refs[-1]
-    n = out.shape[0] // len(others)
+    n = others[0].shape[0]
     for k, other in enumerate(others):
-        out[k * n : (k + 1) * n] = (mine[k * n : (k + 1) * n] + other[...].astype(F32)).astype(BF16)
+        at = slice(k * n, (k + 1) * n)
+        out[at] = (mine[at] + other[...].astype(F32)).astype(BF16)
 
 
 def total_kernel(mine, *refs):
     others, out = refs[:-1], refs[-1]
-    first, rest = others[:SPLIT], others[SPLIT:]
-    n = out.shape[0] // len(first)
-    for k, other in enumerate(first):
-        total = mine[k * n : (k + 1) * n] + other[...].astype(F32)
-        for ref in rest:
-            total = total + ref[k * n : (k + 1) * n].astype(F32)
-        out[k * n : (k + 1) * n] = total
-
-
-def final_kernel(*refs):
-    *done, mine = refs[: CHUNKS]
-    others, out_ref = refs[CHUNKS:-1], refs[-1]
-    first, rest = others[:SPLIT], others[SPLIT:]
+    total = mine[...]
+    for ref in others:
+        total = total + ref[...].astype(F32)
+    out[...] = total
+
+
+def final_kernel(done, mine, *refs):
+    others, out_ref = refs[:-1], refs[-1]
     part = mine.shape[1] // 2
-    n = mine.shape[0] // SPLIT
     for j in range(out_ref.shape[1]):
         for p in range(2):
             lanes = slice(p * part, (p + 1) * part)
-            total = mine[j, lanes, :] + first[j // n][j % n, lanes, :].astype(F32)
-            for ref in rest:
+            total = mine[j, lanes, :]
+            for ref in others:
                 total = total + ref[j, lanes, :].astype(F32)
-            pieces = [ref[j, lanes, :] for ref in done] + [total]
-            out_ref[p, j] = jnp.concatenate(pieces, 0).T.astype(out_ref.dtype)
-
-
-def forward_kernel(rs, helps, z_offsets, ranks, *refs):
+            out_ref[p, j] = jnp.concatenate([done[j, lanes, :], total], 0).T.astype(out_ref.dtype)
+
+
+def forward_kernel(rs, helps, z_offsets, n_groups, ranks, *refs):
     n_pieces = rs * helps
-    pieces = refs[:n_pieces]
-    second, basis, keep_out, send_out, waves, coef, fwd = refs[n_pieces:]
+    groups = [refs[k * n_pieces : (k + 1) * n_pieces] for k in range(n_groups)]
+    second, basis, keep_out, *sends, waves, coef, fwd = refs[n_groups * n_pieces :]
+    n_send = sends[0].shape[0]
     z, r, here = lax.axis_index("col"), lax.axis_index("row"), lax.axis_index("help")
-    columns, quarter, width = pieces[0].shape
+    _, quarter, width = groups[0][0].shape
+    spots = [(group, j) for group in groups for j in range(group[0].shape[0])]
+    columns = len(spots)
     rows = basis.shape[1]
     terms = second.shape[1] // (2 * rows)
     half = rows * terms
     row_index = lax.broadcasted_iota(jnp.int32, (terms, width), 0)
-    for j in range(columns):
-        for n, piece in enumerate(pieces):
-            spot = (r ^ (n % rs)) * helps + (here ^ (n // rs))
-            waves[j, pl.ds(pl.multiple_of(spot * quarter, quarter), quarter), :] = piece[j]
-        out = jnp.dot(second[j], waves[j], preferred_element_type=F32)
+    places = [((r ^ (n % rs)) * helps + (here ^ (n // rs))) * quarter for n in range(n_pieces)]
+    places = [pl.multiple_of(at, quarter) for at in places]
+    for j, (group, at_j) in enumerate(spots):
+        if quarter % LANES == 0:
+            left = jnp.concatenate([second[j, :, pl.ds(at, quarter)] for at in places], 1)
+            right = jnp.concatenate([piece[at_j] for piece in group], 0)
+        else:
+            for at, piece in zip(places, group):
+                waves[j, pl.ds(at, quarter), :] = piece[at_j]
+            left, right = second[j], waves[j]
+        out = jnp.dot(left, right, preferred_element_type=F32)
         value = out[:half] + turn(out[half:], 1.0, -1.0)
         for i in range(rows):
             left = ranks[i, j] - here * terms
@@ -160,16 +169,16 @@
     dims = (((0,), (0,)), ((), ()))
     for i in range(rows):
         value = coef[i]
-        turned = turn(value, -1.0, 1.0)
-        out = lax.dot_general(value.astype(BF16), basis[0, i], dims, preferred_element_type=F32)
-        out = out + lax.dot_general(turned.astype(BF16), basis[1, i], dims, preferred_element_type=F32)
+        left = jnp.concatenate([value, turn(value, -1.0, 1.0)], 0).astype(BF16)
+        right = jnp.concatenate([basis[0, i], basis[1, i]], 0)
+        out = lax.dot_general(left, right, dims, preferred_element_type=F32)
         fwd[i] = out.T
         for n, offset in enumerate(z_offsets):
             block = (z ^ offset) * helps
             at = pl.multiple_of((block + here) * span, span)
             keep_out[n, i] = fwd[i, pl.ds(at, span), :].astype(keep_out.dtype)
             at = pl.multiple_of((block + 1 - here) * span, span)
-            send_out[n, i] = fwd[i, pl.ds(at, span), :].astype(send_out.dtype)
+            sends[n // n_send][n % n_send, i] = fwd[i, pl.ds(at, span), :].astype(BF16)
 
 
 def adjoint_kernel(rs, helps, spots, ranks, *refs):
@@ -189,8 +198,8 @@
                 resid[i, pl.ds(pl.multiple_of(spot * span, span), span), :] = piece[e, i]
         value = resid[i]
         turned = turn(value.astype(F32), 1.0, -1.0).astype(BF16)
-        out = jnp.dot(basis[0, i], value, preferred_element_type=F32)
-        out = out + jnp.dot(basis[1, i], turned, preferred_element_type=F32)
+        left = jnp.concatenate([basis[0, i], basis[1, i]], 1)
+        out = jnp.dot(left, jnp.concatenate([value, turned], 0), preferred_element_type=F32)
         for j in range(columns):
             left = ranks[i, j] - here * terms
             part = out[j * terms : (j + 1) * terms]
@@ -200,22 +209,31 @@
     def keep(d, j, value):
         keeps[d][j] = value
 
+    parts = (len(sends) - 1) // (rs - 1)
+
     def send(d, j, value):
-        refs = sends[d * SPLIT : (d + 1) * SPLIT]
+        refs = sends[:1] if d == 0 else sends[1 + (d - 1) * parts : 1 + d * parts]
         n = refs[0].shape[0]
         refs[j // n][j % n] = value.astype(BF16)
 
+    half = back.shape[1]
     for j in range(columns):
-        value = back[j]
-        left = jnp.concatenate([value, turn(value, -1.0, 1.0)], 0).T.astype(BF16)
+        real = back[j].astype(BF16).T
+        turned = jnp.concatenate([-real[width // 2 :], real[: width // 2]], 0)
+
+        def product(right):
+            out = jnp.dot(real, right[:half], preferred_element_type=F32)
+            return out + jnp.dot(turned, right[half:], preferred_element_type=F32)
+
         if quarter % LANES == 0:
             for put, h in ((keep, here), (send, 1 - here)):
+                places = [((r ^ d) * helps + h) * quarter for d in range(rs)]
+                places = [pl.multiple_of(at, quarter) for at in places]
+                out = product(jnp.concatenate([second[j, :, pl.ds(at, quarter)] for at in places], 1))
                 for d in range(rs):
-                    at = pl.multiple_of(((r ^ d) * helps + h) * quarter, quarter)
-                    out = jnp.dot(left, second[j, :, pl.ds(at, quarter)], preferred_element_type=F32)
-                    put(d, j, out)
+                    put(d, j, out[:, d * quarter : (d + 1) * quarter])
         else:
-            out = jnp.dot(left, second[j], preferred_element_type=F32)
+            out = product(second[j])
             for n in range(rs):
                 for h in range(helps):
                     part = out[:, (n * helps + h) * quarter : (n * helps + h + 1) * quarter]
@@ -238,11 +256,17 @@
     def share(pieces):
         return pieces + [swap("help", d, m) for d in range(1, helps) for m in pieces]
 
+    sizes = [[5 * columns // 8, 3 * columns // 8]] + [[columns]] * (CHUNKS - 1)
     waves = call(
-        waves_kernel, "split_waves", [((columns, quarter, width), BF16)] * CHUNKS, [wavefield]
+        waves_kernel,
+        "split_waves",
+        [((n, quarter, width), BF16) for ns in sizes for n in ns],
+        [wavefield],
     )
-    gathered = [[w] + [swap("row", d, w) for d in range(1, rs)] for w in waves]
-    data = [observed, swap("col", far, observed), amplitude, swap("col", far, amplitude)]
+    waves = [waves[:2]] + [[w] for w in waves[2:]]
+    gathered = [[[w] + [swap("row", d, w) for d in range(1, rs)] for w in ws] for ws in waves]
+    data = [observed, amplitude]
+    data = [m for d in data for m in (d, swap("col", far, after(d, waves[0][0])))]
     second, basis = call(
         load_kernel,
         "load_factors",
@@ -256,12 +280,12 @@
     basis = basis.reshape(2, rows, columns * terms, tile)
 
     def forward(c, mine):
-        shape = (zs, rows, span, width)
-        pieces = share(mine)
+        shape, piece = (zs, rows, span, width), (zs // SPLIT, rows, span, width)
+        pieces = [m for group in mine for m in share(group)]
         return call(
-            functools.partial(forward_kernel, rs, helps, z_offsets),
+            functools.partial(forward_kernel, rs, helps, z_offsets, len(mine)),
             "forward_product",
-            [(shape, F32), (shape, BF16)],
+            [(shape, F32)] + [(piece, BF16)] * SPLIT,
             [tile_ranks, *pieces, second, basis],
             in_specs=[SM] + [VM] * (len(pieces) + 2),
             scratch=[
@@ -273,12 +297,14 @@
             cost=LARGE if c else 1,
         )
 
-    def backward(pieces, spots):
-        whole, piece = (columns, width, quarter), (columns // SPLIT, width, quarter)
+    def backward(c, pieces, spots):
+        whole = (columns, width, quarter)
+        parts = 2
+        piece = (columns // parts, width, quarter)
         outs = call(
             functools.partial(adjoint_kernel, rs, helps, spots),
             "adjoint_product",
-            [(whole, F32)] * rs + [(piece, BF16)] * (rs * SPLIT),
+            [(whole, F32)] * rs + [(whole, BF16)] + [(piece, BF16)] * ((rs - 1) * parts),
             [tile_ranks, *pieces, basis, second],
             in_specs=[SM] + [VM] * (len(pieces) + 2),
             scratch=[
@@ -286,31 +312,31 @@
                 pltpu.VMEM((columns, rows * terms, width), F32),
             ],
             limit=16 * MIB,
-            cost=LARGE,
+            cost=1 if c + 1 == CHUNKS else LARGE,
         )
         sends = outs[rs:]
-        return outs[:rs], [sends[d * SPLIT : (d + 1) * SPLIT] for d in range(rs)]
-
-    halved, mirrored, residuals, shared, totals = [], [], [], [], []
+        return outs[:rs], [sends[:1]] + [sends[1 + d * parts : 1 + (d + 1) * parts] for d in range(rs - 1)]
+
+    halved, mirrored, residuals, sent, totals = [], [], [], [], []
 
     def front(c):
-        earlier = (halved[-1],) if c else (second, data[1], data[3])
-        mine = [gathered[c][0]] + [after(m, *earlier) for m in gathered[c][1:]]
+        earlier = (mirrored[-1][1],) if c else (second, data[1], data[3])
+        mine = [[group[0]] + [after(m, *earlier) for m in group[1:]] for group in gathered[c]]
         if c:
-            mine[0] = after(mine[0], mirrored[-1][1])
-        keep, send = forward(c, mine)
+            mine[0][0] = after(mine[0][0], mirrored[-1][1])
+        keep, *sends = forward(c, mine)
         if c:
-            residual_of(c - 1, send)
+            residual_of(c - 1, sends[-1])
             keep = after(keep, residuals[c - 1])
-        other = swap("help", 1, send)
+        others = [swap("help", 1, send) for send in sends]
         for d in near:
             shape = (keep.shape[0] // 2, rows, span, width)
             keep, send = call(
-                halve_kernel, "halve", [(shape, F32), (shape, BF16)], [keep, other], cost=LARGE if c else 1
+                halve_kernel, "halve", [(shape, F32), (shape, BF16)], [keep, *others], cost=LARGE if c else 1
             )
-            other = swap("col", d, send)
+            others = [swap("col", d, send)]
         halved.append(send)
-        mirrored.append(call(mirror_kernel, "mirror", [(shape, F32), (shape, BF16)], [keep, other]))
+        mirrored.append(call(mirror_kernel, "mirror", [(shape, F32), (shape, BF16)], [keep, *others]))
 
     def residual_of(c, *earlier):
         keep, send = mirrored[c]
@@ -329,29 +355,35 @@
         for d in reversed(near):
             pieces = pieces + [swap("col", d, m) for m in pieces]
             offsets = offsets + [o ^ d for o in offsets]
+        last = c + 1 == CHUNKS
+        if last:
+            pieces[1:] = [after(m, *sent) for m in pieces[1:]]
         pieces = share(pieces)
         spots = [((o, o ^ far), e) for e in range(helps) for o in offsets]
-        last = c + 1 == CHUNKS
-        pieces[0] = after(pieces[0], *(shared[-1] if last else [mirrored[c + 1][1]]))
-        keeps, sends = backward(pieces, spots)
+        if not last:
+            pieces[0] = after(pieces[0], mirrored[c + 1][1])
+        keeps, sends = backward(c, pieces, spots)
         if not last:
             residual_of(c + 1, sends[-1][-1])
             keeps = [keeps[0]] + [after(k, residuals[c + 1]) for k in keeps[1:]]
         shape = (columns, width, quarter)
-        shared.append(
-            [
-                call(
-                    share_kernel, "adjoint_share", [(shape, BF16)], [k, *[swap("help", 1, m) for m in s]]
-                )[0]
-                for k, s in zip(keeps[1:], sends[1:])
-            ]
-        )
+        shared = [
+            call(
+                share_kernel,
+                "adjoint_share",
+                [(shape, BF16)],
+                [k, *[swap("help", 1, m) for m in s]],
+            )[0]
+            for k, s in zip(keeps[1:], sends[1:])
+        ]
         if last:
-            totals[-1] = [after(totals[-1][0], *shared[-1])] + totals[-1][1:]
+            totals[-1][0] = after(totals[-1][0], *shared)
             totals[-1] = call(total_kernel, "total", [(shape, F32)], totals[-1], cost=LARGE)
+        else:
+            sent.extend(shared)
         totals.append(
-            [keeps[0], *[swap("help", 1, m) for m in sends[0]]]
-            + [swap("row", d + 1, m) for d, m in enumerate(shared[-1])]
+            [keeps[0], swap("help", 1, after(sends[0][0], *shared))]
+            + [swap("row", d + 1, m) for d, m in enumerate(shared)]
         )
 
     for c in range(CHUNKS):
@@ -359,7 +391,7 @@
     for c in range(CHUNKS):
         rear(c)
 
-    residual = call(join_kernel, "join", [(observed.shape, BF16)], residuals, cost=LARGE)[0]
+    residual = call(join_kernel, "join", [(observed.shape, BF16)], residuals, cost=1)[0]
     adjoint = call(
         final_kernel, "adjoint_sum", [(wavefield.shape, BF16)], [*totals[0], *totals[1]]
     )[0]

time: 92.1 us -> 85.4 us (0.927)
  starting transfers between devices: 23.6 us -> 19.3 us
  Pallas kernels: 21.7 us -> 18.8 us
    ppermute x30 -> x33, starting transfers between devices: 23.6 us -> 19.3 us  [swap(): return lax.ppermute(value, axis_name, [(i, i ^ step) for i in range(size)])]
    pallas_call x17, Pallas kernels: 21.7 us -> 18.8 us  [call(): pl.pallas_call(kernel, out_shape=[jax.ShapeDtypeStruct(shape, kind) for s...]
    ppermute x30 -> x33, waiting for transfers between devices: 39.6 us -> 40 us  [swap(): return lax.ppermute(value, axis_name, [(i, i ^ step) for i in range(size)])]
  transfers between devices with their start and end apart: 30 -> 33, of which waited for: 14 -> 19; matrix products, arithmetic and copies ran while one was open for 0% -> 0% of each run, Pallas kernels for 22% -> 20%
where the time goes in v4:
time: 85.4 us; the launch traced here: 85.2 us
  waiting for transfers between devices  40 us (47%)
  starting transfers between devices  19.3 us (23%)
  Pallas kernels  18.8 us (22%)
  local copies, waits for them, and re-layouts  6.21 us (7%)
    ppermute x33, waiting for transfers between devices, swap(): return lax.ppermute(value, axis_name, [(i, i ^ step) for i in range(size)])  40 us
    ppermute x33, starting transfers between devices, swap(): return lax.ppermute(value, axis_name, [(i, i ^ step) for i in range(size)])  19.3 us
    pallas_call x17, Pallas kernels, call(): pl.pallas_call(kernel, out_shape=[jax.ShapeDtypeStruct(shape, kind) for s...  18.8 us
    unnamed x12, local copies, waits for them, and re-layouts  6.21 us
  transfers between devices with their start and end apart: 33, of which 19 were waited for; matrix products, arithmetic and copies ran while one was open for 0% of the time, Pallas kernels for 20%

profile of v4, /device:TPU:0, one launch (start us, length us, event | category | flops | bytes accessed | tf_op | source)
XLA Modules:
  0.0 85.2 jit_solution(15397817823401799406)
XLA Ops:
  0.6 1.2 %copy-done = bf16[2,16,128,128]{3,2,1,0:T(8,128)(2,1)S(1)} copy-done((bf16[2,16,128,128]{3,2,1,0:T(8,128)(2,1)S(1)}, bf16[2,16,128,128]{3,2,1,0:T(8,128)(2,1)}, u32[]{:S(2)}) %copy-start) | copy-done | bytes 1048600
  1.9 0.3 split_waves.1
  2.2 0.5 collective-permute-start.3
  2.7 2.6 %collective-permute-start = (bf16[10,128,128]{2,1,0:T(8,128)(2,1)S(1)}, bf16[10,128,128]{2,1,0:T(8,128)(2,1)S(1)}, u32[]{:S(2)}, u32[]{:S(2)}) collective-permute-start(bf16[10,128,128]{2,1,0:T(8,128)(2,1)S(1)} %get-tuple-element.46.refs_0_), channel_id=1, source_target_pairs={{0,2},{2,0},{1,3},{3,1},{4,6},{6,4},{5,7},{7,5},{8,10},{10,8},{9,1... | collective-permute-start | bytes 983048 | tf_op jit(solution)/shard_map/ppermute | solution.py:37
  5.3 2.6 %collective-permute-start.2 = (bf16[4,64,128]{2,1,0:T(8,128)(2,1)}, bf16[4,64,128]{2,1,0:T(8,128)(2,1)S(1)}, u32[]{:S(2)}, u32[]{:S(2)}) collective-permute-start(bf16[4,64,128]{2,1,0:T(8,128)(2,1)} %refs_2_.3), channel_id=1, source_target_pairs={{0,8},{4,12},{8,0},{12,4},{1,9},{5,13},{9,1},{13,5},{2,10},{6,14},... | collective-permute-start | bytes 196616 | tf_op jit(solution)/shard_map/ppermute | solution.py:37
  7.9 0.3 collective-permute-start.1
  8.2 0.2 collective-permute-start.5
  8.4 2.5 %copy-done.2 = bf16[2,4,16,40,512]{4,3,2,1,0:T(8,128)(2,1)S(1)} copy-done((bf16[2,4,16,40,512]{4,3,2,1,0:T(8,128)(2,1)S(1)}, bf16[2,4,16,40,512]{4,3,2,1,0:T(8,128)(2,1)}, u32[]{:S(2)}) %copy-start.2) | copy-done | bytes 5242904
  10.9 2.5 %copy-done.3 = bf16[2,4,16,40,512]{4,3,2,1,0:T(8,128)(2,1)S(1)} copy-done((bf16[2,4,16,40,512]{4,3,2,1,0:T(8,128)(2,1)S(1)}, bf16[2,4,16,40,512]{4,3,2,1,0:T(8,128)(2,1)}, u32[]{:S(2)}) %copy-start.3) | copy-done | bytes 5242904
  13.4 2.2 %load_factors.1 = (bf16[16,8,40,512]{3,2,1,0:T(8,128)(2,1)S(1)}, bf16[2,4,16,40,512]{4,3,2,1,0:T(8,128)(2,1)S(1)}) custom-call(bf16[2,4,16,40,512]{4,3,2,1,0:T(8,128)(2,1)S(1)} %copy-done.2, bf16[2,4,16,40,512]{4,3,2,1,0:T(8,128)(2,1)S(1)} %copy-done.3), custom_call_target="tpu_custom_call" | custom-call | flops 10000000000 | bytes 10000 | tf_op jit(solution)/shard_map/load_factors/pallas_call | solution.py:23
  15.6 2.1 %collective-permute-done.1.refs_1_ = bf16[2,4,64,128]{3,2,1,0:T(8,128)(2,1)S(1)} collective-permute-done((bf16[2,4,64,128]{3,2,1,0:T(8,128)(2,1)}, bf16[2,4,64,128]{3,2,1,0:T(8,128)(2,1)S(1)}, u32[]{:S(2)}, u32[]{:S(2)}) %collective-permute-start.1) | collective-permute-done | bytes 131104 | tf_op jit(solution)/shard_map/ppermute | solution.py:37
  17.7 0.4 collective-permute-start.11
  18.1 0.2 collective-permute-start.6
  18.3 0.3 collective-permute-start.7
  18.6 1.0 %collective-permute-done.6.refs_6_ = bf16[6,128,128]{2,1,0:T(8,128)(2,1)S(1)} collective-permute-done((bf16[6,128,128]{2,1,0:T(8,128)(2,1)S(1)}, bf16[6,128,128]{2,1,0:T(8,128)(2,1)S(1)}, u32[]{:S(2)}, u32[]{:S(2)}) %collective-permute-start.6) | collective-permute-done | bytes 196640 | tf_op jit(solution)/shard_map/ppermute | solution.py:37
  19.6 0.3 collective-permute-done.7.refs_7_
  19.9 3.4 %forward_product.2 = (f32[4,4,64,128]{3,2,1,0:T(8,128)S(1)}, bf16[2,4,64,128]{3,2,1,0:T(8,128)(2,1)S(1)}, bf16[2,4,64,128]{3,2,1,0:T(8,128)(2,1)S(1)}) custom-call(s32[4,16]{1,0:T(4,128)S(1)} %copy-done.1, bf16[10,128,128]{2,1,0:T(8,128)(2,1)S(1)} %get-tuple-element.46.refs_0_, bf16[10,128,128]{2,1,0:T(8,128)(2,1)S(1)} %collective-permute-done.refs_1_, ...), custom_call_target="tpu_custom_call" | custom-call | flops 1 | bytes 10000 | tf_op jit(solution)/shard_map/forward_product/pallas_call | solution.py:23
  23.5 0.4 collective-permute-start.9
  23.9 0.8 collective-permute-done.8.refs_0_
  25.0 1.3 %collective-permute-start.10 = (bf16[2,4,64,128]{3,2,1,0:T(8,128)(2,1)S(1)}, bf16[2,4,64,128]{3,2,1,0:T(8,128)(2,1)S(1)}, u32[]{:S(2)}, u32[]{:S(2)}) collective-permute-start(bf16[2,4,64,128]{3,2,1,0:T(8,128)(2,1)S(1)} %get-tuple-element.58), channel_id=1, source_target_pairs={{0,4},{4,0},{8,12},{12,8},{1,5},{5,1},{9,13},{13,9},{2,6},{6,2},{1... | collective-permute-start | bytes 393224 | tf_op jit(solution)/shard_map/ppermute | solution.py:37
  26.2 4.5 %collective-permute-done.10.refs_0_ = bf16[2,4,64,128]{3,2,1,0:T(8,128)(2,1)S(1)} collective-permute-done((bf16[2,4,64,128]{3,2,1,0:T(8,128)(2,1)S(1)}, bf16[2,4,64,128]{3,2,1,0:T(8,128)(2,1)S(1)}, u32[]{:S(2)}, u32[]{:S(2)}) %collective-permute-start.10) | collective-permute-done | bytes 131104 | tf_op jit(solution)/shard_map/ppermute | solution.py:37
  30.8 1.2 %collective-permute-done.11.refs_1_ = bf16[16,128,128]{2,1,0:T(8,128)(2,1)S(1)} collective-permute-done((bf16[16,128,128]{2,1,0:T(8,128)(2,1)S(1)}, bf16[16,128,128]{2,1,0:T(8,128)(2,1)S(1)}, u32[]{:S(2)}, u32[]{:S(2)}) %collective-permute-start.11) | collective-permute-done | bytes 524320 | tf_op jit(solution)/shard_map/ppermute | solution.py:37
  32.0 0.5 collective-permute-start.13
  32.5 1.2 %collective-permute-start.14 = (bf16[2,4,64,128]{3,2,1,0:T(8,128)(2,1)S(1)}, bf16[2,4,64,128]{3,2,1,0:T(8,128)(2,1)S(1)}, u32[]{:S(2)}, u32[]{:S(2)}) collective-permute-start(bf16[2,4,64,128]{3,2,1,0:T(8,128)(2,1)S(1)} %get-tuple-element.61), channel_id=1, source_target_pairs={{0,8},{4,12},{8,0},{12,4},{1,9},{5,13},{9,1},{13,5},{2,10},{6,14},... | collective-permute-start | bytes 393224 | tf_op jit(solution)/shard_map/ppermute | solution.py:37
  33.9 0.7 collective-permute-done.13.refs_3_
  34.7 3.4 %forward_product.3 = (f32[4,4,64,128]{3,2,1,0:T(8,128)S(1)}, bf16[2,4,64,128]{3,2,1,0:T(8,128)(2,1)S(1)}, bf16[2,4,64,128]{3,2,1,0:T(8,128)(2,1)S(1)}) custom-call(s32[4,16]{1,0:T(4,128)S(1)} %copy-done.1, bf16[16,128,128]{2,1,0:T(8,128)(2,1)S(1)} %get-tuple-element.62.refs_0_, bf16[16,128,128]{2,1,0:T(8,128)(2,1)S(1)} %collective-permute-done.11.refs_1_, ...), custom_call_target="tpu_custom_call" | custom-call | flops 10000000000 | bytes 10000 | tf_op jit(solution)/shard_map/forward_product/pallas_call | solution.py:23
  38.3 0.4 collective-permute-start.15
  38.7 3.0 %collective-permute-done.14.other = bf16[2,4,64,128]{3,2,1,0:T(8,128)(2,1)S(1)} collective-permute-done((bf16[2,4,64,128]{3,2,1,0:T(8,128)(2,1)S(1)}, bf16[2,4,64,128]{3,2,1,0:T(8,128)(2,1)S(1)}, u32[]{:S(2)}, u32[]{:S(2)}) %collective-permute-start.14) | collective-permute-done | bytes 131104 | tf_op jit(solution)/shard_map/ppermute | solution.py:37
  42.0 2.1 %collective-permute-start.17 = (bf16[2,4,64,128]{3,2,1,0:T(8,128)(2,1)S(1)}, bf16[2,4,64,128]{3,2,1,0:T(8,128)(2,1)S(1)}, u32[]{:S(2)}, u32[]{:S(2)}) collective-permute-start(bf16[2,4,64,128]{3,2,1,0:T(8,128)(2,1)S(1)} %get-tuple-element.70), channel_id=1, source_target_pairs={{0,4},{4,0},{8,12},{12,8},{1,5},{5,1},{9,13},{13,9},{2,6},{6,2},{1... | collective-permute-start | bytes 393224 | tf_op jit(solution)/shard_map/ppermute | solution.py:37
  44.0 3.9 %collective-permute-done.18.refs_1_ = bf16[2,4,64,128]{3,2,1,0:T(8,128)(2,1)S(1)} collective-permute-done((bf16[2,4,64,128]{3,2,1,0:T(8,128)(2,1)S(1)}, bf16[2,4,64,128]{3,2,1,0:T(8,128)(2,1)S(1)}, u32[]{:S(2)}, u32[]{:S(2)}) %collective-permute-start.18) | collective-permute-done | bytes 131104 | tf_op jit(solution)/shard_map/ppermute | solution.py:37
  47.9 1.4 %collective-permute-done.17.refs_0_ = bf16[2,4,64,128]{3,2,1,0:T(8,128)(2,1)S(1)} collective-permute-done((bf16[2,4,64,128]{3,2,1,0:T(8,128)(2,1)S(1)}, bf16[2,4,64,128]{3,2,1,0:T(8,128)(2,1)S(1)}, u32[]{:S(2)}, u32[]{:S(2)}) %collective-permute-start.17) | collective-permute-done | bytes 131104 | tf_op jit(solution)/shard_map/ppermute | solution.py:37
  49.4 1.8 %collective-permute-start.21 = (bf16[2,4,64,128]{3,2,1,0:T(8,128)(2,1)S(1)}, bf16[2,4,64,128]{3,2,1,0:T(8,128)(2,1)S(1)}, u32[]{:S(2)}, u32[]{:S(2)}) collective-permute-start(bf16[2,4,64,128]{3,2,1,0:T(8,128)(2,1)S(1)} %get-tuple-element.72), channel_id=1, source_target_pairs={{0,8},{4,12},{8,0},{12,4},{1,9},{5,13},{9,1},{13,5},{2,10},{6,14},... | collective-permute-start | bytes 393224 | tf_op jit(solution)/shard_map/ppermute | solution.py:37
  51.2 3.3 %adjoint_product.2 = (f32[16,128,128]{2,1,0:T(8,128)S(1)}, f32[16,128,128]{2,1,0:T(8,128)S(1)}, bf16[16,128,128]{2,1,0:T(8,128)(2,1)S(1)}, bf16[8,128,128]{2,1,0:T(8,128)(2,1)S(1)}, bf16[8,128,128]{2,1,0:T(8,128)(2,1)S(1)}) custom-call(s32[4,16]{1,0:T(4,128)S(1)} %copy-done.1, bf16[2,4,64,128]{3,2,1,0:T(8,128)(2,1)S(1)} %residual.2.refs_0_, ...), custom_call_target="tpu_custom_call" | custom-call | flops 10000000000 | bytes 10000 | tf_op jit(solution)/shard_map/adjoint_product/pallas_call | solution.py:23
  54.6 0.5 collective-permute-start.23
  55.1 2.6 %collective-permute-done.21.other = bf16[2,4,64,128]{3,2,1,0:T(8,128)(2,1)S(1)} collective-permute-done((bf16[2,4,64,128]{3,2,1,0:T(8,128)(2,1)S(1)}, bf16[2,4,64,128]{3,2,1,0:T(8,128)(2,1)S(1)}, u32[]{:S(2)}, u32[]{:S(2)}) %collective-permute-start.21) | collective-permute-done | bytes 131104 | tf_op jit(solution)/shard_map/ppermute | solution.py:37
  57.8 0.2 collective-permute-start.22
  58.2 1.6 %collective-permute-start.30 = (bf16[16,128,128]{2,1,0:T(8,128)(2,1)S(1)}, bf16[16,128,128]{2,1,0:T(8,128)(2,1)S(1)}, u32[]{:S(2)}, u32[]{:S(2)}) collective-permute-start(bf16[16,128,128]{2,1,0:T(8,128)(2,1)S(1)} %adjoint_share.2), channel_id=1, source_target_pairs={{0,2},{2,0},{1,3},{3,1},{4,6},{6,4},{5,7},{7,5},{8,10},{10,8},{9,1... | collective-permute-start | bytes 1572872 | tf_op jit(solution)/shard_map/ppermute | solution.py:37
  60.0 2.9 %collective-permute-done.22.refs_1_ = bf16[2,4,64,128]{3,2,1,0:T(8,128)(2,1)S(1)} collective-permute-done((bf16[2,4,64,128]{3,2,1,0:T(8,128)(2,1)S(1)}, bf16[2,4,64,128]{3,2,1,0:T(8,128)(2,1)S(1)}, u32[]{:S(2)}, u32[]{:S(2)}) %collective-permute-start.22) | collective-permute-done | bytes 131104 | tf_op jit(solution)/shard_map/ppermute | solution.py:37
  62.9 1.3 %collective-permute-done.26.refs_3_ = bf16[2,4,64,128]{3,2,1,0:T(8,128)(2,1)S(1)} collective-permute-done((bf16[2,4,64,128]{3,2,1,0:T(8,128)(2,1)S(1)}, bf16[2,4,64,128]{3,2,1,0:T(8,128)(2,1)S(1)}, u32[]{:S(2)}, u32[]{:S(2)}) %collective-permute-start.26) | collective-permute-done | bytes 131104 | tf_op jit(solution)/shard_map/ppermute | solution.py:37
  64.2 3.3 %adjoint_product.3 = (f32[16,128,128]{2,1,0:T(8,128)S(1)}, f32[16,128,128]{2,1,0:T(8,128)S(1)}, bf16[16,128,128]{2,1,0:T(8,128)(2,1)S(1)}, bf16[8,128,128]{2,1,0:T(8,128)(2,1)S(1)}, bf16[8,128,128]{2,1,0:T(8,128)(2,1)S(1)}) custom-call(s32[4,16]{1,0:T(4,128)S(1)} %copy-done.1, bf16[2,4,64,128]{3,2,1,0:T(8,128)(2,1)S(1)} %residual.3.refs_1_.refs_0_, ...), custom_call_target="tpu_custom_call" | custom-call | flops 1 | bytes 10000 | tf_op jit(solution)/shard_map/adjoint_product/pallas_call | solution.py:23
  67.8 0.4 collective-permute-start.28
  68.1 0.8 join.1
  68.9 0.3 collective-permute-done.27.refs_0_
  69.1 0.4 collective-permute-done.28.refs_1_
  69.6 1.0 %collective-permute-start.32 = (bf16[16,128,128]{2,1,0:T(8,128)(2,1)S(1)}, bf16[16,128,128]{2,1,0:T(8,128)(2,1)S(1)}, u32[]{:S(2)}, u32[]{:S(2)}) collective-permute-start(bf16[16,128,128]{2,1,0:T(8,128)(2,1)S(1)} %adjoint_share.3), channel_id=1, source_target_pairs={{0,2},{2,0},{1,3},{3,1},{4,6},{6,4},{5,7},{7,5},{8,10},{10,8},{9,1... | collective-permute-start | bytes 1572872 | tf_op jit(solution)/shard_map/ppermute | solution.py:37
  70.6 2.0 %collective-permute-done.30.refs_1_ = bf16[16,128,128]{2,1,0:T(8,128)(2,1)S(1)} collective-permute-done((bf16[16,128,128]{2,1,0:T(8,128)(2,1)S(1)}, bf16[16,128,128]{2,1,0:T(8,128)(2,1)S(1)}, u32[]{:S(2)}, u32[]{:S(2)}) %collective-permute-start.30) | collective-permute-done | bytes 524320 | tf_op jit(solution)/shard_map/ppermute | solution.py:37
  72.8 11.0 %collective-permute-done.32.refs_1_ = bf16[16,128,128]{2,1,0:T(8,128)(2,1)S(1)} collective-permute-done((bf16[16,128,128]{2,1,0:T(8,128)(2,1)S(1)}, bf16[16,128,128]{2,1,0:T(8,128)(2,1)S(1)}, u32[]{:S(2)}, u32[]{:S(2)}) %collective-permute-start.32) | collective-permute-done | bytes 524320 | tf_op jit(solution)/shard_map/ppermute | solution.py:37
  83.8 1.4 %adjoint_sum.1 = bf16[2,16,128,128]{3,2,1,0:T(8,128)(2,1)} custom-call(f32[16,128,128]{2,1,0:T(8,128)S(1)} %total.1.done, f32[16,128,128]{2,1,0:T(8,128)S(1)} %get-tuple-element.87.mine, bf16[16,128,128]{2,1,0:T(8,128)(2,1)S(1)} %collective-permute-done.31.refs_0_, bf16[16,128,128]{2,1,0:T(8,128)(2,1)S(1)} %collective-permute-done.32.refs_1_), custom_call_target="tpu_custom_call" | custom-call | flops 1000000 | bytes 10000 | tf_op jit(solution)/shard_map/adjoint_sum/pallas_call | solution.py:23
  (47 shorter events, 2.3 us)
Async XLA Ops:
  0.6 1.2 %copy-start = (bf16[2,16,128,128]{3,2,1,0:T(8,128)(2,1)S(1)}, bf16[2,16,128,128]{3,2,1,0:T(8,128)(2,1)}, u32[]{:S(2)}) copy-start(bf16[2,16,128,128]{3,2,1,0:T(8,128)(2,1)} %source.1) | copy-start | bytes 3145732
  2.2 17.4 %collective-permute-start.3 = (bf16[10,128,128]{2,1,0:T(8,128)(2,1)S(1)}, bf16[10,128,128]{2,1,0:T(8,128)(2,1)S(1)}, u32[]{:S(2)}, u32[]{:S(2)}) collective-permute-start(bf16[10,128,128]{2,1,0:T(8,128)(2,1)S(1)} %get-tuple-element.46.refs_0_), channel_id=1, source_target_pairs={{0,1},{1,0},{2,3},{3,2},{4,5},{5,4},{6,7},{7,6},{8,9},{9,8},{10,11... | collective-permute-start | bytes 983048 | tf_op jit(solution)/shard_map/ppermute | solution.py:37
  2.7 15.0 %collective-permute-start = (bf16[10,128,128]{2,1,0:T(8,128)(2,1)S(1)}, bf16[10,128,128]{2,1,0:T(8,128)(2,1)S(1)}, u32[]{:S(2)}, u32[]{:S(2)}) collective-permute-start(bf16[10,128,128]{2,1,0:T(8,128)(2,1)S(1)} %get-tuple-element.46.refs_0_), channel_id=1, source_target_pairs={{0,2},{2,0},{1,3},{3,1},{4,6},{6,4},{5,7},{7,5},{8,10},{10,8},{9,1... | collective-permute-start | bytes 983048 | tf_op jit(solution)/shard_map/ppermute | solution.py:37
  5.3 10.3 %collective-permute-start.2 = (bf16[4,64,128]{2,1,0:T(8,128)(2,1)}, bf16[4,64,128]{2,1,0:T(8,128)(2,1)S(1)}, u32[]{:S(2)}, u32[]{:S(2)}) collective-permute-start(bf16[4,64,128]{2,1,0:T(8,128)(2,1)} %refs_2_.3), channel_id=1, source_target_pairs={{0,8},{4,12},{8,0},{12,4},{1,9},{5,13},{9,1},{13,5},{2,10},{6,14},... | collective-permute-start | bytes 196616 | tf_op jit(solution)/shard_map/ppermute | solution.py:37
  7.9 9.8 %collective-permute-start.1 = (bf16[2,4,64,128]{3,2,1,0:T(8,128)(2,1)}, bf16[2,4,64,128]{3,2,1,0:T(8,128)(2,1)S(1)}, u32[]{:S(2)}, u32[]{:S(2)}) collective-permute-start(bf16[2,4,64,128]{3,2,1,0:T(8,128)(2,1)} %refs_0_.3), channel_id=1, source_target_pairs={{0,8},{4,12},{8,0},{12,4},{1,9},{5,13},{9,1},{13,5},{2,10},{6,14},... | collective-permute-start | bytes 393224 | tf_op jit(solution)/shard_map/ppermute | solution.py:37
  8.2 11.7 %copy-start.1 = (s32[4,16]{1,0:T(4,128)S(1)}, s32[4,16]{1,0:T(4,128)}, u32[]{:S(2)}) copy-start(s32[4,16]{1,0:T(4,128)} %ranks.7) | copy-start | bytes 772
  8.2 10.1 %collective-permute-start.5 = (bf16[6,128,128]{2,1,0:T(8,128)(2,1)S(1)}, bf16[6,128,128]{2,1,0:T(8,128)(2,1)S(1)}, u32[]{:S(2)}, u32[]{:S(2)}) collective-permute-start(bf16[6,128,128]{2,1,0:T(8,128)(2,1)S(1)} %get-tuple-element.51.refs_4_), channel_id=1, source_target_pairs={{0,2},{2,0},{1,3},{3,1},{4,6},{6,4},{5,7},{7,5},{8,10},{10,8},{9,1... | collective-permute-start | bytes 589832 | tf_op jit(solution)/shard_map/ppermute | solution.py:37
  8.4 2.5 %copy-start.2 = (bf16[2,4,16,40,512]{4,3,2,1,0:T(8,128)(2,1)S(1)}, bf16[2,4,16,40,512]{4,3,2,1,0:T(8,128)(2,1)}, u32[]{:S(2)}) copy-start(bf16[2,4,16,40,512]{4,3,2,1,0:T(8,128)(2,1)} %second_in.1) | copy-start | bytes 15728644
  10.9 2.5 %copy-start.3 = (bf16[2,4,16,40,512]{4,3,2,1,0:T(8,128)(2,1)S(1)}, bf16[2,4,16,40,512]{4,3,2,1,0:T(8,128)(2,1)}, u32[]{:S(2)}) copy-start(bf16[2,4,16,40,512]{4,3,2,1,0:T(8,128)(2,1)} %basis_in.1) | copy-start | bytes 15728644
  17.7 2.2 %collective-permute-start.4 = (bf16[10,128,128]{2,1,0:T(8,128)(2,1)S(1)}, bf16[10,128,128]{2,1,0:T(8,128)(2,1)S(1)}, u32[]{:S(2)}, u32[]{:S(2)}) collective-permute-start(bf16[10,128,128]{2,1,0:T(8,128)(2,1)S(1)} %collective-permute-done.refs_1_), channel_id=1, source_target_pairs={{0,1},{1,0},{2,3},{3,2},{4,5},{5,4},{6,7},{7,6},{8,9},{9,8},{10,11... | collective-permute-start | bytes 983048 | tf_op jit(solution)/shard_map/ppermute | solution.py:37
  17.7 14.3 %collective-permute-start.11 = (bf16[16,128,128]{2,1,0:T(8,128)(2,1)S(1)}, bf16[16,128,128]{2,1,0:T(8,128)(2,1)S(1)}, u32[]{:S(2)}, u32[]{:S(2)}) collective-permute-start(bf16[16,128,128]{2,1,0:T(8,128)(2,1)S(1)} %get-tuple-element.62.refs_0_), channel_id=1, source_target_pairs={{0,2},{2,0},{1,3},{3,1},{4,6},{6,4},{5,7},{7,5},{8,10},{10,8},{9,1... | collective-permute-start | bytes 1572872 | tf_op jit(solution)/shard_map/ppermute | solution.py:37
  18.1 1.5 %collective-permute-start.6 = (bf16[6,128,128]{2,1,0:T(8,128)(2,1)S(1)}, bf16[6,128,128]{2,1,0:T(8,128)(2,1)S(1)}, u32[]{:S(2)}, u32[]{:S(2)}) collective-permute-start(bf16[6,128,128]{2,1,0:T(8,128)(2,1)S(1)} %get-tuple-element.51.refs_4_), channel_id=1, source_target_pairs={{0,1},{1,0},{2,3},{3,2},{4,5},{5,4},{6,7},{7,6},{8,9},{9,8},{10,11... | collective-permute-start | bytes 589832 | tf_op jit(solution)/shard_map/ppermute | solution.py:37
  18.3 1.6 %collective-permute-start.7 = (bf16[6,128,128]{2,1,0:T(8,128)(2,1)S(1)}, bf16[6,128,128]{2,1,0:T(8,128)(2,1)S(1)}, u32[]{:S(2)}, u32[]{:S(2)}) collective-permute-start(bf16[6,128,128]{2,1,0:T(8,128)(2,1)S(1)} %collective-permute-done.5.refs_5_), channel_id=1, source_target_pairs={{0,1},{1,0},{2,3},{3,2},{4,5},{5,4},{6,7},{7,6},{8,9},{9,8},{10,11... | collective-permute-start | bytes 589832 | tf_op jit(solution)/shard_map/ppermute | solution.py:37
  23.3 1.4 %collective-permute-start.8 = (bf16[2,4,64,128]{3,2,1,0:T(8,128)(2,1)S(1)}, bf16[2,4,64,128]{3,2,1,0:T(8,128)(2,1)S(1)}, u32[]{:S(2)}, u32[]{:S(2)}) collective-permute-start(bf16[2,4,64,128]{3,2,1,0:T(8,128)(2,1)S(1)} %get-tuple-element.55), channel_id=1, source_target_pairs={{0,1},{1,0},{2,3},{3,2},{4,5},{5,4},{6,7},{7,6},{8,9},{9,8},{10,11... | collective-permute-start | bytes 393224 | tf_op jit(solution)/shard_map/ppermute | solution.py:37
  23.5 1.4 %collective-permute-start.9 = (bf16[2,4,64,128]{3,2,1,0:T(8,128)(2,1)S(1)}, bf16[2,4,64,128]{3,2,1,0:T(8,128)(2,1)S(1)}, u32[]{:S(2)}, u32[]{:S(2)}) collective-permute-start(bf16[2,4,64,128]{3,2,1,0:T(8,128)(2,1)S(1)} %get-tuple-element.56), channel_id=1, source_target_pairs={{0,1},{1,0},{2,3},{3,2},{4,5},{5,4},{6,7},{7,6},{8,9},{9,8},{10,11... | collective-permute-start | bytes 393224 | tf_op jit(solution)/shard_map/ppermute | solution.py:37
  25.0 5.8 %collective-permute-start.10 = (bf16[2,4,64,128]{3,2,1,0:T(8,128)(2,1)S(1)}, bf16[2,4,64,128]{3,2,1,0:T(8,128)(2,1)S(1)}, u32[]{:S(2)}, u32[]{:S(2)}) collective-permute-start(bf16[2,4,64,128]{3,2,1,0:T(8,128)(2,1)S(1)} %get-tuple-element.58), channel_id=1, source_target_pairs={{0,4},{4,0},{8,12},{12,8},{1,5},{5,1},{9,13},{13,9},{2,6},{6,2},{1... | collective-permute-start | bytes 393224 | tf_op jit(solution)/shard_map/ppermute | solution.py:37
  30.8 10.9 %copy-start.4 = (bf16[2,4,64,128]{3,2,1,0:T(8,128)(2,1)S(1)}, bf16[2,4,64,128]{3,2,1,0:T(8,128)(2,1)}, u32[]{:S(2)}) copy-start(bf16[2,4,64,128]{3,2,1,0:T(8,128)(2,1)} %refs_0_.3) | copy-start | bytes 393220
  30.8 10.9 %copy-start.5 = (bf16[4,64,128]{2,1,0:T(8,128)(2,1)S(1)}, bf16[4,64,128]{2,1,0:T(8,128)(2,1)}, u32[]{:S(2)}) copy-start(bf16[4,64,128]{2,1,0:T(8,128)(2,1)} %refs_2_.3) | copy-start | bytes 196612
  32.0 1.9 %collective-permute-start.12 = (bf16[16,128,128]{2,1,0:T(8,128)(2,1)S(1)}, bf16[16,128,128]{2,1,0:T(8,128)(2,1)S(1)}, u32[]{:S(2)}, u32[]{:S(2)}) collective-permute-start(bf16[16,128,128]{2,1,0:T(8,128)(2,1)S(1)} %get-tuple-element.62.refs_0_), channel_id=1, source_target_pairs={{0,1},{1,0},{2,3},{3,2},{4,5},{5,4},{6,7},{7,6},{8,9},{9,8},{10,11... | collective-permute-start | bytes 1572872 | tf_op jit(solution)/shard_map/ppermute | solution.py:37
  32.0 2.7 %collective-permute-start.13 = (bf16[16,128,128]{2,1,0:T(8,128)(2,1)S(1)}, bf16[16,128,128]{2,1,0:T(8,128)(2,1)S(1)}, u32[]{:S(2)}, u32[]{:S(2)}) collective-permute-start(bf16[16,128,128]{2,1,0:T(8,128)(2,1)S(1)} %collective-permute-done.11.refs_1_), channel_id=1, source_target_pairs={{0,1},{1,0},{2,3},{3,2},{4,5},{5,4},{6,7},{7,6},{8,9},{9,8},{10,11... | collective-permute-start | bytes 1572872 | tf_op jit(solution)/shard_map/ppermute | solution.py:37
  32.5 9.1 %collective-permute-start.14 = (bf16[2,4,64,128]{3,2,1,0:T(8,128)(2,1)S(1)}, bf16[2,4,64,128]{3,2,1,0:T(8,128)(2,1)S(1)}, u32[]{:S(2)}, u32[]{:S(2)}) collective-permute-start(bf16[2,4,64,128]{3,2,1,0:T(8,128)(2,1)S(1)} %get-tuple-element.61), channel_id=1, source_target_pairs={{0,8},{4,12},{8,0},{12,4},{1,9},{5,13},{9,1},{13,5},{2,10},{6,14},... | collective-permute-start | bytes 393224 | tf_op jit(solution)/shard_map/ppermute | solution.py:37
  38.1 3.8 %collective-permute-start.16 = (bf16[2,4,64,128]{3,2,1,0:T(8,128)(2,1)S(1)}, bf16[2,4,64,128]{3,2,1,0:T(8,128)(2,1)S(1)}, u32[]{:S(2)}, u32[]{:S(2)}) collective-permute-start(bf16[2,4,64,128]{3,2,1,0:T(8,128)(2,1)S(1)} %get-tuple-element.64), channel_id=1, source_target_pairs={{0,1},{1,0},{2,3},{3,2},{4,5},{5,4},{6,7},{7,6},{8,9},{9,8},{10,11... | collective-permute-start | bytes 393224 | tf_op jit(solution)/shard_map/ppermute | solution.py:37
  38.3 3.6 %collective-permute-start.15 = (bf16[2,4,64,128]{3,2,1,0:T(8,128)(2,1)S(1)}, bf16[2,4,64,128]{3,2,1,0:T(8,128)(2,1)S(1)}, u32[]{:S(2)}, u32[]{:S(2)}) collective-permute-start(bf16[2,4,64,128]{3,2,1,0:T(8,128)(2,1)S(1)} %get-tuple-element.68), channel_id=1, source_target_pairs={{0,1},{1,0},{2,3},{3,2},{4,5},{5,4},{6,7},{7,6},{8,9},{9,8},{10,11... | collective-permute-start | bytes 393224 | tf_op jit(solution)/shard_map/ppermute | solution.py:37
  41.8 6.1 %collective-permute-start.18 = (bf16[2,4,64,128]{3,2,1,0:T(8,128)(2,1)S(1)}, bf16[2,4,64,128]{3,2,1,0:T(8,128)(2,1)S(1)}, u32[]{:S(2)}, u32[]{:S(2)}) collective-permute-start(bf16[2,4,64,128]{3,2,1,0:T(8,128)(2,1)S(1)} %residual.2.refs_0_), channel_id=1, source_target_pairs={{0,4},{4,0},{8,12},{12,8},{1,5},{5,1},{9,13},{13,9},{2,6},{6,2},{1... | collective-permute-start | bytes 393224 | tf_op jit(solution)/shard_map/ppermute | solution.py:37
  42.0 7.4 %collective-permute-start.17 = (bf16[2,4,64,128]{3,2,1,0:T(8,128)(2,1)S(1)}, bf16[2,4,64,128]{3,2,1,0:T(8,128)(2,1)S(1)}, u32[]{:S(2)}, u32[]{:S(2)}) collective-permute-start(bf16[2,4,64,128]{3,2,1,0:T(8,128)(2,1)S(1)} %get-tuple-element.70), channel_id=1, source_target_pairs={{0,4},{4,0},{8,12},{12,8},{1,5},{5,1},{9,13},{13,9},{2,6},{6,2},{1... | collective-permute-start | bytes 393224 | tf_op jit(solution)/shard_map/ppermute | solution.py:37
  44.0 7.2 %collective-permute-start.19 = (bf16[2,4,64,128]{3,2,1,0:T(8,128)(2,1)S(1)}, bf16[2,4,64,128]{3,2,1,0:T(8,128)(2,1)S(1)}, u32[]{:S(2)}, u32[]{:S(2)}) collective-permute-start(bf16[2,4,64,128]{3,2,1,0:T(8,128)(2,1)S(1)} %residual.2.refs_0_), channel_id=1, source_target_pairs={{0,1},{1,0},{2,3},{3,2},{4,5},{5,4},{6,7},{7,6},{8,9},{9,8},{10,11... | collective-permute-start | bytes 393224 | tf_op jit(solution)/shard_map/ppermute | solution.py:37
  47.9 3.2 %collective-permute-start.20 = (bf16[2,4,64,128]{3,2,1,0:T(8,128)(2,1)S(1)}, bf16[2,4,64,128]{3,2,1,0:T(8,128)(2,1)S(1)}, u32[]{:S(2)}, u32[]{:S(2)}) collective-permute-start(bf16[2,4,64,128]{3,2,1,0:T(8,128)(2,1)S(1)} %collective-permute-done.18.refs_1_), channel_id=1, source_target_pairs={{0,1},{1,0},{2,3},{3,2},{4,5},{5,4},{6,7},{7,6},{8,9},{9,8},{10,11... | collective-permute-start | bytes 393224 | tf_op jit(solution)/shard_map/ppermute | solution.py:37
  49.4 8.3 %collective-permute-start.21 = (bf16[2,4,64,128]{3,2,1,0:T(8,128)(2,1)S(1)}, bf16[2,4,64,128]{3,2,1,0:T(8,128)(2,1)S(1)}, u32[]{:S(2)}, u32[]{:S(2)}) collective-permute-start(bf16[2,4,64,128]{3,2,1,0:T(8,128)(2,1)S(1)} %get-tuple-element.72), channel_id=1, source_target_pairs={{0,8},{4,12},{8,0},{12,4},{1,9},{5,13},{9,1},{13,5},{2,10},{6,14},... | collective-permute-start | bytes 393224 | tf_op jit(solution)/shard_map/ppermute | solution.py:37
  54.5 3.6 %collective-permute-start.24 = (bf16[8,128,128]{2,1,0:T(8,128)(2,1)S(1)}, bf16[8,128,128]{2,1,0:T(8,128)(2,1)S(1)}, u32[]{:S(2)}, u32[]{:S(2)}) collective-permute-start(bf16[8,128,128]{2,1,0:T(8,128)(2,1)S(1)} %get-tuple-element.74), channel_id=1, source_target_pairs={{0,1},{1,0},{2,3},{3,2},{4,5},{5,4},{6,7},{7,6},{8,9},{9,8},{10,11... | collective-permute-start | bytes 786440 | tf_op jit(solution)/shard_map/ppermute | solution.py:37
  54.6 3.5 %collective-permute-start.23 = (bf16[8,128,128]{2,1,0:T(8,128)(2,1)S(1)}, bf16[8,128,128]{2,1,0:T(8,128)(2,1)S(1)}, u32[]{:S(2)}, u32[]{:S(2)}) collective-permute-start(bf16[8,128,128]{2,1,0:T(8,128)(2,1)S(1)} %get-tuple-element.79), channel_id=1, source_target_pairs={{0,1},{1,0},{2,3},{3,2},{4,5},{5,4},{6,7},{7,6},{8,9},{9,8},{10,11... | collective-permute-start | bytes 786440 | tf_op jit(solution)/shard_map/ppermute | solution.py:37
  57.8 5.1 %collective-permute-start.22 = (bf16[2,4,64,128]{3,2,1,0:T(8,128)(2,1)S(1)}, bf16[2,4,64,128]{3,2,1,0:T(8,128)(2,1)S(1)}, u32[]{:S(2)}, u32[]{:S(2)}) collective-permute-start(bf16[2,4,64,128]{3,2,1,0:T(8,128)(2,1)S(1)} %residual.3.refs_1_.refs_0_), channel_id=1, source_target_pairs={{0,4},{4,0},{8,12},{12,8},{1,5},{5,1},{9,13},{13,9},{2,6},{6,2},{1... | collective-permute-start | bytes 393224 | tf_op jit(solution)/shard_map/ppermute | solution.py:37
  58.2 12.5 %collective-permute-start.29 = (bf16[16,128,128]{2,1,0:T(8,128)(2,1)S(1)}, bf16[16,128,128]{2,1,0:T(8,128)(2,1)S(1)}, u32[]{:S(2)}, u32[]{:S(2)}) collective-permute-start(bf16[16,128,128]{2,1,0:T(8,128)(2,1)S(1)} %get-tuple-element.86), channel_id=1, source_target_pairs={{0,1},{1,0},{2,3},{3,2},{4,5},{5,4},{6,7},{7,6},{8,9},{9,8},{10,11... | collective-permute-start | bytes 1572872 | tf_op jit(solution)/shard_map/ppermute | solution.py:37
  58.2 14.4 %collective-permute-start.30 = (bf16[16,128,128]{2,1,0:T(8,128)(2,1)S(1)}, bf16[16,128,128]{2,1,0:T(8,128)(2,1)S(1)}, u32[]{:S(2)}, u32[]{:S(2)}) collective-permute-start(bf16[16,128,128]{2,1,0:T(8,128)(2,1)S(1)} %adjoint_share.2), channel_id=1, source_target_pairs={{0,2},{2,0},{1,3},{3,1},{4,6},{6,4},{5,7},{7,5},{8,10},{10,8},{9,1... | collective-permute-start | bytes 1572872 | tf_op jit(solution)/shard_map/ppermute | solution.py:37
  59.8 3.1 %collective-permute-start.25 = (bf16[2,4,64,128]{3,2,1,0:T(8,128)(2,1)S(1)}, bf16[2,4,64,128]{3,2,1,0:T(8,128)(2,1)S(1)}, u32[]{:S(2)}, u32[]{:S(2)}) collective-permute-start(bf16[2,4,64,128]{3,2,1,0:T(8,128)(2,1)S(1)} %residual.3.refs_1_.refs_0_), channel_id=1, source_target_pairs={{0,1},{1,0},{2,3},{3,2},{4,5},{5,4},{6,7},{7,6},{8,9},{9,8},{10,11... | collective-permute-start | bytes 393224 | tf_op jit(solution)/shard_map/ppermute | solution.py:37
  62.9 1.3 %collective-permute-start.26 = (bf16[2,4,64,128]{3,2,1,0:T(8,128)(2,1)S(1)}, bf16[2,4,64,128]{3,2,1,0:T(8,128)(2,1)S(1)}, u32[]{:S(2)}, u32[]{:S(2)}) collective-permute-start(bf16[2,4,64,128]{3,2,1,0:T(8,128)(2,1)S(1)} %collective-permute-done.22.refs_1_), channel_id=1, source_target_pairs={{0,1},{1,0},{2,3},{3,2},{4,5},{5,4},{6,7},{7,6},{8,9},{9,8},{10,11... | collective-permute-start | bytes 393224 | tf_op jit(solution)/shard_map/ppermute | solution.py:37
  67.5 1.6 %collective-permute-start.27 = (bf16[8,128,128]{2,1,0:T(8,128)(2,1)S(1)}, bf16[8,128,128]{2,1,0:T(8,128)(2,1)S(1)}, u32[]{:S(2)}, u32[]{:S(2)}) collective-permute-start(bf16[8,128,128]{2,1,0:T(8,128)(2,1)S(1)} %get-tuple-element.82), channel_id=1, source_target_pairs={{0,1},{1,0},{2,3},{3,2},{4,5},{5,4},{6,7},{7,6},{8,9},{9,8},{10,11... | collective-permute-start | bytes 786440 | tf_op jit(solution)/shard_map/ppermute | solution.py:37
  67.8 1.8 %collective-permute-start.28 = (bf16[8,128,128]{2,1,0:T(8,128)(2,1)S(1)}, bf16[8,128,128]{2,1,0:T(8,128)(2,1)S(1)}, u32[]{:S(2)}, u32[]{:S(2)}) collective-permute-start(bf16[8,128,128]{2,1,0:T(8,128)(2,1)S(1)} %get-tuple-element.83), channel_id=1, source_target_pairs={{0,1},{1,0},{2,3},{3,2},{4,5},{5,4},{6,7},{7,6},{8,9},{9,8},{10,11... | collective-permute-start | bytes 786440 | tf_op jit(solution)/shard_map/ppermute | solution.py:37
  69.6 14.2 %collective-permute-start.32 = (bf16[16,128,128]{2,1,0:T(8,128)(2,1)S(1)}, bf16[16,128,128]{2,1,0:T(8,128)(2,1)S(1)}, u32[]{:S(2)}, u32[]{:S(2)}) collective-permute-start(bf16[16,128,128]{2,1,0:T(8,128)(2,1)S(1)} %adjoint_share.3), channel_id=1, source_target_pairs={{0,2},{2,0},{1,3},{3,1},{4,6},{6,4},{5,7},{7,5},{8,10},{10,8},{9,1... | collective-permute-start | bytes 1572872 | tf_op jit(solution)/shard_map/ppermute | solution.py:37
  70.6 2.2 %collective-permute-start.31 = (bf16[16,128,128]{2,1,0:T(8,128)(2,1)S(1)}, bf16[16,128,128]{2,1,0:T(8,128)(2,1)S(1)}, u32[]{:S(2)}, u32[]{:S(2)}) collective-permute-start(bf16[16,128,128]{2,1,0:T(8,128)(2,1)S(1)} %get-tuple-element.89), channel_id=1, source_target_pairs={{0,1},{1,0},{2,3},{3,2},{4,5},{5,4},{6,7},{7,6},{8,9},{9,8},{10,11... | collective-permute-start | bytes 1572872 | tf_op jit(solution)/shard_map/ppermute | solution.py:37

commit v5 on v4

--- a/solution.py
+++ b/solution.py
@@ -13,10 +13,12 @@
 LANES = 128
 VM = pl.BlockSpec(memory_space=pltpu.VMEM)
 SM = pl.BlockSpec(memory_space=pltpu.SMEM)
+HBM = pl.BlockSpec(memory_space=pltpu.HBM)
 ANY = pl.BlockSpec(memory_space=pl.ANY)
 MIB = 1024 * 1024
 LARGE = 10**10
 SPLIT = 2
+BLOCKS = (1, 2)
 
 
 def call(kernel, name, outs, ins, in_specs=None, scratch=(), limit=6 * MIB, cost=10**6):
@@ -32,6 +34,10 @@
     )(*ins)
 
 
+def in_hbm(value):
+    return pltpu.with_memory_space_constraint(value, pltpu.HBM)
+
+
 def swap(axis_name, step, value):
     size = lax.axis_size(axis_name)
     return lax.ppermute(value, axis_name, [(i, i ^ step) for i in range(size)])
@@ -48,15 +54,42 @@
     return pltpu.roll(value, width // 2, value.ndim - 1) * sign
 
 
-def waves_kernel(source, *outs):
-    part = outs[0].shape[-1] // 2
-    at = 0
-    for out in outs:
-        for j in range(out.shape[0]):
-            c, row = divmod(at, source.shape[1])
-            lanes = slice(c * part, (c + 1) * part)
-            out[j] = jnp.concatenate([source[0, row, :, lanes], source[1, row, :, lanes]], -1)
-            at += 1
+def side_by_side(source, j, c, part):
+    lanes = slice(c * part, (c + 1) * part)
+    return jnp.concatenate([source[0, j, :, lanes], source[1, j, :, lanes]], -1)
+
+
+def first_kernel(source, out, held, sems):
+    n = out.shape[0]
+    copies = [pltpu.make_async_copy(source.at[p, :n], held.at[p], sems.at[p]) for p in range(2)]
+    for copy in copies:
+        copy.start()
+    for copy in copies:
+        copy.wait()
+    for j in range(n):
+        out[j] = side_by_side(held, j, 0, out.shape[-1] // 2)
+
+
+def waves_kernel(source, rest, whole, *others):
+    columns, part = whole.shape[0], whole.shape[-1] // 2
+    first = columns - rest.shape[0]
+    for j in range(columns):
+        whole[j] = side_by_side(source, j, 0, part)
+        if j >= first:
+            rest[j - first] = whole[j]
+        for c, other in enumerate(others):
+            other[j] = side_by_side(source, j, c + 1, part)
+
+
+def data_kernel(observed, amplitude, out, sems):
+    copies = [
+        pltpu.make_async_copy(observed, out.at[:2], sems.at[0]),
+        pltpu.make_async_copy(amplitude, out.at[2], sems.at[1]),
+    ]
+    for copy in copies:
+        copy.start()
+    for copy in copies:
+        copy.wait()
 
 
 def load_kernel(second_in, basis_in, second, basis, sems):
@@ -91,14 +124,15 @@
 
 
 def residual_kernel(c, mine, other, *refs):
-    observed, amplitude, out = refs[:2], refs[2:4], refs[4]
-    part = out.shape[-1] // 2
+    arrays, outs = refs[:2], refs[2:]
+    part = outs[0].shape[-1] // 2
     lanes = slice(c * part, (c + 1) * part)
     for e in range(2):
         total = mine[e] + other[e].astype(F32)
-        data = jnp.concatenate([observed[e][0, :, :, lanes], observed[e][1, :, :, lanes]], -1)
-        weight = jnp.concatenate([amplitude[e][:, :, lanes]] * 2, -1)
-        out[e] = (weight.astype(F32) * (total - data.astype(F32))).astype(BF16)
+        data = jnp.concatenate([arrays[e][p, :, :, lanes] for p in range(2)], -1)
+        weight = jnp.concatenate([arrays[e][2, :, :, lanes]] * 2, -1)
+        value = (weight.astype(F32) * (total - data.astype(F32))).astype(BF16)
+        outs[e // outs[0].shape[0]][e % outs[0].shape[0]] = value
 
 
 def join_kernel(*refs):
@@ -133,31 +167,34 @@
             total = mine[j, lanes, :]
             for ref in others:
                 total = total + ref[j, lanes, :].astype(F32)
-            out_ref[p, j] = jnp.concatenate([done[j, lanes, :], total], 0).T.astype(out_ref.dtype)
-
-
-def forward_kernel(rs, helps, z_offsets, n_groups, ranks, *refs):
+            out_ref[p, j] = jnp.concatenate([done[j, lanes, :], total], 0).astype(out_ref.dtype).T
+
+
+def forward_kernel(rs, helps, z_offsets, counts, ranks, *refs):
     n_pieces = rs * helps
-    groups = [refs[k * n_pieces : (k + 1) * n_pieces] for k in range(n_groups)]
-    second, basis, keep_out, *sends, waves, coef, fwd = refs[n_groups * n_pieces :]
+    slots, at = [], 0
+    for count in counts:
+        slots.append([(ref, j) for ref in refs[at : at + count] for j in range(ref.shape[0])])
+        at += count
+    second, basis, keep_out, *sends, waves, coef, fwd = refs[at:]
     n_send = sends[0].shape[0]
     z, r, here = lax.axis_index("col"), lax.axis_index("row"), lax.axis_index("help")
-    _, quarter, width = groups[0][0].shape
-    spots = [(group, j) for group in groups for j in range(group[0].shape[0])]
-    columns = len(spots)
+    _, quarter, width = refs[0].shape
+    columns = len(slots[0])
     rows = basis.shape[1]
     terms = second.shape[1] // (2 * rows)
     half = rows * terms
     row_index = lax.broadcasted_iota(jnp.int32, (terms, width), 0)
     places = [((r ^ (n % rs)) * helps + (here ^ (n // rs))) * quarter for n in range(n_pieces)]
     places = [pl.multiple_of(at, quarter) for at in places]
-    for j, (group, at_j) in enumerate(spots):
+    for j in range(columns):
+        parts = [ref[n] for ref, n in (slot[j] for slot in slots)]
         if quarter % LANES == 0:
             left = jnp.concatenate([second[j, :, pl.ds(at, quarter)] for at in places], 1)
-            right = jnp.concatenate([piece[at_j] for piece in group], 0)
+            right = jnp.concatenate(parts, 0)
         else:
-            for at, piece in zip(places, group):
-                waves[j, pl.ds(at, quarter), :] = piece[at_j]
+            for at, part in zip(places, parts):
+                waves[j, pl.ds(at, quarter), :] = part
             left, right = second[j], waves[j]
         out = jnp.dot(left, right, preferred_element_type=F32)
         value = out[:half] + turn(out[half:], 1.0, -1.0)
@@ -187,7 +224,7 @@
     keeps, sends = refs[n_pieces + 2 : n_pieces + 2 + rs], refs[n_pieces + 2 + rs : -2]
     resid, back = refs[-2:]
     z, r, here = lax.axis_index("col"), lax.axis_index("row"), lax.axis_index("help")
-    blocks, rows, span, width = pieces[0].shape
+    _, rows, span, width = pieces[0].shape
     columns = second.shape[0]
     terms = second.shape[1] // (2 * rows)
     row_index = lax.broadcasted_iota(jnp.int32, (terms, width), 0)
@@ -256,23 +293,43 @@
     def share(pieces):
         return pieces + [swap("help", d, m) for d in range(1, helps) for m in pieces]
 
-    sizes = [[5 * columns // 8, 3 * columns // 8]] + [[columns]] * (CHUNKS - 1)
+    first = 5 * columns // 8
+    shapes = [((n, quarter, width), BF16) for n in (first, columns - first, columns)]
     waves = call(
+        first_kernel,
+        "first_waves",
+        shapes[:1],
+        [in_hbm(wavefield)],
+        in_specs=[HBM],
+        scratch=[pltpu.VMEM((2, first, quarter, rhs), BF16), pltpu.SemaphoreType.DMA((2,))],
+    )
+    data = call(
+        data_kernel,
+        "join_data",
+        [((3, rows, span, rhs), BF16)],
+        [after(in_hbm(observed), *waves), in_hbm(amplitude)],
+        in_specs=[HBM] * 2,
+        scratch=[pltpu.SemaphoreType.DMA((2,))],
+        cost=LARGE,
+    )[0]
+    data = [data, swap("col", far, data)]
+    rest, whole, *others = call(
         waves_kernel,
-        "split_waves",
-        [((n, quarter, width), BF16) for ns in sizes for n in ns],
-        [wavefield],
+        "other_waves",
+        shapes[1:] + shapes[2:] * (CHUNKS - 1),
+        [after(wavefield, data[0])],
+        cost=LARGE,
     )
-    waves = [waves[:2]] + [[w] for w in waves[2:]]
-    gathered = [[[w] + [swap("row", d, w) for d in range(1, rs)] for w in ws] for ws in waves]
-    data = [observed, amplitude]
-    data = [m for d in data for m in (d, swap("col", far, after(d, waves[0][0])))]
+    waves = [[*waves, rest]] + [[w] for w in others]
+    gathered = [[[swap("row", d, w) for w in ws] for d in range(1, rs)] for ws in waves]
+    wholes = [whole, *others]
+
     second, basis = call(
         load_kernel,
         "load_factors",
         [((columns, 2 * rows, terms, tile), BF16), ((2, rows, columns, terms, tile), BF16)],
         [second_factor, basis_factor],
-        in_specs=[pl.BlockSpec(memory_space=pltpu.HBM)] * 2,
+        in_specs=[HBM] * 2,
         scratch=[pltpu.SemaphoreType.DMA((2, 2 * rows))],
         cost=LARGE,
     )
@@ -280,12 +337,13 @@
     basis = basis.reshape(2, rows, columns * terms, tile)
 
     def forward(c, mine):
-        shape, piece = (zs, rows, span, width), (zs // SPLIT, rows, span, width)
-        pieces = [m for group in mine for m in share(group)]
+        split = zs if c else SPLIT
+        shape, piece = (zs, rows, span, width), (zs // split, rows, span, width)
+        pieces = [m for slot in mine for m in slot]
         return call(
-            functools.partial(forward_kernel, rs, helps, z_offsets, len(mine)),
+            functools.partial(forward_kernel, rs, helps, z_offsets, [len(slot) for slot in mine]),
             "forward_product",
-            [(shape, F32)] + [(piece, BF16)] * SPLIT,
+            [(shape, F32)] + [(piece, BF16)] * split,
             [tile_ranks, *pieces, second, basis],
             in_specs=[SM] + [VM] * (len(pieces) + 2),
             scratch=[
@@ -312,7 +370,7 @@
                 pltpu.VMEM((columns, rows * terms, width), F32),
             ],
             limit=16 * MIB,
-            cost=1 if c + 1 == CHUNKS else LARGE,
+            cost=1,
         )
         sends = outs[rs:]
         return outs[:rs], [sends[:1]] + [sends[1 + d * parts : 1 + (d + 1) * parts] for d in range(rs - 1)]
@@ -320,52 +378,60 @@
     halved, mirrored, residuals, sent, totals = [], [], [], [], []
 
     def front(c):
-        earlier = (mirrored[-1][1],) if c else (second, data[1], data[3])
-        mine = [[group[0]] + [after(m, *earlier) for m in group[1:]] for group in gathered[c]]
+        earlier = [(mirrored[-1][1],)] if c else [(second,), (second, data[1])]
+        far_pieces = [[after(m, *e) for m, e in zip(slot, earlier)] for slot in gathered[c]]
+        mine = [waves[c]] + far_pieces
+        for d in range(1, helps):
+            mine.append([swap("help", d, wholes[c])])
+            mine.extend([swap("help", d, m) for m in slot] for slot in far_pieces)
+        mine = [list(slot) for slot in mine]
         if c:
             mine[0][0] = after(mine[0][0], mirrored[-1][1])
         keep, *sends = forward(c, mine)
-        if c:
-            residual_of(c - 1, sends[-1])
-            keep = after(keep, residuals[c - 1])
         others = [swap("help", 1, send) for send in sends]
         for d in near:
             shape = (keep.shape[0] // 2, rows, span, width)
             keep, send = call(
-                halve_kernel, "halve", [(shape, F32), (shape, BF16)], [keep, *others], cost=LARGE if c else 1
+                halve_kernel, "halve", [(shape, F32), (shape, BF16)], [keep, *others], cost=1
             )
             others = [swap("col", d, send)]
         halved.append(send)
+        if c:
+            residual_of(c - 1, send)
+            keep = after(keep, *residuals[c - 1])
         mirrored.append(call(mirror_kernel, "mirror", [(shape, F32), (shape, BF16)], [keep, *others]))
 
     def residual_of(c, *earlier):
         keep, send = mirrored[c]
-        residuals.extend(
+        b = BLOCKS[c > 0]
+        residuals.append(
             call(
                 functools.partial(residual_kernel, c),
                 "residual",
-                [((2, rows, span, width), BF16)],
+                [((b, rows, span, width), BF16)] * (2 // b),
                 [after(keep, *earlier), swap("col", far, send), *data],
                 cost=LARGE,
             )
         )
 
     def rear(c):
-        pieces, offsets = [residuals[c]], [0]
+        pieces = list(residuals[c])
+        offsets = [[0], [far]] if len(pieces) == 2 else [[0, far]]
+        own = len(pieces)
         for d in reversed(near):
             pieces = pieces + [swap("col", d, m) for m in pieces]
-            offsets = offsets + [o ^ d for o in offsets]
+            offsets = offsets + [[o ^ d for o in os] for os in offsets]
         last = c + 1 == CHUNKS
-        if last:
-            pieces[1:] = [after(m, *sent) for m in pieces[1:]]
+        earlier = sent if last else [mirrored[c + 1][1]]
+        pieces[own:] = [after(m, *earlier) for m in pieces[own:]]
         pieces = share(pieces)
-        spots = [((o, o ^ far), e) for e in range(helps) for o in offsets]
+        spots = [(o, e) for e in range(helps) for o in offsets]
         if not last:
             pieces[0] = after(pieces[0], mirrored[c + 1][1])
         keeps, sends = backward(c, pieces, spots)
         if not last:
             residual_of(c + 1, sends[-1][-1])
-            keeps = [keeps[0]] + [after(k, residuals[c + 1]) for k in keeps[1:]]
+            keeps = [keeps[0]] + [after(k, *residuals[c + 1]) for k in keeps[1:]]
         shape = (columns, width, quarter)
         shared = [
             call(
@@ -391,7 +457,7 @@
     for c in range(CHUNKS):
         rear(c)
 
-    residual = call(join_kernel, "join", [(observed.shape, BF16)], residuals, cost=1)[0]
+    residual = call(join_kernel, "join", [(observed.shape, BF16)], [r[0] for r in residuals], cost=1)[0]
     adjoint = call(
         final_kernel, "adjoint_sum", [(wavefield.shape, BF16)], [*totals[0], *totals[1]]
     )[0]

time: 85.4 us -> 81.2 us (0.951)
  waiting for transfers between devices: 40 us -> 33.3 us
  starting transfers between devices: 19.3 us -> 25.7 us
  local copies, waits for them, and re-layouts: 6.21 us -> 0.03 us
  Pallas kernels: 18.8 us -> 21.1 us
    ppermute x33 -> x36, waiting for transfers between devices: 40 us -> 33.3 us  [swap(): return lax.ppermute(value, axis_name, [(i, i ^ step) for i in range(size)])]
    ppermute x33 -> x36, starting transfers between devices: 19.3 us -> 25.7 us  [swap(): return lax.ppermute(value, axis_name, [(i, i ^ step) for i in range(size)])]
    unnamed x12, local copies, waits for them, and re-layouts: 6.21 us -> 0.03 us
    pallas_call x17 -> x19, Pallas kernels: 18.8 us -> 21.1 us  [call(): pl.pallas_call(kernel, out_shape=[jax.ShapeDtypeStruct(shape, kind) for s...]
  transfers between devices with their start and end apart: 33 -> 36, of which waited for: 19 -> 23; matrix products, arithmetic and copies ran while one was open for 0% -> 0% of each run, Pallas kernels for 20% -> 23%
where the time goes in v5:
time: 81.2 us; the launch traced here: 81.1 us
  waiting for transfers between devices  33.3 us (41%)
  starting transfers between devices  25.7 us (32%)
  Pallas kernels  21.1 us (26%)
  between operations  0.86 us (1%)
    ppermute x36, waiting for transfers between devices, swap(): return lax.ppermute(value, axis_name, [(i, i ^ step) for i in range(size)])  33.3 us
    ppermute x36, starting transfers between devices, swap(): return lax.ppermute(value, axis_name, [(i, i ^ step) for i in range(size)])  25.7 us
    pallas_call x19, Pallas kernels, call(): pl.pallas_call(kernel, out_shape=[jax.ShapeDtypeStruct(shape, kind) for s...  21.1 us
  transfers between devices with their start and end apart: 36, of which 23 were waited for; matrix products, arithmetic and copies ran while one was open for 0% of the time, Pallas kernels for 23%

profile of v5, /device:TPU:0, one launch (start us, length us, event | category | flops | bytes accessed | tf_op | source)
XLA Modules:
  0.0 81.1 jit_solution(16704321101840570402)
XLA Ops:
  0.6 1.2 %first_waves.1.refs_0_ = bf16[10,128,128]{2,1,0:T(8,128)(2,1)S(1)} custom-call(bf16[2,16,128,128]{3,2,1,0:T(8,128)(2,1)} %source.2), custom_call_target="tpu_custom_call" | custom-call | flops 1000000 | bytes 10000 | tf_op jit(solution)/shard_map/first_waves/pallas_call | solution.py:25
  1.9 3.0 %collective-permute-start = (bf16[10,128,128]{2,1,0:T(8,128)(2,1)S(1)}, bf16[10,128,128]{2,1,0:T(8,128)(2,1)S(1)}, u32[]{:S(2)}, u32[]{:S(2)}) collective-permute-start(bf16[10,128,128]{2,1,0:T(8,128)(2,1)S(1)} %first_waves.1.refs_0_), channel_id=1, source_target_pairs={{0,2},{2,0},{1,3},{3,1},{4,6},{6,4},{5,7},{7,5},{8,10},{10,8},{9,1... | collective-permute-start | bytes 983048 | tf_op jit(solution)/shard_map/ppermute | solution.py:43
  4.9 1.1 %join_data.1.refs_0_ = bf16[3,4,64,128]{3,2,1,0:T(8,128)(2,1)S(1)} custom-call(bf16[2,4,64,128]{3,2,1,0:T(8,128)(2,1)} %observed, bf16[4,64,128]{2,1,0:T(8,128)(2,1)} %amplitude.1), custom_call_target="tpu_custom_call" | custom-call | flops 10000000000 | bytes 10000 | tf_op jit(solution)/shard_map/join_data/pallas_call | solution.py:25
  6.0 2.7 %collective-permute-start.2 = (bf16[3,4,64,128]{3,2,1,0:T(8,128)(2,1)S(1)}, bf16[3,4,64,128]{3,2,1,0:T(8,128)(2,1)S(1)}, u32[]{:S(2)}, u32[]{:S(2)}) collective-permute-start(bf16[3,4,64,128]{3,2,1,0:T(8,128)(2,1)S(1)} %join_data.1.refs_0_), channel_id=1, source_target_pairs={{0,8},{4,12},{8,0},{12,4},{1,9},{5,13},{9,1},{13,5},{2,10},{6,14},... | collective-permute-start | bytes 589832 | tf_op jit(solution)/shard_map/ppermute | solution.py:43
  8.7 0.4 other_waves.1
  9.0 0.6 collective-permute-start.1
  9.7 2.2 %load_factors.1 = (bf16[16,8,40,512]{3,2,1,0:T(8,128)(2,1)S(1)}, bf16[2,4,16,40,512]{4,3,2,1,0:T(8,128)(2,1)S(1)}) custom-call(bf16[2,4,16,40,512]{4,3,2,1,0:T(8,128)(2,1)S(1)} %bitcast.11, bf16[2,4,16,40,512]{4,3,2,1,0:T(8,128)(2,1)S(1)} %bitcast.13), custom_call_target="tpu_custom_call" | custom-call | flops 10000000000 | bytes 10000 | tf_op jit(solution)/shard_map/load_factors/pallas_call | solution.py:25
  11.9 1.6 %collective-permute-done.refs_2_ = bf16[10,128,128]{2,1,0:T(8,128)(2,1)S(1)} collective-permute-done((bf16[10,128,128]{2,1,0:T(8,128)(2,1)S(1)}, bf16[10,128,128]{2,1,0:T(8,128)(2,1)S(1)}, u32[]{:S(2)}, u32[]{:S(2)}) %collective-permute-start) | collective-permute-done | bytes 327712 | tf_op jit(solution)/shard_map/ppermute | solution.py:43
  13.4 2.1 %collective-permute-start.9 = (bf16[16,128,128]{2,1,0:T(8,128)(2,1)S(1)}, bf16[16,128,128]{2,1,0:T(8,128)(2,1)S(1)}, u32[]{:S(2)}, u32[]{:S(2)}) collective-permute-start(bf16[16,128,128]{2,1,0:T(8,128)(2,1)S(1)} %get-tuple-element.68.refs_0_), channel_id=1, source_target_pairs={{0,2},{2,0},{1,3},{3,1},{4,6},{6,4},{5,7},{7,5},{8,10},{10,8},{9,1... | collective-permute-start | bytes 1572872 | tf_op jit(solution)/shard_map/ppermute | solution.py:43
  15.5 1.3 %collective-permute-done.1.refs_3_ = bf16[6,128,128]{2,1,0:T(8,128)(2,1)S(1)} collective-permute-done((bf16[6,128,128]{2,1,0:T(8,128)(2,1)S(1)}, bf16[6,128,128]{2,1,0:T(8,128)(2,1)S(1)}, u32[]{:S(2)}, u32[]{:S(2)}) %collective-permute-start.1) | collective-permute-done | bytes 196640 | tf_op jit(solution)/shard_map/ppermute | solution.py:43
  16.8 0.7 collective-permute-done.2.refs_1_
  17.6 1.4 %collective-permute-done.5.refs_6_ = bf16[6,128,128]{2,1,0:T(8,128)(2,1)S(1)} collective-permute-done((bf16[6,128,128]{2,1,0:T(8,128)(2,1)S(1)}, bf16[6,128,128]{2,1,0:T(8,128)(2,1)S(1)}, u32[]{:S(2)}, u32[]{:S(2)}) %collective-permute-start.5) | collective-permute-done | bytes 196640 | tf_op jit(solution)/shard_map/ppermute | solution.py:43
  19.0 3.4 %forward_product.2 = (f32[4,4,64,128]{3,2,1,0:T(8,128)S(1)}, bf16[2,4,64,128]{3,2,1,0:T(8,128)(2,1)S(1)}, bf16[2,4,64,128]{3,2,1,0:T(8,128)(2,1)S(1)}) custom-call(s32[4,16]{1,0:T(4,128)S(1)} %copy-done.1, bf16[10,128,128]{2,1,0:T(8,128)(2,1)S(1)} %first_waves.1.refs_0_, bf16[6,128,128]{2,1,0:T(8,128)(2,1)S(1)} %get-tuple-element.54.refs_1_, ...), custom_call_target="tpu_custom_call" | custom-call | flops 1 | bytes 10000 | tf_op jit(solution)/shard_map/forward_product/pallas_call | solution.py:25
  22.6 0.4 collective-permute-start.7
  23.0 0.8 %collective-permute-done.6.refs_0_ = bf16[2,4,64,128]{3,2,1,0:T(8,128)(2,1)S(1)} collective-permute-done((bf16[2,4,64,128]{3,2,1,0:T(8,128)(2,1)S(1)}, bf16[2,4,64,128]{3,2,1,0:T(8,128)(2,1)S(1)}, u32[]{:S(2)}, u32[]{:S(2)}) %collective-permute-start.6) | collective-permute-done | bytes 131104 | tf_op jit(solution)/shard_map/ppermute | solution.py:43
  24.1 1.2 %collective-permute-start.8 = (bf16[2,4,64,128]{3,2,1,0:T(8,128)(2,1)S(1)}, bf16[2,4,64,128]{3,2,1,0:T(8,128)(2,1)S(1)}, u32[]{:S(2)}, u32[]{:S(2)}) collective-permute-start(bf16[2,4,64,128]{3,2,1,0:T(8,128)(2,1)S(1)} %get-tuple-element.64), channel_id=1, source_target_pairs={{0,4},{4,0},{8,12},{12,8},{1,5},{5,1},{9,13},{13,9},{2,6},{6,2},{1... | collective-permute-start | bytes 393224 | tf_op jit(solution)/shard_map/ppermute | solution.py:43
  25.3 4.6 %collective-permute-done.8.refs_0_ = bf16[2,4,64,128]{3,2,1,0:T(8,128)(2,1)S(1)} collective-permute-done((bf16[2,4,64,128]{3,2,1,0:T(8,128)(2,1)S(1)}, bf16[2,4,64,128]{3,2,1,0:T(8,128)(2,1)S(1)}, u32[]{:S(2)}, u32[]{:S(2)}) %collective-permute-start.8) | collective-permute-done | bytes 131104 | tf_op jit(solution)/shard_map/ppermute | solution.py:43
  30.0 2.4 %collective-permute-start.16 = (bf16[2,4,64,128]{3,2,1,0:T(8,128)(2,1)S(1)}, bf16[2,4,64,128]{3,2,1,0:T(8,128)(2,1)S(1)}, u32[]{:S(2)}, u32[]{:S(2)}) collective-permute-start(bf16[2,4,64,128]{3,2,1,0:T(8,128)(2,1)S(1)} %get-tuple-element.67), channel_id=1, source_target_pairs={{0,8},{4,12},{8,0},{12,4},{1,9},{5,13},{9,1},{13,5},{2,10},{6,14},... | collective-permute-start | bytes 393224 | tf_op jit(solution)/shard_map/ppermute | solution.py:43
  32.4 3.4 %forward_product.3 = (f32[4,4,64,128]{3,2,1,0:T(8,128)S(1)}, bf16[1,4,64,128]{3,2,1,0:T(8,128)(2,1)S(1)}, bf16[1,4,64,128]{3,2,1,0:T(8,128)(2,1)S(1)}, bf16[1,4,...) custom-call(s32[4,16]{1,0:T(4,128)S(1)} %copy-done.1, bf16[16,128,128]{2,1,0:T(8,128)(2,1)S(1)} %get-tuple-element.68.refs_0_, ...), custom_call_target="tpu_custom_call" | custom-call | flops 10000000000 | bytes 10000 | tf_op jit(solution)/shard_map/forward_product/pallas_call | solution.py:25
  35.8 0.2 collective-permute-start.12
  36.0 0.3 collective-permute-start.13
  36.5 0.3 collective-permute-start.15
  36.9 0.2 collective-permute-done.12.refs_0_
  37.3 0.3 collective-permute-done.14.refs_2_
  37.9 1.8 %collective-permute-start.17 = (bf16[2,4,64,128]{3,2,1,0:T(8,128)(2,1)S(1)}, bf16[2,4,64,128]{3,2,1,0:T(8,128)(2,1)S(1)}, u32[]{:S(2)}, u32[]{:S(2)}) collective-permute-start(bf16[2,4,64,128]{3,2,1,0:T(8,128)(2,1)S(1)} %get-tuple-element.75), channel_id=1, source_target_pairs={{0,4},{4,0},{8,12},{12,8},{1,5},{5,1},{9,13},{13,9},{2,6},{6,2},{1... | collective-permute-start | bytes 393224 | tf_op jit(solution)/shard_map/ppermute | solution.py:43
  39.8 0.4 collective-permute-start.19
  40.3 1.7 %collective-permute-start.18 = (bf16[1,4,64,128]{3,2,1,0:T(8,128)(2,1)S(1)}, bf16[1,4,64,128]{3,2,1,0:T(8,128)(2,1)S(1)}, u32[]{:S(2)}, u32[]{:S(2)}) collective-permute-start(bf16[1,4,64,128]{3,2,1,0:T(8,128)(2,1)S(1)} %get-tuple-element.83.refs_0_), channel_id=1, source_target_pairs={{0,4},{4,0},{8,12},{12,8},{1,5},{5,1},{9,13},{13,9},{2,6},{6,2},{1... | collective-permute-start | bytes 196616 | tf_op jit(solution)/shard_map/ppermute | solution.py:43
  41.9 2.3 %collective-permute-done.17.refs_0_ = bf16[2,4,64,128]{3,2,1,0:T(8,128)(2,1)S(1)} collective-permute-done((bf16[2,4,64,128]{3,2,1,0:T(8,128)(2,1)S(1)}, bf16[2,4,64,128]{3,2,1,0:T(8,128)(2,1)S(1)}, u32[]{:S(2)}, u32[]{:S(2)}) %collective-permute-start.17) | collective-permute-done | bytes 131104 | tf_op jit(solution)/shard_map/ppermute | solution.py:43
  44.3 1.9 %collective-permute-start.24 = (bf16[2,4,64,128]{3,2,1,0:T(8,128)(2,1)S(1)}, bf16[2,4,64,128]{3,2,1,0:T(8,128)(2,1)S(1)}, u32[]{:S(2)}, u32[]{:S(2)}) collective-permute-start(bf16[2,4,64,128]{3,2,1,0:T(8,128)(2,1)S(1)} %get-tuple-element.82), channel_id=1, source_target_pairs={{0,8},{4,12},{8,0},{12,4},{1,9},{5,13},{9,1},{13,5},{2,10},{6,14},... | collective-permute-start | bytes 393224 | tf_op jit(solution)/shard_map/ppermute | solution.py:43
  46.2 0.5 collective-permute-start.21
  46.7 0.5 collective-permute-start.22
  47.6 0.4 collective-permute-done.23.refs_7_
  48.1 3.3 %adjoint_product.2 = (f32[16,128,128]{2,1,0:T(8,128)S(1)}, f32[16,128,128]{2,1,0:T(8,128)S(1)}, bf16[16,128,128]{2,1,0:T(8,128)(2,1)S(1)}, bf16[8,128,128]{2,1,0:T(8,128)(2,1)S(1)}, bf16[8,128,128]{2,1,0:T(8,128)(2,1)S(1)}) custom-call(s32[4,16]{1,0:T(4,128)S(1)} %copy-done.1, bf16[1,4,64,128]{3,2,1,0:T(8,128)(2,1)S(1)} %get-tuple-element.83.refs_0_, ...), custom_call_target="tpu_custom_call" | custom-call | flops 1 | bytes 10000 | tf_op jit(solution)/shard_map/adjoint_product/pallas_call | solution.py:25
  51.4 0.4 collective-permute-start.27
  52.0 0.5 collective-permute-done.24.other
  52.6 1.4 %collective-permute-start.25 = (bf16[2,4,64,128]{3,2,1,0:T(8,128)(2,1)S(1)}, bf16[2,4,64,128]{3,2,1,0:T(8,128)(2,1)S(1)}, u32[]{:S(2)}, u32[]{:S(2)}) collective-permute-start(bf16[2,4,64,128]{3,2,1,0:T(8,128)(2,1)S(1)} %residual.3.refs_1_.refs_0_), channel_id=1, source_target_pairs={{0,4},{4,0},{8,12},{12,8},{1,5},{5,1},{9,13},{13,9},{2,6},{6,2},{1... | collective-permute-start | bytes 393224 | tf_op jit(solution)/shard_map/ppermute | solution.py:43
  54.2 1.1 %collective-permute-start.33 = (bf16[16,128,128]{2,1,0:T(8,128)(2,1)S(1)}, bf16[16,128,128]{2,1,0:T(8,128)(2,1)S(1)}, u32[]{:S(2)}, u32[]{:S(2)}) collective-permute-start(bf16[16,128,128]{2,1,0:T(8,128)(2,1)S(1)} %adjoint_share.2), channel_id=1, source_target_pairs={{0,2},{2,0},{1,3},{3,1},{4,6},{6,4},{5,7},{7,5},{8,10},{10,8},{9,1... | collective-permute-start | bytes 1572872 | tf_op jit(solution)/shard_map/ppermute | solution.py:43
  55.5 2.5 %collective-permute-done.25.refs_1_ = bf16[2,4,64,128]{3,2,1,0:T(8,128)(2,1)S(1)} collective-permute-done((bf16[2,4,64,128]{3,2,1,0:T(8,128)(2,1)S(1)}, bf16[2,4,64,128]{3,2,1,0:T(8,128)(2,1)S(1)}, u32[]{:S(2)}, u32[]{:S(2)}) %collective-permute-start.25) | collective-permute-done | bytes 131104 | tf_op jit(solution)/shard_map/ppermute | solution.py:43
  57.9 1.3 %collective-permute-done.29.refs_3_ = bf16[2,4,64,128]{3,2,1,0:T(8,128)(2,1)S(1)} collective-permute-done((bf16[2,4,64,128]{3,2,1,0:T(8,128)(2,1)S(1)}, bf16[2,4,64,128]{3,2,1,0:T(8,128)(2,1)S(1)}, u32[]{:S(2)}, u32[]{:S(2)}) %collective-permute-start.29) | collective-permute-done | bytes 131104 | tf_op jit(solution)/shard_map/ppermute | solution.py:43
  59.3 3.3 %adjoint_product.3 = (f32[16,128,128]{2,1,0:T(8,128)S(1)}, f32[16,128,128]{2,1,0:T(8,128)S(1)}, bf16[16,128,128]{2,1,0:T(8,128)(2,1)S(1)}, bf16[8,128,128]{2,1,0:T(8,128)(2,1)S(1)}, bf16[8,128,128]{2,1,0:T(8,128)(2,1)S(1)}) custom-call(s32[4,16]{1,0:T(4,128)S(1)} %copy-done.1, bf16[2,4,64,128]{3,2,1,0:T(8,128)(2,1)S(1)} %residual.3.refs_1_.refs_0_, ...), custom_call_target="tpu_custom_call" | custom-call | flops 1 | bytes 10000 | tf_op jit(solution)/shard_map/adjoint_product/pallas_call | solution.py:25
  62.8 0.4 collective-permute-start.31
  63.2 0.8 join.1
  63.9 0.3 collective-permute-done.30.refs_0_
  64.2 0.4 collective-permute-done.31.refs_1_
  64.7 1.4 %collective-permute-start.35 = (bf16[16,128,128]{2,1,0:T(8,128)(2,1)S(1)}, bf16[16,128,128]{2,1,0:T(8,128)(2,1)S(1)}, u32[]{:S(2)}, u32[]{:S(2)}) collective-permute-start(bf16[16,128,128]{2,1,0:T(8,128)(2,1)S(1)} %adjoint_share.3), channel_id=1, source_target_pairs={{0,2},{2,0},{1,3},{3,1},{4,6},{6,4},{5,7},{7,5},{8,10},{10,8},{9,1... | collective-permute-start | bytes 1572872 | tf_op jit(solution)/shard_map/ppermute | solution.py:43
  66.0 2.9 %collective-permute-done.33.refs_1_ = bf16[16,128,128]{2,1,0:T(8,128)(2,1)S(1)} collective-permute-done((bf16[16,128,128]{2,1,0:T(8,128)(2,1)S(1)}, bf16[16,128,128]{2,1,0:T(8,128)(2,1)S(1)}, u32[]{:S(2)}, u32[]{:S(2)}) %collective-permute-start.33) | collective-permute-done | bytes 524320 | tf_op jit(solution)/shard_map/ppermute | solution.py:43
  69.1 10.6 %collective-permute-done.35.refs_1_ = bf16[16,128,128]{2,1,0:T(8,128)(2,1)S(1)} collective-permute-done((bf16[16,128,128]{2,1,0:T(8,128)(2,1)S(1)}, bf16[16,128,128]{2,1,0:T(8,128)(2,1)S(1)}, u32[]{:S(2)}, u32[]{:S(2)}) %collective-permute-start.35) | collective-permute-done | bytes 524320 | tf_op jit(solution)/shard_map/ppermute | solution.py:43
  79.7 1.3 %adjoint_sum.1 = bf16[2,16,128,128]{3,2,1,0:T(8,128)(2,1)} custom-call(f32[16,128,128]{2,1,0:T(8,128)S(1)} %total.1.done, f32[16,128,128]{2,1,0:T(8,128)S(1)} %get-tuple-element.99.mine, bf16[16,128,128]{2,1,0:T(8,128)(2,1)S(1)} %collective-permute-done.34.refs_0_, bf16[16,128,128]{2,1,0:T(8,128)(2,1)S(1)} %collective-permute-done.35.refs_1_), custom_call_target="tpu_custom_call" | custom-call | flops 1000000 | bytes 10000 | tf_op jit(solution)/shard_map/adjoint_sum/pallas_call | solution.py:25
  (57 shorter events, 3.1 us)
Async XLA Ops:
  1.9 6.8 %copy-start = (bf16[2,16,128,128]{3,2,1,0:T(8,128)(2,1)S(1)}, bf16[2,16,128,128]{3,2,1,0:T(8,128)(2,1)}, u32[]{:S(2)}) copy-start(bf16[2,16,128,128]{3,2,1,0:T(8,128)(2,1)} %source.2) | copy-start | bytes 3145732
  1.9 11.5 %collective-permute-start = (bf16[10,128,128]{2,1,0:T(8,128)(2,1)S(1)}, bf16[10,128,128]{2,1,0:T(8,128)(2,1)S(1)}, u32[]{:S(2)}, u32[]{:S(2)}) collective-permute-start(bf16[10,128,128]{2,1,0:T(8,128)(2,1)S(1)} %first_waves.1.refs_0_), channel_id=1, source_target_pairs={{0,2},{2,0},{1,3},{3,1},{4,6},{6,4},{5,7},{7,5},{8,10},{10,8},{9,1... | collective-permute-start | bytes 983048 | tf_op jit(solution)/shard_map/ppermute | solution.py:43
  4.9 4.7 %slice-start = ((s8[5242880]{0:T(1024)(128)(4,1)}), s8[4194304]{0:T(1024)(128)(4,1)S(1)}, s32[]{:S(2)}) async-start(s8[5242880]{0:T(1024)(128)(4,1)} %bitcast.10), calls=%async_computation | async-start | bytes 8388608
  4.9 4.7 %slice-start.2 = ((s8[5242880]{0:T(1024)(128)(4,1)}), s8[4194304]{0:T(1024)(128)(4,1)S(1)}, s32[]{:S(2)}) async-start(s8[5242880]{0:T(1024)(128)(4,1)} %bitcast.12), calls=%async_computation.2 | async-start | bytes 8388608
  6.0 3.7 %slice-start.1 = ((s8[5242880]{0:T(1024)(128)(4,1)}), s8[1048576]{0:T(1024)(128)(4,1)S(1)}, s32[]{:S(2)}) async-start(s8[5242880]{0:T(1024)(128)(4,1)} %bitcast.10), calls=%async_computation.1 | async-start | bytes 2097152
  6.0 3.7 %slice-start.3 = ((s8[5242880]{0:T(1024)(128)(4,1)}), s8[1048576]{0:T(1024)(128)(4,1)S(1)}, s32[]{:S(2)}) async-start(s8[5242880]{0:T(1024)(128)(4,1)} %bitcast.12), calls=%async_computation.3 | async-start | bytes 2097152
  6.0 11.5 %collective-permute-start.2 = (bf16[3,4,64,128]{3,2,1,0:T(8,128)(2,1)S(1)}, bf16[3,4,64,128]{3,2,1,0:T(8,128)(2,1)S(1)}, u32[]{:S(2)}, u32[]{:S(2)}) collective-permute-start(bf16[3,4,64,128]{3,2,1,0:T(8,128)(2,1)S(1)} %join_data.1.refs_0_), channel_id=1, source_target_pairs={{0,8},{4,12},{8,0},{12,4},{1,9},{5,13},{9,1},{13,5},{2,10},{6,14},... | collective-permute-start | bytes 589832 | tf_op jit(solution)/shard_map/ppermute | solution.py:43
  9.0 7.8 %collective-permute-start.1 = (bf16[6,128,128]{2,1,0:T(8,128)(2,1)S(1)}, bf16[6,128,128]{2,1,0:T(8,128)(2,1)S(1)}, u32[]{:S(2)}, u32[]{:S(2)}) collective-permute-start(bf16[6,128,128]{2,1,0:T(8,128)(2,1)S(1)} %get-tuple-element.54.refs_1_), channel_id=1, source_target_pairs={{0,2},{2,0},{1,3},{3,1},{4,6},{6,4},{5,7},{7,5},{8,10},{10,8},{9,1... | collective-permute-start | bytes 589832 | tf_op jit(solution)/shard_map/ppermute | solution.py:43
  9.6 9.4 %copy-start.1 = (s32[4,16]{1,0:T(4,128)S(1)}, s32[4,16]{1,0:T(4,128)}, u32[]{:S(2)}) copy-start(s32[4,16]{1,0:T(4,128)} %ranks.7) | copy-start | bytes 772
  9.6 9.4 %collective-permute-start.3 = (bf16[16,128,128]{2,1,0:T(8,128)(2,1)S(1)}, bf16[16,128,128]{2,1,0:T(8,128)(2,1)S(1)}, u32[]{:S(2)}, u32[]{:S(2)}) collective-permute-start(bf16[16,128,128]{2,1,0:T(8,128)(2,1)S(1)} %get-tuple-element.58), channel_id=1, source_target_pairs={{0,1},{1,0},{2,3},{3,2},{4,5},{5,4},{6,7},{7,6},{8,9},{9,8},{10,11... | collective-permute-start | bytes 1572872 | tf_op jit(solution)/shard_map/ppermute | solution.py:43
  13.4 5.6 %collective-permute-start.4 = (bf16[10,128,128]{2,1,0:T(8,128)(2,1)S(1)}, bf16[10,128,128]{2,1,0:T(8,128)(2,1)S(1)}, u32[]{:S(2)}, u32[]{:S(2)}) collective-permute-start(bf16[10,128,128]{2,1,0:T(8,128)(2,1)S(1)} %collective-permute-done.refs_2_), channel_id=1, source_target_pairs={{0,1},{1,0},{2,3},{3,2},{4,5},{5,4},{6,7},{7,6},{8,9},{9,8},{10,11... | collective-permute-start | bytes 983048 | tf_op jit(solution)/shard_map/ppermute | solution.py:43
  13.4 16.5 %collective-permute-start.9 = (bf16[16,128,128]{2,1,0:T(8,128)(2,1)S(1)}, bf16[16,128,128]{2,1,0:T(8,128)(2,1)S(1)}, u32[]{:S(2)}, u32[]{:S(2)}) collective-permute-start(bf16[16,128,128]{2,1,0:T(8,128)(2,1)S(1)} %get-tuple-element.68.refs_0_), channel_id=1, source_target_pairs={{0,2},{2,0},{1,3},{3,1},{4,6},{6,4},{5,7},{7,5},{8,10},{10,8},{9,1... | collective-permute-start | bytes 1572872 | tf_op jit(solution)/shard_map/ppermute | solution.py:43
  17.5 1.4 %collective-permute-start.5 = (bf16[6,128,128]{2,1,0:T(8,128)(2,1)S(1)}, bf16[6,128,128]{2,1,0:T(8,128)(2,1)S(1)}, u32[]{:S(2)}, u32[]{:S(2)}) collective-permute-start(bf16[6,128,128]{2,1,0:T(8,128)(2,1)S(1)} %collective-permute-done.1.refs_3_), channel_id=1, source_target_pairs={{0,1},{1,0},{2,3},{3,2},{4,5},{5,4},{6,7},{7,6},{8,9},{9,8},{10,11... | collective-permute-start | bytes 589832 | tf_op jit(solution)/shard_map/ppermute | solution.py:43
  22.4 1.4 %collective-permute-start.6 = (bf16[2,4,64,128]{3,2,1,0:T(8,128)(2,1)S(1)}, bf16[2,4,64,128]{3,2,1,0:T(8,128)(2,1)S(1)}, u32[]{:S(2)}, u32[]{:S(2)}) collective-permute-start(bf16[2,4,64,128]{3,2,1,0:T(8,128)(2,1)S(1)} %get-tuple-element.61), channel_id=1, source_target_pairs={{0,1},{1,0},{2,3},{3,2},{4,5},{5,4},{6,7},{7,6},{8,9},{9,8},{10,11... | collective-permute-start | bytes 393224 | tf_op jit(solution)/shard_map/ppermute | solution.py:43
  22.6 1.4 %collective-permute-start.7 = (bf16[2,4,64,128]{3,2,1,0:T(8,128)(2,1)S(1)}, bf16[2,4,64,128]{3,2,1,0:T(8,128)(2,1)S(1)}, u32[]{:S(2)}, u32[]{:S(2)}) collective-permute-start(bf16[2,4,64,128]{3,2,1,0:T(8,128)(2,1)S(1)} %get-tuple-element.62), channel_id=1, source_target_pairs={{0,1},{1,0},{2,3},{3,2},{4,5},{5,4},{6,7},{7,6},{8,9},{9,8},{10,11... | collective-permute-start | bytes 393224 | tf_op jit(solution)/shard_map/ppermute | solution.py:43
  24.1 5.8 %collective-permute-start.8 = (bf16[2,4,64,128]{3,2,1,0:T(8,128)(2,1)S(1)}, bf16[2,4,64,128]{3,2,1,0:T(8,128)(2,1)S(1)}, u32[]{:S(2)}, u32[]{:S(2)}) collective-permute-start(bf16[2,4,64,128]{3,2,1,0:T(8,128)(2,1)S(1)} %get-tuple-element.64), channel_id=1, source_target_pairs={{0,4},{4,0},{8,12},{12,8},{1,5},{5,1},{9,13},{13,9},{2,6},{6,2},{1... | collective-permute-start | bytes 393224 | tf_op jit(solution)/shard_map/ppermute | solution.py:43
  25.3 7.1 %collective-permute-start.10 = (bf16[16,128,128]{2,1,0:T(8,128)(2,1)S(1)}, bf16[16,128,128]{2,1,0:T(8,128)(2,1)S(1)}, u32[]{:S(2)}, u32[]{:S(2)}) collective-permute-start(bf16[16,128,128]{2,1,0:T(8,128)(2,1)S(1)} %get-tuple-element.68.refs_0_), channel_id=1, source_target_pairs={{0,1},{1,0},{2,3},{3,2},{4,5},{5,4},{6,7},{7,6},{8,9},{9,8},{10,11... | collective-permute-start | bytes 1572872 | tf_op jit(solution)/shard_map/ppermute | solution.py:43
  29.9 2.5 %collective-permute-start.11 = (bf16[16,128,128]{2,1,0:T(8,128)(2,1)S(1)}, bf16[16,128,128]{2,1,0:T(8,128)(2,1)S(1)}, u32[]{:S(2)}, u32[]{:S(2)}) collective-permute-start(bf16[16,128,128]{2,1,0:T(8,128)(2,1)S(1)} %collective-permute-done.9.refs_1_), channel_id=1, source_target_pairs={{0,1},{1,0},{2,3},{3,2},{4,5},{5,4},{6,7},{7,6},{8,9},{9,8},{10,11... | collective-permute-start | bytes 1572872 | tf_op jit(solution)/shard_map/ppermute | solution.py:43
  30.0 9.7 %collective-permute-start.16 = (bf16[2,4,64,128]{3,2,1,0:T(8,128)(2,1)S(1)}, bf16[2,4,64,128]{3,2,1,0:T(8,128)(2,1)S(1)}, u32[]{:S(2)}, u32[]{:S(2)}) collective-permute-start(bf16[2,4,64,128]{3,2,1,0:T(8,128)(2,1)S(1)} %get-tuple-element.67), channel_id=1, source_target_pairs={{0,8},{4,12},{8,0},{12,4},{1,9},{5,13},{9,1},{13,5},{2,10},{6,14},... | collective-permute-start | bytes 393224 | tf_op jit(solution)/shard_map/ppermute | solution.py:43
  35.8 1.3 %collective-permute-start.12 = (bf16[1,4,64,128]{3,2,1,0:T(8,128)(2,1)S(1)}, bf16[1,4,64,128]{3,2,1,0:T(8,128)(2,1)S(1)}, u32[]{:S(2)}, u32[]{:S(2)}) collective-permute-start(bf16[1,4,64,128]{3,2,1,0:T(8,128)(2,1)S(1)} %get-tuple-element.71), channel_id=1, source_target_pairs={{0,1},{1,0},{2,3},{3,2},{4,5},{5,4},{6,7},{7,6},{8,9},{9,8},{10,11... | collective-permute-start | bytes 196616 | tf_op jit(solution)/shard_map/ppermute | solution.py:43
  36.0 1.3 %collective-permute-start.13 = (bf16[1,4,64,128]{3,2,1,0:T(8,128)(2,1)S(1)}, bf16[1,4,64,128]{3,2,1,0:T(8,128)(2,1)S(1)}, u32[]{:S(2)}, u32[]{:S(2)}) collective-permute-start(bf16[1,4,64,128]{3,2,1,0:T(8,128)(2,1)S(1)} %get-tuple-element.72), channel_id=1, source_target_pairs={{0,1},{1,0},{2,3},{3,2},{4,5},{5,4},{6,7},{7,6},{8,9},{9,8},{10,11... | collective-permute-start | bytes 196616 | tf_op jit(solution)/shard_map/ppermute | solution.py:43
  36.4 1.3 %collective-permute-start.14 = (bf16[1,4,64,128]{3,2,1,0:T(8,128)(2,1)S(1)}, bf16[1,4,64,128]{3,2,1,0:T(8,128)(2,1)S(1)}, u32[]{:S(2)}, u32[]{:S(2)}) collective-permute-start(bf16[1,4,64,128]{3,2,1,0:T(8,128)(2,1)S(1)} %get-tuple-element.73), channel_id=1, source_target_pairs={{0,1},{1,0},{2,3},{3,2},{4,5},{5,4},{6,7},{7,6},{8,9},{9,8},{10,11... | collective-permute-start | bytes 196616 | tf_op jit(solution)/shard_map/ppermute | solution.py:43
  36.5 1.3 %collective-permute-start.15 = (bf16[1,4,64,128]{3,2,1,0:T(8,128)(2,1)S(1)}, bf16[1,4,64,128]{3,2,1,0:T(8,128)(2,1)S(1)}, u32[]{:S(2)}, u32[]{:S(2)}) collective-permute-start(bf16[1,4,64,128]{3,2,1,0:T(8,128)(2,1)S(1)} %get-tuple-element.74), channel_id=1, source_target_pairs={{0,1},{1,0},{2,3},{3,2},{4,5},{5,4},{6,7},{7,6},{8,9},{9,8},{10,11... | collective-permute-start | bytes 196616 | tf_op jit(solution)/shard_map/ppermute | solution.py:43
  37.9 6.4 %collective-permute-start.17 = (bf16[2,4,64,128]{3,2,1,0:T(8,128)(2,1)S(1)}, bf16[2,4,64,128]{3,2,1,0:T(8,128)(2,1)S(1)}, u32[]{:S(2)}, u32[]{:S(2)}) collective-permute-start(bf16[2,4,64,128]{3,2,1,0:T(8,128)(2,1)S(1)} %get-tuple-element.75), channel_id=1, source_target_pairs={{0,4},{4,0},{8,12},{12,8},{1,5},{5,1},{9,13},{13,9},{2,6},{6,2},{1... | collective-permute-start | bytes 393224 | tf_op jit(solution)/shard_map/ppermute | solution.py:43
  39.8 6.9 %collective-permute-start.19 = (bf16[1,4,64,128]{3,2,1,0:T(8,128)(2,1)S(1)}, bf16[1,4,64,128]{3,2,1,0:T(8,128)(2,1)S(1)}, u32[]{:S(2)}, u32[]{:S(2)}) collective-permute-start(bf16[1,4,64,128]{3,2,1,0:T(8,128)(2,1)S(1)} %get-tuple-element.79.refs_1_), channel_id=1, source_target_pairs={{0,4},{4,0},{8,12},{12,8},{1,5},{5,1},{9,13},{13,9},{2,6},{6,2},{1... | collective-permute-start | bytes 196616 | tf_op jit(solution)/shard_map/ppermute | solution.py:43
  40.3 6.4 %collective-permute-start.18 = (bf16[1,4,64,128]{3,2,1,0:T(8,128)(2,1)S(1)}, bf16[1,4,64,128]{3,2,1,0:T(8,128)(2,1)S(1)}, u32[]{:S(2)}, u32[]{:S(2)}) collective-permute-start(bf16[1,4,64,128]{3,2,1,0:T(8,128)(2,1)S(1)} %get-tuple-element.83.refs_0_), channel_id=1, source_target_pairs={{0,4},{4,0},{8,12},{12,8},{1,5},{5,1},{9,13},{13,9},{2,6},{6,2},{1... | collective-permute-start | bytes 196616 | tf_op jit(solution)/shard_map/ppermute | solution.py:43
  44.3 8.2 %collective-permute-start.24 = (bf16[2,4,64,128]{3,2,1,0:T(8,128)(2,1)S(1)}, bf16[2,4,64,128]{3,2,1,0:T(8,128)(2,1)S(1)}, u32[]{:S(2)}, u32[]{:S(2)}) collective-permute-start(bf16[2,4,64,128]{3,2,1,0:T(8,128)(2,1)S(1)} %get-tuple-element.82), channel_id=1, source_target_pairs={{0,8},{4,12},{8,0},{12,4},{1,9},{5,13},{9,1},{13,5},{2,10},{6,14},... | collective-permute-start | bytes 393224 | tf_op jit(solution)/shard_map/ppermute | solution.py:43
  46.2 1.3 %collective-permute-start.20 = (bf16[1,4,64,128]{3,2,1,0:T(8,128)(2,1)S(1)}, bf16[1,4,64,128]{3,2,1,0:T(8,128)(2,1)S(1)}, u32[]{:S(2)}, u32[]{:S(2)}) collective-permute-start(bf16[1,4,64,128]{3,2,1,0:T(8,128)(2,1)S(1)} %get-tuple-element.83.refs_0_), channel_id=1, source_target_pairs={{0,1},{1,0},{2,3},{3,2},{4,5},{5,4},{6,7},{7,6},{8,9},{9,8},{10,11... | collective-permute-start | bytes 196616 | tf_op jit(solution)/shard_map/ppermute | solution.py:43
  46.2 1.4 %collective-permute-start.21 = (bf16[1,4,64,128]{3,2,1,0:T(8,128)(2,1)S(1)}, bf16[1,4,64,128]{3,2,1,0:T(8,128)(2,1)S(1)}, u32[]{:S(2)}, u32[]{:S(2)}) collective-permute-start(bf16[1,4,64,128]{3,2,1,0:T(8,128)(2,1)S(1)} %get-tuple-element.79.refs_1_), channel_id=1, source_target_pairs={{0,1},{1,0},{2,3},{3,2},{4,5},{5,4},{6,7},{7,6},{8,9},{9,8},{10,11... | collective-permute-start | bytes 196616 | tf_op jit(solution)/shard_map/ppermute | solution.py:43
  46.7 1.3 %collective-permute-start.23 = (bf16[1,4,64,128]{3,2,1,0:T(8,128)(2,1)S(1)}, bf16[1,4,64,128]{3,2,1,0:T(8,128)(2,1)S(1)}, u32[]{:S(2)}, u32[]{:S(2)}) collective-permute-start(bf16[1,4,64,128]{3,2,1,0:T(8,128)(2,1)S(1)} %collective-permute-done.19.refs_3_), channel_id=1, source_target_pairs={{0,1},{1,0},{2,3},{3,2},{4,5},{5,4},{6,7},{7,6},{8,9},{9,8},{10,11... | collective-permute-start | bytes 196616 | tf_op jit(solution)/shard_map/ppermute | solution.py:43
  46.7 1.4 %collective-permute-start.22 = (bf16[1,4,64,128]{3,2,1,0:T(8,128)(2,1)S(1)}, bf16[1,4,64,128]{3,2,1,0:T(8,128)(2,1)S(1)}, u32[]{:S(2)}, u32[]{:S(2)}) collective-permute-start(bf16[1,4,64,128]{3,2,1,0:T(8,128)(2,1)S(1)} %collective-permute-done.18.refs_2_), channel_id=1, source_target_pairs={{0,1},{1,0},{2,3},{3,2},{4,5},{5,4},{6,7},{7,6},{8,9},{9,8},{10,11... | collective-permute-start | bytes 196616 | tf_op jit(solution)/shard_map/ppermute | solution.py:43
  51.4 2.6 %collective-permute-start.27 = (bf16[8,128,128]{2,1,0:T(8,128)(2,1)S(1)}, bf16[8,128,128]{2,1,0:T(8,128)(2,1)S(1)}, u32[]{:S(2)}, u32[]{:S(2)}) collective-permute-start(bf16[8,128,128]{2,1,0:T(8,128)(2,1)S(1)} %get-tuple-element.86), channel_id=1, source_target_pairs={{0,1},{1,0},{2,3},{3,2},{4,5},{5,4},{6,7},{7,6},{8,9},{9,8},{10,11... | collective-permute-start | bytes 786440 | tf_op jit(solution)/shard_map/ppermute | solution.py:43
  51.8 2.2 %collective-permute-start.26 = (bf16[8,128,128]{2,1,0:T(8,128)(2,1)S(1)}, bf16[8,128,128]{2,1,0:T(8,128)(2,1)S(1)}, u32[]{:S(2)}, u32[]{:S(2)}) collective-permute-start(bf16[8,128,128]{2,1,0:T(8,128)(2,1)S(1)} %get-tuple-element.91), channel_id=1, source_target_pairs={{0,1},{1,0},{2,3},{3,2},{4,5},{5,4},{6,7},{7,6},{8,9},{9,8},{10,11... | collective-permute-start | bytes 786440 | tf_op jit(solution)/shard_map/ppermute | solution.py:43
  52.6 5.4 %collective-permute-start.25 = (bf16[2,4,64,128]{3,2,1,0:T(8,128)(2,1)S(1)}, bf16[2,4,64,128]{3,2,1,0:T(8,128)(2,1)S(1)}, u32[]{:S(2)}, u32[]{:S(2)}) collective-permute-start(bf16[2,4,64,128]{3,2,1,0:T(8,128)(2,1)S(1)} %residual.3.refs_1_.refs_0_), channel_id=1, source_target_pairs={{0,4},{4,0},{8,12},{12,8},{1,5},{5,1},{9,13},{13,9},{2,6},{6,2},{1... | collective-permute-start | bytes 393224 | tf_op jit(solution)/shard_map/ppermute | solution.py:43
  54.1 11.9 %collective-permute-start.32 = (bf16[16,128,128]{2,1,0:T(8,128)(2,1)S(1)}, bf16[16,128,128]{2,1,0:T(8,128)(2,1)S(1)}, u32[]{:S(2)}, u32[]{:S(2)}) collective-permute-start(bf16[16,128,128]{2,1,0:T(8,128)(2,1)S(1)} %get-tuple-element.98), channel_id=1, source_target_pairs={{0,1},{1,0},{2,3},{3,2},{4,5},{5,4},{6,7},{7,6},{8,9},{9,8},{10,11... | collective-permute-start | bytes 1572872 | tf_op jit(solution)/shard_map/ppermute | solution.py:43
  54.2 14.8 %collective-permute-start.33 = (bf16[16,128,128]{2,1,0:T(8,128)(2,1)S(1)}, bf16[16,128,128]{2,1,0:T(8,128)(2,1)S(1)}, u32[]{:S(2)}, u32[]{:S(2)}) collective-permute-start(bf16[16,128,128]{2,1,0:T(8,128)(2,1)S(1)} %adjoint_share.2), channel_id=1, source_target_pairs={{0,2},{2,0},{1,3},{3,1},{4,6},{6,4},{5,7},{7,5},{8,10},{10,8},{9,1... | collective-permute-start | bytes 1572872 | tf_op jit(solution)/shard_map/ppermute | solution.py:43
  55.3 2.6 %collective-permute-start.28 = (bf16[2,4,64,128]{3,2,1,0:T(8,128)(2,1)S(1)}, bf16[2,4,64,128]{3,2,1,0:T(8,128)(2,1)S(1)}, u32[]{:S(2)}, u32[]{:S(2)}) collective-permute-start(bf16[2,4,64,128]{3,2,1,0:T(8,128)(2,1)S(1)} %residual.3.refs_1_.refs_0_), channel_id=1, source_target_pairs={{0,1},{1,0},{2,3},{3,2},{4,5},{5,4},{6,7},{7,6},{8,9},{9,8},{10,11... | collective-permute-start | bytes 393224 | tf_op jit(solution)/shard_map/ppermute | solution.py:43
  57.9 1.3 %collective-permute-start.29 = (bf16[2,4,64,128]{3,2,1,0:T(8,128)(2,1)S(1)}, bf16[2,4,64,128]{3,2,1,0:T(8,128)(2,1)S(1)}, u32[]{:S(2)}, u32[]{:S(2)}) collective-permute-start(bf16[2,4,64,128]{3,2,1,0:T(8,128)(2,1)S(1)} %collective-permute-done.25.refs_1_), channel_id=1, source_target_pairs={{0,1},{1,0},{2,3},{3,2},{4,5},{5,4},{6,7},{7,6},{8,9},{9,8},{10,11... | collective-permute-start | bytes 393224 | tf_op jit(solution)/shard_map/ppermute | solution.py:43
  62.6 1.6 %collective-permute-start.30 = (bf16[8,128,128]{2,1,0:T(8,128)(2,1)S(1)}, bf16[8,128,128]{2,1,0:T(8,128)(2,1)S(1)}, u32[]{:S(2)}, u32[]{:S(2)}) collective-permute-start(bf16[8,128,128]{2,1,0:T(8,128)(2,1)S(1)} %get-tuple-element.94), channel_id=1, source_target_pairs={{0,1},{1,0},{2,3},{3,2},{4,5},{5,4},{6,7},{7,6},{8,9},{9,8},{10,11... | collective-permute-start | bytes 786440 | tf_op jit(solution)/shard_map/ppermute | solution.py:43
  62.8 1.8 %collective-permute-start.31 = (bf16[8,128,128]{2,1,0:T(8,128)(2,1)S(1)}, bf16[8,128,128]{2,1,0:T(8,128)(2,1)S(1)}, u32[]{:S(2)}, u32[]{:S(2)}) collective-permute-start(bf16[8,128,128]{2,1,0:T(8,128)(2,1)S(1)} %get-tuple-element.95), channel_id=1, source_target_pairs={{0,1},{1,0},{2,3},{3,2},{4,5},{5,4},{6,7},{7,6},{8,9},{9,8},{10,11... | collective-permute-start | bytes 786440 | tf_op jit(solution)/shard_map/ppermute | solution.py:43
  64.7 15.1 %collective-permute-start.35 = (bf16[16,128,128]{2,1,0:T(8,128)(2,1)S(1)}, bf16[16,128,128]{2,1,0:T(8,128)(2,1)S(1)}, u32[]{:S(2)}, u32[]{:S(2)}) collective-permute-start(bf16[16,128,128]{2,1,0:T(8,128)(2,1)S(1)} %adjoint_share.3), channel_id=1, source_target_pairs={{0,2},{2,0},{1,3},{3,1},{4,6},{6,4},{5,7},{7,5},{8,10},{10,8},{9,1... | collective-permute-start | bytes 1572872 | tf_op jit(solution)/shard_map/ppermute | solution.py:43
  66.0 3.1 %collective-permute-start.34 = (bf16[16,128,128]{2,1,0:T(8,128)(2,1)S(1)}, bf16[16,128,128]{2,1,0:T(8,128)(2,1)S(1)}, u32[]{:S(2)}, u32[]{:S(2)}) collective-permute-start(bf16[16,128,128]{2,1,0:T(8,128)(2,1)S(1)} %get-tuple-element.101), channel_id=1, source_target_pairs={{0,1},{1,0},{2,3},{3,2},{4,5},{5,4},{6,7},{7,6},{8,9},{9,8},{10,11... | collective-permute-start | bytes 1572872 | tf_op jit(solution)/shard_map/ppermute | solution.py:43

commit v6 on v5

v6 whole, which is shorter than its diff:
```python
import functools

import jax
import jax.numpy as jnp
from jax import lax
from jax.experimental import pallas as pl
from jax.experimental.pallas import tpu as pltpu
from jax.sharding import PartitionSpec as P

BF16 = jnp.bfloat16
F32 = jnp.float32
CHUNKS = 2
LANES = 128
VM = pl.BlockSpec(memory_space=pltpu.VMEM)
SM = pl.BlockSpec(memory_space=pltpu.SMEM)
HBM = pl.BlockSpec(memory_space=pltpu.HBM)
ANY = pl.BlockSpec(memory_space=pl.ANY)
MIB = 1024 * 1024
LARGE = 10**10
SPLIT = 2
HEAD = 1
OWN = 1


def call(kernel, name, outs, ins, in_specs=None, out_specs=None, scratch=(), limit=6 * MIB, cost=10**6):
    return pl.pallas_call(
        kernel,
        out_shape=[jax.ShapeDtypeStruct(shape, kind) for shape, kind in outs],
        in_specs=in_specs or [VM] * len(ins),
        out_specs=out_specs or [VM] * len(outs),
        scratch_shapes=list(scratch),
        compiler_params=pltpu.CompilerParams(vmem_limit_bytes=limit),
        cost_estimate=pl.CostEstimate(flops=cost, bytes_accessed=10**4, transcendentals=0),
        name=name,
    )(*ins)


def in_hbm(value):
    return pltpu.with_memory_space_constraint(value, pltpu.HBM)


def swap(axis_name, step, value):
    size = lax.axis_size(axis_name)
    return lax.ppermute(value, axis_name, [(i, i ^ step) for i in range(size)])


def after(value, *earlier):
    return lax.optimization_barrier((value, *earlier))[0]


def turn(value, first, second):
    width = value.shape[-1]
    lane = lax.broadcasted_iota(jnp.int32, value.shape, value.ndim - 1)
    sign = jnp.where(lane < width // 2, first, second).astype(F32)
    return pltpu.roll(value, width // 2, value.ndim - 1) * sign


def side_by_side(source, j, c, part):
    lanes = slice(c * part, (c + 1) * part)
    return jnp.concatenate([source[0, j, :, lanes], source[1, j, :, lanes]], -1)


def first_kernel(source, observed, amplitude, out, data, held, sems):
    n = out.shape[0]
    copies = [pltpu.make_async_copy(source.at[p, :n], held.at[p], sems.at[p]) for p in range(2)]
    copies.append(pltpu.make_async_copy(observed, data.at[:2], sems.at[2]))
    copies.append(pltpu.make_async_copy(amplitude, data.at[2], sems.at[3]))
    for copy in copies:
        copy.start()
    for copy in copies[:2]:
        copy.wait()
    for j in range(n):
        out[j] = side_by_side(held, j, 0, out.shape[-1] // 2)
    for copy in copies[2:]:
        copy.wait()


def relay_kernel(source, out):
    out[...] = source[...]


def waves_kernel(source, rest, whole, *others):
    columns, part = whole.shape[0], whole.shape[-1] // 2
    first = columns - rest.shape[0]
    for j in range(columns):
        whole[j] = side_by_side(source, j, 0, part)
        if j >= first:
            rest[j - first] = whole[j]
        for c, other in enumerate(others):
            other[j] = side_by_side(source, j, c + 1, part)


def load_kernel(second_in, basis_in, second, basis, sems):
    rows = second_in.shape[1]
    copies = []
    for p in range(2):
        for i in range(rows):
            n = p * rows + i
            copies.append(pltpu.make_async_copy(second_in.at[p, i], second.at[:, n], sems.at[0, n]))
            copies.append(pltpu.make_async_copy(basis_in.at[p, i], basis.at[p, i], sems.at[1, n]))
    for copy in copies:
        copy.start()
    for copy in copies:
        copy.wait()


def halve_kernel(mine, *refs):
    others, keep, send = refs[:-2], refs[-2], refs[-1]
    n = keep.shape[0]
    total = jnp.concatenate([other[...] for other in others], 0).astype(F32) + mine[...]
    keep[...] = total[:n]
    send[...] = total[n:].astype(BF16)


def mirror_kernel(mine, *refs):
    others, keep, send = refs[:-2], refs[-2], refs[-1]
    total = jnp.concatenate([other[...] for other in others], 0).astype(F32) + mine[...]
    keep[...] = total
    n = keep.shape[0]
    for e in range(n):
        send[e] = total[n - 1 - e].astype(BF16)


def residual_kernel(c, mine, other, *refs):
    arrays, out = refs[:2], refs[2]
    part = out.shape[-1] // 2
    lanes = slice(c * part, (c + 1) * part)
    for e in range(2):
        total = mine[e] + other[e].astype(F32)
        data = jnp.concatenate([arrays[e][p, :, :, lanes] for p in range(2)], -1)
        weight = jnp.concatenate([arrays[e][2, :, :, lanes]] * 2, -1)
        value = (weight.astype(F32) * (total - data.astype(F32))).astype(BF16)
        out[e] = value


def spread_kernel(source, *outs):
    for e, out in enumerate(outs):
        out[0] = source[e]


def join_kernel(*refs):
    out = refs[-1]
    part = out.shape[-1] // (len(refs) - 1)
    for p in range(2):
        out[p] = jnp.concatenate([ref[0, :, :, p * part : (p + 1) * part] for ref in refs[:-1]], -1)


def share_kernel(mine, *refs):
    others, out = refs[:-1], refs[-1]
    n = others[0].shape[0]
    for k, other in enumerate(others):
        at = slice(k * n, (k + 1) * n)
        out[at] = (mine[at] + other[...].astype(F32)).astype(BF16)


def total_kernel(mine, *refs):
    others, out = refs[:-1], refs[-1]
    total = mine[...]
    for ref in others:
        total = total + ref[...].astype(F32)
    out[...] = total


def final_kernel(done, mine, *refs):
    *others, out, out_ref, sems = refs
    part = mine.shape[1] // 2
    columns = out_ref.shape[1]
    copies = []
    for j in range(columns):
        for p in range(2):
            lanes = slice(p * part, (p + 1) * part)
            total = mine[j, lanes, :]
            for ref in others:
                total = total + ref[j, lanes, :].astype(F32)
            out_ref[p, j] = jnp.concatenate([done[j, lanes, :], total], 0).astype(out_ref.dtype).T
        n = len(copies)
        if j + 1 == (n + 1) * columns // sems.shape[0]:
            at = slice(n * columns // sems.shape[0], j + 1)
            copies.append(pltpu.make_async_copy(out_ref.at[:, at], out.at[:, at], sems.at[n]))
            copies[-1].start()
    for copy in copies:
        copy.wait()


def slots_of(counts, refs):
    slots, at = [], 0
    for count in counts:
        slots.append([(ref, j) for ref in refs[at : at + count] for j in range(ref.shape[0])])
        at += count
    return slots, refs[at:]


def products(slots, places, columns, second, waves):
    _, quarter, width = slots[0][0][0].shape
    half = second.shape[1] // 2
    at_all = [pl.multiple_of(at * quarter, quarter) for at in places]
    for n, j in enumerate(columns):
        parts = [ref[k] for ref, k in (slot[n if len(slot) == len(columns) else j] for slot in slots)]
        if quarter % LANES == 0:
            left = jnp.concatenate([second[j, :, pl.ds(at, quarter)] for at in at_all], 1)
            right = jnp.concatenate(parts, 0)
        else:
            waves[n] = jnp.zeros(waves.shape[1:], BF16)
            for at, part in zip(at_all, parts):
                waves[n, pl.ds(at, quarter), :] = part
            left, right = second[j], waves[n]
        out = jnp.dot(left, right, preferred_element_type=F32)
        yield n, j, out[:half] + turn(out[half:], 1.0, -1.0)


def near_kernel(second, *refs):
    r, here = lax.axis_index("row"), lax.axis_index("help")
    helps = lax.axis_size("help")
    *refs, waves = refs
    parts = len(refs) // (helps + 1)
    for c in range(parts):
        out = refs[parts * helps + c]
        slots = [[(ref, j) for j in range(ref.shape[0])] for ref in refs[c * helps : (c + 1) * helps]]
        places = [r * helps + (here ^ d) for d in range(helps)]
        rows = out.shape[0]
        for n, j, value in products(slots, places, range(second.shape[0]), second, waves):
            terms = value.shape[0] // rows
            for i in range(rows):
                out[i, j * terms : (j + 1) * terms, :] = value[i * terms : (i + 1) * terms]


def coefficients(slots, columns, ranks, second, near, waves, coef):
    rs, helps = lax.axis_size("row"), lax.axis_size("help")
    r, here = lax.axis_index("row"), lax.axis_index("help")
    rows = coef.shape[0]
    terms = second.shape[1] // (2 * rows)
    row_index = lax.broadcasted_iota(jnp.int32, (terms, coef.shape[2]), 0)
    places = [(r ^ d) * helps + (here ^ e) for e in range(helps) for d in range(1, rs)]
    for n, j, value in products(slots, places, columns, second, waves):
        for i in range(rows):
            left = ranks[i, j] - here * terms
            part = value[i * terms : (i + 1) * terms] + near[i, j * terms : (j + 1) * terms, :]
            coef[i, n * terms : (n + 1) * terms, :] = jnp.where(row_index < left, part, 0.0)


def head_kernel(counts, ranks, *refs):
    slots, (second, near, coef, waves) = slots_of(counts, refs)
    coefficients(slots, range(len(slots[0])), ranks, second, near, waves, coef)


def forward_kernel(z_offsets, counts, n_heads, ranks, *refs):
    slots, refs = slots_of(counts, refs)
    (second, basis, near), heads, refs = refs[:3], refs[3 : 3 + n_heads], refs[3 + n_heads :]
    keep_out, *sends, waves, coef, fwd = refs
    n_send = sends[0].shape[0]
    helps = lax.axis_size("help")
    z, here = lax.axis_index("col"), lax.axis_index("help")
    columns = second.shape[0]
    coefficients(slots, range(columns - len(slots[0]), columns), ranks, second, near, waves, coef)
    rows = basis.shape[1]
    _, _, span, _ = keep_out.shape
    dims = (((0,), (0,)), ((), ()))
    for i in range(rows):
        value = jnp.concatenate([head[i] for head in heads] + [coef[i]], 0)
        left = jnp.concatenate([value, turn(value, -1.0, 1.0)], 0).astype(BF16)
        right = jnp.concatenate([basis[0, i], basis[1, i]], 0)
        out = lax.dot_general(left, right, dims, preferred_element_type=F32)
        fwd[i] = out.T
        for n, offset in enumerate(z_offsets):
            block = (z ^ offset) * helps
            at = pl.multiple_of((block + here) * span, span)
            keep_out[n, i] = fwd[i, pl.ds(at, span), :].astype(keep_out.dtype)
            at = pl.multiple_of((block + 1 - here) * span, span)
            sends[n // n_send][n % n_send, i] = fwd[i, pl.ds(at, span), :].astype(BF16)


def adjoint_terms(offsets, back, second, keeps, sends):
    rs, helps = lax.axis_size("row"), lax.axis_size("help")
    r, here = lax.axis_index("row"), lax.axis_index("help")
    _, width, quarter = keeps[0].shape
    parts = len(sends) // len(offsets)
    half = back.shape[1]

    def keep(d, j, value):
        keeps[d][j] = value

    def send(d, j, value):
        refs = sends[d * parts : (d + 1) * parts]
        n = refs[0].shape[0]
        refs[j // n][j % n] = value.astype(BF16)

    for j in range(back.shape[0]):
        real = back[j].astype(BF16).T
        turned = jnp.concatenate([-real[width // 2 :], real[: width // 2]], 0)

        def product(right):
            out = jnp.dot(real, right[:half], preferred_element_type=F32)
            return out + jnp.dot(turned, right[half:], preferred_element_type=F32)

        if quarter % LANES == 0:
            for n, d in enumerate(offsets):
                places = [((r ^ d) * helps + h) * quarter for h in (here, 1 - here)]
                places = [pl.multiple_of(at, quarter) for at in places]
                out = product(jnp.concatenate([second[j, :, pl.ds(at, quarter)] for at in places], 1))
                keep(n, j, out[:, :quarter])
                send(n, j, out[:, quarter:])
        else:
            out = product(second[j])
            for m in range(rs):
                for h in range(helps):
                    part = out[:, (m * helps + h) * quarter : (m * helps + h + 1) * quarter]
                    for n, d in enumerate(offsets):
                        pl.when((here == h) & (m ^ r == d))(functools.partial(keep, n, j, part))
                        pl.when((here != h) & (m ^ r == d))(functools.partial(send, n, j, part))


def adjoint_kernel(offsets, spots, ranks, *refs):
    n_pieces, n = len(spots), len(offsets)
    pieces, (basis, second), refs = refs[:n_pieces], refs[n_pieces : n_pieces + 2], refs[n_pieces + 2 :]
    back_out, keeps, sends, (resid, back) = refs[0], refs[1 : 1 + n], refs[1 + n : -2], refs[-2:]
    helps = lax.axis_size("help")
    z, here = lax.axis_index("col"), lax.axis_index("help")
    _, rows, span, width = pieces[0].shape
    columns = second.shape[0]
    terms = second.shape[1] // (2 * rows)
    row_index = lax.broadcasted_iota(jnp.int32, (terms, width), 0)
    for i in range(rows):
        for piece, (z_offsets, h_offset) in zip(pieces, spots):
            for e, offset in enumerate(z_offsets):
                spot = (z ^ offset) * helps + (here ^ h_offset)
                resid[i, pl.ds(pl.multiple_of(spot * span, span), span), :] = piece[e, i]
        value = resid[i]
        turned = turn(value.astype(F32), 1.0, -1.0).astype(BF16)
        left = jnp.concatenate([basis[0, i], basis[1, i]], 1)
        out = jnp.dot(left, jnp.concatenate([value, turned], 0), preferred_element_type=F32)
        for j in range(columns):
            left = ranks[i, j] - here * terms
            part = out[j * terms : (j + 1) * terms]
            back[j, i * terms : (i + 1) * terms, :] = jnp.where(row_index < left, part, 0.0)
    back_out[...] = back[...].astype(BF16)
    adjoint_terms(offsets, back, second, keeps, sends)


def own_kernel(back, second, keep, send):
    adjoint_terms([0], back, second, [keep], [send])


def body(wavefield, basis_factor, second_factor, tile_ranks, observed, amplitude):
    _, columns, quarter, rhs = wavefield.shape
    _, rows, _, terms, tile = basis_factor.shape
    span = observed.shape[2]
    zs, rs, helps = lax.axis_size("col"), lax.axis_size("row"), lax.axis_size("help")
    width = 2 * rhs // CHUNKS
    bits = zs.bit_length() - 1
    far = zs // 2
    near = [1 << b for b in range(bits - 1)]
    z_offsets = [int(format(n, f"0{bits}b")[::-1], 2) for n in range(zs)]

    def share(pieces):
        return pieces + [swap("help", d, m) for d in range(1, helps) for m in pieces]

    first = 5 * columns // 8
    shapes = [((n, quarter, width), BF16) for n in (first, columns - first, columns)]
    head, data = call(
        first_kernel,
        "first_waves",
        shapes[:1] + [((3, rows, span, rhs), BF16)],
        [in_hbm(wavefield), in_hbm(observed), in_hbm(amplitude)],
        in_specs=[HBM] * 3,
        scratch=[pltpu.VMEM((2, first, quarter, rhs), BF16), pltpu.SemaphoreType.DMA((4,))],
    )
    data = call(relay_kernel, "relay_data", [(data.shape, BF16)], [after(data, head)], cost=LARGE)[0]
    data = [data, swap("col", far, data)]
    rest, whole, *others = call(
        waves_kernel,
        "other_waves",
        shapes[1:] + shapes[2:] * (CHUNKS - 1),
        [after(wavefield, data[0])],
        cost=LARGE,
    )
    waves = [[head, rest]] + [[w] for w in others]
    gathered = [[[swap("row", d, w) for w in ws] for d in range(1, rs)] for ws in waves]
    wholes = [whole, *others]

    second, basis = call(
        load_kernel,
        "load_factors",
        [((columns, 2 * rows, terms, tile), BF16), ((2, rows, columns, terms, tile), BF16)],
        [second_factor, basis_factor],
        in_specs=[HBM] * 2,
        scratch=[pltpu.SemaphoreType.DMA((2, 2 * rows))],
        cost=LARGE,
    )
    second = second.reshape(columns, 2 * rows * terms, tile)
    basis = basis.reshape(2, rows, columns * terms, tile)
    nears = call(
        near_kernel,
        "near_products",
        [((rows, columns * terms, width), F32)] * CHUNKS,
        [second, *[m for w in wholes for m in share([w])]],
        scratch=[pltpu.VMEM((columns, tile, width), BF16)],
        limit=16 * MIB,
        cost=1,
    )

    def forward(c, mine, heads):
        split = zs if c else SPLIT
        shape, piece = (zs, rows, span, width), (zs // split, rows, span, width)
        pieces = [m for slot in mine for m in slot]
        n = sum(m.shape[0] for m in mine[0])
        return call(
            functools.partial(forward_kernel, z_offsets, [len(slot) for slot in mine], len(heads)),
            "forward_product",
            [(shape, F32)] + [(piece, BF16)] * split,
            [tile_ranks, *pieces, second, basis, nears[c], *heads],
            in_specs=[SM] + [VM] * (len(pieces) + 3 + len(heads)),
            scratch=[
                pltpu.VMEM((n, tile, width), BF16),
                pltpu.VMEM((rows, n * terms, width), F32),
                pltpu.VMEM((rows, tile, width), F32),
            ],
            limit=16 * MIB,
            cost=LARGE if c else 1,
        )

    def backward(c, pieces, spots):
        whole, parts = (columns, width, quarter), 2
        piece = (columns // parts, width, quarter)
        back, *outs = call(
            functools.partial(adjoint_kernel, list(range(1, rs)), spots),
            "adjoint_product",
            [((columns, rows * terms, width), BF16)]
            + [(whole, F32)] * (rs - 1)
            + [(piece, BF16)] * ((rs - 1) * parts),
            [tile_ranks, *pieces, basis, second],
            in_specs=[SM] + [VM] * (len(pieces) + 2),
            scratch=[
                pltpu.VMEM((rows, tile, width), BF16),
                pltpu.VMEM((columns, rows * terms, width), F32),
            ],
            limit=16 * MIB,
            cost=1,
        )
        keeps, sends = outs[: rs - 1], outs[rs - 1 :]
        own = call(
            own_kernel, "own_quarter", [(whole, F32), (whole, BF16)], [back, second], limit=16 * MIB, cost=OWN
        )
        return [own[0], *keeps], [own[1:]] + [sends[d * parts : (d + 1) * parts] for d in range(rs - 1)]

    halved, mirrored, residuals, sent, totals, joined = [], [], [], [], [], []

    def front(c):
        earlier = [(mirrored[-1][1],)] if c else [(second, *nears), (second, data[1])]
        far_pieces = [[after(m, *e) for m, e in zip(slot, earlier)] for slot in gathered[c]]
        mine = list(far_pieces)
        for d in range(1, helps):
            mine.extend([swap("help", d, m) for m in slot] for slot in far_pieces)
        heads = []
        if c:
            mine[0][0] = after(mine[0][0], mirrored[-1][1])
        else:
            pieces = [slot[0] for slot in mine]
            heads = call(
                functools.partial(head_kernel, [1] * len(pieces)),
                "first_coefficients",
                [((rows, first * terms, width), F32)],
                [tile_ranks, *pieces, second, nears[0]],
                in_specs=[SM] + [VM] * (len(pieces) + 2),
                scratch=[pltpu.VMEM((first, tile, width), BF16)],
                limit=16 * MIB,
                cost=HEAD,
            )
            mine = [slot[1:] or slot for slot in mine]
        keep, *sends = forward(c, mine, heads)
        others = [swap("help", 1, send) for send in sends]
        for d in near:
            shape = (keep.shape[0] // 2, rows, span, width)
            keep, send = call(
                halve_kernel, "halve", [(shape, F32), (shape, BF16)], [keep, *others], cost=1
            )
            others = [swap("col", d, send)]
        halved.append(send)
        if c:
            residual_of(c - 1, send)
            keep = after(keep, *residuals[c - 1])
        mirrored.append(call(mirror_kernel, "mirror", [(shape, F32), (shape, BF16)], [keep, *others]))

    def residual_of(c, *earlier):
        keep, send = mirrored[c]
        residuals.append(
            call(
                functools.partial(residual_kernel, c),
                "residual",
                [((2, rows, span, width), BF16)],
                [after(keep, *earlier), swap("col", far, send), *data],
                cost=LARGE,
            )
        )

    def rear(c):
        pieces, offsets = list(residuals[c]), [[0, far]]
        for d in reversed(near):
            pieces = pieces + [swap("col", d, m) for m in pieces]
            offsets = offsets + [[o ^ d for o in os] for os in offsets]
        last = c + 1 == CHUNKS
        earlier = sent if last else [mirrored[c + 1][1]]
        pieces[1:] = [after(m, *earlier) for m in pieces[1:]]
        passed = list(pieces)
        if not last:
            block = ((1, rows, span, width), BF16)
            for m in pieces[1:]:
                passed.extend(call(spread_kernel, "spread", [block] * 2, [m], cost=1))
            passed[1 : len(pieces)] = []
            passed_offsets = offsets[:1] + [[o] for os in offsets[1:] for o in os]
        else:
            passed_offsets = offsets
        pieces = pieces + [swap("help", d, m) for d in range(1, helps) for m in passed]
        spots = [(o, 0) for o in offsets] + [(o, e) for e in range(1, helps) for o in passed_offsets]
        if not last:
            pieces[0] = after(pieces[0], mirrored[c + 1][1])
        else:
            joined.extend(call(join_kernel, "join", [(observed.shape, BF16)], [r[0] for r in residuals]))
            pieces[0] = after(pieces[0], *joined)
        keeps, sends = backward(c, pieces, spots)
        if not last:
            residual_of(c + 1, sends[0][0])
            keeps = [keeps[0]] + [after(k, *residuals[c + 1]) for k in keeps[1:]]
        shape = (columns, width, quarter)
        shared = [
            call(
                share_kernel,
                "adjoint_share",
                [(shape, BF16)],
                [k, *[swap("help", 1, m) for m in s]],
            )[0]
            for k, s in zip(keeps[1:], sends[1:])
        ]
        if last:
            totals[-1][0] = after(totals[-1][0], *shared)
            mine, theirs, *others = totals[-1]
            mine = call(total_kernel, "total", [(shape, F32)], [mine, *others], cost=1)[0]
            totals[-1] = call(total_kernel, "total", [(shape, F32)], [mine, theirs], cost=LARGE)
        else:
            sent.extend(shared)
        totals.append(
            [keeps[0], swap("help", 1, after(sends[0][0], *shared))]
            + [swap("row", d + 1, m) for d, m in enumerate(shared)]
        )

    for c in range(CHUNKS):
        front(c)
    for c in range(CHUNKS):
        rear(c)

    adjoint = call(
        final_kernel,
        "adjoint_sum",
        [(wavefield.shape, BF16)],
        [*totals[0], *totals[1]],
        out_specs=[HBM],
        scratch=[pltpu.VMEM(wavefield.shape, BF16), pltpu.SemaphoreType.DMA((4,))],
    )[0]
    return joined[0], adjoint


def solution(mesh):
    return jax.shard_map(
        body,
        mesh=mesh,
        in_specs=(
            P("freq", "col", ("row", "help"), None),
            P("freq", "row", "col", "help", None),
            P("freq", "row", "col", "help", None),
            P(("freq", "row"), "col"),
            P("freq", "row", ("col", "help"), None),
            P(("freq", "row"), ("col", "help"), None),
        ),
        out_specs=(
            P("freq", "row", ("col", "help"), None),
            P("freq", "col", ("row", "help"), None),
        ),
        check_vma=False,
    )
```

time: 81.2 us -> 79.6 us (0.980)
  waiting for transfers between devices: 33.3 us -> 29.3 us
  Pallas kernels: 21.1 us -> 22.4 us
  starting transfers between devices: 25.7 us -> 26.6 us
    ppermute x36 -> x34, waiting for transfers between devices: 33.3 us -> 29.3 us  [swap(): return lax.ppermute(value, axis_name, [(i, i ^ step) for i in range(size)])]
    pallas_call x19 -> x25, Pallas kernels: 21.1 us -> 22.4 us  [call(): pl.pallas_call(kernel, out_shape=[jax.ShapeDtypeStruct(shape, kind) for s...]
    ppermute x36 -> x34, starting transfers between devices: 25.7 us -> 26.6 us  [swap(): return lax.ppermute(value, axis_name, [(i, i ^ step) for i in range(size)])]
  transfers between devices with their start and end apart: 36 -> 34, of which waited for: 23 -> 22; matrix products, arithmetic and copies ran while one was open for 0% -> 0% of each run, Pallas kernels for 23% -> 25%
where the time goes in v6:
time: 79.6 us; the launch traced here: 79.4 us
  waiting for transfers between devices  29.3 us (37%)
  starting transfers between devices  26.6 us (33%)
  Pallas kernels  22.4 us (28%)
  between operations  1.07 us (1%)
    ppermute x34, waiting for transfers between devices, swap(): return lax.ppermute(value, axis_name, [(i, i ^ step) for i in range(size)])  29.3 us
    ppermute x34, starting transfers between devices, swap(): return lax.ppermute(value, axis_name, [(i, i ^ step) for i in range(size)])  26.6 us
    pallas_call x25, Pallas kernels, call(): pl.pallas_call(kernel, out_shape=[jax.ShapeDtypeStruct(shape, kind) for s...  22.4 us
  transfers between devices with their start and end apart: 34, of which 22 were waited for; matrix products, arithmetic and copies ran while one was open for 0% of the time, Pallas kernels for 25%

profile of v6, /device:TPU:0, one launch (start us, length us, event | category | flops | bytes accessed | tf_op | source)
XLA Modules:
  0.0 79.4 jit_solution(8347629781413993961)
XLA Ops:
  0.6 1.3 %first_waves.1 = (bf16[10,128,128]{2,1,0:T(8,128)(2,1)S(1)}, bf16[3,4,64,128]{3,2,1,0:T(8,128)(2,1)S(1)}) custom-call(bf16[2,16,128,128]{3,2,1,0:T(8,128)(2,1)} %source.2, bf16[2,4,64,128]{3,2,1,0:T(8,128)(2,1)} %observed.1, bf16[4,64,128]{2,1,0:T(8,128)(2,1)} %amplitude.1), custom_call_target="tpu_custom_call" | custom-call | flops 1000000 | bytes 10000 | tf_op jit(solution)/shard_map/first_waves/pallas_call | solution.py:26
  1.9 3.0 %collective-permute-start.5 = (bf16[10,128,128]{2,1,0:T(8,128)(2,1)S(1)}, bf16[10,128,128]{2,1,0:T(8,128)(2,1)S(1)}, u32[]{:S(2)}, u32[]{:S(2)}) collective-permute-start(bf16[10,128,128]{2,1,0:T(8,128)(2,1)S(1)} %get-tuple-element.59), channel_id=1, source_target_pairs={{0,2},{2,0},{1,3},{3,1},{4,6},{6,4},{5,7},{7,5},{8,10},{10,8},{9,1... | collective-permute-start | bytes 983048 | tf_op jit(solution)/shard_map/ppermute | solution.py:44
  5.0 2.7 %collective-permute-start.1 = (bf16[3,4,64,128]{3,2,1,0:T(8,128)(2,1)S(1)}, bf16[3,4,64,128]{3,2,1,0:T(8,128)(2,1)S(1)}, u32[]{:S(2)}, u32[]{:S(2)}) collective-permute-start(bf16[3,4,64,128]{3,2,1,0:T(8,128)(2,1)S(1)} %relay_data.1.refs_0_), channel_id=1, source_target_pairs={{0,8},{4,12},{8,0},{12,4},{1,9},{5,13},{9,1},{13,5},{2,10},{6,14},... | collective-permute-start | bytes 589832 | tf_op jit(solution)/shard_map/ppermute | solution.py:44
  7.6 0.4 other_waves.1
  8.1 0.5 collective-permute-start.3
  8.6 0.5 collective-permute-start
  9.2 2.2 %load_factors.1 = (bf16[16,8,40,512]{3,2,1,0:T(8,128)(2,1)S(1)}, bf16[2,4,16,40,512]{4,3,2,1,0:T(8,128)(2,1)S(1)}) custom-call(bf16[2,4,16,40,512]{4,3,2,1,0:T(8,128)(2,1)S(1)} %bitcast.15, bf16[2,4,16,40,512]{4,3,2,1,0:T(8,128)(2,1)S(1)} %bitcast.17), custom_call_target="tpu_custom_call" | custom-call | flops 10000000000 | bytes 10000 | tf_op jit(solution)/shard_map/load_factors/pallas_call | solution.py:26
  11.4 1.7 %near_products.1 = (f32[4,640,128]{2,1,0:T(8,128)S(1)}, f32[4,640,128]{2,1,0:T(8,128)S(1)}) custom-call(bf16[16,320,512]{2,1,0:T(8,128)(2,1)S(1)} %bitcast.2, bf16[16,128,128]{2,1,0:T(8,128)(2,1)S(1)} %get-tuple-element.66.refs_0_, bf16[16,128,128]{2,1,0:T(8,128)(2,1)S(1)} %collective-permute-done.3.refs_1_, ...), custom_call_target="tpu_custom_call" | custom-call | flops 1 | bytes 10000 | tf_op jit(solution)/shard_map/near_products/pallas_call | solution.py:26
  13.1 0.4 collective-permute-done.5.refs_0_
  13.4 2.1 %collective-permute-start.10 = (bf16[16,128,128]{2,1,0:T(8,128)(2,1)S(1)}, bf16[16,128,128]{2,1,0:T(8,128)(2,1)S(1)}, u32[]{:S(2)}, u32[]{:S(2)}) collective-permute-start(bf16[16,128,128]{2,1,0:T(8,128)(2,1)S(1)} %get-tuple-element.67.refs_2_), channel_id=1, source_target_pairs={{0,2},{2,0},{1,3},{3,1},{4,6},{6,4},{5,7},{7,5},{8,10},{10,8},{9,1... | collective-permute-start | bytes 1572872 | tf_op jit(solution)/shard_map/ppermute | solution.py:44
  15.5 1.3 %collective-permute-done.refs_0_ = bf16[6,128,128]{2,1,0:T(8,128)(2,1)S(1)} collective-permute-done((bf16[6,128,128]{2,1,0:T(8,128)(2,1)S(1)}, bf16[6,128,128]{2,1,0:T(8,128)(2,1)S(1)}, u32[]{:S(2)}, u32[]{:S(2)}) %collective-permute-start) | collective-permute-done | bytes 196640 | tf_op jit(solution)/shard_map/ppermute | solution.py:44
  16.9 1.2 %first_coefficients.1.refs_5_ = f32[4,400,128]{2,1,0:T(8,128)S(1)} custom-call(s32[4,16]{1,0:T(4,128)S(1)} %copy-done.1, bf16[10,128,128]{2,1,0:T(8,128)(2,1)S(1)} %collective-permute-done.5.refs_0_, bf16[10,128,128]{2,1,0:T(8,128)(2,1)S(1)} %collective-permute-done.6.refs_1_, bf16[16,320,512]{2,1,0:T(8,128)(2,1)S(1)} %bitcast.3, ...), custom_call_target="tpu_custom_call" | custom-call | flops 1 | bytes 10000 | tf_op jit(solution)/shard_map/first_coefficients/pallas_call | solution.py:26
  18.3 2.7 %forward_product.2 = (f32[4,4,64,128]{3,2,1,0:T(8,128)S(1)}, bf16[2,4,64,128]{3,2,1,0:T(8,128)(2,1)S(1)}, bf16[2,4,64,128]{3,2,1,0:T(8,128)(2,1)S(1)}) custom-call(s32[4,16]{1,0:T(4,128)S(1)} %copy-done.1, bf16[6,128,128]{2,1,0:T(8,128)(2,1)S(1)} %collective-permute-done.refs_0_, bf16[6,128,128]{2,1,0:T(8,128)(2,1)S(1)} %collective-permute-done.2.refs_1_, ...), custom_call_target="tpu_custom_call" | custom-call | flops 1 | bytes 10000 | tf_op jit(solution)/shard_map/forward_product/pallas_call | solution.py:26
  21.0 0.4 collective-permute-start.7
  21.6 0.8 %collective-permute-done.7.refs_0_ = bf16[2,4,64,128]{3,2,1,0:T(8,128)(2,1)S(1)} collective-permute-done((bf16[2,4,64,128]{3,2,1,0:T(8,128)(2,1)S(1)}, bf16[2,4,64,128]{3,2,1,0:T(8,128)(2,1)S(1)}, u32[]{:S(2)}, u32[]{:S(2)}) %collective-permute-start.7) | collective-permute-done | bytes 131104 | tf_op jit(solution)/shard_map/ppermute | solution.py:44
  22.4 0.3 collective-permute-done.8.refs_1_
  22.8 1.9 %collective-permute-start.9 = (bf16[2,4,64,128]{3,2,1,0:T(8,128)(2,1)S(1)}, bf16[2,4,64,128]{3,2,1,0:T(8,128)(2,1)S(1)}, u32[]{:S(2)}, u32[]{:S(2)}) collective-permute-start(bf16[2,4,64,128]{3,2,1,0:T(8,128)(2,1)S(1)} %get-tuple-element.75), channel_id=1, source_target_pairs={{0,4},{4,0},{8,12},{12,8},{1,5},{5,1},{9,13},{13,9},{2,6},{6,2},{1... | collective-permute-start | bytes 393224 | tf_op jit(solution)/shard_map/ppermute | solution.py:44
  24.7 3.8 %collective-permute-done.9.refs_0_ = bf16[2,4,64,128]{3,2,1,0:T(8,128)(2,1)S(1)} collective-permute-done((bf16[2,4,64,128]{3,2,1,0:T(8,128)(2,1)S(1)}, bf16[2,4,64,128]{3,2,1,0:T(8,128)(2,1)S(1)}, u32[]{:S(2)}, u32[]{:S(2)}) %collective-permute-start.9) | collective-permute-done | bytes 131104 | tf_op jit(solution)/shard_map/ppermute | solution.py:44
  28.7 2.8 %collective-permute-start.16 = (bf16[2,4,64,128]{3,2,1,0:T(8,128)(2,1)S(1)}, bf16[2,4,64,128]{3,2,1,0:T(8,128)(2,1)S(1)}, u32[]{:S(2)}, u32[]{:S(2)}) collective-permute-start(bf16[2,4,64,128]{3,2,1,0:T(8,128)(2,1)S(1)} %get-tuple-element.77), channel_id=1, source_target_pairs={{0,8},{4,12},{8,0},{12,4},{1,9},{5,13},{9,1},{13,5},{2,10},{6,14},... | collective-permute-start | bytes 393224 | tf_op jit(solution)/shard_map/ppermute | solution.py:44
  31.5 3.0 %forward_product.3 = (f32[4,4,64,128]{3,2,1,0:T(8,128)S(1)}, bf16[1,4,64,128]{3,2,1,0:T(8,128)(2,1)S(1)}, bf16[1,4,64,128]{3,2,1,0:T(8,128)(2,1)S(1)}, bf16[1,4,...) custom-call(s32[4,16]{1,0:T(4,128)S(1)} %copy-done.1, bf16[16,128,128]{2,1,0:T(8,128)(2,1)S(1)} %collective-permute-done.10.refs_0_, ...), custom_call_target="tpu_custom_call" | custom-call | flops 10000000000 | bytes 10000 | tf_op jit(solution)/shard_map/forward_product/pallas_call | solution.py:26
  34.8 0.4 collective-permute-start.13
  35.3 0.4 collective-permute-start.15
  36.0 0.4 collective-permute-done.14.refs_2_
  36.6 1.6 %collective-permute-start.17 = (bf16[2,4,64,128]{3,2,1,0:T(8,128)(2,1)S(1)}, bf16[2,4,64,128]{3,2,1,0:T(8,128)(2,1)S(1)}, u32[]{:S(2)}, u32[]{:S(2)}) collective-permute-start(bf16[2,4,64,128]{3,2,1,0:T(8,128)(2,1)S(1)} %get-tuple-element.85), channel_id=1, source_target_pairs={{0,4},{4,0},{8,12},{12,8},{1,5},{5,1},{9,13},{13,9},{2,6},{6,2},{1... | collective-permute-start | bytes 393224 | tf_op jit(solution)/shard_map/ppermute | solution.py:44
  38.6 0.8 %collective-permute-start.18 = (bf16[2,4,64,128]{3,2,1,0:T(8,128)(2,1)S(1)}, bf16[2,4,64,128]{3,2,1,0:T(8,128)(2,1)S(1)}, u32[]{:S(2)}, u32[]{:S(2)}) collective-permute-start(bf16[2,4,64,128]{3,2,1,0:T(8,128)(2,1)S(1)} %residual.2.refs_0_), channel_id=1, source_target_pairs={{0,4},{4,0},{8,12},{12,8},{1,5},{5,1},{9,13},{13,9},{2,6},{6,2},{1... | collective-permute-start | bytes 393224 | tf_op jit(solution)/shard_map/ppermute | solution.py:44
  39.4 3.6 %collective-permute-done.17.refs_0_ = bf16[2,4,64,128]{3,2,1,0:T(8,128)(2,1)S(1)} collective-permute-done((bf16[2,4,64,128]{3,2,1,0:T(8,128)(2,1)S(1)}, bf16[2,4,64,128]{3,2,1,0:T(8,128)(2,1)S(1)}, u32[]{:S(2)}, u32[]{:S(2)}) %collective-permute-start.17) | collective-permute-done | bytes 131104 | tf_op jit(solution)/shard_map/ppermute | solution.py:44
  43.0 1.8 %collective-permute-start.22 = (bf16[2,4,64,128]{3,2,1,0:T(8,128)(2,1)S(1)}, bf16[2,4,64,128]{3,2,1,0:T(8,128)(2,1)S(1)}, u32[]{:S(2)}, u32[]{:S(2)}) collective-permute-start(bf16[2,4,64,128]{3,2,1,0:T(8,128)(2,1)S(1)} %get-tuple-element.90), channel_id=1, source_target_pairs={{0,8},{4,12},{8,0},{12,4},{1,9},{5,13},{9,1},{13,5},{2,10},{6,14},... | collective-permute-start | bytes 393224 | tf_op jit(solution)/shard_map/ppermute | solution.py:44
  44.8 0.4 collective-permute-done.18.source.refs_1_
  45.3 0.5 collective-permute-start.21
  45.8 0.7 collective-permute-done.20.refs_3_
  46.7 2.7 %adjoint_product.2 = (bf16[16,160,128]{2,1,0:T(8,128)(2,1)S(1)}, f32[16,128,128]{2,1,0:T(8,128)S(1)}, bf16[8,128,128]{2,1,0:T(8,128)(2,1)S(1)}, bf16[8,128,128]{2,1,0:T(8,128)(2,1)S(1)}) custom-call(s32[4,16]{1,0:T(4,128)S(1)} %copy-done.1, bf16[2,4,64,128]{3,2,1,0:T(8,128)(2,1)S(1)} %residual.2.refs_0_, ...), custom_call_target="tpu_custom_call" | custom-call | flops 1 | bytes 10000 | tf_op jit(solution)/shard_map/adjoint_product/pallas_call | solution.py:26
  49.5 0.8 own_quarter.2
  50.2 0.4 collective-permute-start.24
  50.8 0.4 collective-permute-done.22.other
  51.3 1.5 %collective-permute-start.23 = (bf16[2,4,64,128]{3,2,1,0:T(8,128)(2,1)S(1)}, bf16[2,4,64,128]{3,2,1,0:T(8,128)(2,1)S(1)}, u32[]{:S(2)}, u32[]{:S(2)}) collective-permute-start(bf16[2,4,64,128]{3,2,1,0:T(8,128)(2,1)S(1)} %residual.3.refs_1_.refs_0_), channel_id=1, source_target_pairs={{0,4},{4,0},{8,12},{12,8},{1,5},{5,1},{9,13},{13,9},{2,6},{6,2},{1... | collective-permute-start | bytes 393224 | tf_op jit(solution)/shard_map/ppermute | solution.py:44
  52.9 1.6 %collective-permute-start.30 = (bf16[16,128,128]{2,1,0:T(8,128)(2,1)S(1)}, bf16[16,128,128]{2,1,0:T(8,128)(2,1)S(1)}, u32[]{:S(2)}, u32[]{:S(2)}) collective-permute-start(bf16[16,128,128]{2,1,0:T(8,128)(2,1)S(1)} %adjoint_share.2), channel_id=1, source_target_pairs={{0,2},{2,0},{1,3},{3,1},{4,6},{6,4},{5,7},{7,5},{8,10},{10,8},{9,1... | collective-permute-start | bytes 1572872 | tf_op jit(solution)/shard_map/ppermute | solution.py:44
  54.5 0.5 collective-permute-start.26
  55.1 1.8 %collective-permute-done.23.refs_1_ = bf16[2,4,64,128]{3,2,1,0:T(8,128)(2,1)S(1)} collective-permute-done((bf16[2,4,64,128]{3,2,1,0:T(8,128)(2,1)S(1)}, bf16[2,4,64,128]{3,2,1,0:T(8,128)(2,1)S(1)}, u32[]{:S(2)}, u32[]{:S(2)}) %collective-permute-start.23) | collective-permute-done | bytes 131104 | tf_op jit(solution)/shard_map/ppermute | solution.py:44
  56.8 0.8 join.1
  57.6 0.6 collective-permute-done.27.refs_3_
  58.2 2.9 %adjoint_product.3 = (bf16[16,160,128]{2,1,0:T(8,128)(2,1)S(1)}, f32[16,128,128]{2,1,0:T(8,128)S(1)}, bf16[8,128,128]{2,1,0:T(8,128)(2,1)S(1)}, bf16[8,128,128]{2,1,0:T(8,128)(2,1)S(1)}) custom-call(s32[4,16]{1,0:T(4,128)S(1)} %copy-done.1, bf16[2,4,64,128]{3,2,1,0:T(8,128)(2,1)S(1)} %residual.3.refs_1_.refs_0_, ...), custom_call_target="tpu_custom_call" | custom-call | flops 1 | bytes 10000 | tf_op jit(solution)/shard_map/adjoint_product/pallas_call | solution.py:26
  61.3 0.4 collective-permute-start.29
  61.7 0.8 own_quarter.3
  62.7 0.4 collective-permute-done.29.refs_1_
  63.2 1.6 %collective-permute-start.33 = (bf16[16,128,128]{2,1,0:T(8,128)(2,1)S(1)}, bf16[16,128,128]{2,1,0:T(8,128)(2,1)S(1)}, u32[]{:S(2)}, u32[]{:S(2)}) collective-permute-start(bf16[16,128,128]{2,1,0:T(8,128)(2,1)S(1)} %adjoint_share.3), channel_id=1, source_target_pairs={{0,2},{2,0},{1,3},{3,1},{4,6},{6,4},{5,7},{7,5},{8,10},{10,8},{9,1... | collective-permute-start | bytes 1572872 | tf_op jit(solution)/shard_map/ppermute | solution.py:44
  64.8 2.9 %collective-permute-done.30.refs_0_ = bf16[16,128,128]{2,1,0:T(8,128)(2,1)S(1)} collective-permute-done((bf16[16,128,128]{2,1,0:T(8,128)(2,1)S(1)}, bf16[16,128,128]{2,1,0:T(8,128)(2,1)S(1)}, u32[]{:S(2)}, u32[]{:S(2)}) %collective-permute-start.30) | collective-permute-done | bytes 524320 | tf_op jit(solution)/shard_map/ppermute | solution.py:44
  67.9 10.2 %collective-permute-done.33.refs_1_ = bf16[16,128,128]{2,1,0:T(8,128)(2,1)S(1)} collective-permute-done((bf16[16,128,128]{2,1,0:T(8,128)(2,1)S(1)}, bf16[16,128,128]{2,1,0:T(8,128)(2,1)S(1)}, u32[]{:S(2)}, u32[]{:S(2)}) %collective-permute-start.33) | collective-permute-done | bytes 524320 | tf_op jit(solution)/shard_map/ppermute | solution.py:44
  78.1 1.1 %adjoint_sum.1 = bf16[2,16,128,128]{3,2,1,0:T(8,128)(2,1)} custom-call(f32[16,128,128]{2,1,0:T(8,128)S(1)} %total.3.done, f32[16,128,128]{2,1,0:T(8,128)S(1)} %get-tuple-element.111.mine, bf16[16,128,128]{2,1,0:T(8,128)(2,1)S(1)} %collective-permute-done.32.refs_0_, bf16[16,128,128]{2,1,0:T(8,128)(2,1)S(1)} %collective-permute-done.33.refs_1_), custom_call_target="tpu_custom_call" | custom-call | flops 1000000 | bytes 10000 | tf_op jit(solution)/shard_map/adjoint_sum/pallas_call | solution.py:26
  (59 shorter events, 3.5 us)
Async XLA Ops:
  1.9 11.5 %collective-permute-start.5 = (bf16[10,128,128]{2,1,0:T(8,128)(2,1)S(1)}, bf16[10,128,128]{2,1,0:T(8,128)(2,1)S(1)}, u32[]{:S(2)}, u32[]{:S(2)}) collective-permute-start(bf16[10,128,128]{2,1,0:T(8,128)(2,1)S(1)} %get-tuple-element.59), channel_id=1, source_target_pairs={{0,2},{2,0},{1,3},{3,1},{4,6},{6,4},{5,7},{7,5},{8,10},{10,8},{9,1... | collective-permute-start | bytes 983048 | tf_op jit(solution)/shard_map/ppermute | solution.py:44
  4.9 2.7 %copy-start = (bf16[2,16,128,128]{3,2,1,0:T(8,128)(2,1)S(1)}, bf16[2,16,128,128]{3,2,1,0:T(8,128)(2,1)}, u32[]{:S(2)}) copy-start(bf16[2,16,128,128]{3,2,1,0:T(8,128)(2,1)} %source.2) | copy-start | bytes 3145732
  4.9 4.2 %slice-start = ((s8[5242880]{0:T(1024)(128)(4,1)}), s8[4194304]{0:T(1024)(128)(4,1)S(1)}, s32[]{:S(2)}) async-start(s8[5242880]{0:T(1024)(128)(4,1)} %bitcast.14), calls=%async_computation | async-start | bytes 8388608
  4.9 4.2 %slice-start.2 = ((s8[5242880]{0:T(1024)(128)(4,1)}), s8[4194304]{0:T(1024)(128)(4,1)S(1)}, s32[]{:S(2)}) async-start(s8[5242880]{0:T(1024)(128)(4,1)} %bitcast.16), calls=%async_computation.2 | async-start | bytes 8388608
  4.9 4.2 %slice-start.1 = ((s8[5242880]{0:T(1024)(128)(4,1)}), s8[1048576]{0:T(1024)(128)(4,1)S(1)}, s32[]{:S(2)}) async-start(s8[5242880]{0:T(1024)(128)(4,1)} %bitcast.14), calls=%async_computation.1 | async-start | bytes 2097152
  4.9 4.3 %slice-start.3 = ((s8[5242880]{0:T(1024)(128)(4,1)}), s8[1048576]{0:T(1024)(128)(4,1)S(1)}, s32[]{:S(2)}) async-start(s8[5242880]{0:T(1024)(128)(4,1)} %bitcast.16), calls=%async_computation.3 | async-start | bytes 2097152
  5.0 11.9 %collective-permute-start.1 = (bf16[3,4,64,128]{3,2,1,0:T(8,128)(2,1)S(1)}, bf16[3,4,64,128]{3,2,1,0:T(8,128)(2,1)S(1)}, u32[]{:S(2)}, u32[]{:S(2)}) collective-permute-start(bf16[3,4,64,128]{3,2,1,0:T(8,128)(2,1)S(1)} %relay_data.1.refs_0_), channel_id=1, source_target_pairs={{0,8},{4,12},{8,0},{12,4},{1,9},{5,13},{9,1},{13,5},{2,10},{6,14},... | collective-permute-start | bytes 589832 | tf_op jit(solution)/shard_map/ppermute | solution.py:44
  8.0 3.4 %collective-permute-start.4 = (bf16[16,128,128]{2,1,0:T(8,128)(2,1)S(1)}, bf16[16,128,128]{2,1,0:T(8,128)(2,1)S(1)}, u32[]{:S(2)}, u32[]{:S(2)}) collective-permute-start(bf16[16,128,128]{2,1,0:T(8,128)(2,1)S(1)} %get-tuple-element.67.refs_2_), channel_id=1, source_target_pairs={{0,1},{1,0},{2,3},{3,2},{4,5},{5,4},{6,7},{7,6},{8,9},{9,8},{10,11... | collective-permute-start | bytes 1572872 | tf_op jit(solution)/shard_map/ppermute | solution.py:44
  8.1 3.4 %collective-permute-start.3 = (bf16[16,128,128]{2,1,0:T(8,128)(2,1)S(1)}, bf16[16,128,128]{2,1,0:T(8,128)(2,1)S(1)}, u32[]{:S(2)}, u32[]{:S(2)}) collective-permute-start(bf16[16,128,128]{2,1,0:T(8,128)(2,1)S(1)} %get-tuple-element.66.refs_0_), channel_id=1, source_target_pairs={{0,1},{1,0},{2,3},{3,2},{4,5},{5,4},{6,7},{7,6},{8,9},{9,8},{10,11... | collective-permute-start | bytes 1572872 | tf_op jit(solution)/shard_map/ppermute | solution.py:44
  8.6 8.3 %collective-permute-start = (bf16[6,128,128]{2,1,0:T(8,128)(2,1)S(1)}, bf16[6,128,128]{2,1,0:T(8,128)(2,1)S(1)}, u32[]{:S(2)}, u32[]{:S(2)}) collective-permute-start(bf16[6,128,128]{2,1,0:T(8,128)(2,1)S(1)} %get-tuple-element.62), channel_id=1, source_target_pairs={{0,2},{2,0},{1,3},{3,1},{4,6},{6,4},{5,7},{7,5},{8,10},{10,8},{9,1... | collective-permute-start | bytes 589832 | tf_op jit(solution)/shard_map/ppermute | solution.py:44
  11.4 5.5 %copy-start.1 = (s32[4,16]{1,0:T(4,128)S(1)}, s32[4,16]{1,0:T(4,128)}, u32[]{:S(2)}) copy-start(s32[4,16]{1,0:T(4,128)} %ranks.9) | copy-start | bytes 772
  13.4 3.4 %collective-permute-start.6 = (bf16[10,128,128]{2,1,0:T(8,128)(2,1)S(1)}, bf16[10,128,128]{2,1,0:T(8,128)(2,1)S(1)}, u32[]{:S(2)}, u32[]{:S(2)}) collective-permute-start(bf16[10,128,128]{2,1,0:T(8,128)(2,1)S(1)} %collective-permute-done.5.refs_0_), channel_id=1, source_target_pairs={{0,1},{1,0},{2,3},{3,2},{4,5},{5,4},{6,7},{7,6},{8,9},{9,8},{10,11... | collective-permute-start | bytes 983048 | tf_op jit(solution)/shard_map/ppermute | solution.py:44
  13.4 15.1 %collective-permute-start.10 = (bf16[16,128,128]{2,1,0:T(8,128)(2,1)S(1)}, bf16[16,128,128]{2,1,0:T(8,128)(2,1)S(1)}, u32[]{:S(2)}, u32[]{:S(2)}) collective-permute-start(bf16[16,128,128]{2,1,0:T(8,128)(2,1)S(1)} %get-tuple-element.67.refs_2_), channel_id=1, source_target_pairs={{0,2},{2,0},{1,3},{3,1},{4,6},{6,4},{5,7},{7,5},{8,10},{10,8},{9,1... | collective-permute-start | bytes 1572872 | tf_op jit(solution)/shard_map/ppermute | solution.py:44
  16.8 1.4 %collective-permute-start.2 = (bf16[6,128,128]{2,1,0:T(8,128)(2,1)S(1)}, bf16[6,128,128]{2,1,0:T(8,128)(2,1)S(1)}, u32[]{:S(2)}, u32[]{:S(2)}) collective-permute-start(bf16[6,128,128]{2,1,0:T(8,128)(2,1)S(1)} %collective-permute-done.refs_0_), channel_id=1, source_target_pairs={{0,1},{1,0},{2,3},{3,2},{4,5},{5,4},{6,7},{7,6},{8,9},{9,8},{10,11... | collective-permute-start | bytes 589832 | tf_op jit(solution)/shard_map/ppermute | solution.py:44
  21.0 1.4 %collective-permute-start.7 = (bf16[2,4,64,128]{3,2,1,0:T(8,128)(2,1)S(1)}, bf16[2,4,64,128]{3,2,1,0:T(8,128)(2,1)S(1)}, u32[]{:S(2)}, u32[]{:S(2)}) collective-permute-start(bf16[2,4,64,128]{3,2,1,0:T(8,128)(2,1)S(1)} %get-tuple-element.72), channel_id=1, source_target_pairs={{0,1},{1,0},{2,3},{3,2},{4,5},{5,4},{6,7},{7,6},{8,9},{9,8},{10,11... | collective-permute-start | bytes 393224 | tf_op jit(solution)/shard_map/ppermute | solution.py:44
  21.4 1.3 %collective-permute-start.8 = (bf16[2,4,64,128]{3,2,1,0:T(8,128)(2,1)S(1)}, bf16[2,4,64,128]{3,2,1,0:T(8,128)(2,1)S(1)}, u32[]{:S(2)}, u32[]{:S(2)}) collective-permute-start(bf16[2,4,64,128]{3,2,1,0:T(8,128)(2,1)S(1)} %get-tuple-element.73), channel_id=1, source_target_pairs={{0,1},{1,0},{2,3},{3,2},{4,5},{5,4},{6,7},{7,6},{8,9},{9,8},{10,11... | collective-permute-start | bytes 393224 | tf_op jit(solution)/shard_map/ppermute | solution.py:44
  22.8 5.7 %collective-permute-start.9 = (bf16[2,4,64,128]{3,2,1,0:T(8,128)(2,1)S(1)}, bf16[2,4,64,128]{3,2,1,0:T(8,128)(2,1)S(1)}, u32[]{:S(2)}, u32[]{:S(2)}) collective-permute-start(bf16[2,4,64,128]{3,2,1,0:T(8,128)(2,1)S(1)} %get-tuple-element.75), channel_id=1, source_target_pairs={{0,4},{4,0},{8,12},{12,8},{1,5},{5,1},{9,13},{13,9},{2,6},{6,2},{1... | collective-permute-start | bytes 393224 | tf_op jit(solution)/shard_map/ppermute | solution.py:44
  28.6 2.9 %collective-permute-start.11 = (bf16[16,128,128]{2,1,0:T(8,128)(2,1)S(1)}, bf16[16,128,128]{2,1,0:T(8,128)(2,1)S(1)}, u32[]{:S(2)}, u32[]{:S(2)}) collective-permute-start(bf16[16,128,128]{2,1,0:T(8,128)(2,1)S(1)} %collective-permute-done.10.refs_0_), channel_id=1, source_target_pairs={{0,1},{1,0},{2,3},{3,2},{4,5},{5,4},{6,7},{7,6},{8,9},{9,8},{10,11... | collective-permute-start | bytes 1572872 | tf_op jit(solution)/shard_map/ppermute | solution.py:44
  28.7 9.7 %collective-permute-start.16 = (bf16[2,4,64,128]{3,2,1,0:T(8,128)(2,1)S(1)}, bf16[2,4,64,128]{3,2,1,0:T(8,128)(2,1)S(1)}, u32[]{:S(2)}, u32[]{:S(2)}) collective-permute-start(bf16[2,4,64,128]{3,2,1,0:T(8,128)(2,1)S(1)} %get-tuple-element.77), channel_id=1, source_target_pairs={{0,8},{4,12},{8,0},{12,4},{1,9},{5,13},{9,1},{13,5},{2,10},{6,14},... | collective-permute-start | bytes 393224 | tf_op jit(solution)/shard_map/ppermute | solution.py:44
  34.5 1.3 %collective-permute-start.12 = (bf16[1,4,64,128]{3,2,1,0:T(8,128)(2,1)S(1)}, bf16[1,4,64,128]{3,2,1,0:T(8,128)(2,1)S(1)}, u32[]{:S(2)}, u32[]{:S(2)}) collective-permute-start(bf16[1,4,64,128]{3,2,1,0:T(8,128)(2,1)S(1)} %get-tuple-element.81), channel_id=1, source_target_pairs={{0,1},{1,0},{2,3},{3,2},{4,5},{5,4},{6,7},{7,6},{8,9},{9,8},{10,11... | collective-permute-start | bytes 196616 | tf_op jit(solution)/shard_map/ppermute | solution.py:44
  34.8 1.3 %collective-permute-start.13 = (bf16[1,4,64,128]{3,2,1,0:T(8,128)(2,1)S(1)}, bf16[1,4,64,128]{3,2,1,0:T(8,128)(2,1)S(1)}, u32[]{:S(2)}, u32[]{:S(2)}) collective-permute-start(bf16[1,4,64,128]{3,2,1,0:T(8,128)(2,1)S(1)} %get-tuple-element.82), channel_id=1, source_target_pairs={{0,1},{1,0},{2,3},{3,2},{4,5},{5,4},{6,7},{7,6},{8,9},{9,8},{10,11... | collective-permute-start | bytes 196616 | tf_op jit(solution)/shard_map/ppermute | solution.py:44
  35.1 1.3 %collective-permute-start.14 = (bf16[1,4,64,128]{3,2,1,0:T(8,128)(2,1)S(1)}, bf16[1,4,64,128]{3,2,1,0:T(8,128)(2,1)S(1)}, u32[]{:S(2)}, u32[]{:S(2)}) collective-permute-start(bf16[1,4,64,128]{3,2,1,0:T(8,128)(2,1)S(1)} %get-tuple-element.83), channel_id=1, source_target_pairs={{0,1},{1,0},{2,3},{3,2},{4,5},{5,4},{6,7},{7,6},{8,9},{9,8},{10,11... | collective-permute-start | bytes 196616 | tf_op jit(solution)/shard_map/ppermute | solution.py:44
  35.3 1.3 %collective-permute-start.15 = (bf16[1,4,64,128]{3,2,1,0:T(8,128)(2,1)S(1)}, bf16[1,4,64,128]{3,2,1,0:T(8,128)(2,1)S(1)}, u32[]{:S(2)}, u32[]{:S(2)}) collective-permute-start(bf16[1,4,64,128]{3,2,1,0:T(8,128)(2,1)S(1)} %get-tuple-element.84), channel_id=1, source_target_pairs={{0,1},{1,0},{2,3},{3,2},{4,5},{5,4},{6,7},{7,6},{8,9},{9,8},{10,11... | collective-permute-start | bytes 196616 | tf_op jit(solution)/shard_map/ppermute | solution.py:44
  36.6 6.4 %collective-permute-start.17 = (bf16[2,4,64,128]{3,2,1,0:T(8,128)(2,1)S(1)}, bf16[2,4,64,128]{3,2,1,0:T(8,128)(2,1)S(1)}, u32[]{:S(2)}, u32[]{:S(2)}) collective-permute-start(bf16[2,4,64,128]{3,2,1,0:T(8,128)(2,1)S(1)} %get-tuple-element.85), channel_id=1, source_target_pairs={{0,4},{4,0},{8,12},{12,8},{1,5},{5,1},{9,13},{13,9},{2,6},{6,2},{1... | collective-permute-start | bytes 393224 | tf_op jit(solution)/shard_map/ppermute | solution.py:44
  38.6 6.6 %collective-permute-start.18 = (bf16[2,4,64,128]{3,2,1,0:T(8,128)(2,1)S(1)}, bf16[2,4,64,128]{3,2,1,0:T(8,128)(2,1)S(1)}, u32[]{:S(2)}, u32[]{:S(2)}) collective-permute-start(bf16[2,4,64,128]{3,2,1,0:T(8,128)(2,1)S(1)} %residual.2.refs_0_), channel_id=1, source_target_pairs={{0,4},{4,0},{8,12},{12,8},{1,5},{5,1},{9,13},{13,9},{2,6},{6,2},{1... | collective-permute-start | bytes 393224 | tf_op jit(solution)/shard_map/ppermute | solution.py:44
  39.4 6.4 %collective-permute-start.19 = (bf16[2,4,64,128]{3,2,1,0:T(8,128)(2,1)S(1)}, bf16[2,4,64,128]{3,2,1,0:T(8,128)(2,1)S(1)}, u32[]{:S(2)}, u32[]{:S(2)}) collective-permute-start(bf16[2,4,64,128]{3,2,1,0:T(8,128)(2,1)S(1)} %residual.2.refs_0_), channel_id=1, source_target_pairs={{0,1},{1,0},{2,3},{3,2},{4,5},{5,4},{6,7},{7,6},{8,9},{9,8},{10,11... | collective-permute-start | bytes 393224 | tf_op jit(solution)/shard_map/ppermute | solution.py:44
  43.0 8.2 %collective-permute-start.22 = (bf16[2,4,64,128]{3,2,1,0:T(8,128)(2,1)S(1)}, bf16[2,4,64,128]{3,2,1,0:T(8,128)(2,1)S(1)}, u32[]{:S(2)}, u32[]{:S(2)}) collective-permute-start(bf16[2,4,64,128]{3,2,1,0:T(8,128)(2,1)S(1)} %get-tuple-element.90), channel_id=1, source_target_pairs={{0,8},{4,12},{8,0},{12,4},{1,9},{5,13},{9,1},{13,5},{2,10},{6,14},... | collective-permute-start | bytes 393224 | tf_op jit(solution)/shard_map/ppermute | solution.py:44
  45.2 1.3 %collective-permute-start.20 = (bf16[1,4,64,128]{3,2,1,0:T(8,128)(2,1)S(1)}, bf16[1,4,64,128]{3,2,1,0:T(8,128)(2,1)S(1)}, u32[]{:S(2)}, u32[]{:S(2)}) collective-permute-start(bf16[1,4,64,128]{3,2,1,0:T(8,128)(2,1)S(1)} %get-tuple-element.93), channel_id=1, source_target_pairs={{0,1},{1,0},{2,3},{3,2},{4,5},{5,4},{6,7},{7,6},{8,9},{9,8},{10,11... | collective-permute-start | bytes 196616 | tf_op jit(solution)/shard_map/ppermute | solution.py:44
  45.3 1.4 %collective-permute-start.21 = (bf16[1,4,64,128]{3,2,1,0:T(8,128)(2,1)S(1)}, bf16[1,4,64,128]{3,2,1,0:T(8,128)(2,1)S(1)}, u32[]{:S(2)}, u32[]{:S(2)}) collective-permute-start(bf16[1,4,64,128]{3,2,1,0:T(8,128)(2,1)S(1)} %get-tuple-element.94), channel_id=1, source_target_pairs={{0,1},{1,0},{2,3},{3,2},{4,5},{5,4},{6,7},{7,6},{8,9},{9,8},{10,11... | collective-permute-start | bytes 196616 | tf_op jit(solution)/shard_map/ppermute | solution.py:44
  50.2 2.6 %collective-permute-start.24 = (bf16[8,128,128]{2,1,0:T(8,128)(2,1)S(1)}, bf16[8,128,128]{2,1,0:T(8,128)(2,1)S(1)}, u32[]{:S(2)}, u32[]{:S(2)}) collective-permute-start(bf16[8,128,128]{2,1,0:T(8,128)(2,1)S(1)} %get-tuple-element.102), channel_id=1, source_target_pairs={{0,1},{1,0},{2,3},{3,2},{4,5},{5,4},{6,7},{7,6},{8,9},{9,8},{10,11... | collective-permute-start | bytes 786440 | tf_op jit(solution)/shard_map/ppermute | solution.py:44
  50.6 2.2 %collective-permute-start.25 = (bf16[8,128,128]{2,1,0:T(8,128)(2,1)S(1)}, bf16[8,128,128]{2,1,0:T(8,128)(2,1)S(1)}, u32[]{:S(2)}, u32[]{:S(2)}) collective-permute-start(bf16[8,128,128]{2,1,0:T(8,128)(2,1)S(1)} %get-tuple-element.103), channel_id=1, source_target_pairs={{0,1},{1,0},{2,3},{3,2},{4,5},{5,4},{6,7},{7,6},{8,9},{9,8},{10,11... | collective-permute-start | bytes 786440 | tf_op jit(solution)/shard_map/ppermute | solution.py:44
  51.3 5.5 %collective-permute-start.23 = (bf16[2,4,64,128]{3,2,1,0:T(8,128)(2,1)S(1)}, bf16[2,4,64,128]{3,2,1,0:T(8,128)(2,1)S(1)}, u32[]{:S(2)}, u32[]{:S(2)}) collective-permute-start(bf16[2,4,64,128]{3,2,1,0:T(8,128)(2,1)S(1)} %residual.3.refs_1_.refs_0_), channel_id=1, source_target_pairs={{0,4},{4,0},{8,12},{12,8},{1,5},{5,1},{9,13},{13,9},{2,6},{6,2},{1... | collective-permute-start | bytes 393224 | tf_op jit(solution)/shard_map/ppermute | solution.py:44
  52.9 14.8 %collective-permute-start.30 = (bf16[16,128,128]{2,1,0:T(8,128)(2,1)S(1)}, bf16[16,128,128]{2,1,0:T(8,128)(2,1)S(1)}, u32[]{:S(2)}, u32[]{:S(2)}) collective-permute-start(bf16[16,128,128]{2,1,0:T(8,128)(2,1)S(1)} %adjoint_share.2), channel_id=1, source_target_pairs={{0,2},{2,0},{1,3},{3,1},{4,6},{6,4},{5,7},{7,5},{8,10},{10,8},{9,1... | collective-permute-start | bytes 1572872 | tf_op jit(solution)/shard_map/ppermute | solution.py:44
  54.5 13.2 %collective-permute-start.31 = (bf16[16,128,128]{2,1,0:T(8,128)(2,1)S(1)}, bf16[16,128,128]{2,1,0:T(8,128)(2,1)S(1)}, u32[]{:S(2)}, u32[]{:S(2)}) collective-permute-start(bf16[16,128,128]{2,1,0:T(8,128)(2,1)S(1)} %get-tuple-element.109), channel_id=1, source_target_pairs={{0,1},{1,0},{2,3},{3,2},{4,5},{5,4},{6,7},{7,6},{8,9},{9,8},{10,11... | collective-permute-start | bytes 1572872 | tf_op jit(solution)/shard_map/ppermute | solution.py:44
  54.5 3.0 %collective-permute-start.26 = (bf16[2,4,64,128]{3,2,1,0:T(8,128)(2,1)S(1)}, bf16[2,4,64,128]{3,2,1,0:T(8,128)(2,1)S(1)}, u32[]{:S(2)}, u32[]{:S(2)}) collective-permute-start(bf16[2,4,64,128]{3,2,1,0:T(8,128)(2,1)S(1)} %residual.3.refs_1_.refs_0_), channel_id=1, source_target_pairs={{0,1},{1,0},{2,3},{3,2},{4,5},{5,4},{6,7},{7,6},{8,9},{9,8},{10,11... | collective-permute-start | bytes 393224 | tf_op jit(solution)/shard_map/ppermute | solution.py:44
  56.8 1.3 %collective-permute-start.27 = (bf16[2,4,64,128]{3,2,1,0:T(8,128)(2,1)S(1)}, bf16[2,4,64,128]{3,2,1,0:T(8,128)(2,1)S(1)}, u32[]{:S(2)}, u32[]{:S(2)}) collective-permute-start(bf16[2,4,64,128]{3,2,1,0:T(8,128)(2,1)S(1)} %collective-permute-done.23.refs_1_), channel_id=1, source_target_pairs={{0,1},{1,0},{2,3},{3,2},{4,5},{5,4},{6,7},{7,6},{8,9},{9,8},{10,11... | collective-permute-start | bytes 393224 | tf_op jit(solution)/shard_map/ppermute | solution.py:44
  61.1 1.6 %collective-permute-start.28 = (bf16[8,128,128]{2,1,0:T(8,128)(2,1)S(1)}, bf16[8,128,128]{2,1,0:T(8,128)(2,1)S(1)}, u32[]{:S(2)}, u32[]{:S(2)}) collective-permute-start(bf16[8,128,128]{2,1,0:T(8,128)(2,1)S(1)} %get-tuple-element.106), channel_id=1, source_target_pairs={{0,1},{1,0},{2,3},{3,2},{4,5},{5,4},{6,7},{7,6},{8,9},{9,8},{10,11... | collective-permute-start | bytes 786440 | tf_op jit(solution)/shard_map/ppermute | solution.py:44
  61.3 1.8 %collective-permute-start.29 = (bf16[8,128,128]{2,1,0:T(8,128)(2,1)S(1)}, bf16[8,128,128]{2,1,0:T(8,128)(2,1)S(1)}, u32[]{:S(2)}, u32[]{:S(2)}) collective-permute-start(bf16[8,128,128]{2,1,0:T(8,128)(2,1)S(1)} %get-tuple-element.107), channel_id=1, source_target_pairs={{0,1},{1,0},{2,3},{3,2},{4,5},{5,4},{6,7},{7,6},{8,9},{9,8},{10,11... | collective-permute-start | bytes 786440 | tf_op jit(solution)/shard_map/ppermute | solution.py:44
  63.2 14.9 %collective-permute-start.33 = (bf16[16,128,128]{2,1,0:T(8,128)(2,1)S(1)}, bf16[16,128,128]{2,1,0:T(8,128)(2,1)S(1)}, u32[]{:S(2)}, u32[]{:S(2)}) collective-permute-start(bf16[16,128,128]{2,1,0:T(8,128)(2,1)S(1)} %adjoint_share.3), channel_id=1, source_target_pairs={{0,2},{2,0},{1,3},{3,1},{4,6},{6,4},{5,7},{7,5},{8,10},{10,8},{9,1... | collective-permute-start | bytes 1572872 | tf_op jit(solution)/shard_map/ppermute | solution.py:44
  64.8 3.1 %collective-permute-start.32 = (bf16[16,128,128]{2,1,0:T(8,128)(2,1)S(1)}, bf16[16,128,128]{2,1,0:T(8,128)(2,1)S(1)}, u32[]{:S(2)}, u32[]{:S(2)}) collective-permute-start(bf16[16,128,128]{2,1,0:T(8,128)(2,1)S(1)} %get-tuple-element.113), channel_id=1, source_target_pairs={{0,1},{1,0},{2,3},{3,2},{4,5},{5,4},{6,7},{7,6},{8,9},{9,8},{10,11... | collective-permute-start | bytes 1572872 | tf_op jit(solution)/shard_map/ppermute | solution.py:44

commit v7 on v6

--- a/solution.py
+++ b/solution.py
@@ -110,6 +110,23 @@
     total = jnp.concatenate([other[...] for other in others], 0).astype(F32) + mine[...]
     keep[...] = total[:n]
     send[...] = total[n:].astype(BF16)
+
+
+def sums_kernel(mine, *refs):
+    others, send = refs[:-1], refs[-1]
+    n = send.shape[0]
+    total = jnp.concatenate([other[...] for other in others], 0).astype(F32) + mine[n:]
+    send[...] = total.astype(BF16)
+
+
+def stay_kernel(mine, *refs):
+    *others, arrived, keep, send = refs
+    n = keep.shape[0]
+    total = jnp.concatenate([other[...] for other in others], 0).astype(F32) + mine[:n]
+    total = total + arrived[...].astype(F32)
+    keep[...] = total
+    for e in range(n):
+        send[e] = total[n - 1 - e].astype(BF16)
 
 
 def mirror_kernel(mine, *refs):
@@ -442,7 +459,7 @@
         )
         return [own[0], *keeps], [own[1:]] + [sends[d * parts : (d + 1) * parts] for d in range(rs - 1)]
 
-    halved, mirrored, residuals, sent, totals, joined = [], [], [], [], [], []
+    mirrored, residuals, sent, totals, joined = [], [], [], [], []
 
     def front(c):
         earlier = [(mirrored[-1][1],)] if c else [(second, *nears), (second, data[1])]
@@ -468,17 +485,25 @@
             mine = [slot[1:] or slot for slot in mine]
         keep, *sends = forward(c, mine, heads)
         others = [swap("help", 1, send) for send in sends]
-        for d in near:
+        kernel, stay = mirror_kernel, []
+        if len(near) == 1:
+            kernel, n = stay_kernel, len(others) // 2
             shape = (keep.shape[0] // 2, rows, span, width)
-            keep, send = call(
-                halve_kernel, "halve", [(shape, F32), (shape, BF16)], [keep, *others], cost=1
-            )
-            others = [swap("col", d, send)]
-        halved.append(send)
+            stay, others = others[:n], others[n:]
+            send = call(sums_kernel, "halve", [(shape, BF16)], [keep, *others], cost=1)[0]
+            others = [swap("col", near[0], send)]
+        else:
+            for d in near:
+                shape = (keep.shape[0] // 2, rows, span, width)
+                keep, send = call(halve_kernel, "halve", [(shape, F32), (shape, BF16)], [keep, *others], cost=1)
+                others = [swap("col", d, send)]
         if c:
             residual_of(c - 1, send)
             keep = after(keep, *residuals[c - 1])
-        mirrored.append(call(mirror_kernel, "mirror", [(shape, F32), (shape, BF16)], [keep, *others]))
+        shape = (2, rows, span, width)
+        mirrored.append(
+            call(kernel, "mirror", [(shape, F32), (shape, BF16)], [keep, *stay, *others])
+        )
 
     def residual_of(c, *earlier):
         keep, send = mirrored[c]

time: 79.6 us -> 78.6 us (0.987)
  starting transfers between devices: 26.6 us -> 25.7 us
    ppermute x34, starting transfers between devices: 26.6 us -> 25.7 us  [swap(): return lax.ppermute(value, axis_name, [(i, i ^ step) for i in range(size)])]
  transfers between devices with their start and end apart: 34 -> 34, of which waited for: 22 -> 21; matrix products, arithmetic and copies ran while one was open for 0% -> 0% of each run, Pallas kernels for 25% -> 25%
where the time goes in v7:
time: 78.6 us; the launch traced here: 78.4 us
  waiting for transfers between devices  29.1 us (37%)
  starting transfers between devices  25.7 us (33%)
  Pallas kernels  22.3 us (28%)
  between operations  1.07 us (1%)
    ppermute x34, waiting for transfers between devices, swap(): return lax.ppermute(value, axis_name, [(i, i ^ step) for i in range(size)])  29.1 us
    ppermute x34, starting transfers between devices, swap(): return lax.ppermute(value, axis_name, [(i, i ^ step) for i in range(size)])  25.7 us
    pallas_call x25, Pallas kernels, call(): pl.pallas_call(kernel, out_shape=[jax.ShapeDtypeStruct(shape, kind) for s...  22.3 us
  transfers between devices with their start and end apart: 34, of which 21 were waited for; matrix products, arithmetic and copies ran while one was open for 0% of the time, Pallas kernels for 25%

profile of v7, /device:TPU:0, one launch (start us, length us, event | category | flops | bytes accessed | tf_op | source)
XLA Modules:
  0.0 78.4 jit_solution(3551614867008813067)
XLA Ops:
  0.6 1.3 %first_waves.1 = (bf16[10,128,128]{2,1,0:T(8,128)(2,1)S(1)}, bf16[3,4,64,128]{3,2,1,0:T(8,128)(2,1)S(1)}) custom-call(bf16[2,16,128,128]{3,2,1,0:T(8,128)(2,1)} %source.2, bf16[2,4,64,128]{3,2,1,0:T(8,128)(2,1)} %observed.1, bf16[4,64,128]{2,1,0:T(8,128)(2,1)} %amplitude.1), custom_call_target="tpu_custom_call" | custom-call | flops 1000000 | bytes 10000 | tf_op jit(solution)/shard_map/first_waves/pallas_call | solution.py:26
  1.9 3.0 %collective-permute-start.5 = (bf16[10,128,128]{2,1,0:T(8,128)(2,1)S(1)}, bf16[10,128,128]{2,1,0:T(8,128)(2,1)S(1)}, u32[]{:S(2)}, u32[]{:S(2)}) collective-permute-start(bf16[10,128,128]{2,1,0:T(8,128)(2,1)S(1)} %get-tuple-element.55), channel_id=1, source_target_pairs={{0,2},{2,0},{1,3},{3,1},{4,6},{6,4},{5,7},{7,5},{8,10},{10,8},{9,1... | collective-permute-start | bytes 983048 | tf_op jit(solution)/shard_map/ppermute | solution.py:44
  5.0 2.7 %collective-permute-start.1 = (bf16[3,4,64,128]{3,2,1,0:T(8,128)(2,1)S(1)}, bf16[3,4,64,128]{3,2,1,0:T(8,128)(2,1)S(1)}, u32[]{:S(2)}, u32[]{:S(2)}) collective-permute-start(bf16[3,4,64,128]{3,2,1,0:T(8,128)(2,1)S(1)} %relay_data.1.refs_0_), channel_id=1, source_target_pairs={{0,8},{4,12},{8,0},{12,4},{1,9},{5,13},{9,1},{13,5},{2,10},{6,14},... | collective-permute-start | bytes 589832 | tf_op jit(solution)/shard_map/ppermute | solution.py:44
  7.6 0.4 other_waves.1
  8.1 0.5 collective-permute-start.3
  8.6 0.5 collective-permute-start
  9.2 2.2 %load_factors.1 = (bf16[16,8,40,512]{3,2,1,0:T(8,128)(2,1)S(1)}, bf16[2,4,16,40,512]{4,3,2,1,0:T(8,128)(2,1)S(1)}) custom-call(bf16[2,4,16,40,512]{4,3,2,1,0:T(8,128)(2,1)S(1)} %bitcast.15, bf16[2,4,16,40,512]{4,3,2,1,0:T(8,128)(2,1)S(1)} %bitcast.17), custom_call_target="tpu_custom_call" | custom-call | flops 10000000000 | bytes 10000 | tf_op jit(solution)/shard_map/load_factors/pallas_call | solution.py:26
  11.4 1.7 %near_products.1 = (f32[4,640,128]{2,1,0:T(8,128)S(1)}, f32[4,640,128]{2,1,0:T(8,128)S(1)}) custom-call(bf16[16,320,512]{2,1,0:T(8,128)(2,1)S(1)} %bitcast.2, bf16[16,128,128]{2,1,0:T(8,128)(2,1)S(1)} %get-tuple-element.62.refs_0_, bf16[16,128,128]{2,1,0:T(8,128)(2,1)S(1)} %collective-permute-done.3.refs_1_, ...), custom_call_target="tpu_custom_call" | custom-call | flops 1 | bytes 10000 | tf_op jit(solution)/shard_map/near_products/pallas_call | solution.py:26
  13.1 0.4 collective-permute-done.5.refs_0_
  13.4 2.1 %collective-permute-start.10 = (bf16[16,128,128]{2,1,0:T(8,128)(2,1)S(1)}, bf16[16,128,128]{2,1,0:T(8,128)(2,1)S(1)}, u32[]{:S(2)}, u32[]{:S(2)}) collective-permute-start(bf16[16,128,128]{2,1,0:T(8,128)(2,1)S(1)} %get-tuple-element.63.refs_2_), channel_id=1, source_target_pairs={{0,2},{2,0},{1,3},{3,1},{4,6},{6,4},{5,7},{7,5},{8,10},{10,8},{9,1... | collective-permute-start | bytes 1572872 | tf_op jit(solution)/shard_map/ppermute | solution.py:44
  15.5 1.3 %collective-permute-done.refs_0_ = bf16[6,128,128]{2,1,0:T(8,128)(2,1)S(1)} collective-permute-done((bf16[6,128,128]{2,1,0:T(8,128)(2,1)S(1)}, bf16[6,128,128]{2,1,0:T(8,128)(2,1)S(1)}, u32[]{:S(2)}, u32[]{:S(2)}) %collective-permute-start) | collective-permute-done | bytes 196640 | tf_op jit(solution)/shard_map/ppermute | solution.py:44
  16.9 1.2 %first_coefficients.1.refs_5_ = f32[4,400,128]{2,1,0:T(8,128)S(1)} custom-call(s32[4,16]{1,0:T(4,128)S(1)} %copy-done.1, bf16[10,128,128]{2,1,0:T(8,128)(2,1)S(1)} %collective-permute-done.5.refs_0_, bf16[10,128,128]{2,1,0:T(8,128)(2,1)S(1)} %collective-permute-done.6.refs_1_, bf16[16,320,512]{2,1,0:T(8,128)(2,1)S(1)} %bitcast.3, ...), custom_call_target="tpu_custom_call" | custom-call | flops 1 | bytes 10000 | tf_op jit(solution)/shard_map/first_coefficients/pallas_call | solution.py:26
  18.3 2.7 %forward_product.2 = (f32[4,4,64,128]{3,2,1,0:T(8,128)S(1)}, bf16[2,4,64,128]{3,2,1,0:T(8,128)(2,1)S(1)}, bf16[2,4,64,128]{3,2,1,0:T(8,128)(2,1)S(1)}) custom-call(s32[4,16]{1,0:T(4,128)S(1)} %copy-done.1, bf16[6,128,128]{2,1,0:T(8,128)(2,1)S(1)} %collective-permute-done.refs_0_, bf16[6,128,128]{2,1,0:T(8,128)(2,1)S(1)} %collective-permute-done.2.refs_1_, ...), custom_call_target="tpu_custom_call" | custom-call | flops 1 | bytes 10000 | tf_op jit(solution)/shard_map/forward_product/pallas_call | solution.py:26
  21.0 0.4 collective-permute-start.8
  21.6 0.8 %collective-permute-done.8.refs_0_ = bf16[2,4,64,128]{3,2,1,0:T(8,128)(2,1)S(1)} collective-permute-done((bf16[2,4,64,128]{3,2,1,0:T(8,128)(2,1)S(1)}, bf16[2,4,64,128]{3,2,1,0:T(8,128)(2,1)S(1)}, u32[]{:S(2)}, u32[]{:S(2)}) %collective-permute-start.8) | collective-permute-done | bytes 131104 | tf_op jit(solution)/shard_map/ppermute | solution.py:44
  22.5 1.9 %collective-permute-start.9 = (bf16[2,4,64,128]{3,2,1,0:T(8,128)(2,1)S(1)}, bf16[2,4,64,128]{3,2,1,0:T(8,128)(2,1)S(1)}, u32[]{:S(2)}, u32[]{:S(2)}) collective-permute-start(bf16[2,4,64,128]{3,2,1,0:T(8,128)(2,1)S(1)} %halve.2), channel_id=1, source_target_pairs={{0,4},{4,0},{8,12},{12,8},{1,5},{5,1},{9,13},{13,9},{2,6},{6,2},{1... | collective-permute-start | bytes 393224 | tf_op jit(solution)/shard_map/ppermute | solution.py:44
  24.3 4.0 %collective-permute-done.9.refs_1_ = bf16[2,4,64,128]{3,2,1,0:T(8,128)(2,1)S(1)} collective-permute-done((bf16[2,4,64,128]{3,2,1,0:T(8,128)(2,1)S(1)}, bf16[2,4,64,128]{3,2,1,0:T(8,128)(2,1)S(1)}, u32[]{:S(2)}, u32[]{:S(2)}) %collective-permute-start.9) | collective-permute-done | bytes 131104 | tf_op jit(solution)/shard_map/ppermute | solution.py:44
  28.5 2.8 %collective-permute-start.14 = (bf16[2,4,64,128]{3,2,1,0:T(8,128)(2,1)S(1)}, bf16[2,4,64,128]{3,2,1,0:T(8,128)(2,1)S(1)}, u32[]{:S(2)}, u32[]{:S(2)}) collective-permute-start(bf16[2,4,64,128]{3,2,1,0:T(8,128)(2,1)S(1)} %get-tuple-element.71), channel_id=1, source_target_pairs={{0,8},{4,12},{8,0},{12,4},{1,9},{5,13},{9,1},{13,5},{2,10},{6,14},... | collective-permute-start | bytes 393224 | tf_op jit(solution)/shard_map/ppermute | solution.py:44
  31.3 3.0 %forward_product.3 = (f32[4,4,64,128]{3,2,1,0:T(8,128)S(1)}, bf16[1,4,64,128]{3,2,1,0:T(8,128)(2,1)S(1)}, bf16[1,4,64,128]{3,2,1,0:T(8,128)(2,1)S(1)}, bf16[1,4,...) custom-call(s32[4,16]{1,0:T(4,128)S(1)} %copy-done.1, bf16[16,128,128]{2,1,0:T(8,128)(2,1)S(1)} %collective-permute-done.10.refs_0_, ...), custom_call_target="tpu_custom_call" | custom-call | flops 10000000000 | bytes 10000 | tf_op jit(solution)/shard_map/forward_product/pallas_call | solution.py:26
  34.9 0.7 collective-permute-done.12.refs_0_
  35.8 1.6 %collective-permute-start.17 = (bf16[2,4,64,128]{3,2,1,0:T(8,128)(2,1)S(1)}, bf16[2,4,64,128]{3,2,1,0:T(8,128)(2,1)S(1)}, u32[]{:S(2)}, u32[]{:S(2)}) collective-permute-start(bf16[2,4,64,128]{3,2,1,0:T(8,128)(2,1)S(1)} %halve.3), channel_id=1, source_target_pairs={{0,4},{4,0},{8,12},{12,8},{1,5},{5,1},{9,13},{13,9},{2,6},{6,2},{1... | collective-permute-start | bytes 393224 | tf_op jit(solution)/shard_map/ppermute | solution.py:44
  37.5 0.7 collective-permute-done.14.other
  38.3 0.8 %collective-permute-start.18 = (bf16[2,4,64,128]{3,2,1,0:T(8,128)(2,1)S(1)}, bf16[2,4,64,128]{3,2,1,0:T(8,128)(2,1)S(1)}, u32[]{:S(2)}, u32[]{:S(2)}) collective-permute-start(bf16[2,4,64,128]{3,2,1,0:T(8,128)(2,1)S(1)} %residual.2.refs_0_), channel_id=1, source_target_pairs={{0,4},{4,0},{8,12},{12,8},{1,5},{5,1},{9,13},{13,9},{2,6},{6,2},{1... | collective-permute-start | bytes 393224 | tf_op jit(solution)/shard_map/ppermute | solution.py:44
  39.2 0.5 collective-permute-start.16
  39.7 0.7 collective-permute-done.15.refs_0_
  40.6 1.6 %collective-permute-done.17.refs_2_ = bf16[2,4,64,128]{3,2,1,0:T(8,128)(2,1)S(1)} collective-permute-done((bf16[2,4,64,128]{3,2,1,0:T(8,128)(2,1)S(1)}, bf16[2,4,64,128]{3,2,1,0:T(8,128)(2,1)S(1)}, u32[]{:S(2)}, u32[]{:S(2)}) %collective-permute-start.17) | collective-permute-done | bytes 131104 | tf_op jit(solution)/shard_map/ppermute | solution.py:44
  42.3 1.8 %collective-permute-start.22 = (bf16[2,4,64,128]{3,2,1,0:T(8,128)(2,1)S(1)}, bf16[2,4,64,128]{3,2,1,0:T(8,128)(2,1)S(1)}, u32[]{:S(2)}, u32[]{:S(2)}) collective-permute-start(bf16[2,4,64,128]{3,2,1,0:T(8,128)(2,1)S(1)} %get-tuple-element.82), channel_id=1, source_target_pairs={{0,8},{4,12},{8,0},{12,4},{1,9},{5,13},{9,1},{13,5},{2,10},{6,14},... | collective-permute-start | bytes 393224 | tf_op jit(solution)/shard_map/ppermute | solution.py:44
  44.1 0.4 collective-permute-done.18.source.refs_1_
  44.5 0.5 collective-permute-start.21
  45.0 0.7 collective-permute-done.20.refs_3_
  45.9 2.7 %adjoint_product.2 = (bf16[16,160,128]{2,1,0:T(8,128)(2,1)S(1)}, f32[16,128,128]{2,1,0:T(8,128)S(1)}, bf16[8,128,128]{2,1,0:T(8,128)(2,1)S(1)}, bf16[8,128,128]{2,1,0:T(8,128)(2,1)S(1)}) custom-call(s32[4,16]{1,0:T(4,128)S(1)} %copy-done.1, bf16[2,4,64,128]{3,2,1,0:T(8,128)(2,1)S(1)} %residual.2.refs_0_, ...), custom_call_target="tpu_custom_call" | custom-call | flops 1 | bytes 10000 | tf_op jit(solution)/shard_map/adjoint_product/pallas_call | solution.py:26
  48.7 0.8 own_quarter.2
  49.5 0.4 collective-permute-start.24
  50.0 0.9 %collective-permute-done.22.other = bf16[2,4,64,128]{3,2,1,0:T(8,128)(2,1)S(1)} collective-permute-done((bf16[2,4,64,128]{3,2,1,0:T(8,128)(2,1)S(1)}, bf16[2,4,64,128]{3,2,1,0:T(8,128)(2,1)S(1)}, u32[]{:S(2)}, u32[]{:S(2)}) %collective-permute-start.22) | collective-permute-done | bytes 131104 | tf_op jit(solution)/shard_map/ppermute | solution.py:44
  51.1 0.8 %collective-permute-start.23 = (bf16[2,4,64,128]{3,2,1,0:T(8,128)(2,1)S(1)}, bf16[2,4,64,128]{3,2,1,0:T(8,128)(2,1)S(1)}, u32[]{:S(2)}, u32[]{:S(2)}) collective-permute-start(bf16[2,4,64,128]{3,2,1,0:T(8,128)(2,1)S(1)} %residual.3.refs_1_.refs_0_), channel_id=1, source_target_pairs={{0,4},{4,0},{8,12},{12,8},{1,5},{5,1},{9,13},{13,9},{2,6},{6,2},{1... | collective-permute-start | bytes 393224 | tf_op jit(solution)/shard_map/ppermute | solution.py:44
  51.9 1.6 %collective-permute-start.30 = (bf16[16,128,128]{2,1,0:T(8,128)(2,1)S(1)}, bf16[16,128,128]{2,1,0:T(8,128)(2,1)S(1)}, u32[]{:S(2)}, u32[]{:S(2)}) collective-permute-start(bf16[16,128,128]{2,1,0:T(8,128)(2,1)S(1)} %adjoint_share.2), channel_id=1, source_target_pairs={{0,2},{2,0},{1,3},{3,1},{4,6},{6,4},{5,7},{7,5},{8,10},{10,8},{9,1... | collective-permute-start | bytes 1572872 | tf_op jit(solution)/shard_map/ppermute | solution.py:44
  53.6 0.5 collective-permute-start.26
  54.1 2.0 %collective-permute-done.23.refs_1_ = bf16[2,4,64,128]{3,2,1,0:T(8,128)(2,1)S(1)} collective-permute-done((bf16[2,4,64,128]{3,2,1,0:T(8,128)(2,1)S(1)}, bf16[2,4,64,128]{3,2,1,0:T(8,128)(2,1)S(1)}, u32[]{:S(2)}, u32[]{:S(2)}) %collective-permute-start.23) | collective-permute-done | bytes 131104 | tf_op jit(solution)/shard_map/ppermute | solution.py:44
  56.1 0.8 join.1
  56.8 0.6 collective-permute-done.27.refs_3_
  57.4 3.0 %adjoint_product.3 = (bf16[16,160,128]{2,1,0:T(8,128)(2,1)S(1)}, f32[16,128,128]{2,1,0:T(8,128)S(1)}, bf16[8,128,128]{2,1,0:T(8,128)(2,1)S(1)}, bf16[8,128,128]{2,1,0:T(8,128)(2,1)S(1)}) custom-call(s32[4,16]{1,0:T(4,128)S(1)} %copy-done.1, bf16[2,4,64,128]{3,2,1,0:T(8,128)(2,1)S(1)} %residual.3.refs_1_.refs_0_, ...), custom_call_target="tpu_custom_call" | custom-call | flops 1 | bytes 10000 | tf_op jit(solution)/shard_map/adjoint_product/pallas_call | solution.py:26
  60.6 0.4 collective-permute-start.29
  61.0 0.8 own_quarter.3
  62.0 0.4 collective-permute-done.29.refs_1_
  62.5 1.6 %collective-permute-start.33 = (bf16[16,128,128]{2,1,0:T(8,128)(2,1)S(1)}, bf16[16,128,128]{2,1,0:T(8,128)(2,1)S(1)}, u32[]{:S(2)}, u32[]{:S(2)}) collective-permute-start(bf16[16,128,128]{2,1,0:T(8,128)(2,1)S(1)} %adjoint_share.3), channel_id=1, source_target_pairs={{0,2},{2,0},{1,3},{3,1},{4,6},{6,4},{5,7},{7,5},{8,10},{10,8},{9,1... | collective-permute-start | bytes 1572872 | tf_op jit(solution)/shard_map/ppermute | solution.py:44
  64.0 2.4 %collective-permute-done.30.refs_0_ = bf16[16,128,128]{2,1,0:T(8,128)(2,1)S(1)} collective-permute-done((bf16[16,128,128]{2,1,0:T(8,128)(2,1)S(1)}, bf16[16,128,128]{2,1,0:T(8,128)(2,1)S(1)}, u32[]{:S(2)}, u32[]{:S(2)}) %collective-permute-start.30) | collective-permute-done | bytes 524320 | tf_op jit(solution)/shard_map/ppermute | solution.py:44
  66.7 10.5 %collective-permute-done.33.refs_1_ = bf16[16,128,128]{2,1,0:T(8,128)(2,1)S(1)} collective-permute-done((bf16[16,128,128]{2,1,0:T(8,128)(2,1)S(1)}, bf16[16,128,128]{2,1,0:T(8,128)(2,1)S(1)}, u32[]{:S(2)}, u32[]{:S(2)}) %collective-permute-start.33) | collective-permute-done | bytes 524320 | tf_op jit(solution)/shard_map/ppermute | solution.py:44
  77.1 1.1 %adjoint_sum.1 = bf16[2,16,128,128]{3,2,1,0:T(8,128)(2,1)} custom-call(f32[16,128,128]{2,1,0:T(8,128)S(1)} %total.3.done, f32[16,128,128]{2,1,0:T(8,128)S(1)} %get-tuple-element.103.mine, bf16[16,128,128]{2,1,0:T(8,128)(2,1)S(1)} %collective-permute-done.32.refs_0_, bf16[16,128,128]{2,1,0:T(8,128)(2,1)S(1)} %collective-permute-done.33.refs_1_), custom_call_target="tpu_custom_call" | custom-call | flops 1000000 | bytes 10000 | tf_op jit(solution)/shard_map/adjoint_sum/pallas_call | solution.py:26
  (59 shorter events, 3.2 us)
Async XLA Ops:
  1.9 11.5 %collective-permute-start.5 = (bf16[10,128,128]{2,1,0:T(8,128)(2,1)S(1)}, bf16[10,128,128]{2,1,0:T(8,128)(2,1)S(1)}, u32[]{:S(2)}, u32[]{:S(2)}) collective-permute-start(bf16[10,128,128]{2,1,0:T(8,128)(2,1)S(1)} %get-tuple-element.55), channel_id=1, source_target_pairs={{0,2},{2,0},{1,3},{3,1},{4,6},{6,4},{5,7},{7,5},{8,10},{10,8},{9,1... | collective-permute-start | bytes 983048 | tf_op jit(solution)/shard_map/ppermute | solution.py:44
  4.9 2.7 %copy-start = (bf16[2,16,128,128]{3,2,1,0:T(8,128)(2,1)S(1)}, bf16[2,16,128,128]{3,2,1,0:T(8,128)(2,1)}, u32[]{:S(2)}) copy-start(bf16[2,16,128,128]{3,2,1,0:T(8,128)(2,1)} %source.2) | copy-start | bytes 3145732
  4.9 4.2 %slice-start = ((s8[5242880]{0:T(1024)(128)(4,1)}), s8[4194304]{0:T(1024)(128)(4,1)S(1)}, s32[]{:S(2)}) async-start(s8[5242880]{0:T(1024)(128)(4,1)} %bitcast.14), calls=%async_computation | async-start | bytes 8388608
  4.9 4.2 %slice-start.2 = ((s8[5242880]{0:T(1024)(128)(4,1)}), s8[4194304]{0:T(1024)(128)(4,1)S(1)}, s32[]{:S(2)}) async-start(s8[5242880]{0:T(1024)(128)(4,1)} %bitcast.16), calls=%async_computation.2 | async-start | bytes 8388608
  4.9 4.2 %slice-start.1 = ((s8[5242880]{0:T(1024)(128)(4,1)}), s8[1048576]{0:T(1024)(128)(4,1)S(1)}, s32[]{:S(2)}) async-start(s8[5242880]{0:T(1024)(128)(4,1)} %bitcast.14), calls=%async_computation.1 | async-start | bytes 2097152
  4.9 4.3 %slice-start.3 = ((s8[5242880]{0:T(1024)(128)(4,1)}), s8[1048576]{0:T(1024)(128)(4,1)S(1)}, s32[]{:S(2)}) async-start(s8[5242880]{0:T(1024)(128)(4,1)} %bitcast.16), calls=%async_computation.3 | async-start | bytes 2097152
  5.0 11.9 %collective-permute-start.1 = (bf16[3,4,64,128]{3,2,1,0:T(8,128)(2,1)S(1)}, bf16[3,4,64,128]{3,2,1,0:T(8,128)(2,1)S(1)}, u32[]{:S(2)}, u32[]{:S(2)}) collective-permute-start(bf16[3,4,64,128]{3,2,1,0:T(8,128)(2,1)S(1)} %relay_data.1.refs_0_), channel_id=1, source_target_pairs={{0,8},{4,12},{8,0},{12,4},{1,9},{5,13},{9,1},{13,5},{2,10},{6,14},... | collective-permute-start | bytes 589832 | tf_op jit(solution)/shard_map/ppermute | solution.py:44
  8.0 3.4 %collective-permute-start.4 = (bf16[16,128,128]{2,1,0:T(8,128)(2,1)S(1)}, bf16[16,128,128]{2,1,0:T(8,128)(2,1)S(1)}, u32[]{:S(2)}, u32[]{:S(2)}) collective-permute-start(bf16[16,128,128]{2,1,0:T(8,128)(2,1)S(1)} %get-tuple-element.63.refs_2_), channel_id=1, source_target_pairs={{0,1},{1,0},{2,3},{3,2},{4,5},{5,4},{6,7},{7,6},{8,9},{9,8},{10,11... | collective-permute-start | bytes 1572872 | tf_op jit(solution)/shard_map/ppermute | solution.py:44
  8.1 3.4 %collective-permute-start.3 = (bf16[16,128,128]{2,1,0:T(8,128)(2,1)S(1)}, bf16[16,128,128]{2,1,0:T(8,128)(2,1)S(1)}, u32[]{:S(2)}, u32[]{:S(2)}) collective-permute-start(bf16[16,128,128]{2,1,0:T(8,128)(2,1)S(1)} %get-tuple-element.62.refs_0_), channel_id=1, source_target_pairs={{0,1},{1,0},{2,3},{3,2},{4,5},{5,4},{6,7},{7,6},{8,9},{9,8},{10,11... | collective-permute-start | bytes 1572872 | tf_op jit(solution)/shard_map/ppermute | solution.py:44
  8.6 8.3 %collective-permute-start = (bf16[6,128,128]{2,1,0:T(8,128)(2,1)S(1)}, bf16[6,128,128]{2,1,0:T(8,128)(2,1)S(1)}, u32[]{:S(2)}, u32[]{:S(2)}) collective-permute-start(bf16[6,128,128]{2,1,0:T(8,128)(2,1)S(1)} %get-tuple-element.58), channel_id=1, source_target_pairs={{0,2},{2,0},{1,3},{3,1},{4,6},{6,4},{5,7},{7,5},{8,10},{10,8},{9,1... | collective-permute-start | bytes 589832 | tf_op jit(solution)/shard_map/ppermute | solution.py:44
  11.4 5.5 %copy-start.1 = (s32[4,16]{1,0:T(4,128)S(1)}, s32[4,16]{1,0:T(4,128)}, u32[]{:S(2)}) copy-start(s32[4,16]{1,0:T(4,128)} %ranks.9) | copy-start | bytes 772
  13.4 3.4 %collective-permute-start.6 = (bf16[10,128,128]{2,1,0:T(8,128)(2,1)S(1)}, bf16[10,128,128]{2,1,0:T(8,128)(2,1)S(1)}, u32[]{:S(2)}, u32[]{:S(2)}) collective-permute-start(bf16[10,128,128]{2,1,0:T(8,128)(2,1)S(1)} %collective-permute-done.5.refs_0_), channel_id=1, source_target_pairs={{0,1},{1,0},{2,3},{3,2},{4,5},{5,4},{6,7},{7,6},{8,9},{9,8},{10,11... | collective-permute-start | bytes 983048 | tf_op jit(solution)/shard_map/ppermute | solution.py:44
  13.4 14.9 %collective-permute-start.10 = (bf16[16,128,128]{2,1,0:T(8,128)(2,1)S(1)}, bf16[16,128,128]{2,1,0:T(8,128)(2,1)S(1)}, u32[]{:S(2)}, u32[]{:S(2)}) collective-permute-start(bf16[16,128,128]{2,1,0:T(8,128)(2,1)S(1)} %get-tuple-element.63.refs_2_), channel_id=1, source_target_pairs={{0,2},{2,0},{1,3},{3,1},{4,6},{6,4},{5,7},{7,5},{8,10},{10,8},{9,1... | collective-permute-start | bytes 1572872 | tf_op jit(solution)/shard_map/ppermute | solution.py:44
  16.8 1.4 %collective-permute-start.2 = (bf16[6,128,128]{2,1,0:T(8,128)(2,1)S(1)}, bf16[6,128,128]{2,1,0:T(8,128)(2,1)S(1)}, u32[]{:S(2)}, u32[]{:S(2)}) collective-permute-start(bf16[6,128,128]{2,1,0:T(8,128)(2,1)S(1)} %collective-permute-done.refs_0_), channel_id=1, source_target_pairs={{0,1},{1,0},{2,3},{3,2},{4,5},{5,4},{6,7},{7,6},{8,9},{9,8},{10,11... | collective-permute-start | bytes 589832 | tf_op jit(solution)/shard_map/ppermute | solution.py:44
  21.0 1.4 %collective-permute-start.8 = (bf16[2,4,64,128]{3,2,1,0:T(8,128)(2,1)S(1)}, bf16[2,4,64,128]{3,2,1,0:T(8,128)(2,1)S(1)}, u32[]{:S(2)}, u32[]{:S(2)}) collective-permute-start(bf16[2,4,64,128]{3,2,1,0:T(8,128)(2,1)S(1)} %get-tuple-element.69), channel_id=1, source_target_pairs={{0,1},{1,0},{2,3},{3,2},{4,5},{5,4},{6,7},{7,6},{8,9},{9,8},{10,11... | collective-permute-start | bytes 393224 | tf_op jit(solution)/shard_map/ppermute | solution.py:44
  21.4 2.9 %collective-permute-start.7 = (bf16[2,4,64,128]{3,2,1,0:T(8,128)(2,1)S(1)}, bf16[2,4,64,128]{3,2,1,0:T(8,128)(2,1)S(1)}, u32[]{:S(2)}, u32[]{:S(2)}) collective-permute-start(bf16[2,4,64,128]{3,2,1,0:T(8,128)(2,1)S(1)} %get-tuple-element.68), channel_id=1, source_target_pairs={{0,1},{1,0},{2,3},{3,2},{4,5},{5,4},{6,7},{7,6},{8,9},{9,8},{10,11... | collective-permute-start | bytes 393224 | tf_op jit(solution)/shard_map/ppermute | solution.py:44
  22.5 5.9 %collective-permute-start.9 = (bf16[2,4,64,128]{3,2,1,0:T(8,128)(2,1)S(1)}, bf16[2,4,64,128]{3,2,1,0:T(8,128)(2,1)S(1)}, u32[]{:S(2)}, u32[]{:S(2)}) collective-permute-start(bf16[2,4,64,128]{3,2,1,0:T(8,128)(2,1)S(1)} %halve.2), channel_id=1, source_target_pairs={{0,4},{4,0},{8,12},{12,8},{1,5},{5,1},{9,13},{13,9},{2,6},{6,2},{1... | collective-permute-start | bytes 393224 | tf_op jit(solution)/shard_map/ppermute | solution.py:44
  28.4 2.9 %collective-permute-start.11 = (bf16[16,128,128]{2,1,0:T(8,128)(2,1)S(1)}, bf16[16,128,128]{2,1,0:T(8,128)(2,1)S(1)}, u32[]{:S(2)}, u32[]{:S(2)}) collective-permute-start(bf16[16,128,128]{2,1,0:T(8,128)(2,1)S(1)} %collective-permute-done.10.refs_0_), channel_id=1, source_target_pairs={{0,1},{1,0},{2,3},{3,2},{4,5},{5,4},{6,7},{7,6},{8,9},{9,8},{10,11... | collective-permute-start | bytes 1572872 | tf_op jit(solution)/shard_map/ppermute | solution.py:44
  28.5 9.7 %collective-permute-start.14 = (bf16[2,4,64,128]{3,2,1,0:T(8,128)(2,1)S(1)}, bf16[2,4,64,128]{3,2,1,0:T(8,128)(2,1)S(1)}, u32[]{:S(2)}, u32[]{:S(2)}) collective-permute-start(bf16[2,4,64,128]{3,2,1,0:T(8,128)(2,1)S(1)} %get-tuple-element.71), channel_id=1, source_target_pairs={{0,8},{4,12},{8,0},{12,4},{1,9},{5,13},{9,1},{13,5},{2,10},{6,14},... | collective-permute-start | bytes 393224 | tf_op jit(solution)/shard_map/ppermute | solution.py:44
  34.3 1.3 %collective-permute-start.12 = (bf16[1,4,64,128]{3,2,1,0:T(8,128)(2,1)S(1)}, bf16[1,4,64,128]{3,2,1,0:T(8,128)(2,1)S(1)}, u32[]{:S(2)}, u32[]{:S(2)}) collective-permute-start(bf16[1,4,64,128]{3,2,1,0:T(8,128)(2,1)S(1)} %get-tuple-element.75), channel_id=1, source_target_pairs={{0,1},{1,0},{2,3},{3,2},{4,5},{5,4},{6,7},{7,6},{8,9},{9,8},{10,11... | collective-permute-start | bytes 196616 | tf_op jit(solution)/shard_map/ppermute | solution.py:44
  34.5 1.3 %collective-permute-start.13 = (bf16[1,4,64,128]{3,2,1,0:T(8,128)(2,1)S(1)}, bf16[1,4,64,128]{3,2,1,0:T(8,128)(2,1)S(1)}, u32[]{:S(2)}, u32[]{:S(2)}) collective-permute-start(bf16[1,4,64,128]{3,2,1,0:T(8,128)(2,1)S(1)} %get-tuple-element.76), channel_id=1, source_target_pairs={{0,1},{1,0},{2,3},{3,2},{4,5},{5,4},{6,7},{7,6},{8,9},{9,8},{10,11... | collective-permute-start | bytes 196616 | tf_op jit(solution)/shard_map/ppermute | solution.py:44
  35.8 6.4 %collective-permute-start.17 = (bf16[2,4,64,128]{3,2,1,0:T(8,128)(2,1)S(1)}, bf16[2,4,64,128]{3,2,1,0:T(8,128)(2,1)S(1)}, u32[]{:S(2)}, u32[]{:S(2)}) collective-permute-start(bf16[2,4,64,128]{3,2,1,0:T(8,128)(2,1)S(1)} %halve.3), channel_id=1, source_target_pairs={{0,4},{4,0},{8,12},{12,8},{1,5},{5,1},{9,13},{13,9},{2,6},{6,2},{1... | collective-permute-start | bytes 393224 | tf_op jit(solution)/shard_map/ppermute | solution.py:44
  38.3 6.1 %collective-permute-start.18 = (bf16[2,4,64,128]{3,2,1,0:T(8,128)(2,1)S(1)}, bf16[2,4,64,128]{3,2,1,0:T(8,128)(2,1)S(1)}, u32[]{:S(2)}, u32[]{:S(2)}) collective-permute-start(bf16[2,4,64,128]{3,2,1,0:T(8,128)(2,1)S(1)} %residual.2.refs_0_), channel_id=1, source_target_pairs={{0,4},{4,0},{8,12},{12,8},{1,5},{5,1},{9,13},{13,9},{2,6},{6,2},{1... | collective-permute-start | bytes 393224 | tf_op jit(solution)/shard_map/ppermute | solution.py:44
  39.2 1.3 %collective-permute-start.15 = (bf16[1,4,64,128]{3,2,1,0:T(8,128)(2,1)S(1)}, bf16[1,4,64,128]{3,2,1,0:T(8,128)(2,1)S(1)}, u32[]{:S(2)}, u32[]{:S(2)}) collective-permute-start(bf16[1,4,64,128]{3,2,1,0:T(8,128)(2,1)S(1)} %get-tuple-element.79), channel_id=1, source_target_pairs={{0,1},{1,0},{2,3},{3,2},{4,5},{5,4},{6,7},{7,6},{8,9},{9,8},{10,11... | collective-permute-start | bytes 196616 | tf_op jit(solution)/shard_map/ppermute | solution.py:44
  39.2 1.4 %collective-permute-start.16 = (bf16[1,4,64,128]{3,2,1,0:T(8,128)(2,1)S(1)}, bf16[1,4,64,128]{3,2,1,0:T(8,128)(2,1)S(1)}, u32[]{:S(2)}, u32[]{:S(2)}) collective-permute-start(bf16[1,4,64,128]{3,2,1,0:T(8,128)(2,1)S(1)} %get-tuple-element.80), channel_id=1, source_target_pairs={{0,1},{1,0},{2,3},{3,2},{4,5},{5,4},{6,7},{7,6},{8,9},{9,8},{10,11... | collective-permute-start | bytes 196616 | tf_op jit(solution)/shard_map/ppermute | solution.py:44
  39.7 5.4 %collective-permute-start.19 = (bf16[2,4,64,128]{3,2,1,0:T(8,128)(2,1)S(1)}, bf16[2,4,64,128]{3,2,1,0:T(8,128)(2,1)S(1)}, u32[]{:S(2)}, u32[]{:S(2)}) collective-permute-start(bf16[2,4,64,128]{3,2,1,0:T(8,128)(2,1)S(1)} %residual.2.refs_0_), channel_id=1, source_target_pairs={{0,1},{1,0},{2,3},{3,2},{4,5},{5,4},{6,7},{7,6},{8,9},{9,8},{10,11... | collective-permute-start | bytes 393224 | tf_op jit(solution)/shard_map/ppermute | solution.py:44
  42.3 8.6 %collective-permute-start.22 = (bf16[2,4,64,128]{3,2,1,0:T(8,128)(2,1)S(1)}, bf16[2,4,64,128]{3,2,1,0:T(8,128)(2,1)S(1)}, u32[]{:S(2)}, u32[]{:S(2)}) collective-permute-start(bf16[2,4,64,128]{3,2,1,0:T(8,128)(2,1)S(1)} %get-tuple-element.82), channel_id=1, source_target_pairs={{0,8},{4,12},{8,0},{12,4},{1,9},{5,13},{9,1},{13,5},{2,10},{6,14},... | collective-permute-start | bytes 393224 | tf_op jit(solution)/shard_map/ppermute | solution.py:44
  44.5 1.3 %collective-permute-start.20 = (bf16[1,4,64,128]{3,2,1,0:T(8,128)(2,1)S(1)}, bf16[1,4,64,128]{3,2,1,0:T(8,128)(2,1)S(1)}, u32[]{:S(2)}, u32[]{:S(2)}) collective-permute-start(bf16[1,4,64,128]{3,2,1,0:T(8,128)(2,1)S(1)} %get-tuple-element.85), channel_id=1, source_target_pairs={{0,1},{1,0},{2,3},{3,2},{4,5},{5,4},{6,7},{7,6},{8,9},{9,8},{10,11... | collective-permute-start | bytes 196616 | tf_op jit(solution)/shard_map/ppermute | solution.py:44
  44.5 1.4 %collective-permute-start.21 = (bf16[1,4,64,128]{3,2,1,0:T(8,128)(2,1)S(1)}, bf16[1,4,64,128]{3,2,1,0:T(8,128)(2,1)S(1)}, u32[]{:S(2)}, u32[]{:S(2)}) collective-permute-start(bf16[1,4,64,128]{3,2,1,0:T(8,128)(2,1)S(1)} %get-tuple-element.86), channel_id=1, source_target_pairs={{0,1},{1,0},{2,3},{3,2},{4,5},{5,4},{6,7},{7,6},{8,9},{9,8},{10,11... | collective-permute-start | bytes 196616 | tf_op jit(solution)/shard_map/ppermute | solution.py:44
  49.5 2.4 %collective-permute-start.24 = (bf16[8,128,128]{2,1,0:T(8,128)(2,1)S(1)}, bf16[8,128,128]{2,1,0:T(8,128)(2,1)S(1)}, u32[]{:S(2)}, u32[]{:S(2)}) collective-permute-start(bf16[8,128,128]{2,1,0:T(8,128)(2,1)S(1)} %get-tuple-element.94), channel_id=1, source_target_pairs={{0,1},{1,0},{2,3},{3,2},{4,5},{5,4},{6,7},{7,6},{8,9},{9,8},{10,11... | collective-permute-start | bytes 786440 | tf_op jit(solution)/shard_map/ppermute | solution.py:44
  49.9 2.0 %collective-permute-start.25 = (bf16[8,128,128]{2,1,0:T(8,128)(2,1)S(1)}, bf16[8,128,128]{2,1,0:T(8,128)(2,1)S(1)}, u32[]{:S(2)}, u32[]{:S(2)}) collective-permute-start(bf16[8,128,128]{2,1,0:T(8,128)(2,1)S(1)} %get-tuple-element.95), channel_id=1, source_target_pairs={{0,1},{1,0},{2,3},{3,2},{4,5},{5,4},{6,7},{7,6},{8,9},{9,8},{10,11... | collective-permute-start | bytes 786440 | tf_op jit(solution)/shard_map/ppermute | solution.py:44
  51.1 5.0 %collective-permute-start.23 = (bf16[2,4,64,128]{3,2,1,0:T(8,128)(2,1)S(1)}, bf16[2,4,64,128]{3,2,1,0:T(8,128)(2,1)S(1)}, u32[]{:S(2)}, u32[]{:S(2)}) collective-permute-start(bf16[2,4,64,128]{3,2,1,0:T(8,128)(2,1)S(1)} %residual.3.refs_1_.refs_0_), channel_id=1, source_target_pairs={{0,4},{4,0},{8,12},{12,8},{1,5},{5,1},{9,13},{13,9},{2,6},{6,2},{1... | collective-permute-start | bytes 393224 | tf_op jit(solution)/shard_map/ppermute | solution.py:44
  51.9 14.5 %collective-permute-start.30 = (bf16[16,128,128]{2,1,0:T(8,128)(2,1)S(1)}, bf16[16,128,128]{2,1,0:T(8,128)(2,1)S(1)}, u32[]{:S(2)}, u32[]{:S(2)}) collective-permute-start(bf16[16,128,128]{2,1,0:T(8,128)(2,1)S(1)} %adjoint_share.2), channel_id=1, source_target_pairs={{0,2},{2,0},{1,3},{3,1},{4,6},{6,4},{5,7},{7,5},{8,10},{10,8},{9,1... | collective-permute-start | bytes 1572872 | tf_op jit(solution)/shard_map/ppermute | solution.py:44
  53.6 13.0 %collective-permute-start.31 = (bf16[16,128,128]{2,1,0:T(8,128)(2,1)S(1)}, bf16[16,128,128]{2,1,0:T(8,128)(2,1)S(1)}, u32[]{:S(2)}, u32[]{:S(2)}) collective-permute-start(bf16[16,128,128]{2,1,0:T(8,128)(2,1)S(1)} %get-tuple-element.101), channel_id=1, source_target_pairs={{0,1},{1,0},{2,3},{3,2},{4,5},{5,4},{6,7},{7,6},{8,9},{9,8},{10,11... | collective-permute-start | bytes 1572872 | tf_op jit(solution)/shard_map/ppermute | solution.py:44
  53.6 3.3 %collective-permute-start.26 = (bf16[2,4,64,128]{3,2,1,0:T(8,128)(2,1)S(1)}, bf16[2,4,64,128]{3,2,1,0:T(8,128)(2,1)S(1)}, u32[]{:S(2)}, u32[]{:S(2)}) collective-permute-start(bf16[2,4,64,128]{3,2,1,0:T(8,128)(2,1)S(1)} %residual.3.refs_1_.refs_0_), channel_id=1, source_target_pairs={{0,1},{1,0},{2,3},{3,2},{4,5},{5,4},{6,7},{7,6},{8,9},{9,8},{10,11... | collective-permute-start | bytes 393224 | tf_op jit(solution)/shard_map/ppermute | solution.py:44
  56.1 1.3 %collective-permute-start.27 = (bf16[2,4,64,128]{3,2,1,0:T(8,128)(2,1)S(1)}, bf16[2,4,64,128]{3,2,1,0:T(8,128)(2,1)S(1)}, u32[]{:S(2)}, u32[]{:S(2)}) collective-permute-start(bf16[2,4,64,128]{3,2,1,0:T(8,128)(2,1)S(1)} %collective-permute-done.23.refs_1_), channel_id=1, source_target_pairs={{0,1},{1,0},{2,3},{3,2},{4,5},{5,4},{6,7},{7,6},{8,9},{9,8},{10,11... | collective-permute-start | bytes 393224 | tf_op jit(solution)/shard_map/ppermute | solution.py:44
  60.4 1.6 %collective-permute-start.28 = (bf16[8,128,128]{2,1,0:T(8,128)(2,1)S(1)}, bf16[8,128,128]{2,1,0:T(8,128)(2,1)S(1)}, u32[]{:S(2)}, u32[]{:S(2)}) collective-permute-start(bf16[8,128,128]{2,1,0:T(8,128)(2,1)S(1)} %get-tuple-element.98), channel_id=1, source_target_pairs={{0,1},{1,0},{2,3},{3,2},{4,5},{5,4},{6,7},{7,6},{8,9},{9,8},{10,11... | collective-permute-start | bytes 786440 | tf_op jit(solution)/shard_map/ppermute | solution.py:44
  60.6 1.8 %collective-permute-start.29 = (bf16[8,128,128]{2,1,0:T(8,128)(2,1)S(1)}, bf16[8,128,128]{2,1,0:T(8,128)(2,1)S(1)}, u32[]{:S(2)}, u32[]{:S(2)}) collective-permute-start(bf16[8,128,128]{2,1,0:T(8,128)(2,1)S(1)} %get-tuple-element.99), channel_id=1, source_target_pairs={{0,1},{1,0},{2,3},{3,2},{4,5},{5,4},{6,7},{7,6},{8,9},{9,8},{10,11... | collective-permute-start | bytes 786440 | tf_op jit(solution)/shard_map/ppermute | solution.py:44
  62.5 14.7 %collective-permute-start.33 = (bf16[16,128,128]{2,1,0:T(8,128)(2,1)S(1)}, bf16[16,128,128]{2,1,0:T(8,128)(2,1)S(1)}, u32[]{:S(2)}, u32[]{:S(2)}) collective-permute-start(bf16[16,128,128]{2,1,0:T(8,128)(2,1)S(1)} %adjoint_share.3), channel_id=1, source_target_pairs={{0,2},{2,0},{1,3},{3,1},{4,6},{6,4},{5,7},{7,5},{8,10},{10,8},{9,1... | collective-permute-start | bytes 1572872 | tf_op jit(solution)/shard_map/ppermute | solution.py:44
  64.0 2.6 %collective-permute-start.32 = (bf16[16,128,128]{2,1,0:T(8,128)(2,1)S(1)}, bf16[16,128,128]{2,1,0:T(8,128)(2,1)S(1)}, u32[]{:S(2)}, u32[]{:S(2)}) collective-permute-start(bf16[16,128,128]{2,1,0:T(8,128)(2,1)S(1)} %get-tuple-element.105), channel_id=1, source_target_pairs={{0,1},{1,0},{2,3},{3,2},{4,5},{5,4},{6,7},{7,6},{8,9},{9,8},{10,11... | collective-permute-start | bytes 1572872 | tf_op jit(solution)/shard_map/ppermute | solution.py:44

commit v8 on v7

--- a/solution.py
+++ b/solution.py
@@ -498,7 +498,7 @@
                 keep, send = call(halve_kernel, "halve", [(shape, F32), (shape, BF16)], [keep, *others], cost=1)
                 others = [swap("col", d, send)]
         if c:
-            residual_of(c - 1, send)
+            residual_of(c - 1, send, *stay)
             keep = after(keep, *residuals[c - 1])
         shape = (2, rows, span, width)
         mirrored.append(

time: 78.6 us -> 78.8 us (level)
  transfers between devices with their start and end apart: 34 -> 34, of which waited for: 21 -> 19; matrix products, arithmetic and copies ran while one was open for 0% -> 0% of each run, Pallas kernels for 25% -> 25%
where the time goes in v8:
time: 78.8 us; the launch traced here: 78.6 us
  waiting for transfers between devices  29 us (37%)
  starting transfers between devices  26 us (33%)
  Pallas kernels  22.3 us (28%)
  between operations  1.07 us (1%)
    ppermute x34, waiting for transfers between devices, swap(): return lax.ppermute(value, axis_name, [(i, i ^ step) for i in range(size)])  29 us
    ppermute x34, starting transfers between devices, swap(): return lax.ppermute(value, axis_name, [(i, i ^ step) for i in range(size)])  26 us
    pallas_call x25, Pallas kernels, call(): pl.pallas_call(kernel, out_shape=[jax.ShapeDtypeStruct(shape, kind) for s...  22.3 us
  transfers between devices with their start and end apart: 34, of which 19 were waited for; matrix products, arithmetic and copies ran while one was open for 0% of the time, Pallas kernels for 25%

profile of v8, /device:TPU:0, one launch (start us, length us, event | category | flops | bytes accessed | tf_op | source)
XLA Modules:
  0.0 78.6 jit_solution(17873745674364846954)
XLA Ops:
  0.6 1.3 %first_waves.1 = (bf16[10,128,128]{2,1,0:T(8,128)(2,1)S(1)}, bf16[3,4,64,128]{3,2,1,0:T(8,128)(2,1)S(1)}) custom-call(bf16[2,16,128,128]{3,2,1,0:T(8,128)(2,1)} %source.2, bf16[2,4,64,128]{3,2,1,0:T(8,128)(2,1)} %observed.1, bf16[4,64,128]{2,1,0:T(8,128)(2,1)} %amplitude.1), custom_call_target="tpu_custom_call" | custom-call | flops 1000000 | bytes 10000 | tf_op jit(solution)/shard_map/first_waves/pallas_call | solution.py:26
  1.9 3.0 %collective-permute-start.5 = (bf16[10,128,128]{2,1,0:T(8,128)(2,1)S(1)}, bf16[10,128,128]{2,1,0:T(8,128)(2,1)S(1)}, u32[]{:S(2)}, u32[]{:S(2)}) collective-permute-start(bf16[10,128,128]{2,1,0:T(8,128)(2,1)S(1)} %get-tuple-element.55), channel_id=1, source_target_pairs={{0,2},{2,0},{1,3},{3,1},{4,6},{6,4},{5,7},{7,5},{8,10},{10,8},{9,1... | collective-permute-start | bytes 983048 | tf_op jit(solution)/shard_map/ppermute | solution.py:44
  5.0 2.7 %collective-permute-start.1 = (bf16[3,4,64,128]{3,2,1,0:T(8,128)(2,1)S(1)}, bf16[3,4,64,128]{3,2,1,0:T(8,128)(2,1)S(1)}, u32[]{:S(2)}, u32[]{:S(2)}) collective-permute-start(bf16[3,4,64,128]{3,2,1,0:T(8,128)(2,1)S(1)} %relay_data.1.refs_0_), channel_id=1, source_target_pairs={{0,8},{4,12},{8,0},{12,4},{1,9},{5,13},{9,1},{13,5},{2,10},{6,14},... | collective-permute-start | bytes 589832 | tf_op jit(solution)/shard_map/ppermute | solution.py:44
  7.6 0.4 other_waves.1
  8.1 0.5 collective-permute-start.3
  8.6 0.5 collective-permute-start
  9.2 2.2 %load_factors.1 = (bf16[16,8,40,512]{3,2,1,0:T(8,128)(2,1)S(1)}, bf16[2,4,16,40,512]{4,3,2,1,0:T(8,128)(2,1)S(1)}) custom-call(bf16[2,4,16,40,512]{4,3,2,1,0:T(8,128)(2,1)S(1)} %bitcast.15, bf16[2,4,16,40,512]{4,3,2,1,0:T(8,128)(2,1)S(1)} %bitcast.17), custom_call_target="tpu_custom_call" | custom-call | flops 10000000000 | bytes 10000 | tf_op jit(solution)/shard_map/load_factors/pallas_call | solution.py:26
  11.4 1.7 %near_products.1 = (f32[4,640,128]{2,1,0:T(8,128)S(1)}, f32[4,640,128]{2,1,0:T(8,128)S(1)}) custom-call(bf16[16,320,512]{2,1,0:T(8,128)(2,1)S(1)} %bitcast.2, bf16[16,128,128]{2,1,0:T(8,128)(2,1)S(1)} %get-tuple-element.62.refs_0_, bf16[16,128,128]{2,1,0:T(8,128)(2,1)S(1)} %collective-permute-done.3.refs_1_, ...), custom_call_target="tpu_custom_call" | custom-call | flops 1 | bytes 10000 | tf_op jit(solution)/shard_map/near_products/pallas_call | solution.py:26
  13.1 0.4 collective-permute-done.5.refs_0_
  13.4 2.1 %collective-permute-start.10 = (bf16[16,128,128]{2,1,0:T(8,128)(2,1)S(1)}, bf16[16,128,128]{2,1,0:T(8,128)(2,1)S(1)}, u32[]{:S(2)}, u32[]{:S(2)}) collective-permute-start(bf16[16,128,128]{2,1,0:T(8,128)(2,1)S(1)} %get-tuple-element.63.refs_2_), channel_id=1, source_target_pairs={{0,2},{2,0},{1,3},{3,1},{4,6},{6,4},{5,7},{7,5},{8,10},{10,8},{9,1... | collective-permute-start | bytes 1572872 | tf_op jit(solution)/shard_map/ppermute | solution.py:44
  15.5 1.3 %collective-permute-done.refs_0_ = bf16[6,128,128]{2,1,0:T(8,128)(2,1)S(1)} collective-permute-done((bf16[6,128,128]{2,1,0:T(8,128)(2,1)S(1)}, bf16[6,128,128]{2,1,0:T(8,128)(2,1)S(1)}, u32[]{:S(2)}, u32[]{:S(2)}) %collective-permute-start) | collective-permute-done | bytes 196640 | tf_op jit(solution)/shard_map/ppermute | solution.py:44
  16.9 1.2 %first_coefficients.1.refs_5_ = f32[4,400,128]{2,1,0:T(8,128)S(1)} custom-call(s32[4,16]{1,0:T(4,128)S(1)} %copy-done.1, bf16[10,128,128]{2,1,0:T(8,128)(2,1)S(1)} %collective-permute-done.5.refs_0_, bf16[10,128,128]{2,1,0:T(8,128)(2,1)S(1)} %collective-permute-done.6.refs_1_, bf16[16,320,512]{2,1,0:T(8,128)(2,1)S(1)} %bitcast.3, ...), custom_call_target="tpu_custom_call" | custom-call | flops 1 | bytes 10000 | tf_op jit(solution)/shard_map/first_coefficients/pallas_call | solution.py:26
  18.3 2.7 %forward_product.2 = (f32[4,4,64,128]{3,2,1,0:T(8,128)S(1)}, bf16[2,4,64,128]{3,2,1,0:T(8,128)(2,1)S(1)}, bf16[2,4,64,128]{3,2,1,0:T(8,128)(2,1)S(1)}) custom-call(s32[4,16]{1,0:T(4,128)S(1)} %copy-done.1, bf16[6,128,128]{2,1,0:T(8,128)(2,1)S(1)} %collective-permute-done.refs_0_, bf16[6,128,128]{2,1,0:T(8,128)(2,1)S(1)} %collective-permute-done.2.refs_1_, ...), custom_call_target="tpu_custom_call" | custom-call | flops 1 | bytes 10000 | tf_op jit(solution)/shard_map/forward_product/pallas_call | solution.py:26
  21.0 0.4 collective-permute-start.8
  21.6 0.8 %collective-permute-done.8.refs_0_ = bf16[2,4,64,128]{3,2,1,0:T(8,128)(2,1)S(1)} collective-permute-done((bf16[2,4,64,128]{3,2,1,0:T(8,128)(2,1)S(1)}, bf16[2,4,64,128]{3,2,1,0:T(8,128)(2,1)S(1)}, u32[]{:S(2)}, u32[]{:S(2)}) %collective-permute-start.8) | collective-permute-done | bytes 131104 | tf_op jit(solution)/shard_map/ppermute | solution.py:44
  22.5 1.9 %collective-permute-start.9 = (bf16[2,4,64,128]{3,2,1,0:T(8,128)(2,1)S(1)}, bf16[2,4,64,128]{3,2,1,0:T(8,128)(2,1)S(1)}, u32[]{:S(2)}, u32[]{:S(2)}) collective-permute-start(bf16[2,4,64,128]{3,2,1,0:T(8,128)(2,1)S(1)} %halve.2), channel_id=1, source_target_pairs={{0,4},{4,0},{8,12},{12,8},{1,5},{5,1},{9,13},{13,9},{2,6},{6,2},{1... | collective-permute-start | bytes 393224 | tf_op jit(solution)/shard_map/ppermute | solution.py:44
  24.3 4.0 %collective-permute-done.9.refs_1_ = bf16[2,4,64,128]{3,2,1,0:T(8,128)(2,1)S(1)} collective-permute-done((bf16[2,4,64,128]{3,2,1,0:T(8,128)(2,1)S(1)}, bf16[2,4,64,128]{3,2,1,0:T(8,128)(2,1)S(1)}, u32[]{:S(2)}, u32[]{:S(2)}) %collective-permute-start.9) | collective-permute-done | bytes 131104 | tf_op jit(solution)/shard_map/ppermute | solution.py:44
  28.5 2.8 %collective-permute-start.16 = (bf16[2,4,64,128]{3,2,1,0:T(8,128)(2,1)S(1)}, bf16[2,4,64,128]{3,2,1,0:T(8,128)(2,1)S(1)}, u32[]{:S(2)}, u32[]{:S(2)}) collective-permute-start(bf16[2,4,64,128]{3,2,1,0:T(8,128)(2,1)S(1)} %get-tuple-element.71), channel_id=1, source_target_pairs={{0,8},{4,12},{8,0},{12,4},{1,9},{5,13},{9,1},{13,5},{2,10},{6,14},... | collective-permute-start | bytes 393224 | tf_op jit(solution)/shard_map/ppermute | solution.py:44
  31.3 3.0 %forward_product.3 = (f32[4,4,64,128]{3,2,1,0:T(8,128)S(1)}, bf16[1,4,64,128]{3,2,1,0:T(8,128)(2,1)S(1)}, bf16[1,4,64,128]{3,2,1,0:T(8,128)(2,1)S(1)}, bf16[1,4,...) custom-call(s32[4,16]{1,0:T(4,128)S(1)} %copy-done.1, bf16[16,128,128]{2,1,0:T(8,128)(2,1)S(1)} %collective-permute-done.10.refs_0_, ...), custom_call_target="tpu_custom_call" | custom-call | flops 10000000000 | bytes 10000 | tf_op jit(solution)/shard_map/forward_product/pallas_call | solution.py:26
  34.5 0.3 collective-permute-start.13
  35.1 0.3 collective-permute-start.15
  35.8 1.6 %collective-permute-start.17 = (bf16[2,4,64,128]{3,2,1,0:T(8,128)(2,1)S(1)}, bf16[2,4,64,128]{3,2,1,0:T(8,128)(2,1)S(1)}, u32[]{:S(2)}, u32[]{:S(2)}) collective-permute-start(bf16[2,4,64,128]{3,2,1,0:T(8,128)(2,1)S(1)} %halve.3), channel_id=1, source_target_pairs={{0,4},{4,0},{8,12},{12,8},{1,5},{5,1},{9,13},{13,9},{2,6},{6,2},{1... | collective-permute-start | bytes 393224 | tf_op jit(solution)/shard_map/ppermute | solution.py:44
  37.5 0.7 collective-permute-done.16.other
  38.3 0.8 %collective-permute-start.18 = (bf16[2,4,64,128]{3,2,1,0:T(8,128)(2,1)S(1)}, bf16[2,4,64,128]{3,2,1,0:T(8,128)(2,1)S(1)}, u32[]{:S(2)}, u32[]{:S(2)}) collective-permute-start(bf16[2,4,64,128]{3,2,1,0:T(8,128)(2,1)S(1)} %residual.2.refs_0_), channel_id=1, source_target_pairs={{0,4},{4,0},{8,12},{12,8},{1,5},{5,1},{9,13},{13,9},{2,6},{6,2},{1... | collective-permute-start | bytes 393224 | tf_op jit(solution)/shard_map/ppermute | solution.py:44
  39.2 3.0 %collective-permute-done.17.refs_2_ = bf16[2,4,64,128]{3,2,1,0:T(8,128)(2,1)S(1)} collective-permute-done((bf16[2,4,64,128]{3,2,1,0:T(8,128)(2,1)S(1)}, bf16[2,4,64,128]{3,2,1,0:T(8,128)(2,1)S(1)}, u32[]{:S(2)}, u32[]{:S(2)}) %collective-permute-start.17) | collective-permute-done | bytes 131104 | tf_op jit(solution)/shard_map/ppermute | solution.py:44
  42.3 1.3 %collective-permute-start.22 = (bf16[2,4,64,128]{3,2,1,0:T(8,128)(2,1)S(1)}, bf16[2,4,64,128]{3,2,1,0:T(8,128)(2,1)S(1)}, u32[]{:S(2)}, u32[]{:S(2)}) collective-permute-start(bf16[2,4,64,128]{3,2,1,0:T(8,128)(2,1)S(1)} %get-tuple-element.82), channel_id=1, source_target_pairs={{0,8},{4,12},{8,0},{12,4},{1,9},{5,13},{9,1},{13,5},{2,10},{6,14},... | collective-permute-start | bytes 393224 | tf_op jit(solution)/shard_map/ppermute | solution.py:44
  43.6 0.9 %collective-permute-done.18.source.refs_1_ = bf16[2,4,64,128]{3,2,1,0:T(8,128)(2,1)S(1)} collective-permute-done((bf16[2,4,64,128]{3,2,1,0:T(8,128)(2,1)S(1)}, bf16[2,4,64,128]{3,2,1,0:T(8,128)(2,1)S(1)}, u32[]{:S(2)}, u32[]{:S(2)}) %collective-permute-start.18) | collective-permute-done | bytes 131104 | tf_op jit(solution)/shard_map/ppermute | solution.py:44
  44.5 0.5 collective-permute-start.21
  45.0 0.7 collective-permute-done.20.refs_3_
  45.9 2.7 %adjoint_product.2 = (bf16[16,160,128]{2,1,0:T(8,128)(2,1)S(1)}, f32[16,128,128]{2,1,0:T(8,128)S(1)}, bf16[8,128,128]{2,1,0:T(8,128)(2,1)S(1)}, bf16[8,128,128]{2,1,0:T(8,128)(2,1)S(1)}) custom-call(s32[4,16]{1,0:T(4,128)S(1)} %copy-done.1, bf16[2,4,64,128]{3,2,1,0:T(8,128)(2,1)S(1)} %residual.2.refs_0_, ...), custom_call_target="tpu_custom_call" | custom-call | flops 1 | bytes 10000 | tf_op jit(solution)/shard_map/adjoint_product/pallas_call | solution.py:26
  48.7 0.8 own_quarter.2
  49.5 0.4 collective-permute-start.24
  50.0 0.4 collective-permute-done.22.other
  50.6 1.5 %collective-permute-start.23 = (bf16[2,4,64,128]{3,2,1,0:T(8,128)(2,1)S(1)}, bf16[2,4,64,128]{3,2,1,0:T(8,128)(2,1)S(1)}, u32[]{:S(2)}, u32[]{:S(2)}) collective-permute-start(bf16[2,4,64,128]{3,2,1,0:T(8,128)(2,1)S(1)} %residual.3.refs_1_.refs_0_), channel_id=1, source_target_pairs={{0,4},{4,0},{8,12},{12,8},{1,5},{5,1},{9,13},{13,9},{2,6},{6,2},{1... | collective-permute-start | bytes 393224 | tf_op jit(solution)/shard_map/ppermute | solution.py:44
  52.1 1.6 %collective-permute-start.30 = (bf16[16,128,128]{2,1,0:T(8,128)(2,1)S(1)}, bf16[16,128,128]{2,1,0:T(8,128)(2,1)S(1)}, u32[]{:S(2)}, u32[]{:S(2)}) collective-permute-start(bf16[16,128,128]{2,1,0:T(8,128)(2,1)S(1)} %adjoint_share.2), channel_id=1, source_target_pairs={{0,2},{2,0},{1,3},{3,1},{4,6},{6,4},{5,7},{7,5},{8,10},{10,8},{9,1... | collective-permute-start | bytes 1572872 | tf_op jit(solution)/shard_map/ppermute | solution.py:44
  53.8 0.5 collective-permute-start.26
  54.3 1.7 %collective-permute-done.23.refs_1_ = bf16[2,4,64,128]{3,2,1,0:T(8,128)(2,1)S(1)} collective-permute-done((bf16[2,4,64,128]{3,2,1,0:T(8,128)(2,1)S(1)}, bf16[2,4,64,128]{3,2,1,0:T(8,128)(2,1)S(1)}, u32[]{:S(2)}, u32[]{:S(2)}) %collective-permute-start.23) | collective-permute-done | bytes 131104 | tf_op jit(solution)/shard_map/ppermute | solution.py:44
  56.0 0.8 join.1
  56.8 0.6 collective-permute-done.27.refs_3_
  57.4 3.0 %adjoint_product.3 = (bf16[16,160,128]{2,1,0:T(8,128)(2,1)S(1)}, f32[16,128,128]{2,1,0:T(8,128)S(1)}, bf16[8,128,128]{2,1,0:T(8,128)(2,1)S(1)}, bf16[8,128,128]{2,1,0:T(8,128)(2,1)S(1)}) custom-call(s32[4,16]{1,0:T(4,128)S(1)} %copy-done.1, bf16[2,4,64,128]{3,2,1,0:T(8,128)(2,1)S(1)} %residual.3.refs_1_.refs_0_, ...), custom_call_target="tpu_custom_call" | custom-call | flops 1 | bytes 10000 | tf_op jit(solution)/shard_map/adjoint_product/pallas_call | solution.py:26
  60.6 0.4 collective-permute-start.29
  60.9 0.8 own_quarter.3
  61.7 0.2 collective-permute-done.28.refs_0_
  62.0 0.4 collective-permute-done.29.refs_1_
  62.4 1.6 %collective-permute-start.33 = (bf16[16,128,128]{2,1,0:T(8,128)(2,1)S(1)}, bf16[16,128,128]{2,1,0:T(8,128)(2,1)S(1)}, u32[]{:S(2)}, u32[]{:S(2)}) collective-permute-start(bf16[16,128,128]{2,1,0:T(8,128)(2,1)S(1)} %adjoint_share.3), channel_id=1, source_target_pairs={{0,2},{2,0},{1,3},{3,1},{4,6},{6,4},{5,7},{7,5},{8,10},{10,8},{9,1... | collective-permute-start | bytes 1572872 | tf_op jit(solution)/shard_map/ppermute | solution.py:44
  64.1 2.8 %collective-permute-done.30.refs_0_ = bf16[16,128,128]{2,1,0:T(8,128)(2,1)S(1)} collective-permute-done((bf16[16,128,128]{2,1,0:T(8,128)(2,1)S(1)}, bf16[16,128,128]{2,1,0:T(8,128)(2,1)S(1)}, u32[]{:S(2)}, u32[]{:S(2)}) %collective-permute-start.30) | collective-permute-done | bytes 524320 | tf_op jit(solution)/shard_map/ppermute | solution.py:44
  67.1 10.2 %collective-permute-done.33.refs_1_ = bf16[16,128,128]{2,1,0:T(8,128)(2,1)S(1)} collective-permute-done((bf16[16,128,128]{2,1,0:T(8,128)(2,1)S(1)}, bf16[16,128,128]{2,1,0:T(8,128)(2,1)S(1)}, u32[]{:S(2)}, u32[]{:S(2)}) %collective-permute-start.33) | collective-permute-done | bytes 524320 | tf_op jit(solution)/shard_map/ppermute | solution.py:44
  77.3 1.1 %adjoint_sum.1 = bf16[2,16,128,128]{3,2,1,0:T(8,128)(2,1)} custom-call(f32[16,128,128]{2,1,0:T(8,128)S(1)} %total.3.done, f32[16,128,128]{2,1,0:T(8,128)S(1)} %get-tuple-element.103.mine, bf16[16,128,128]{2,1,0:T(8,128)(2,1)S(1)} %collective-permute-done.32.refs_0_, bf16[16,128,128]{2,1,0:T(8,128)(2,1)S(1)} %collective-permute-done.33.refs_1_), custom_call_target="tpu_custom_call" | custom-call | flops 1000000 | bytes 10000 | tf_op jit(solution)/shard_map/adjoint_sum/pallas_call | solution.py:26
  (59 shorter events, 2.9 us)
Async XLA Ops:
  1.9 11.5 %collective-permute-start.5 = (bf16[10,128,128]{2,1,0:T(8,128)(2,1)S(1)}, bf16[10,128,128]{2,1,0:T(8,128)(2,1)S(1)}, u32[]{:S(2)}, u32[]{:S(2)}) collective-permute-start(bf16[10,128,128]{2,1,0:T(8,128)(2,1)S(1)} %get-tuple-element.55), channel_id=1, source_target_pairs={{0,2},{2,0},{1,3},{3,1},{4,6},{6,4},{5,7},{7,5},{8,10},{10,8},{9,1... | collective-permute-start | bytes 983048 | tf_op jit(solution)/shard_map/ppermute | solution.py:44
  4.9 2.7 %copy-start = (bf16[2,16,128,128]{3,2,1,0:T(8,128)(2,1)S(1)}, bf16[2,16,128,128]{3,2,1,0:T(8,128)(2,1)}, u32[]{:S(2)}) copy-start(bf16[2,16,128,128]{3,2,1,0:T(8,128)(2,1)} %source.2) | copy-start | bytes 3145732
  4.9 4.2 %slice-start = ((s8[5242880]{0:T(1024)(128)(4,1)}), s8[4194304]{0:T(1024)(128)(4,1)S(1)}, s32[]{:S(2)}) async-start(s8[5242880]{0:T(1024)(128)(4,1)} %bitcast.14), calls=%async_computation | async-start | bytes 8388608
  4.9 4.2 %slice-start.2 = ((s8[5242880]{0:T(1024)(128)(4,1)}), s8[4194304]{0:T(1024)(128)(4,1)S(1)}, s32[]{:S(2)}) async-start(s8[5242880]{0:T(1024)(128)(4,1)} %bitcast.16), calls=%async_computation.2 | async-start | bytes 8388608
  4.9 4.2 %slice-start.1 = ((s8[5242880]{0:T(1024)(128)(4,1)}), s8[1048576]{0:T(1024)(128)(4,1)S(1)}, s32[]{:S(2)}) async-start(s8[5242880]{0:T(1024)(128)(4,1)} %bitcast.14), calls=%async_computation.1 | async-start | bytes 2097152
  4.9 4.3 %slice-start.3 = ((s8[5242880]{0:T(1024)(128)(4,1)}), s8[1048576]{0:T(1024)(128)(4,1)S(1)}, s32[]{:S(2)}) async-start(s8[5242880]{0:T(1024)(128)(4,1)} %bitcast.16), calls=%async_computation.3 | async-start | bytes 2097152
  5.0 11.9 %collective-permute-start.1 = (bf16[3,4,64,128]{3,2,1,0:T(8,128)(2,1)S(1)}, bf16[3,4,64,128]{3,2,1,0:T(8,128)(2,1)S(1)}, u32[]{:S(2)}, u32[]{:S(2)}) collective-permute-start(bf16[3,4,64,128]{3,2,1,0:T(8,128)(2,1)S(1)} %relay_data.1.refs_0_), channel_id=1, source_target_pairs={{0,8},{4,12},{8,0},{12,4},{1,9},{5,13},{9,1},{13,5},{2,10},{6,14},... | collective-permute-start | bytes 589832 | tf_op jit(solution)/shard_map/ppermute | solution.py:44
  8.0 3.4 %collective-permute-start.4 = (bf16[16,128,128]{2,1,0:T(8,128)(2,1)S(1)}, bf16[16,128,128]{2,1,0:T(8,128)(2,1)S(1)}, u32[]{:S(2)}, u32[]{:S(2)}) collective-permute-start(bf16[16,128,128]{2,1,0:T(8,128)(2,1)S(1)} %get-tuple-element.63.refs_2_), channel_id=1, source_target_pairs={{0,1},{1,0},{2,3},{3,2},{4,5},{5,4},{6,7},{7,6},{8,9},{9,8},{10,11... | collective-permute-start | bytes 1572872 | tf_op jit(solution)/shard_map/ppermute | solution.py:44
  8.1 3.4 %collective-permute-start.3 = (bf16[16,128,128]{2,1,0:T(8,128)(2,1)S(1)}, bf16[16,128,128]{2,1,0:T(8,128)(2,1)S(1)}, u32[]{:S(2)}, u32[]{:S(2)}) collective-permute-start(bf16[16,128,128]{2,1,0:T(8,128)(2,1)S(1)} %get-tuple-element.62.refs_0_), channel_id=1, source_target_pairs={{0,1},{1,0},{2,3},{3,2},{4,5},{5,4},{6,7},{7,6},{8,9},{9,8},{10,11... | collective-permute-start | bytes 1572872 | tf_op jit(solution)/shard_map/ppermute | solution.py:44
  8.6 8.3 %collective-permute-start = (bf16[6,128,128]{2,1,0:T(8,128)(2,1)S(1)}, bf16[6,128,128]{2,1,0:T(8,128)(2,1)S(1)}, u32[]{:S(2)}, u32[]{:S(2)}) collective-permute-start(bf16[6,128,128]{2,1,0:T(8,128)(2,1)S(1)} %get-tuple-element.58), channel_id=1, source_target_pairs={{0,2},{2,0},{1,3},{3,1},{4,6},{6,4},{5,7},{7,5},{8,10},{10,8},{9,1... | collective-permute-start | bytes 589832 | tf_op jit(solution)/shard_map/ppermute | solution.py:44
  11.4 5.5 %copy-start.1 = (s32[4,16]{1,0:T(4,128)S(1)}, s32[4,16]{1,0:T(4,128)}, u32[]{:S(2)}) copy-start(s32[4,16]{1,0:T(4,128)} %ranks.9) | copy-start | bytes 772
  13.4 3.4 %collective-permute-start.6 = (bf16[10,128,128]{2,1,0:T(8,128)(2,1)S(1)}, bf16[10,128,128]{2,1,0:T(8,128)(2,1)S(1)}, u32[]{:S(2)}, u32[]{:S(2)}) collective-permute-start(bf16[10,128,128]{2,1,0:T(8,128)(2,1)S(1)} %collective-permute-done.5.refs_0_), channel_id=1, source_target_pairs={{0,1},{1,0},{2,3},{3,2},{4,5},{5,4},{6,7},{7,6},{8,9},{9,8},{10,11... | collective-permute-start | bytes 983048 | tf_op jit(solution)/shard_map/ppermute | solution.py:44
  13.4 14.9 %collective-permute-start.10 = (bf16[16,128,128]{2,1,0:T(8,128)(2,1)S(1)}, bf16[16,128,128]{2,1,0:T(8,128)(2,1)S(1)}, u32[]{:S(2)}, u32[]{:S(2)}) collective-permute-start(bf16[16,128,128]{2,1,0:T(8,128)(2,1)S(1)} %get-tuple-element.63.refs_2_), channel_id=1, source_target_pairs={{0,2},{2,0},{1,3},{3,1},{4,6},{6,4},{5,7},{7,5},{8,10},{10,8},{9,1... | collective-permute-start | bytes 1572872 | tf_op jit(solution)/shard_map/ppermute | solution.py:44
  16.8 1.4 %collective-permute-start.2 = (bf16[6,128,128]{2,1,0:T(8,128)(2,1)S(1)}, bf16[6,128,128]{2,1,0:T(8,128)(2,1)S(1)}, u32[]{:S(2)}, u32[]{:S(2)}) collective-permute-start(bf16[6,128,128]{2,1,0:T(8,128)(2,1)S(1)} %collective-permute-done.refs_0_), channel_id=1, source_target_pairs={{0,1},{1,0},{2,3},{3,2},{4,5},{5,4},{6,7},{7,6},{8,9},{9,8},{10,11... | collective-permute-start | bytes 589832 | tf_op jit(solution)/shard_map/ppermute | solution.py:44
  21.0 1.4 %collective-permute-start.8 = (bf16[2,4,64,128]{3,2,1,0:T(8,128)(2,1)S(1)}, bf16[2,4,64,128]{3,2,1,0:T(8,128)(2,1)S(1)}, u32[]{:S(2)}, u32[]{:S(2)}) collective-permute-start(bf16[2,4,64,128]{3,2,1,0:T(8,128)(2,1)S(1)} %get-tuple-element.69), channel_id=1, source_target_pairs={{0,1},{1,0},{2,3},{3,2},{4,5},{5,4},{6,7},{7,6},{8,9},{9,8},{10,11... | collective-permute-start | bytes 393224 | tf_op jit(solution)/shard_map/ppermute | solution.py:44
  21.4 2.9 %collective-permute-start.7 = (bf16[2,4,64,128]{3,2,1,0:T(8,128)(2,1)S(1)}, bf16[2,4,64,128]{3,2,1,0:T(8,128)(2,1)S(1)}, u32[]{:S(2)}, u32[]{:S(2)}) collective-permute-start(bf16[2,4,64,128]{3,2,1,0:T(8,128)(2,1)S(1)} %get-tuple-element.68), channel_id=1, source_target_pairs={{0,1},{1,0},{2,3},{3,2},{4,5},{5,4},{6,7},{7,6},{8,9},{9,8},{10,11... | collective-permute-start | bytes 393224 | tf_op jit(solution)/shard_map/ppermute | solution.py:44
  22.5 5.9 %collective-permute-start.9 = (bf16[2,4,64,128]{3,2,1,0:T(8,128)(2,1)S(1)}, bf16[2,4,64,128]{3,2,1,0:T(8,128)(2,1)S(1)}, u32[]{:S(2)}, u32[]{:S(2)}) collective-permute-start(bf16[2,4,64,128]{3,2,1,0:T(8,128)(2,1)S(1)} %halve.2), channel_id=1, source_target_pairs={{0,4},{4,0},{8,12},{12,8},{1,5},{5,1},{9,13},{13,9},{2,6},{6,2},{1... | collective-permute-start | bytes 393224 | tf_op jit(solution)/shard_map/ppermute | solution.py:44
  28.4 2.9 %collective-permute-start.11 = (bf16[16,128,128]{2,1,0:T(8,128)(2,1)S(1)}, bf16[16,128,128]{2,1,0:T(8,128)(2,1)S(1)}, u32[]{:S(2)}, u32[]{:S(2)}) collective-permute-start(bf16[16,128,128]{2,1,0:T(8,128)(2,1)S(1)} %collective-permute-done.10.refs_0_), channel_id=1, source_target_pairs={{0,1},{1,0},{2,3},{3,2},{4,5},{5,4},{6,7},{7,6},{8,9},{9,8},{10,11... | collective-permute-start | bytes 1572872 | tf_op jit(solution)/shard_map/ppermute | solution.py:44
  28.5 9.7 %collective-permute-start.16 = (bf16[2,4,64,128]{3,2,1,0:T(8,128)(2,1)S(1)}, bf16[2,4,64,128]{3,2,1,0:T(8,128)(2,1)S(1)}, u32[]{:S(2)}, u32[]{:S(2)}) collective-permute-start(bf16[2,4,64,128]{3,2,1,0:T(8,128)(2,1)S(1)} %get-tuple-element.71), channel_id=1, source_target_pairs={{0,8},{4,12},{8,0},{12,4},{1,9},{5,13},{9,1},{13,5},{2,10},{6,14},... | collective-permute-start | bytes 393224 | tf_op jit(solution)/shard_map/ppermute | solution.py:44
  34.3 1.3 %collective-permute-start.12 = (bf16[1,4,64,128]{3,2,1,0:T(8,128)(2,1)S(1)}, bf16[1,4,64,128]{3,2,1,0:T(8,128)(2,1)S(1)}, u32[]{:S(2)}, u32[]{:S(2)}) collective-permute-start(bf16[1,4,64,128]{3,2,1,0:T(8,128)(2,1)S(1)} %get-tuple-element.75), channel_id=1, source_target_pairs={{0,1},{1,0},{2,3},{3,2},{4,5},{5,4},{6,7},{7,6},{8,9},{9,8},{10,11... | collective-permute-start | bytes 196616 | tf_op jit(solution)/shard_map/ppermute | solution.py:44
  34.5 1.3 %collective-permute-start.13 = (bf16[1,4,64,128]{3,2,1,0:T(8,128)(2,1)S(1)}, bf16[1,4,64,128]{3,2,1,0:T(8,128)(2,1)S(1)}, u32[]{:S(2)}, u32[]{:S(2)}) collective-permute-start(bf16[1,4,64,128]{3,2,1,0:T(8,128)(2,1)S(1)} %get-tuple-element.76), channel_id=1, source_target_pairs={{0,1},{1,0},{2,3},{3,2},{4,5},{5,4},{6,7},{7,6},{8,9},{9,8},{10,11... | collective-permute-start | bytes 196616 | tf_op jit(solution)/shard_map/ppermute | solution.py:44
  34.9 2.6 %collective-permute-start.14 = (bf16[1,4,64,128]{3,2,1,0:T(8,128)(2,1)S(1)}, bf16[1,4,64,128]{3,2,1,0:T(8,128)(2,1)S(1)}, u32[]{:S(2)}, u32[]{:S(2)}) collective-permute-start(bf16[1,4,64,128]{3,2,1,0:T(8,128)(2,1)S(1)} %get-tuple-element.77), channel_id=1, source_target_pairs={{0,1},{1,0},{2,3},{3,2},{4,5},{5,4},{6,7},{7,6},{8,9},{9,8},{10,11... | collective-permute-start | bytes 196616 | tf_op jit(solution)/shard_map/ppermute | solution.py:44
  35.1 2.4 %collective-permute-start.15 = (bf16[1,4,64,128]{3,2,1,0:T(8,128)(2,1)S(1)}, bf16[1,4,64,128]{3,2,1,0:T(8,128)(2,1)S(1)}, u32[]{:S(2)}, u32[]{:S(2)}) collective-permute-start(bf16[1,4,64,128]{3,2,1,0:T(8,128)(2,1)S(1)} %get-tuple-element.78), channel_id=1, source_target_pairs={{0,1},{1,0},{2,3},{3,2},{4,5},{5,4},{6,7},{7,6},{8,9},{9,8},{10,11... | collective-permute-start | bytes 196616 | tf_op jit(solution)/shard_map/ppermute | solution.py:44
  35.8 6.4 %collective-permute-start.17 = (bf16[2,4,64,128]{3,2,1,0:T(8,128)(2,1)S(1)}, bf16[2,4,64,128]{3,2,1,0:T(8,128)(2,1)S(1)}, u32[]{:S(2)}, u32[]{:S(2)}) collective-permute-start(bf16[2,4,64,128]{3,2,1,0:T(8,128)(2,1)S(1)} %halve.3), channel_id=1, source_target_pairs={{0,4},{4,0},{8,12},{12,8},{1,5},{5,1},{9,13},{13,9},{2,6},{6,2},{1... | collective-permute-start | bytes 393224 | tf_op jit(solution)/shard_map/ppermute | solution.py:44
  38.3 6.1 %collective-permute-start.18 = (bf16[2,4,64,128]{3,2,1,0:T(8,128)(2,1)S(1)}, bf16[2,4,64,128]{3,2,1,0:T(8,128)(2,1)S(1)}, u32[]{:S(2)}, u32[]{:S(2)}) collective-permute-start(bf16[2,4,64,128]{3,2,1,0:T(8,128)(2,1)S(1)} %residual.2.refs_0_), channel_id=1, source_target_pairs={{0,4},{4,0},{8,12},{12,8},{1,5},{5,1},{9,13},{13,9},{2,6},{6,2},{1... | collective-permute-start | bytes 393224 | tf_op jit(solution)/shard_map/ppermute | solution.py:44
  39.2 5.9 %collective-permute-start.19 = (bf16[2,4,64,128]{3,2,1,0:T(8,128)(2,1)S(1)}, bf16[2,4,64,128]{3,2,1,0:T(8,128)(2,1)S(1)}, u32[]{:S(2)}, u32[]{:S(2)}) collective-permute-start(bf16[2,4,64,128]{3,2,1,0:T(8,128)(2,1)S(1)} %residual.2.refs_0_), channel_id=1, source_target_pairs={{0,1},{1,0},{2,3},{3,2},{4,5},{5,4},{6,7},{7,6},{8,9},{9,8},{10,11... | collective-permute-start | bytes 393224 | tf_op jit(solution)/shard_map/ppermute | solution.py:44
  42.3 8.2 %collective-permute-start.22 = (bf16[2,4,64,128]{3,2,1,0:T(8,128)(2,1)S(1)}, bf16[2,4,64,128]{3,2,1,0:T(8,128)(2,1)S(1)}, u32[]{:S(2)}, u32[]{:S(2)}) collective-permute-start(bf16[2,4,64,128]{3,2,1,0:T(8,128)(2,1)S(1)} %get-tuple-element.82), channel_id=1, source_target_pairs={{0,8},{4,12},{8,0},{12,4},{1,9},{5,13},{9,1},{13,5},{2,10},{6,14},... | collective-permute-start | bytes 393224 | tf_op jit(solution)/shard_map/ppermute | solution.py:44
  44.5 1.3 %collective-permute-start.20 = (bf16[1,4,64,128]{3,2,1,0:T(8,128)(2,1)S(1)}, bf16[1,4,64,128]{3,2,1,0:T(8,128)(2,1)S(1)}, u32[]{:S(2)}, u32[]{:S(2)}) collective-permute-start(bf16[1,4,64,128]{3,2,1,0:T(8,128)(2,1)S(1)} %get-tuple-element.85), channel_id=1, source_target_pairs={{0,1},{1,0},{2,3},{3,2},{4,5},{5,4},{6,7},{7,6},{8,9},{9,8},{10,11... | collective-permute-start | bytes 196616 | tf_op jit(solution)/shard_map/ppermute | solution.py:44
  44.5 1.4 %collective-permute-start.21 = (bf16[1,4,64,128]{3,2,1,0:T(8,128)(2,1)S(1)}, bf16[1,4,64,128]{3,2,1,0:T(8,128)(2,1)S(1)}, u32[]{:S(2)}, u32[]{:S(2)}) collective-permute-start(bf16[1,4,64,128]{3,2,1,0:T(8,128)(2,1)S(1)} %get-tuple-element.86), channel_id=1, source_target_pairs={{0,1},{1,0},{2,3},{3,2},{4,5},{5,4},{6,7},{7,6},{8,9},{9,8},{10,11... | collective-permute-start | bytes 196616 | tf_op jit(solution)/shard_map/ppermute | solution.py:44
  49.5 2.6 %collective-permute-start.24 = (bf16[8,128,128]{2,1,0:T(8,128)(2,1)S(1)}, bf16[8,128,128]{2,1,0:T(8,128)(2,1)S(1)}, u32[]{:S(2)}, u32[]{:S(2)}) collective-permute-start(bf16[8,128,128]{2,1,0:T(8,128)(2,1)S(1)} %get-tuple-element.94), channel_id=1, source_target_pairs={{0,1},{1,0},{2,3},{3,2},{4,5},{5,4},{6,7},{7,6},{8,9},{9,8},{10,11... | collective-permute-start | bytes 786440 | tf_op jit(solution)/shard_map/ppermute | solution.py:44
  49.9 2.1 %collective-permute-start.25 = (bf16[8,128,128]{2,1,0:T(8,128)(2,1)S(1)}, bf16[8,128,128]{2,1,0:T(8,128)(2,1)S(1)}, u32[]{:S(2)}, u32[]{:S(2)}) collective-permute-start(bf16[8,128,128]{2,1,0:T(8,128)(2,1)S(1)} %get-tuple-element.95), channel_id=1, source_target_pairs={{0,1},{1,0},{2,3},{3,2},{4,5},{5,4},{6,7},{7,6},{8,9},{9,8},{10,11... | collective-permute-start | bytes 786440 | tf_op jit(solution)/shard_map/ppermute | solution.py:44
  50.6 5.5 %collective-permute-start.23 = (bf16[2,4,64,128]{3,2,1,0:T(8,128)(2,1)S(1)}, bf16[2,4,64,128]{3,2,1,0:T(8,128)(2,1)S(1)}, u32[]{:S(2)}, u32[]{:S(2)}) collective-permute-start(bf16[2,4,64,128]{3,2,1,0:T(8,128)(2,1)S(1)} %residual.3.refs_1_.refs_0_), channel_id=1, source_target_pairs={{0,4},{4,0},{8,12},{12,8},{1,5},{5,1},{9,13},{13,9},{2,6},{6,2},{1... | collective-permute-start | bytes 393224 | tf_op jit(solution)/shard_map/ppermute | solution.py:44
  52.1 14.8 %collective-permute-start.30 = (bf16[16,128,128]{2,1,0:T(8,128)(2,1)S(1)}, bf16[16,128,128]{2,1,0:T(8,128)(2,1)S(1)}, u32[]{:S(2)}, u32[]{:S(2)}) collective-permute-start(bf16[16,128,128]{2,1,0:T(8,128)(2,1)S(1)} %adjoint_share.2), channel_id=1, source_target_pairs={{0,2},{2,0},{1,3},{3,1},{4,6},{6,4},{5,7},{7,5},{8,10},{10,8},{9,1... | collective-permute-start | bytes 1572872 | tf_op jit(solution)/shard_map/ppermute | solution.py:44
  53.8 13.2 %collective-permute-start.31 = (bf16[16,128,128]{2,1,0:T(8,128)(2,1)S(1)}, bf16[16,128,128]{2,1,0:T(8,128)(2,1)S(1)}, u32[]{:S(2)}, u32[]{:S(2)}) collective-permute-start(bf16[16,128,128]{2,1,0:T(8,128)(2,1)S(1)} %get-tuple-element.101), channel_id=1, source_target_pairs={{0,1},{1,0},{2,3},{3,2},{4,5},{5,4},{6,7},{7,6},{8,9},{9,8},{10,11... | collective-permute-start | bytes 1572872 | tf_op jit(solution)/shard_map/ppermute | solution.py:44
  53.8 3.0 %collective-permute-start.26 = (bf16[2,4,64,128]{3,2,1,0:T(8,128)(2,1)S(1)}, bf16[2,4,64,128]{3,2,1,0:T(8,128)(2,1)S(1)}, u32[]{:S(2)}, u32[]{:S(2)}) collective-permute-start(bf16[2,4,64,128]{3,2,1,0:T(8,128)(2,1)S(1)} %residual.3.refs_1_.refs_0_), channel_id=1, source_target_pairs={{0,1},{1,0},{2,3},{3,2},{4,5},{5,4},{6,7},{7,6},{8,9},{9,8},{10,11... | collective-permute-start | bytes 393224 | tf_op jit(solution)/shard_map/ppermute | solution.py:44
  56.0 1.3 %collective-permute-start.27 = (bf16[2,4,64,128]{3,2,1,0:T(8,128)(2,1)S(1)}, bf16[2,4,64,128]{3,2,1,0:T(8,128)(2,1)S(1)}, u32[]{:S(2)}, u32[]{:S(2)}) collective-permute-start(bf16[2,4,64,128]{3,2,1,0:T(8,128)(2,1)S(1)} %collective-permute-done.23.refs_1_), channel_id=1, source_target_pairs={{0,1},{1,0},{2,3},{3,2},{4,5},{5,4},{6,7},{7,6},{8,9},{9,8},{10,11... | collective-permute-start | bytes 393224 | tf_op jit(solution)/shard_map/ppermute | solution.py:44
  60.4 1.6 %collective-permute-start.28 = (bf16[8,128,128]{2,1,0:T(8,128)(2,1)S(1)}, bf16[8,128,128]{2,1,0:T(8,128)(2,1)S(1)}, u32[]{:S(2)}, u32[]{:S(2)}) collective-permute-start(bf16[8,128,128]{2,1,0:T(8,128)(2,1)S(1)} %get-tuple-element.98), channel_id=1, source_target_pairs={{0,1},{1,0},{2,3},{3,2},{4,5},{5,4},{6,7},{7,6},{8,9},{9,8},{10,11... | collective-permute-start | bytes 786440 | tf_op jit(solution)/shard_map/ppermute | solution.py:44
  60.6 1.8 %collective-permute-start.29 = (bf16[8,128,128]{2,1,0:T(8,128)(2,1)S(1)}, bf16[8,128,128]{2,1,0:T(8,128)(2,1)S(1)}, u32[]{:S(2)}, u32[]{:S(2)}) collective-permute-start(bf16[8,128,128]{2,1,0:T(8,128)(2,1)S(1)} %get-tuple-element.99), channel_id=1, source_target_pairs={{0,1},{1,0},{2,3},{3,2},{4,5},{5,4},{6,7},{7,6},{8,9},{9,8},{10,11... | collective-permute-start | bytes 786440 | tf_op jit(solution)/shard_map/ppermute | solution.py:44
  62.4 14.9 %collective-permute-start.33 = (bf16[16,128,128]{2,1,0:T(8,128)(2,1)S(1)}, bf16[16,128,128]{2,1,0:T(8,128)(2,1)S(1)}, u32[]{:S(2)}, u32[]{:S(2)}) collective-permute-start(bf16[16,128,128]{2,1,0:T(8,128)(2,1)S(1)} %adjoint_share.3), channel_id=1, source_target_pairs={{0,2},{2,0},{1,3},{3,1},{4,6},{6,4},{5,7},{7,5},{8,10},{10,8},{9,1... | collective-permute-start | bytes 1572872 | tf_op jit(solution)/shard_map/ppermute | solution.py:44
  64.1 3.0 %collective-permute-start.32 = (bf16[16,128,128]{2,1,0:T(8,128)(2,1)S(1)}, bf16[16,128,128]{2,1,0:T(8,128)(2,1)S(1)}, u32[]{:S(2)}, u32[]{:S(2)}) collective-permute-start(bf16[16,128,128]{2,1,0:T(8,128)(2,1)S(1)} %get-tuple-element.105), channel_id=1, source_target_pairs={{0,1},{1,0},{2,3},{3,2},{4,5},{5,4},{6,7},{7,6},{8,9},{9,8},{10,11... | collective-permute-start | bytes 1572872 | tf_op jit(solution)/shard_map/ppermute | solution.py:44

commit v9 on v7

--- a/solution.py
+++ b/solution.py
@@ -286,7 +286,7 @@
             sends[n // n_send][n % n_send, i] = fwd[i, pl.ds(at, span), :].astype(BF16)
 
 
-def adjoint_terms(offsets, back, second, keeps, sends):
+def adjoint_terms(offsets, back, second, keeps, sends, rounded=None):
     rs, helps = lax.axis_size("row"), lax.axis_size("help")
     r, here = lax.axis_index("row"), lax.axis_index("help")
     _, width, quarter = keeps[0].shape
@@ -302,7 +302,10 @@
         refs[j // n][j % n] = value.astype(BF16)
 
     for j in range(back.shape[0]):
-        real = back[j].astype(BF16).T
+        value = back[j].astype(BF16)
+        if rounded is not None:
+            rounded[j] = value
+        real = value.T
         turned = jnp.concatenate([-real[width // 2 :], real[: width // 2]], 0)
 
         def product(right):
@@ -349,8 +352,7 @@
             left = ranks[i, j] - here * terms
             part = out[j * terms : (j + 1) * terms]
             back[j, i * terms : (i + 1) * terms, :] = jnp.where(row_index < left, part, 0.0)
-    back_out[...] = back[...].astype(BF16)
-    adjoint_terms(offsets, back, second, keeps, sends)
+    adjoint_terms(offsets, back, second, keeps, sends, back_out)
 
 
 def own_kernel(back, second, keep, send):

time: 78.6 us -> 78.6 us (level)
  no operation moved by 1% of the time
where the time goes in v9:
time: 78.6 us; the launch traced here: 78.4 us
  waiting for transfers between devices  29.1 us (37%)
  starting transfers between devices  25.7 us (33%)
  Pallas kernels  22.3 us (28%)
  between operations  1.07 us (1%)
    ppermute x34, waiting for transfers between devices, swap(): return lax.ppermute(value, axis_name, [(i, i ^ step) for i in range(size)])  29.1 us
    ppermute x34, starting transfers between devices, swap(): return lax.ppermute(value, axis_name, [(i, i ^ step) for i in range(size)])  25.7 us
    pallas_call x25, Pallas kernels, call(): pl.pallas_call(kernel, out_shape=[jax.ShapeDtypeStruct(shape, kind) for s...  22.3 us
  transfers between devices with their start and end apart: 34, of which 21 were waited for; matrix products, arithmetic and copies ran while one was open for 0% of the time, Pallas kernels for 25%

profile of v9, /device:TPU:0, one launch (start us, length us, event | category | flops | bytes accessed | tf_op | source)
XLA Modules:
  0.0 78.4 jit_solution(3551614867008813067)
XLA Ops:
  0.6 1.3 %first_waves.1 = (bf16[10,128,128]{2,1,0:T(8,128)(2,1)S(1)}, bf16[3,4,64,128]{3,2,1,0:T(8,128)(2,1)S(1)}) custom-call(bf16[2,16,128,128]{3,2,1,0:T(8,128)(2,1)} %source.2, bf16[2,4,64,128]{3,2,1,0:T(8,128)(2,1)} %observed.1, bf16[4,64,128]{2,1,0:T(8,128)(2,1)} %amplitude.1), custom_call_target="tpu_custom_call" | custom-call | flops 1000000 | bytes 10000 | tf_op jit(solution)/shard_map/first_waves/pallas_call | solution.py:26
  1.9 3.0 %collective-permute-start.5 = (bf16[10,128,128]{2,1,0:T(8,128)(2,1)S(1)}, bf16[10,128,128]{2,1,0:T(8,128)(2,1)S(1)}, u32[]{:S(2)}, u32[]{:S(2)}) collective-permute-start(bf16[10,128,128]{2,1,0:T(8,128)(2,1)S(1)} %get-tuple-element.55), channel_id=1, source_target_pairs={{0,2},{2,0},{1,3},{3,1},{4,6},{6,4},{5,7},{7,5},{8,10},{10,8},{9,1... | collective-permute-start | bytes 983048 | tf_op jit(solution)/shard_map/ppermute | solution.py:44
  5.0 2.7 %collective-permute-start.1 = (bf16[3,4,64,128]{3,2,1,0:T(8,128)(2,1)S(1)}, bf16[3,4,64,128]{3,2,1,0:T(8,128)(2,1)S(1)}, u32[]{:S(2)}, u32[]{:S(2)}) collective-permute-start(bf16[3,4,64,128]{3,2,1,0:T(8,128)(2,1)S(1)} %relay_data.1.refs_0_), channel_id=1, source_target_pairs={{0,8},{4,12},{8,0},{12,4},{1,9},{5,13},{9,1},{13,5},{2,10},{6,14},... | collective-permute-start | bytes 589832 | tf_op jit(solution)/shard_map/ppermute | solution.py:44
  7.6 0.4 other_waves.1
  8.1 0.5 collective-permute-start.3
  8.6 0.5 collective-permute-start
  9.2 2.2 %load_factors.1 = (bf16[16,8,40,512]{3,2,1,0:T(8,128)(2,1)S(1)}, bf16[2,4,16,40,512]{4,3,2,1,0:T(8,128)(2,1)S(1)}) custom-call(bf16[2,4,16,40,512]{4,3,2,1,0:T(8,128)(2,1)S(1)} %bitcast.15, bf16[2,4,16,40,512]{4,3,2,1,0:T(8,128)(2,1)S(1)} %bitcast.17), custom_call_target="tpu_custom_call" | custom-call | flops 10000000000 | bytes 10000 | tf_op jit(solution)/shard_map/load_factors/pallas_call | solution.py:26
  11.4 1.7 %near_products.1 = (f32[4,640,128]{2,1,0:T(8,128)S(1)}, f32[4,640,128]{2,1,0:T(8,128)S(1)}) custom-call(bf16[16,320,512]{2,1,0:T(8,128)(2,1)S(1)} %bitcast.2, bf16[16,128,128]{2,1,0:T(8,128)(2,1)S(1)} %get-tuple-element.62.refs_0_, bf16[16,128,128]{2,1,0:T(8,128)(2,1)S(1)} %collective-permute-done.3.refs_1_, ...), custom_call_target="tpu_custom_call" | custom-call | flops 1 | bytes 10000 | tf_op jit(solution)/shard_map/near_products/pallas_call | solution.py:26
  13.1 0.4 collective-permute-done.5.refs_0_
  13.4 2.1 %collective-permute-start.10 = (bf16[16,128,128]{2,1,0:T(8,128)(2,1)S(1)}, bf16[16,128,128]{2,1,0:T(8,128)(2,1)S(1)}, u32[]{:S(2)}, u32[]{:S(2)}) collective-permute-start(bf16[16,128,128]{2,1,0:T(8,128)(2,1)S(1)} %get-tuple-element.63.refs_2_), channel_id=1, source_target_pairs={{0,2},{2,0},{1,3},{3,1},{4,6},{6,4},{5,7},{7,5},{8,10},{10,8},{9,1... | collective-permute-start | bytes 1572872 | tf_op jit(solution)/shard_map/ppermute | solution.py:44
  15.5 1.3 %collective-permute-done.refs_0_ = bf16[6,128,128]{2,1,0:T(8,128)(2,1)S(1)} collective-permute-done((bf16[6,128,128]{2,1,0:T(8,128)(2,1)S(1)}, bf16[6,128,128]{2,1,0:T(8,128)(2,1)S(1)}, u32[]{:S(2)}, u32[]{:S(2)}) %collective-permute-start) | collective-permute-done | bytes 196640 | tf_op jit(solution)/shard_map/ppermute | solution.py:44
  16.9 1.2 %first_coefficients.1.refs_5_ = f32[4,400,128]{2,1,0:T(8,128)S(1)} custom-call(s32[4,16]{1,0:T(4,128)S(1)} %copy-done.1, bf16[10,128,128]{2,1,0:T(8,128)(2,1)S(1)} %collective-permute-done.5.refs_0_, bf16[10,128,128]{2,1,0:T(8,128)(2,1)S(1)} %collective-permute-done.6.refs_1_, bf16[16,320,512]{2,1,0:T(8,128)(2,1)S(1)} %bitcast.3, ...), custom_call_target="tpu_custom_call" | custom-call | flops 1 | bytes 10000 | tf_op jit(solution)/shard_map/first_coefficients/pallas_call | solution.py:26
  18.3 2.7 %forward_product.2 = (f32[4,4,64,128]{3,2,1,0:T(8,128)S(1)}, bf16[2,4,64,128]{3,2,1,0:T(8,128)(2,1)S(1)}, bf16[2,4,64,128]{3,2,1,0:T(8,128)(2,1)S(1)}) custom-call(s32[4,16]{1,0:T(4,128)S(1)} %copy-done.1, bf16[6,128,128]{2,1,0:T(8,128)(2,1)S(1)} %collective-permute-done.refs_0_, bf16[6,128,128]{2,1,0:T(8,128)(2,1)S(1)} %collective-permute-done.2.refs_1_, ...), custom_call_target="tpu_custom_call" | custom-call | flops 1 | bytes 10000 | tf_op jit(solution)/shard_map/forward_product/pallas_call | solution.py:26
  21.0 0.4 collective-permute-start.8
  21.6 0.8 %collective-permute-done.8.refs_0_ = bf16[2,4,64,128]{3,2,1,0:T(8,128)(2,1)S(1)} collective-permute-done((bf16[2,4,64,128]{3,2,1,0:T(8,128)(2,1)S(1)}, bf16[2,4,64,128]{3,2,1,0:T(8,128)(2,1)S(1)}, u32[]{:S(2)}, u32[]{:S(2)}) %collective-permute-start.8) | collective-permute-done | bytes 131104 | tf_op jit(solution)/shard_map/ppermute | solution.py:44
  22.5 1.9 %collective-permute-start.9 = (bf16[2,4,64,128]{3,2,1,0:T(8,128)(2,1)S(1)}, bf16[2,4,64,128]{3,2,1,0:T(8,128)(2,1)S(1)}, u32[]{:S(2)}, u32[]{:S(2)}) collective-permute-start(bf16[2,4,64,128]{3,2,1,0:T(8,128)(2,1)S(1)} %halve.2), channel_id=1, source_target_pairs={{0,4},{4,0},{8,12},{12,8},{1,5},{5,1},{9,13},{13,9},{2,6},{6,2},{1... | collective-permute-start | bytes 393224 | tf_op jit(solution)/shard_map/ppermute | solution.py:44
  24.3 4.0 %collective-permute-done.9.refs_1_ = bf16[2,4,64,128]{3,2,1,0:T(8,128)(2,1)S(1)} collective-permute-done((bf16[2,4,64,128]{3,2,1,0:T(8,128)(2,1)S(1)}, bf16[2,4,64,128]{3,2,1,0:T(8,128)(2,1)S(1)}, u32[]{:S(2)}, u32[]{:S(2)}) %collective-permute-start.9) | collective-permute-done | bytes 131104 | tf_op jit(solution)/shard_map/ppermute | solution.py:44
  28.5 2.8 %collective-permute-start.14 = (bf16[2,4,64,128]{3,2,1,0:T(8,128)(2,1)S(1)}, bf16[2,4,64,128]{3,2,1,0:T(8,128)(2,1)S(1)}, u32[]{:S(2)}, u32[]{:S(2)}) collective-permute-start(bf16[2,4,64,128]{3,2,1,0:T(8,128)(2,1)S(1)} %get-tuple-element.71), channel_id=1, source_target_pairs={{0,8},{4,12},{8,0},{12,4},{1,9},{5,13},{9,1},{13,5},{2,10},{6,14},... | collective-permute-start | bytes 393224 | tf_op jit(solution)/shard_map/ppermute | solution.py:44
  31.3 3.0 %forward_product.3 = (f32[4,4,64,128]{3,2,1,0:T(8,128)S(1)}, bf16[1,4,64,128]{3,2,1,0:T(8,128)(2,1)S(1)}, bf16[1,4,64,128]{3,2,1,0:T(8,128)(2,1)S(1)}, bf16[1,4,...) custom-call(s32[4,16]{1,0:T(4,128)S(1)} %copy-done.1, bf16[16,128,128]{2,1,0:T(8,128)(2,1)S(1)} %collective-permute-done.10.refs_0_, ...), custom_call_target="tpu_custom_call" | custom-call | flops 10000000000 | bytes 10000 | tf_op jit(solution)/shard_map/forward_product/pallas_call | solution.py:26
  34.9 0.7 collective-permute-done.12.refs_0_
  35.8 1.6 %collective-permute-start.17 = (bf16[2,4,64,128]{3,2,1,0:T(8,128)(2,1)S(1)}, bf16[2,4,64,128]{3,2,1,0:T(8,128)(2,1)S(1)}, u32[]{:S(2)}, u32[]{:S(2)}) collective-permute-start(bf16[2,4,64,128]{3,2,1,0:T(8,128)(2,1)S(1)} %halve.3), channel_id=1, source_target_pairs={{0,4},{4,0},{8,12},{12,8},{1,5},{5,1},{9,13},{13,9},{2,6},{6,2},{1... | collective-permute-start | bytes 393224 | tf_op jit(solution)/shard_map/ppermute | solution.py:44
  37.5 0.7 collective-permute-done.14.other
  38.3 0.8 %collective-permute-start.18 = (bf16[2,4,64,128]{3,2,1,0:T(8,128)(2,1)S(1)}, bf16[2,4,64,128]{3,2,1,0:T(8,128)(2,1)S(1)}, u32[]{:S(2)}, u32[]{:S(2)}) collective-permute-start(bf16[2,4,64,128]{3,2,1,0:T(8,128)(2,1)S(1)} %residual.2.refs_0_), channel_id=1, source_target_pairs={{0,4},{4,0},{8,12},{12,8},{1,5},{5,1},{9,13},{13,9},{2,6},{6,2},{1... | collective-permute-start | bytes 393224 | tf_op jit(solution)/shard_map/ppermute | solution.py:44
  39.2 0.5 collective-permute-start.16
  39.7 0.7 collective-permute-done.15.refs_0_
  40.6 1.6 %collective-permute-done.17.refs_2_ = bf16[2,4,64,128]{3,2,1,0:T(8,128)(2,1)S(1)} collective-permute-done((bf16[2,4,64,128]{3,2,1,0:T(8,128)(2,1)S(1)}, bf16[2,4,64,128]{3,2,1,0:T(8,128)(2,1)S(1)}, u32[]{:S(2)}, u32[]{:S(2)}) %collective-permute-start.17) | collective-permute-done | bytes 131104 | tf_op jit(solution)/shard_map/ppermute | solution.py:44
  42.3 1.8 %collective-permute-start.22 = (bf16[2,4,64,128]{3,2,1,0:T(8,128)(2,1)S(1)}, bf16[2,4,64,128]{3,2,1,0:T(8,128)(2,1)S(1)}, u32[]{:S(2)}, u32[]{:S(2)}) collective-permute-start(bf16[2,4,64,128]{3,2,1,0:T(8,128)(2,1)S(1)} %get-tuple-element.82), channel_id=1, source_target_pairs={{0,8},{4,12},{8,0},{12,4},{1,9},{5,13},{9,1},{13,5},{2,10},{6,14},... | collective-permute-start | bytes 393224 | tf_op jit(solution)/shard_map/ppermute | solution.py:44
  44.1 0.4 collective-permute-done.18.source.refs_1_
  44.5 0.5 collective-permute-start.21
  45.0 0.7 collective-permute-done.20.refs_3_
  45.9 2.7 %adjoint_product.2 = (bf16[16,160,128]{2,1,0:T(8,128)(2,1)S(1)}, f32[16,128,128]{2,1,0:T(8,128)S(1)}, bf16[8,128,128]{2,1,0:T(8,128)(2,1)S(1)}, bf16[8,128,128]{2,1,0:T(8,128)(2,1)S(1)}) custom-call(s32[4,16]{1,0:T(4,128)S(1)} %copy-done.1, bf16[2,4,64,128]{3,2,1,0:T(8,128)(2,1)S(1)} %residual.2.refs_0_, ...), custom_call_target="tpu_custom_call" | custom-call | flops 1 | bytes 10000 | tf_op jit(solution)/shard_map/adjoint_product/pallas_call | solution.py:26
  48.7 0.8 own_quarter.2
  49.5 0.4 collective-permute-start.24
  50.0 0.9 %collective-permute-done.22.other = bf16[2,4,64,128]{3,2,1,0:T(8,128)(2,1)S(1)} collective-permute-done((bf16[2,4,64,128]{3,2,1,0:T(8,128)(2,1)S(1)}, bf16[2,4,64,128]{3,2,1,0:T(8,128)(2,1)S(1)}, u32[]{:S(2)}, u32[]{:S(2)}) %collective-permute-start.22) | collective-permute-done | bytes 131104 | tf_op jit(solution)/shard_map/ppermute | solution.py:44
  51.1 0.8 %collective-permute-start.23 = (bf16[2,4,64,128]{3,2,1,0:T(8,128)(2,1)S(1)}, bf16[2,4,64,128]{3,2,1,0:T(8,128)(2,1)S(1)}, u32[]{:S(2)}, u32[]{:S(2)}) collective-permute-start(bf16[2,4,64,128]{3,2,1,0:T(8,128)(2,1)S(1)} %residual.3.refs_1_.refs_0_), channel_id=1, source_target_pairs={{0,4},{4,0},{8,12},{12,8},{1,5},{5,1},{9,13},{13,9},{2,6},{6,2},{1... | collective-permute-start | bytes 393224 | tf_op jit(solution)/shard_map/ppermute | solution.py:44
  51.9 1.6 %collective-permute-start.30 = (bf16[16,128,128]{2,1,0:T(8,128)(2,1)S(1)}, bf16[16,128,128]{2,1,0:T(8,128)(2,1)S(1)}, u32[]{:S(2)}, u32[]{:S(2)}) collective-permute-start(bf16[16,128,128]{2,1,0:T(8,128)(2,1)S(1)} %adjoint_share.2), channel_id=1, source_target_pairs={{0,2},{2,0},{1,3},{3,1},{4,6},{6,4},{5,7},{7,5},{8,10},{10,8},{9,1... | collective-permute-start | bytes 1572872 | tf_op jit(solution)/shard_map/ppermute | solution.py:44
  53.6 0.5 collective-permute-start.26
  54.1 2.0 %collective-permute-done.23.refs_1_ = bf16[2,4,64,128]{3,2,1,0:T(8,128)(2,1)S(1)} collective-permute-done((bf16[2,4,64,128]{3,2,1,0:T(8,128)(2,1)S(1)}, bf16[2,4,64,128]{3,2,1,0:T(8,128)(2,1)S(1)}, u32[]{:S(2)}, u32[]{:S(2)}) %collective-permute-start.23) | collective-permute-done | bytes 131104 | tf_op jit(solution)/shard_map/ppermute | solution.py:44
  56.1 0.8 join.1
  56.8 0.6 collective-permute-done.27.refs_3_
  57.4 3.0 %adjoint_product.3 = (bf16[16,160,128]{2,1,0:T(8,128)(2,1)S(1)}, f32[16,128,128]{2,1,0:T(8,128)S(1)}, bf16[8,128,128]{2,1,0:T(8,128)(2,1)S(1)}, bf16[8,128,128]{2,1,0:T(8,128)(2,1)S(1)}) custom-call(s32[4,16]{1,0:T(4,128)S(1)} %copy-done.1, bf16[2,4,64,128]{3,2,1,0:T(8,128)(2,1)S(1)} %residual.3.refs_1_.refs_0_, ...), custom_call_target="tpu_custom_call" | custom-call | flops 1 | bytes 10000 | tf_op jit(solution)/shard_map/adjoint_product/pallas_call | solution.py:26
  60.6 0.4 collective-permute-start.29
  61.0 0.8 own_quarter.3
  62.0 0.4 collective-permute-done.29.refs_1_
  62.5 1.6 %collective-permute-start.33 = (bf16[16,128,128]{2,1,0:T(8,128)(2,1)S(1)}, bf16[16,128,128]{2,1,0:T(8,128)(2,1)S(1)}, u32[]{:S(2)}, u32[]{:S(2)}) collective-permute-start(bf16[16,128,128]{2,1,0:T(8,128)(2,1)S(1)} %adjoint_share.3), channel_id=1, source_target_pairs={{0,2},{2,0},{1,3},{3,1},{4,6},{6,4},{5,7},{7,5},{8,10},{10,8},{9,1... | collective-permute-start | bytes 1572872 | tf_op jit(solution)/shard_map/ppermute | solution.py:44
  64.0 2.4 %collective-permute-done.30.refs_0_ = bf16[16,128,128]{2,1,0:T(8,128)(2,1)S(1)} collective-permute-done((bf16[16,128,128]{2,1,0:T(8,128)(2,1)S(1)}, bf16[16,128,128]{2,1,0:T(8,128)(2,1)S(1)}, u32[]{:S(2)}, u32[]{:S(2)}) %collective-permute-start.30) | collective-permute-done | bytes 524320 | tf_op jit(solution)/shard_map/ppermute | solution.py:44
  66.7 10.5 %collective-permute-done.33.refs_1_ = bf16[16,128,128]{2,1,0:T(8,128)(2,1)S(1)} collective-permute-done((bf16[16,128,128]{2,1,0:T(8,128)(2,1)S(1)}, bf16[16,128,128]{2,1,0:T(8,128)(2,1)S(1)}, u32[]{:S(2)}, u32[]{:S(2)}) %collective-permute-start.33) | collective-permute-done | bytes 524320 | tf_op jit(solution)/shard_map/ppermute | solution.py:44
  77.1 1.1 %adjoint_sum.1 = bf16[2,16,128,128]{3,2,1,0:T(8,128)(2,1)} custom-call(f32[16,128,128]{2,1,0:T(8,128)S(1)} %total.3.done, f32[16,128,128]{2,1,0:T(8,128)S(1)} %get-tuple-element.103.mine, bf16[16,128,128]{2,1,0:T(8,128)(2,1)S(1)} %collective-permute-done.32.refs_0_, bf16[16,128,128]{2,1,0:T(8,128)(2,1)S(1)} %collective-permute-done.33.refs_1_), custom_call_target="tpu_custom_call" | custom-call | flops 1000000 | bytes 10000 | tf_op jit(solution)/shard_map/adjoint_sum/pallas_call | solution.py:26
  (59 shorter events, 3.2 us)
Async XLA Ops:
  1.9 11.5 %collective-permute-start.5 = (bf16[10,128,128]{2,1,0:T(8,128)(2,1)S(1)}, bf16[10,128,128]{2,1,0:T(8,128)(2,1)S(1)}, u32[]{:S(2)}, u32[]{:S(2)}) collective-permute-start(bf16[10,128,128]{2,1,0:T(8,128)(2,1)S(1)} %get-tuple-element.55), channel_id=1, source_target_pairs={{0,2},{2,0},{1,3},{3,1},{4,6},{6,4},{5,7},{7,5},{8,10},{10,8},{9,1... | collective-permute-start | bytes 983048 | tf_op jit(solution)/shard_map/ppermute | solution.py:44
  4.9 2.7 %copy-start = (bf16[2,16,128,128]{3,2,1,0:T(8,128)(2,1)S(1)}, bf16[2,16,128,128]{3,2,1,0:T(8,128)(2,1)}, u32[]{:S(2)}) copy-start(bf16[2,16,128,128]{3,2,1,0:T(8,128)(2,1)} %source.2) | copy-start | bytes 3145732
  4.9 4.2 %slice-start = ((s8[5242880]{0:T(1024)(128)(4,1)}), s8[4194304]{0:T(1024)(128)(4,1)S(1)}, s32[]{:S(2)}) async-start(s8[5242880]{0:T(1024)(128)(4,1)} %bitcast.14), calls=%async_computation | async-start | bytes 8388608
  4.9 4.2 %slice-start.2 = ((s8[5242880]{0:T(1024)(128)(4,1)}), s8[4194304]{0:T(1024)(128)(4,1)S(1)}, s32[]{:S(2)}) async-start(s8[5242880]{0:T(1024)(128)(4,1)} %bitcast.16), calls=%async_computation.2 | async-start | bytes 8388608
  4.9 4.2 %slice-start.1 = ((s8[5242880]{0:T(1024)(128)(4,1)}), s8[1048576]{0:T(1024)(128)(4,1)S(1)}, s32[]{:S(2)}) async-start(s8[5242880]{0:T(1024)(128)(4,1)} %bitcast.14), calls=%async_computation.1 | async-start | bytes 2097152
  4.9 4.3 %slice-start.3 = ((s8[5242880]{0:T(1024)(128)(4,1)}), s8[1048576]{0:T(1024)(128)(4,1)S(1)}, s32[]{:S(2)}) async-start(s8[5242880]{0:T(1024)(128)(4,1)} %bitcast.16), calls=%async_computation.3 | async-start | bytes 2097152
  5.0 11.9 %collective-permute-start.1 = (bf16[3,4,64,128]{3,2,1,0:T(8,128)(2,1)S(1)}, bf16[3,4,64,128]{3,2,1,0:T(8,128)(2,1)S(1)}, u32[]{:S(2)}, u32[]{:S(2)}) collective-permute-start(bf16[3,4,64,128]{3,2,1,0:T(8,128)(2,1)S(1)} %relay_data.1.refs_0_), channel_id=1, source_target_pairs={{0,8},{4,12},{8,0},{12,4},{1,9},{5,13},{9,1},{13,5},{2,10},{6,14},... | collective-permute-start | bytes 589832 | tf_op jit(solution)/shard_map/ppermute | solution.py:44
  8.0 3.4 %collective-permute-start.4 = (bf16[16,128,128]{2,1,0:T(8,128)(2,1)S(1)}, bf16[16,128,128]{2,1,0:T(8,128)(2,1)S(1)}, u32[]{:S(2)}, u32[]{:S(2)}) collective-permute-start(bf16[16,128,128]{2,1,0:T(8,128)(2,1)S(1)} %get-tuple-element.63.refs_2_), channel_id=1, source_target_pairs={{0,1},{1,0},{2,3},{3,2},{4,5},{5,4},{6,7},{7,6},{8,9},{9,8},{10,11... | collective-permute-start | bytes 1572872 | tf_op jit(solution)/shard_map/ppermute | solution.py:44
  8.1 3.4 %collective-permute-start.3 = (bf16[16,128,128]{2,1,0:T(8,128)(2,1)S(1)}, bf16[16,128,128]{2,1,0:T(8,128)(2,1)S(1)}, u32[]{:S(2)}, u32[]{:S(2)}) collective-permute-start(bf16[16,128,128]{2,1,0:T(8,128)(2,1)S(1)} %get-tuple-element.62.refs_0_), channel_id=1, source_target_pairs={{0,1},{1,0},{2,3},{3,2},{4,5},{5,4},{6,7},{7,6},{8,9},{9,8},{10,11... | collective-permute-start | bytes 1572872 | tf_op jit(solution)/shard_map/ppermute | solution.py:44
  8.6 8.3 %collective-permute-start = (bf16[6,128,128]{2,1,0:T(8,128)(2,1)S(1)}, bf16[6,128,128]{2,1,0:T(8,128)(2,1)S(1)}, u32[]{:S(2)}, u32[]{:S(2)}) collective-permute-start(bf16[6,128,128]{2,1,0:T(8,128)(2,1)S(1)} %get-tuple-element.58), channel_id=1, source_target_pairs={{0,2},{2,0},{1,3},{3,1},{4,6},{6,4},{5,7},{7,5},{8,10},{10,8},{9,1... | collective-permute-start | bytes 589832 | tf_op jit(solution)/shard_map/ppermute | solution.py:44
  11.4 5.5 %copy-start.1 = (s32[4,16]{1,0:T(4,128)S(1)}, s32[4,16]{1,0:T(4,128)}, u32[]{:S(2)}) copy-start(s32[4,16]{1,0:T(4,128)} %ranks.9) | copy-start | bytes 772
  13.4 3.4 %collective-permute-start.6 = (bf16[10,128,128]{2,1,0:T(8,128)(2,1)S(1)}, bf16[10,128,128]{2,1,0:T(8,128)(2,1)S(1)}, u32[]{:S(2)}, u32[]{:S(2)}) collective-permute-start(bf16[10,128,128]{2,1,0:T(8,128)(2,1)S(1)} %collective-permute-done.5.refs_0_), channel_id=1, source_target_pairs={{0,1},{1,0},{2,3},{3,2},{4,5},{5,4},{6,7},{7,6},{8,9},{9,8},{10,11... | collective-permute-start | bytes 983048 | tf_op jit(solution)/shard_map/ppermute | solution.py:44
  13.4 14.9 %collective-permute-start.10 = (bf16[16,128,128]{2,1,0:T(8,128)(2,1)S(1)}, bf16[16,128,128]{2,1,0:T(8,128)(2,1)S(1)}, u32[]{:S(2)}, u32[]{:S(2)}) collective-permute-start(bf16[16,128,128]{2,1,0:T(8,128)(2,1)S(1)} %get-tuple-element.63.refs_2_), channel_id=1, source_target_pairs={{0,2},{2,0},{1,3},{3,1},{4,6},{6,4},{5,7},{7,5},{8,10},{10,8},{9,1... | collective-permute-start | bytes 1572872 | tf_op jit(solution)/shard_map/ppermute | solution.py:44
  16.8 1.4 %collective-permute-start.2 = (bf16[6,128,128]{2,1,0:T(8,128)(2,1)S(1)}, bf16[6,128,128]{2,1,0:T(8,128)(2,1)S(1)}, u32[]{:S(2)}, u32[]{:S(2)}) collective-permute-start(bf16[6,128,128]{2,1,0:T(8,128)(2,1)S(1)} %collective-permute-done.refs_0_), channel_id=1, source_target_pairs={{0,1},{1,0},{2,3},{3,2},{4,5},{5,4},{6,7},{7,6},{8,9},{9,8},{10,11... | collective-permute-start | bytes 589832 | tf_op jit(solution)/shard_map/ppermute | solution.py:44
  21.0 1.4 %collective-permute-start.8 = (bf16[2,4,64,128]{3,2,1,0:T(8,128)(2,1)S(1)}, bf16[2,4,64,128]{3,2,1,0:T(8,128)(2,1)S(1)}, u32[]{:S(2)}, u32[]{:S(2)}) collective-permute-start(bf16[2,4,64,128]{3,2,1,0:T(8,128)(2,1)S(1)} %get-tuple-element.69), channel_id=1, source_target_pairs={{0,1},{1,0},{2,3},{3,2},{4,5},{5,4},{6,7},{7,6},{8,9},{9,8},{10,11... | collective-permute-start | bytes 393224 | tf_op jit(solution)/shard_map/ppermute | solution.py:44
  21.4 2.9 %collective-permute-start.7 = (bf16[2,4,64,128]{3,2,1,0:T(8,128)(2,1)S(1)}, bf16[2,4,64,128]{3,2,1,0:T(8,128)(2,1)S(1)}, u32[]{:S(2)}, u32[]{:S(2)}) collective-permute-start(bf16[2,4,64,128]{3,2,1,0:T(8,128)(2,1)S(1)} %get-tuple-element.68), channel_id=1, source_target_pairs={{0,1},{1,0},{2,3},{3,2},{4,5},{5,4},{6,7},{7,6},{8,9},{9,8},{10,11... | collective-permute-start | bytes 393224 | tf_op jit(solution)/shard_map/ppermute | solution.py:44
  22.5 5.9 %collective-permute-start.9 = (bf16[2,4,64,128]{3,2,1,0:T(8,128)(2,1)S(1)}, bf16[2,4,64,128]{3,2,1,0:T(8,128)(2,1)S(1)}, u32[]{:S(2)}, u32[]{:S(2)}) collective-permute-start(bf16[2,4,64,128]{3,2,1,0:T(8,128)(2,1)S(1)} %halve.2), channel_id=1, source_target_pairs={{0,4},{4,0},{8,12},{12,8},{1,5},{5,1},{9,13},{13,9},{2,6},{6,2},{1... | collective-permute-start | bytes 393224 | tf_op jit(solution)/shard_map/ppermute | solution.py:44
  28.4 2.9 %collective-permute-start.11 = (bf16[16,128,128]{2,1,0:T(8,128)(2,1)S(1)}, bf16[16,128,128]{2,1,0:T(8,128)(2,1)S(1)}, u32[]{:S(2)}, u32[]{:S(2)}) collective-permute-start(bf16[16,128,128]{2,1,0:T(8,128)(2,1)S(1)} %collective-permute-done.10.refs_0_), channel_id=1, source_target_pairs={{0,1},{1,0},{2,3},{3,2},{4,5},{5,4},{6,7},{7,6},{8,9},{9,8},{10,11... | collective-permute-start | bytes 1572872 | tf_op jit(solution)/shard_map/ppermute | solution.py:44
  28.5 9.7 %collective-permute-start.14 = (bf16[2,4,64,128]{3,2,1,0:T(8,128)(2,1)S(1)}, bf16[2,4,64,128]{3,2,1,0:T(8,128)(2,1)S(1)}, u32[]{:S(2)}, u32[]{:S(2)}) collective-permute-start(bf16[2,4,64,128]{3,2,1,0:T(8,128)(2,1)S(1)} %get-tuple-element.71), channel_id=1, source_target_pairs={{0,8},{4,12},{8,0},{12,4},{1,9},{5,13},{9,1},{13,5},{2,10},{6,14},... | collective-permute-start | bytes 393224 | tf_op jit(solution)/shard_map/ppermute | solution.py:44
  34.3 1.3 %collective-permute-start.12 = (bf16[1,4,64,128]{3,2,1,0:T(8,128)(2,1)S(1)}, bf16[1,4,64,128]{3,2,1,0:T(8,128)(2,1)S(1)}, u32[]{:S(2)}, u32[]{:S(2)}) collective-permute-start(bf16[1,4,64,128]{3,2,1,0:T(8,128)(2,1)S(1)} %get-tuple-element.75), channel_id=1, source_target_pairs={{0,1},{1,0},{2,3},{3,2},{4,5},{5,4},{6,7},{7,6},{8,9},{9,8},{10,11... | collective-permute-start | bytes 196616 | tf_op jit(solution)/shard_map/ppermute | solution.py:44
  34.5 1.3 %collective-permute-start.13 = (bf16[1,4,64,128]{3,2,1,0:T(8,128)(2,1)S(1)}, bf16[1,4,64,128]{3,2,1,0:T(8,128)(2,1)S(1)}, u32[]{:S(2)}, u32[]{:S(2)}) collective-permute-start(bf16[1,4,64,128]{3,2,1,0:T(8,128)(2,1)S(1)} %get-tuple-element.76), channel_id=1, source_target_pairs={{0,1},{1,0},{2,3},{3,2},{4,5},{5,4},{6,7},{7,6},{8,9},{9,8},{10,11... | collective-permute-start | bytes 196616 | tf_op jit(solution)/shard_map/ppermute | solution.py:44
  35.8 6.4 %collective-permute-start.17 = (bf16[2,4,64,128]{3,2,1,0:T(8,128)(2,1)S(1)}, bf16[2,4,64,128]{3,2,1,0:T(8,128)(2,1)S(1)}, u32[]{:S(2)}, u32[]{:S(2)}) collective-permute-start(bf16[2,4,64,128]{3,2,1,0:T(8,128)(2,1)S(1)} %halve.3), channel_id=1, source_target_pairs={{0,4},{4,0},{8,12},{12,8},{1,5},{5,1},{9,13},{13,9},{2,6},{6,2},{1... | collective-permute-start | bytes 393224 | tf_op jit(solution)/shard_map/ppermute | solution.py:44
  38.3 6.1 %collective-permute-start.18 = (bf16[2,4,64,128]{3,2,1,0:T(8,128)(2,1)S(1)}, bf16[2,4,64,128]{3,2,1,0:T(8,128)(2,1)S(1)}, u32[]{:S(2)}, u32[]{:S(2)}) collective-permute-start(bf16[2,4,64,128]{3,2,1,0:T(8,128)(2,1)S(1)} %residual.2.refs_0_), channel_id=1, source_target_pairs={{0,4},{4,0},{8,12},{12,8},{1,5},{5,1},{9,13},{13,9},{2,6},{6,2},{1... | collective-permute-start | bytes 393224 | tf_op jit(solution)/shard_map/ppermute | solution.py:44
  39.2 1.3 %collective-permute-start.15 = (bf16[1,4,64,128]{3,2,1,0:T(8,128)(2,1)S(1)}, bf16[1,4,64,128]{3,2,1,0:T(8,128)(2,1)S(1)}, u32[]{:S(2)}, u32[]{:S(2)}) collective-permute-start(bf16[1,4,64,128]{3,2,1,0:T(8,128)(2,1)S(1)} %get-tuple-element.79), channel_id=1, source_target_pairs={{0,1},{1,0},{2,3},{3,2},{4,5},{5,4},{6,7},{7,6},{8,9},{9,8},{10,11... | collective-permute-start | bytes 196616 | tf_op jit(solution)/shard_map/ppermute | solution.py:44
  39.2 1.4 %collective-permute-start.16 = (bf16[1,4,64,128]{3,2,1,0:T(8,128)(2,1)S(1)}, bf16[1,4,64,128]{3,2,1,0:T(8,128)(2,1)S(1)}, u32[]{:S(2)}, u32[]{:S(2)}) collective-permute-start(bf16[1,4,64,128]{3,2,1,0:T(8,128)(2,1)S(1)} %get-tuple-element.80), channel_id=1, source_target_pairs={{0,1},{1,0},{2,3},{3,2},{4,5},{5,4},{6,7},{7,6},{8,9},{9,8},{10,11... | collective-permute-start | bytes 196616 | tf_op jit(solution)/shard_map/ppermute | solution.py:44
  39.7 5.4 %collective-permute-start.19 = (bf16[2,4,64,128]{3,2,1,0:T(8,128)(2,1)S(1)}, bf16[2,4,64,128]{3,2,1,0:T(8,128)(2,1)S(1)}, u32[]{:S(2)}, u32[]{:S(2)}) collective-permute-start(bf16[2,4,64,128]{3,2,1,0:T(8,128)(2,1)S(1)} %residual.2.refs_0_), channel_id=1, source_target_pairs={{0,1},{1,0},{2,3},{3,2},{4,5},{5,4},{6,7},{7,6},{8,9},{9,8},{10,11... | collective-permute-start | bytes 393224 | tf_op jit(solution)/shard_map/ppermute | solution.py:44
  42.3 8.6 %collective-permute-start.22 = (bf16[2,4,64,128]{3,2,1,0:T(8,128)(2,1)S(1)}, bf16[2,4,64,128]{3,2,1,0:T(8,128)(2,1)S(1)}, u32[]{:S(2)}, u32[]{:S(2)}) collective-permute-start(bf16[2,4,64,128]{3,2,1,0:T(8,128)(2,1)S(1)} %get-tuple-element.82), channel_id=1, source_target_pairs={{0,8},{4,12},{8,0},{12,4},{1,9},{5,13},{9,1},{13,5},{2,10},{6,14},... | collective-permute-start | bytes 393224 | tf_op jit(solution)/shard_map/ppermute | solution.py:44
  44.5 1.3 %collective-permute-start.20 = (bf16[1,4,64,128]{3,2,1,0:T(8,128)(2,1)S(1)}, bf16[1,4,64,128]{3,2,1,0:T(8,128)(2,1)S(1)}, u32[]{:S(2)}, u32[]{:S(2)}) collective-permute-start(bf16[1,4,64,128]{3,2,1,0:T(8,128)(2,1)S(1)} %get-tuple-element.85), channel_id=1, source_target_pairs={{0,1},{1,0},{2,3},{3,2},{4,5},{5,4},{6,7},{7,6},{8,9},{9,8},{10,11... | collective-permute-start | bytes 196616 | tf_op jit(solution)/shard_map/ppermute | solution.py:44
  44.5 1.4 %collective-permute-start.21 = (bf16[1,4,64,128]{3,2,1,0:T(8,128)(2,1)S(1)}, bf16[1,4,64,128]{3,2,1,0:T(8,128)(2,1)S(1)}, u32[]{:S(2)}, u32[]{:S(2)}) collective-permute-start(bf16[1,4,64,128]{3,2,1,0:T(8,128)(2,1)S(1)} %get-tuple-element.86), channel_id=1, source_target_pairs={{0,1},{1,0},{2,3},{3,2},{4,5},{5,4},{6,7},{7,6},{8,9},{9,8},{10,11... | collective-permute-start | bytes 196616 | tf_op jit(solution)/shard_map/ppermute | solution.py:44
  49.5 2.4 %collective-permute-start.24 = (bf16[8,128,128]{2,1,0:T(8,128)(2,1)S(1)}, bf16[8,128,128]{2,1,0:T(8,128)(2,1)S(1)}, u32[]{:S(2)}, u32[]{:S(2)}) collective-permute-start(bf16[8,128,128]{2,1,0:T(8,128)(2,1)S(1)} %get-tuple-element.94), channel_id=1, source_target_pairs={{0,1},{1,0},{2,3},{3,2},{4,5},{5,4},{6,7},{7,6},{8,9},{9,8},{10,11... | collective-permute-start | bytes 786440 | tf_op jit(solution)/shard_map/ppermute | solution.py:44
  49.9 2.0 %collective-permute-start.25 = (bf16[8,128,128]{2,1,0:T(8,128)(2,1)S(1)}, bf16[8,128,128]{2,1,0:T(8,128)(2,1)S(1)}, u32[]{:S(2)}, u32[]{:S(2)}) collective-permute-start(bf16[8,128,128]{2,1,0:T(8,128)(2,1)S(1)} %get-tuple-element.95), channel_id=1, source_target_pairs={{0,1},{1,0},{2,3},{3,2},{4,5},{5,4},{6,7},{7,6},{8,9},{9,8},{10,11... | collective-permute-start | bytes 786440 | tf_op jit(solution)/shard_map/ppermute | solution.py:44
  51.1 5.0 %collective-permute-start.23 = (bf16[2,4,64,128]{3,2,1,0:T(8,128)(2,1)S(1)}, bf16[2,4,64,128]{3,2,1,0:T(8,128)(2,1)S(1)}, u32[]{:S(2)}, u32[]{:S(2)}) collective-permute-start(bf16[2,4,64,128]{3,2,1,0:T(8,128)(2,1)S(1)} %residual.3.refs_1_.refs_0_), channel_id=1, source_target_pairs={{0,4},{4,0},{8,12},{12,8},{1,5},{5,1},{9,13},{13,9},{2,6},{6,2},{1... | collective-permute-start | bytes 393224 | tf_op jit(solution)/shard_map/ppermute | solution.py:44
  51.9 14.5 %collective-permute-start.30 = (bf16[16,128,128]{2,1,0:T(8,128)(2,1)S(1)}, bf16[16,128,128]{2,1,0:T(8,128)(2,1)S(1)}, u32[]{:S(2)}, u32[]{:S(2)}) collective-permute-start(bf16[16,128,128]{2,1,0:T(8,128)(2,1)S(1)} %adjoint_share.2), channel_id=1, source_target_pairs={{0,2},{2,0},{1,3},{3,1},{4,6},{6,4},{5,7},{7,5},{8,10},{10,8},{9,1... | collective-permute-start | bytes 1572872 | tf_op jit(solution)/shard_map/ppermute | solution.py:44
  53.6 13.0 %collective-permute-start.31 = (bf16[16,128,128]{2,1,0:T(8,128)(2,1)S(1)}, bf16[16,128,128]{2,1,0:T(8,128)(2,1)S(1)}, u32[]{:S(2)}, u32[]{:S(2)}) collective-permute-start(bf16[16,128,128]{2,1,0:T(8,128)(2,1)S(1)} %get-tuple-element.101), channel_id=1, source_target_pairs={{0,1},{1,0},{2,3},{3,2},{4,5},{5,4},{6,7},{7,6},{8,9},{9,8},{10,11... | collective-permute-start | bytes 1572872 | tf_op jit(solution)/shard_map/ppermute | solution.py:44
  53.6 3.3 %collective-permute-start.26 = (bf16[2,4,64,128]{3,2,1,0:T(8,128)(2,1)S(1)}, bf16[2,4,64,128]{3,2,1,0:T(8,128)(2,1)S(1)}, u32[]{:S(2)}, u32[]{:S(2)}) collective-permute-start(bf16[2,4,64,128]{3,2,1,0:T(8,128)(2,1)S(1)} %residual.3.refs_1_.refs_0_), channel_id=1, source_target_pairs={{0,1},{1,0},{2,3},{3,2},{4,5},{5,4},{6,7},{7,6},{8,9},{9,8},{10,11... | collective-permute-start | bytes 393224 | tf_op jit(solution)/shard_map/ppermute | solution.py:44
  56.1 1.3 %collective-permute-start.27 = (bf16[2,4,64,128]{3,2,1,0:T(8,128)(2,1)S(1)}, bf16[2,4,64,128]{3,2,1,0:T(8,128)(2,1)S(1)}, u32[]{:S(2)}, u32[]{:S(2)}) collective-permute-start(bf16[2,4,64,128]{3,2,1,0:T(8,128)(2,1)S(1)} %collective-permute-done.23.refs_1_), channel_id=1, source_target_pairs={{0,1},{1,0},{2,3},{3,2},{4,5},{5,4},{6,7},{7,6},{8,9},{9,8},{10,11... | collective-permute-start | bytes 393224 | tf_op jit(solution)/shard_map/ppermute | solution.py:44
  60.4 1.6 %collective-permute-start.28 = (bf16[8,128,128]{2,1,0:T(8,128)(2,1)S(1)}, bf16[8,128,128]{2,1,0:T(8,128)(2,1)S(1)}, u32[]{:S(2)}, u32[]{:S(2)}) collective-permute-start(bf16[8,128,128]{2,1,0:T(8,128)(2,1)S(1)} %get-tuple-element.98), channel_id=1, source_target_pairs={{0,1},{1,0},{2,3},{3,2},{4,5},{5,4},{6,7},{7,6},{8,9},{9,8},{10,11... | collective-permute-start | bytes 786440 | tf_op jit(solution)/shard_map/ppermute | solution.py:44
  60.6 1.8 %collective-permute-start.29 = (bf16[8,128,128]{2,1,0:T(8,128)(2,1)S(1)}, bf16[8,128,128]{2,1,0:T(8,128)(2,1)S(1)}, u32[]{:S(2)}, u32[]{:S(2)}) collective-permute-start(bf16[8,128,128]{2,1,0:T(8,128)(2,1)S(1)} %get-tuple-element.99), channel_id=1, source_target_pairs={{0,1},{1,0},{2,3},{3,2},{4,5},{5,4},{6,7},{7,6},{8,9},{9,8},{10,11... | collective-permute-start | bytes 786440 | tf_op jit(solution)/shard_map/ppermute | solution.py:44
  62.5 14.7 %collective-permute-start.33 = (bf16[16,128,128]{2,1,0:T(8,128)(2,1)S(1)}, bf16[16,128,128]{2,1,0:T(8,128)(2,1)S(1)}, u32[]{:S(2)}, u32[]{:S(2)}) collective-permute-start(bf16[16,128,128]{2,1,0:T(8,128)(2,1)S(1)} %adjoint_share.3), channel_id=1, source_target_pairs={{0,2},{2,0},{1,3},{3,1},{4,6},{6,4},{5,7},{7,5},{8,10},{10,8},{9,1... | collective-permute-start | bytes 1572872 | tf_op jit(solution)/shard_map/ppermute | solution.py:44
  64.0 2.6 %collective-permute-start.32 = (bf16[16,128,128]{2,1,0:T(8,128)(2,1)S(1)}, bf16[16,128,128]{2,1,0:T(8,128)(2,1)S(1)}, u32[]{:S(2)}, u32[]{:S(2)}) collective-permute-start(bf16[16,128,128]{2,1,0:T(8,128)(2,1)S(1)} %get-tuple-element.105), channel_id=1, source_target_pairs={{0,1},{1,0},{2,3},{3,2},{4,5},{5,4},{6,7},{7,6},{8,9},{9,8},{10,11... | collective-permute-start | bytes 1572872 | tf_op jit(solution)/shard_map/ppermute | solution.py:44
